TPU v7x, 32 devices: a whole 2x2x4 slice. The times are simulated.
32 devices in a mesh: len: 4 (over y, x), energy: 4 (over z), mom: 2 (over core).
Axes of the slice: x: 2, y: 2, z: 4, core: 2. Of those that a mesh axis runs over, the one named last changes fastest.
Arguments:
- hamiltonian: float32 [2, 4, 2, 128, 128], P('mom', 'len'), may hold values from -0.5 to 0.5
- sigma_prev: float32 [2, 4, 16, 2, 128, 128], P('mom', 'len', 'energy'), may hold values from -0.25 to 0.25
- coupling: float32 [4, 128, 128], P('len'), may hold values from -1.5 to 1.5
- coupling_pattern: int32 [128, 128], replicated, may hold values 0 or 1
- phonon_shift: int32 [4], replicated, may hold values from 1 to 8
- phonon_weight: float32 [4], replicated, may hold values from 0.5 to 2
Outputs:
- sigma_retarded: float32 [2, 4, 16, 2, 128, 128], P('mom', 'len', 'energy')
- sigma_lesser: float32 [2, 4, 16, 2, 128, 128], P('mom', 'len', 'energy')
All inputs are finite; a program needn't handle non-finite values.
Results may differ from a plain program's by a relative error of at most 0.0001.
Values sent between devices are 32-bit elements; how exact they have to be, the bound alone decides.
No kernel may reach another device: no remote copies, remote signals or barrier semaphores. Data moves between devices by JAX's collectives and lax.ppermute only.
A program may use at most 128 MiB of HBM per device.

v0:
```python
import functools

import jax
import jax.numpy as jnp
from jax import lax
from jax.experimental import pallas as pl
from jax.experimental.pallas import tpu as pltpu
from jax.sharding import PartitionSpec as P

F32 = jnp.float32
BF16 = jnp.bfloat16
VMEM_LIMIT = 16 * 1024 * 1024


def split(x):
    high = x.astype(BF16)
    return high, (x - high.astype(F32)).astype(BF16)


def dot(a, b):
    return jnp.dot(a, b, preferred_element_type=F32)


def dot3(a, b):
    rows = a[0].shape[0]
    both = dot(jnp.concatenate([a[0], a[1]], axis=0), b[0])
    return both[:rows] + (both[rows:] + dot(a[0], b[1]))


def right_form(m):
    n = m.shape[0]
    re, im = m[:, :n], m[:, n:]
    return jnp.concatenate([m, jnp.concatenate([-im, re], axis=1)], axis=0)


def right_pair(m):
    high, low = split(m)
    return right_form(high), right_form(low)


def identity(n):
    rows = lax.broadcasted_iota(jnp.int32, (n, 2 * n), 0)
    cols = lax.broadcasted_iota(jnp.int32, (n, 2 * n), 1)
    return (rows == cols).astype(F32)


def inverse_kernel(total, ham_ref, sig_ref, out_ref):
    local_e, _, n, _ = sig_ref.shape
    start = lax.axis_index("energy") * local_e
    eye = identity(n)
    for e in range(local_e):
        pos = jnp.full((1, n), start + e, jnp.int32).astype(F32)
        zre = 5.0 + 2.0 * pos / total
        mag = zre * zre + 1.0
        qre = zre / mag
        qim = -1.0 / mag
        sre = ham_ref[0] + sig_ref[e, 0]
        sim = ham_ref[1] + sig_ref[e, 1]
        a1 = jnp.concatenate([qre * sre - qim * sim, qre * sim + qim * sre], axis=1)
        a1_pair = split(a1)
        a1_right = (right_form(a1_pair[0]), right_form(a1_pair[1]))
        a2 = dot3(a1_pair, a1_right)
        a2_pair = split(a2)
        a2_right = (right_form(a2_pair[0]), right_form(a2_pair[1]))
        a3 = dot3(a1_pair, a2_right)
        a4 = dot3(a2_pair, a2_right)
        p = eye + (a1 + (a2 + a3))
        x = p + dot3(split(p), right_pair(a4))
        re, im = x[:, :n], x[:, n:]
        out_ref[e, 0] = qre * re - qim * im
        out_ref[e, 1] = qre * im + qim * re


def chain_kernel(g_ref, coupling_ref, pattern_ref, out_ref):
    layers, per, _, n, _ = g_ref.shape
    mask = pattern_ref[...].astype(F32)
    bonds = [None] + [coupling_ref[l] * mask for l in range(1, layers)]
    bonds_t = [None] + [b.T for b in bonds[1:]]
    for p in range(per):
        g = [jnp.concatenate([g_ref[l, p, 0], g_ref[l, p, 1]], axis=1) for l in range(layers)]
        down = [None] * layers
        up = [None] * layers
        for l in range(layers):
            high, low = split(g[l])
            tall = (
                jnp.concatenate([high[:, :n], high[:, n:]], axis=0),
                jnp.concatenate([low[:, :n], low[:, n:]], axis=0),
            )
            wide = (high, low)
            if l > 0:
                u = dot3(tall, split(bonds[l]))
                v = dot3(split(bonds_t[l]), wide)
                down[l] = (split(jnp.concatenate([u[:n], u[n:]], axis=1)), right_pair(v))
            if l + 1 < layers:
                u = dot3(tall, split(bonds_t[l + 1]))
                v = dot3(split(bonds[l + 1]), wide)
                up[l] = (split(jnp.concatenate([u[:n], u[n:]], axis=1)), right_pair(v))
        green = list(g)
        gleft = g[0]
        gright = g[layers - 1]
        for step in range(1, layers):
            l = step
            u, v = down[l]
            term = dot3(split(dot3(u, right_pair(gleft))), v)
            green[l] = green[l] + term
            gleft = g[l] + term
            l = layers - 1 - step
            u, v = up[l]
            term = dot3(split(dot3(u, right_pair(gright))), v)
            green[l] = green[l] + term
            gright = g[l] + term
        for l in range(layers):
            near = [green[m] for m in (l - 1, l + 1) if 0 <= m < layers]
            y = green[l] + 0.5 * sum(near[1:], near[0]) if near else green[l]
            out_ref[l, p, 0] = y[:, :n]
            out_ref[l, p, 1] = y[:, n:]


def occupation(pos, total, n):
    return 1.0 / (1.0 + jnp.exp(8.0 * jnp.full((1, n), pos, jnp.int32).astype(F32) / total - 4.0))


def mix_kernel(total, distances, first, last, shift_ref, weight_ref, *refs):
    count = len(distances)
    own, other = refs[:count], refs[count : 2 * count]
    ret_in, les_in = (None, None) if first else refs[2 * count : 2 * count + 2]
    ret_ref, les_ref = refs[-2:]
    local_e, _, n, _ = own[0].shape
    phonons = shift_ref.shape[0]
    start = lax.axis_index("energy") * local_e
    shifts = [shift_ref[m] for m in range(phonons)]
    weights = [weight_ref[m] for m in range(phonons)]

    def coefficient(t):
        value = 0.0
        for s, w in zip(shifts, weights):
            value = value + jnp.where(s == t, w, 0.0)
        return value

    most = total // 2
    coefficients = {}
    for d in distances:
        for t in range(d * local_e - local_e + 1, d * local_e + local_e):
            if 1 <= t <= most and t not in coefficients:
                coefficients[t] = coefficient(t)
    occ_own = {}
    occ_other = {}
    for d in distances:
        for b in range(local_e):
            occ_own[d, b] = occupation(start - d * local_e + b, total, n)
            occ_other[d, b] = occupation(start + d * local_e + b, total, n)
    for a in range(local_e):
        ret = [jnp.zeros((n, n), F32) if first else ret_in[a, c] for c in range(2)]
        les = [jnp.zeros((n, n), F32) if first else les_in[a, c] for c in range(2)]
        for i, d in enumerate(distances):
            for b in range(local_e):
                for source, t, occ, factor in (
                    (own[i], d * local_e + a - b, occ_own[d, b], 1.0),
                    (other[i], d * local_e + b - a, occ_other[d, b], 0.5),
                ):
                    if not 1 <= t <= most:
                        continue
                    w = coefficients[t] * factor
                    for c in range(2):
                        value = w * source[b, c]
                        ret[c] = ret[c] + value
                        les[c] = les[c] + occ * value
        if last:
            les = [les[0] - les[0].T, les[1] + les[1].T]
        for c in range(2):
            ret_ref[a, c] = ret[c]
            les_ref[a, c] = les[c]


def whole(count):
    return [pl.BlockSpec(memory_space=pltpu.VMEM)] * count


def params():
    return pltpu.CompilerParams(vmem_limit_bytes=VMEM_LIMIT)


def shards(hamiltonian, sigma_prev, coupling, coupling_pattern, phonon_shift, phonon_weight):
    local_e, _, n, _ = sigma_prev.shape[2:]
    layers = lax.axis_size("len")
    count = lax.axis_size("energy")
    moms = lax.axis_size("mom")
    total = local_e * count
    per = local_e // layers
    block = (local_e, 2, n, n)

    couplings = lax.all_gather(coupling[0], "len", axis=0)
    g = pl.pallas_call(
        functools.partial(inverse_kernel, total),
        out_shape=jax.ShapeDtypeStruct(block, F32),
        in_specs=whole(2),
        out_specs=pl.BlockSpec(memory_space=pltpu.VMEM),
        compiler_params=params(),
        name="inverse",
    )(hamiltonian[0, 0], sigma_prev[0, 0])
    g = lax.all_to_all(g, "len", split_axis=0, concat_axis=0, tiled=True)
    y = pl.pallas_call(
        chain_kernel,
        out_shape=jax.ShapeDtypeStruct((layers, per, 2, n, n), F32),
        in_specs=whole(3),
        out_specs=pl.BlockSpec(memory_space=pltpu.VMEM),
        compiler_params=params(),
        name="chains",
    )(g.reshape(layers, per, 2, n, n), couplings, coupling_pattern)
    y = lax.all_to_all(y.reshape(block), "len", split_axis=0, concat_axis=0, tiled=True)

    reach = -(-(total // 2) // local_e)
    both = ("energy", "mom")
    up_pairs = [(z, z + 1) for z in range(count - 1)]
    down_pairs = [(z + 1, z) for z in range(count - 1)]
    cross = [
        ((z + 1) * moms + k, z * moms + (moms - 1 - k)) for z in range(count - 1) for k in range(moms)
    ]
    own = [y]
    other = []
    for d in range(1, reach + 1):
        own.append(lax.ppermute(own[-1], "energy", up_pairs))
        if d == 1:
            other.append(lax.ppermute(y, both, cross))
        else:
            other.append(lax.ppermute(other[-1], "energy", down_pairs))
    other.insert(0, lax.ppermute(y, "mom", [(k, moms - 1 - k) for k in range(moms)]))

    groups = [(0, 1)] + [
        tuple(range(d, min(d + 4, reach + 1))) for d in range(2, reach + 1, 4)
    ]
    smem = pl.BlockSpec(memory_space=pltpu.SMEM)
    sums = []
    for i, group in enumerate(groups):
        blocks = [own[d] for d in group] + [other[d] for d in group] + list(sums)
        sums = pl.pallas_call(
            functools.partial(mix_kernel, total, group, i == 0, i == len(groups) - 1),
            out_shape=[jax.ShapeDtypeStruct(block, F32)] * 2,
            in_specs=[smem, smem] + whole(len(blocks)),
            out_specs=whole(2),
            compiler_params=params(),
            name="mix",
        )(phonon_shift, phonon_weight, *blocks)
    retarded, lesser = sums
    return (retarded[None, None], lesser[None, None])


def solution(mesh):
    in_specs = (
        P("mom", "len", None, None, None),
        P("mom", "len", "energy", None, None, None),
        P("len", None, None),
        P(),
        P(),
        P(),
    )
    out_specs = (
        P("mom", "len", "energy", None, None, None),
        P("mom", "len", "energy", None, None, None),
    )
    return jax.shard_map(shards, mesh=mesh, in_specs=in_specs, out_specs=out_specs, check_vma=False)
```

profile of v0, /device:TPU:0, one launch (start us, length us, event | category | flops | bytes accessed | tf_op | source)
XLA Modules:
  0.0 71.9 jit_solution(14474332012555042904)
XLA Ops:
  0.6 0.0 copy-start
  0.6 1.0 %copy-done = f32[1,1,4,2,128,128]{5,4,3,2,1,0:T(8,128)S(1)} copy-done((f32[1,1,4,2,128,128]{5,4,3,2,1,0:T(8,128)S(1)}, f32[1,1,4,2,128,128]{5,4,3,2,1,0:T(8,128)}, u32[]{:S(2)}) %copy-start) | copy-done | bytes 524312
  1.7 0.0 copy-start.1
  1.7 0.9 %copy-done.1 = f32[1,1,2,128,128]{4,3,2,1,0:T(8,128)S(1)} copy-done((f32[1,1,2,128,128]{4,3,2,1,0:T(8,128)S(1)}, f32[1,1,2,128,128]{4,3,2,1,0:T(8,128)}, u32[]{:S(2)}) %copy-start.1) | copy-done | bytes 131096
  2.6 2.6 %inverse.1 = f32[4,2,128,128]{3,2,1,0:T(8,128)} custom-call(f32[2,128,128]{2,1,0:T(8,128)S(1)} %bitcast.9, f32[4,2,128,128]{3,2,1,0:T(8,128)S(1)} %bitcast.8), custom_call_target="tpu_custom_call" | custom-call | tf_op jit(solution)/shard_map/inverse/pallas_call | solution.py:193
  5.2 0.0 copy-start.5
  5.2 5.3 %all-to-all-start = ((f32[4,2,128,128]{3,2,1,0:T(8,128)}), f32[4,2,128,128]{3,2,1,0:T(8,128)S(1)}, u32[]{:S(2)}, u32[]{:S(2)}) async-start(f32[4,2,128,128]{3,2,1,0:T(8,128)} %inverse.1), calls=%async_computation | async-start | bytes 1048576 | tf_op jit(solution)/shard_map/all_to_all | solution.py:201
  10.5 0.0 copy-done.5
  10.5 0.0 copy-start.2
  10.5 12.4 %all_gather.3.coupling_ref = f32[4,128,128]{2,1,0:T(8,128)S(1)} all-gather(f32[1,128,128]{2,1,0:T(8,128)S(1)} %copy-done.5), channel_id=1, replica_groups=mesh['len'=4,'energy'=4,'mom'=2] {'len'}, dimensions={0}, use_global_device_ids=true | all-gather | bytes 327680 | tf_op jit(solution)/shard_map/all_gather | solution.py:192
  22.9 0.0 all-to-all-done
  22.9 0.0 copy-done.2
  22.9 2.1 %chains.1 = f32[4,1,2,128,128]{4,3,2,1,0:T(8,128)S(1)} custom-call(f32[4,1,2,128,128]{4,3,2,1,0:T(8,128)S(1)} %bitcast.6, f32[4,128,128]{2,1,0:T(8,128)S(1)} %all_gather.3.coupling_ref, s32[128,128]{1,0:T(8,128)S(1)} %copy-done.2), custom_call_target="tpu_custom_call" | custom-call | tf_op jit(solution)/shard_map/chains/pallas_call | solution.py:202
  25.0 0.0 copy-start.3
  25.0 0.0 copy-start.4
  25.0 9.7 %all_to_all.10.refs_0_ = f32[4,2,128,128]{3,2,1,0:T(8,128)S(1)} all-to-all(f32[4,2,128,128]{3,2,1,0:T(8,128)S(1)} %bitcast.7), channel_id=1, replica_groups=mesh['len'=4,'energy'=4,'mom'=2] {'len'}, dimensions={0} | all-to-all | bytes 1048576 | tf_op jit(solution)/shard_map/all_to_all | solution.py:210
  34.7 3.5 %collective-permute-start = (f32[4,2,128,128]{3,2,1,0:T(8,128)S(1)}, f32[4,2,128,128]{3,2,1,0:T(8,128)S(1)}, u32[]{:S(2)}, u32[]{:S(2)}) collective-permute-start(f32[4,2,128,128]{3,2,1,0:T(8,128)S(1)} %all_to_all.10.refs_0_), channel_id=1, source_target_pairs={{0,2},{2,4},{4,6},{1,3},{3,5},{5,7},{8,10},{10,12},{12,14},{9,11},... | collective-permute-start | bytes 1572872 | tf_op jit(solution)/shard_map/ppermute | solution.py:222
  38.2 1.3 %collective-permute-start.2 = (f32[4,2,128,128]{3,2,1,0:T(8,128)S(1)}, f32[4,2,128,128]{3,2,1,0:T(8,128)S(1)}, u32[]{:S(2)}, u32[]{:S(2)}) collective-permute-start(f32[4,2,128,128]{3,2,1,0:T(8,128)S(1)} %all_to_all.10.refs_0_), channel_id=1, source_target_pairs={{2,1},{3,0},{4,3},{5,2},{6,5},{7,4},{10,9},{11,8},{12,11},{13,10},... | collective-permute-start | bytes 1572872 | tf_op jit(solution)/shard_map/ppermute | solution.py:224
  39.5 0.1 collective-permute-start.4
  39.6 6.5 %collective-permute-done.refs_1_ = f32[4,2,128,128]{3,2,1,0:T(8,128)S(1)} collective-permute-done((f32[4,2,128,128]{3,2,1,0:T(8,128)S(1)}, f32[4,2,128,128]{3,2,1,0:T(8,128)S(1)}, u32[]{:S(2)}, u32[]{:S(2)}) %collective-permute-start) | collective-permute-done | bytes 524320 | tf_op jit(solution)/shard_map/ppermute | solution.py:222
  46.0 4.4 %collective-permute-start.1 = (f32[4,2,128,128]{3,2,1,0:T(8,128)S(1)}, f32[4,2,128,128]{3,2,1,0:T(8,128)S(1)}, u32[]{:S(2)}, u32[]{:S(2)}) collective-permute-start(f32[4,2,128,128]{3,2,1,0:T(8,128)S(1)} %collective-permute-done.refs_1_), channel_id=1, source_target_pairs={{0,2},{2,4},{4,6},{1,3},{3,5},{5,7},{8,10},{10,12},{12,14},{9,11},... | collective-permute-start | bytes 1572872 | tf_op jit(solution)/shard_map/ppermute | solution.py:222
  50.5 3.7 %collective-permute-done.2.refs_3_ = f32[4,2,128,128]{3,2,1,0:T(8,128)S(1)} collective-permute-done((f32[4,2,128,128]{3,2,1,0:T(8,128)S(1)}, f32[4,2,128,128]{3,2,1,0:T(8,128)S(1)}, u32[]{:S(2)}, u32[]{:S(2)}) %collective-permute-start.2) | collective-permute-done | bytes 524320 | tf_op jit(solution)/shard_map/ppermute | solution.py:224
  54.2 1.3 %collective-permute-start.3 = (f32[4,2,128,128]{3,2,1,0:T(8,128)S(1)}, f32[4,2,128,128]{3,2,1,0:T(8,128)S(1)}, u32[]{:S(2)}, u32[]{:S(2)}) collective-permute-start(f32[4,2,128,128]{3,2,1,0:T(8,128)S(1)} %collective-permute-done.2.refs_3_), channel_id=1, source_target_pairs={{2,0},{4,2},{6,4},{3,1},{5,3},{7,5},{10,8},{12,10},{14,12},{11,9},... | collective-permute-start | bytes 1572872 | tf_op jit(solution)/shard_map/ppermute | solution.py:226
  55.5 0.0 collective-permute-done.4.refs_2_
  55.5 0.0 copy-done.3
  55.5 0.0 copy-done.4
  55.5 1.4 %mix.2 = (f32[4,2,128,128]{3,2,1,0:T(8,128)S(1)}, f32[4,2,128,128]{3,2,1,0:T(8,128)S(1)}) custom-call(s32[4]{0:T(128)S(1)} %copy-done.3, f32[4]{0:T(128)S(1)} %copy-done.4, f32[4,2,128,128]{3,2,1,0:T(8,128)S(1)} %all_to_all.10.refs_0_, f32[4,2,128,128]{3,2,1,0:T(8,128)S(1)} %collective-permute-done.refs_1_, ...), custom_call_target="tpu_custom_call" | custom-call | tf_op jit(solution)/shard_map/mix/pallas_call | solution.py:236
  56.9 0.5 collective-permute-done.1.refs_0_
  57.4 12.6 %collective-permute-done.3.refs_1_ = f32[4,2,128,128]{3,2,1,0:T(8,128)S(1)} collective-permute-done((f32[4,2,128,128]{3,2,1,0:T(8,128)S(1)}, f32[4,2,128,128]{3,2,1,0:T(8,128)S(1)}, u32[]{:S(2)}, u32[]{:S(2)}) %collective-permute-start.3) | collective-permute-done | bytes 524320 | tf_op jit(solution)/shard_map/ppermute | solution.py:226
  70.0 1.9 %mix.3 = (f32[4,2,128,128]{3,2,1,0:T(8,128)}, f32[4,2,128,128]{3,2,1,0:T(8,128)}) custom-call(s32[4]{0:T(128)S(1)} %copy-done.3, f32[4]{0:T(128)S(1)} %copy-done.4, f32[4,2,128,128]{3,2,1,0:T(8,128)S(1)} %collective-permute-done.1.refs_0_, f32[4,2,128,128]{3,2,1,0:T(8,128)S(1)} %collective-permute-done.3.refs_1_, ...), custom_call_target="tpu_custom_call" | custom-call | tf_op jit(solution)/shard_map/mix/pallas_call | solution.py:236
Async XLA Ops:
  0.6 1.0 %copy-start = (f32[1,1,4,2,128,128]{5,4,3,2,1,0:T(8,128)S(1)}, f32[1,1,4,2,128,128]{5,4,3,2,1,0:T(8,128)}, u32[]{:S(2)}) copy-start(f32[1,1,4,2,128,128]{5,4,3,2,1,0:T(8,128)} %param.7) | copy-start | bytes 1572868
  1.7 0.9 %copy-start.1 = (f32[1,1,2,128,128]{4,3,2,1,0:T(8,128)S(1)}, f32[1,1,2,128,128]{4,3,2,1,0:T(8,128)}, u32[]{:S(2)}) copy-start(f32[1,1,2,128,128]{4,3,2,1,0:T(8,128)} %param.6) | copy-start | bytes 393220
  5.2 5.3 %copy-start.5 = (f32[1,128,128]{2,1,0:T(8,128)S(1)}, f32[1,128,128]{2,1,0:T(8,128)}, u32[]{:S(2)}) copy-start(f32[1,128,128]{2,1,0:T(8,128)} %param.8) | copy-start | bytes 196612
  5.2 17.7 %all-to-all-start = ((f32[4,2,128,128]{3,2,1,0:T(8,128)}), f32[4,2,128,128]{3,2,1,0:T(8,128)S(1)}, u32[]{:S(2)}, u32[]{:S(2)}) async-start(f32[4,2,128,128]{3,2,1,0:T(8,128)} %inverse.1), calls=%async_computation | async-start | bytes 1048576 | tf_op jit(solution)/shard_map/all_to_all | solution.py:201
  10.5 12.4 %copy-start.2 = (s32[128,128]{1,0:T(8,128)S(1)}, s32[128,128]{1,0:T(8,128)}, u32[]{:S(2)}) copy-start(s32[128,128]{1,0:T(8,128)} %pattern_ref.1) | copy-start | bytes 196612
  25.0 30.5 %copy-start.3 = (s32[4]{0:T(128)S(1)}, s32[4]{0:T(128)}, u32[]{:S(2)}) copy-start(s32[4]{0:T(128)} %shift_ref.3) | copy-start | bytes 52
  25.0 30.5 %copy-start.4 = (f32[4]{0:T(128)S(1)}, f32[4]{0:T(128)}, u32[]{:S(2)}) copy-start(f32[4]{0:T(128)} %weight_ref.3) | copy-start | bytes 52
  34.7 11.4 %collective-permute-start = (f32[4,2,128,128]{3,2,1,0:T(8,128)S(1)}, f32[4,2,128,128]{3,2,1,0:T(8,128)S(1)}, u32[]{:S(2)}, u32[]{:S(2)}) collective-permute-start(f32[4,2,128,128]{3,2,1,0:T(8,128)S(1)} %all_to_all.10.refs_0_), channel_id=1, source_target_pairs={{0,2},{2,4},{4,6},{1,3},{3,5},{5,7},{8,10},{10,12},{12,14},{9,11},... | collective-permute-start | bytes 1572872 | tf_op jit(solution)/shard_map/ppermute | solution.py:222
  38.2 16.0 %collective-permute-start.2 = (f32[4,2,128,128]{3,2,1,0:T(8,128)S(1)}, f32[4,2,128,128]{3,2,1,0:T(8,128)S(1)}, u32[]{:S(2)}, u32[]{:S(2)}) collective-permute-start(f32[4,2,128,128]{3,2,1,0:T(8,128)S(1)} %all_to_all.10.refs_0_), channel_id=1, source_target_pairs={{2,1},{3,0},{4,3},{5,2},{6,5},{7,4},{10,9},{11,8},{12,11},{13,10},... | collective-permute-start | bytes 1572872 | tf_op jit(solution)/shard_map/ppermute | solution.py:224
  39.5 16.0 %collective-permute-start.4 = (f32[4,2,128,128]{3,2,1,0:T(8,128)S(1)}, f32[4,2,128,128]{3,2,1,0:T(8,128)S(1)}, u32[]{:S(2)}, u32[]{:S(2)}) collective-permute-start(f32[4,2,128,128]{3,2,1,0:T(8,128)S(1)} %all_to_all.10.refs_0_), channel_id=1, source_target_pairs={{0,1},{1,0},{2,3},{3,2},{4,5},{5,4},{6,7},{7,6},{8,9},{9,8},{10,11... | collective-permute-start | bytes 1572872 | tf_op jit(solution)/shard_map/ppermute | solution.py:227
  46.0 11.3 %collective-permute-start.1 = (f32[4,2,128,128]{3,2,1,0:T(8,128)S(1)}, f32[4,2,128,128]{3,2,1,0:T(8,128)S(1)}, u32[]{:S(2)}, u32[]{:S(2)}) collective-permute-start(f32[4,2,128,128]{3,2,1,0:T(8,128)S(1)} %collective-permute-done.refs_1_), channel_id=1, source_target_pairs={{0,2},{2,4},{4,6},{1,3},{3,5},{5,7},{8,10},{10,12},{12,14},{9,11},... | collective-permute-start | bytes 1572872 | tf_op jit(solution)/shard_map/ppermute | solution.py:222
  54.2 15.8 %collective-permute-start.3 = (f32[4,2,128,128]{3,2,1,0:T(8,128)S(1)}, f32[4,2,128,128]{3,2,1,0:T(8,128)S(1)}, u32[]{:S(2)}, u32[]{:S(2)}) collective-permute-start(f32[4,2,128,128]{3,2,1,0:T(8,128)S(1)} %collective-permute-done.2.refs_3_), channel_id=1, source_target_pairs={{2,0},{4,2},{6,4},{3,1},{5,3},{7,5},{10,8},{12,10},{14,12},{11,9},... | collective-permute-start | bytes 1572872 | tf_op jit(solution)/shard_map/ppermute | solution.py:226
where the time goes:
time: 72.4 us; the launch traced here: 71.9 us
  waiting for transfers between devices  23.3 us (32%)
  blocking collectives  22.1 us (31%)
  starting transfers between devices  15.9 us (22%)
  Pallas kernels  7.98 us (11%)
  local copies, waits for them, and re-layouts  1.96 us (3%)
  between operations  0.75 us (1%)
    ppermute x1, waiting for transfers between devices, shards(): other.append(lax.ppermute(other[-1], 'energy', down_pairs))  12.6 us
    all_gather x1, blocking collectives, shards(): couplings = lax.all_gather(coupling[0], 'len', axis=0)  12.4 us
    all_to_all x1, blocking collectives, shards(): lax.all_to_all(y.reshape(block), 'len', split_axis=0, concat_axis=0, tile...  9.65 us
    ppermute x2, starting transfers between devices, shards(): own.append(lax.ppermute(own[-1], 'energy', up_pairs))  7.92 us
    ppermute x2, waiting for transfers between devices, shards(): own.append(lax.ppermute(own[-1], 'energy', up_pairs))  6.92 us
    all_to_all x1, starting transfers between devices, shards(): g = lax.all_to_all(g, 'len', split_axis=0, concat_axis=0, tiled=True)  5.31 us
    ppermute x1, waiting for transfers between devices, shards(): other.append(lax.ppermute(y, both, cross))  3.74 us
    pallas_call x2, Pallas kernels, shards(): pl.pallas_call(functools.partial(mix_kernel, total, group, i == 0, i == l...  3.31 us
  transfers between devices with their start and end apart: 6, of which 4 were waited for; matrix products, arithmetic and copies ran while one was open for 0% of the time, Pallas kernels for 2%

commit v1 on v0

v1 whole, which is shorter than its diff:
```python
import functools

import jax
import jax.numpy as jnp
from jax import lax
from jax.experimental import pallas as pl
from jax.experimental.pallas import tpu as pltpu
from jax.sharding import PartitionSpec as P

F32 = jnp.float32
BF16 = jnp.bfloat16
VMEM_LIMIT = 16 * 1024 * 1024


def split(x):
    high = x.astype(BF16)
    return high, (x - high.astype(F32)).astype(BF16)


def dot(a, b):
    return jnp.dot(a, b, preferred_element_type=F32)


def dot3(a, b):
    rows = a[0].shape[0]
    both = dot(jnp.concatenate([a[0], a[1]], axis=0), b[0])
    return both[:rows] + (both[rows:] + dot(a[0], b[1]))


def right_form(m):
    n = m.shape[0]
    re, im = m[:, :n], m[:, n:]
    return jnp.concatenate([m, jnp.concatenate([-im, re], axis=1)], axis=0)


def right_pair(m):
    high, low = split(m)
    return right_form(high), right_form(low)


def identity(n):
    rows = lax.broadcasted_iota(jnp.int32, (n, 2 * n), 0)
    cols = lax.broadcasted_iota(jnp.int32, (n, 2 * n), 1)
    return (rows == cols).astype(F32)


def orders(layers):
    first = list(range(1, layers))
    second = list(first)
    if layers > 2:
        second[0], second[1] = second[1], second[0]
    return first, second


def peers(layers):
    here = lax.axis_index("len")
    core = lax.axis_index("mom")
    first, second = orders(layers)
    return [here] + [here ^ jnp.where(core == 0, a, b) for a, b in zip(first, second)]


def inverse_kernel(total, ham_ref, sig_ref, *out_refs):
    local_e, _, n, _ = sig_ref.shape
    layers = len(out_refs)
    per = local_e // layers
    start = lax.axis_index("energy") * local_e
    eye = identity(n)
    for out_ref, peer in reversed(list(zip(out_refs, peers(layers)))):
        for p in range(per):
            e = peer * per + p
            pos = jnp.full((1, n), start + e, jnp.int32).astype(F32)
            zre = 5.0 + 2.0 * pos / total
            mag = zre * zre + 1.0
            qre = zre / mag
            qim = -1.0 / mag
            sre = ham_ref[0] + sig_ref[e, 0]
            sim = ham_ref[1] + sig_ref[e, 1]
            a1 = jnp.concatenate([qre * sre - qim * sim, qre * sim + qim * sre], axis=1)
            a1_pair = split(a1)
            a1_right = (right_form(a1_pair[0]), right_form(a1_pair[1]))
            a2 = dot3(a1_pair, a1_right)
            a2_pair = split(a2)
            a2_right = (right_form(a2_pair[0]), right_form(a2_pair[1]))
            a3 = dot3(a1_pair, a2_right)
            a4 = dot3(a2_pair, a2_right)
            s = eye + (a1 + (a2 + a3))
            x = s + dot3(split(s), right_pair(a4))
            re, im = x[:, :n], x[:, n:]
            out_ref[p, 0] = qre * re - qim * im
            out_ref[p, 1] = qre * im + qim * re


def chain_kernel(layers, *refs):
    g_slots, coupling_slots = refs[:layers], refs[layers : 2 * layers]
    pattern_ref = refs[2 * layers]
    out_slots = refs[2 * layers + 1 : 3 * layers + 1]
    g_ref, bond_ref = refs[3 * layers + 1 :]
    _, per, _, n, _ = g_ref.shape
    mask = pattern_ref[...].astype(F32)
    for peer, g_slot, coupling_slot in zip(peers(layers), g_slots, coupling_slots):
        g_ref[peer] = g_slot[...]
        bond_ref[peer] = coupling_slot[...] * mask
    bonds = [None] + [bond_ref[l] for l in range(1, layers)]
    bonds_t = [None] + [b.T for b in bonds[1:]]
    for p in range(per):
        g = [jnp.concatenate([g_ref[l, p, 0], g_ref[l, p, 1]], axis=1) for l in range(layers)]
        down = [None] * layers
        up = [None] * layers
        for l in range(layers):
            high, low = split(g[l])
            tall = (
                jnp.concatenate([high[:, :n], high[:, n:]], axis=0),
                jnp.concatenate([low[:, :n], low[:, n:]], axis=0),
            )
            wide = (high, low)
            if l > 0:
                u = dot3(tall, split(bonds[l]))
                v = dot3(split(bonds_t[l]), wide)
                down[l] = (split(jnp.concatenate([u[:n], u[n:]], axis=1)), right_pair(v))
            if l + 1 < layers:
                u = dot3(tall, split(bonds_t[l + 1]))
                v = dot3(split(bonds[l + 1]), wide)
                up[l] = (split(jnp.concatenate([u[:n], u[n:]], axis=1)), right_pair(v))
        green = list(g)
        gleft = g[0]
        gright = g[layers - 1]
        for step in range(1, layers):
            l = step
            u, v = down[l]
            term = dot3(split(dot3(u, right_pair(gleft))), v)
            green[l] = green[l] + term
            gleft = g[l] + term
            l = layers - 1 - step
            u, v = up[l]
            term = dot3(split(dot3(u, right_pair(gright))), v)
            green[l] = green[l] + term
            gright = g[l] + term
        for l in range(layers):
            near = [green[m] for m in (l - 1, l + 1) if 0 <= m < layers]
            y = green[l] + 0.5 * sum(near[1:], near[0]) if near else green[l]
            g_ref[l, p, 0] = y[:, :n]
            g_ref[l, p, 1] = y[:, n:]
    for peer, out_slot in zip(peers(layers), out_slots):
        out_slot[...] = g_ref[peer]


def pack_kernel(*refs):
    slots, out_ref = refs[:-1], refs[-1]
    per = slots[0].shape[0]
    for peer, slot in zip(peers(len(slots)), slots):
        for p in range(per):
            out_ref[peer * per + p] = slot[p]


def momenta_kernel(own_ref, other_ref, zero_ref, one_ref):
    core = lax.axis_index("mom")

    @pl.when(core == 0)
    def _():
        zero_ref[...] = own_ref[...]
        one_ref[...] = other_ref[...]

    @pl.when(core != 0)
    def _():
        zero_ref[...] = other_ref[...]
        one_ref[...] = own_ref[...]


def occupation(pos, total, n):
    return 1.0 / (1.0 + jnp.exp(8.0 * jnp.full((1, n), pos, jnp.int32).astype(F32) / total - 4.0))


def mix_kernel(total, distances, first, last, shift_ref, weight_ref, *refs):
    count = len(distances)
    blocks = refs[:count], refs[count : 2 * count]
    sums_in = (None, None) if first else refs[2 * count : 2 * count + 2]
    ret_ref, les_ref = refs[-2:]
    local_e, _, n, _ = blocks[0][0].shape
    phonons = shift_ref.shape[0]
    start = lax.axis_index("energy") * local_e
    core = lax.axis_index("mom")
    shifts = [shift_ref[m] for m in range(phonons)]
    weights = [weight_ref[m] for m in range(phonons)]

    def coefficient(t):
        value = 0.0
        for s, w in zip(shifts, weights):
            value = value + jnp.where(s == t, w, 0.0)
        return value

    def body(own, other):
        ret_in, les_in = sums_in
        most = total // 2
        coefficients = {}
        for d in distances:
            for t in range(d * local_e - local_e + 1, d * local_e + local_e):
                if 1 <= t <= most and t not in coefficients:
                    coefficients[t] = coefficient(t)
        occ_own = {}
        occ_other = {}
        for d in distances:
            for b in range(local_e):
                occ_own[d, b] = occupation(start - d * local_e + b, total, n)
                occ_other[d, b] = occupation(start + d * local_e + b, total, n)
        for a in range(local_e):
            ret = [jnp.zeros((n, n), F32) if first else ret_in[a, c] for c in range(2)]
            les = [jnp.zeros((n, n), F32) if first else les_in[a, c] for c in range(2)]
            for i, d in enumerate(distances):
                for b in range(local_e):
                    for source, t, occ, factor in (
                        (own[i], d * local_e + a - b, occ_own[d, b], 1.0),
                        (other[i], d * local_e + b - a, occ_other[d, b], 0.5),
                    ):
                        if not 1 <= t <= most:
                            continue
                        w = coefficients[t] * factor
                        for c in range(2):
                            value = w * source[b, c]
                            ret[c] = ret[c] + value
                            les[c] = les[c] + occ * value
            if last:
                les = [les[0] - les[0].T, les[1] + les[1].T]
            for c in range(2):
                ret_ref[a, c] = ret[c]
                les_ref[a, c] = les[c]

    @pl.when(core == 0)
    def _():
        body(*blocks)

    @pl.when(core != 0)
    def _():
        body(*blocks[::-1])


def whole(count):
    return [pl.BlockSpec(memory_space=pltpu.VMEM)] * count


def params():
    return pltpu.CompilerParams(vmem_limit_bytes=VMEM_LIMIT)


def shards(hamiltonian, sigma_prev, coupling, coupling_pattern, phonon_shift, phonon_weight):
    local_e, _, n, _ = sigma_prev.shape[2:]
    layers = lax.axis_size("len")
    count = lax.axis_size("energy")
    moms = lax.axis_size("mom")
    total = local_e * count
    per = local_e // layers
    block = jax.ShapeDtypeStruct((local_e, 2, n, n), F32)
    part = jax.ShapeDtypeStruct((per, 2, n, n), F32)

    first, second = orders(layers)

    def exchange(slots):
        received = [slots[0]]
        for slot, a, b in zip(slots[1:], first, second):
            pairs = [
                (l * moms + k, (l ^ (a if k == 0 else b)) * moms + k)
                for l in range(layers)
                for k in range(moms)
            ]
            received.append(lax.ppermute(slot, ("len", "mom"), pairs))
        return received

    couplings = exchange([coupling[0]] * layers)
    g = pl.pallas_call(
        functools.partial(inverse_kernel, total),
        out_shape=[part] * layers,
        in_specs=whole(2),
        out_specs=whole(layers),
        compiler_params=params(),
        name="inverse",
    )(hamiltonian[0, 0], sigma_prev[0, 0])
    y = pl.pallas_call(
        functools.partial(chain_kernel, layers),
        out_shape=[part] * layers,
        in_specs=whole(2 * layers + 1),
        out_specs=whole(layers),
        scratch_shapes=[pltpu.VMEM((layers, per, 2, n, n), F32), pltpu.VMEM((layers, n, n), F32)],
        compiler_params=params(),
        name="chains",
    )(*exchange(g), *couplings, coupling_pattern)
    y = pl.pallas_call(
        pack_kernel,
        out_shape=block,
        in_specs=whole(layers),
        out_specs=whole(1)[0],
        compiler_params=params(),
        name="pack",
    )(*exchange(y))
    swapped = lax.ppermute(y, "mom", [(k, moms - 1 - k) for k in range(moms)])
    zero, one = pl.pallas_call(
        momenta_kernel,
        out_shape=[block] * 2,
        in_specs=whole(2),
        out_specs=whole(2),
        compiler_params=params(),
        name="momenta",
    )(y, swapped)

    reach = -(-(total // 2) // local_e)
    up_down = []
    down_up = []
    for z in range(count - 1):
        low, high = z * moms, (z + 1) * moms
        up_down += [(low, high), (high + 1, low + 1)]
        down_up += [(high, low), (low + 1, high + 1)]
    zeros = [zero]
    ones = [one]
    for d in range(1, reach + 1):
        zeros.append(lax.ppermute(zeros[-1], ("energy", "mom"), up_down))
        ones.append(lax.ppermute(ones[-1], ("energy", "mom"), down_up))

    groups = [(0, 1)] + [
        tuple(range(d, min(d + 4, reach + 1))) for d in range(2, reach + 1, 4)
    ]
    smem = pl.BlockSpec(memory_space=pltpu.SMEM)
    sums = []
    for i, group in enumerate(groups):
        blocks = [zeros[d] for d in group] + [ones[d] for d in group] + list(sums)
        sums = pl.pallas_call(
            functools.partial(mix_kernel, total, group, i == 0, i == len(groups) - 1),
            out_shape=[block] * 2,
            in_specs=[smem, smem] + whole(len(blocks)),
            out_specs=whole(2),
            compiler_params=params(),
            name="mix",
        )(phonon_shift, phonon_weight, *blocks)
    retarded, lesser = sums
    return (retarded[None, None], lesser[None, None])


def solution(mesh):
    in_specs = (
        P("mom", "len", None, None, None),
        P("mom", "len", "energy", None, None, None),
        P("len", None, None),
        P(),
        P(),
        P(),
    )
    out_specs = (
        P("mom", "len", "energy", None, None, None),
        P("mom", "len", "energy", None, None, None),
    )
    return jax.shard_map(shards, mesh=mesh, in_specs=in_specs, out_specs=out_specs, check_vma=False)
```

time: 72.4 us -> 65.8 us (0.909)
  blocking collectives: 22.1 us -> 0 us
  starting transfers between devices: 15.9 us -> 25.3 us
  waiting for transfers between devices: 23.3 us -> 29.7 us
    ppermute x5 -> x14, starting transfers between devices: 10.6 us -> 25.3 us  [the longest x9 14.9 us: exchange(): received.append(lax.ppermute(slot, ('len', 'mom'), pairs))]
    all_gather x1 -> x0, blocking collectives: 12.4 us -> none  [shards(): couplings = lax.all_gather(coupling[0], 'len', axis=0)]
    all_to_all x1 -> x0, blocking collectives: 9.65 us -> none  [shards(): lax.all_to_all(y.reshape(block), 'len', split_axis=0, concat_axis=0, tile...]
    ppermute x5 -> x14, waiting for transfers between devices: 23.3 us -> 29.7 us  [the longest x2 18.7 us: shards(): zeros.append(lax.ppermute(zeros[-1], ('energy', 'mom'), up_down))]
    all_to_all x1 -> x0, starting transfers between devices: 5.31 us -> none  [shards(): g = lax.all_to_all(g, 'len', split_axis=0, concat_axis=0, tiled=True)]
    pallas_call x2 -> x4, Pallas kernels: 4.67 us -> 4.15 us  [the longest x1 2.22 us: shards(): pl.pallas_call(functools.partial(chain_kernel, layers), out_shape=[part]...]
  transfers between devices with their start and end apart: 6 -> 14, of which waited for: 4 -> 9; matrix products, arithmetic and copies ran while one was open for 0% -> 0% of each run, Pallas kernels for 2% -> 2%
where the time goes in v1:
time: 65.8 us; the launch traced here: 65.4 us
  waiting for transfers between devices  29.7 us (45%)
  starting transfers between devices  25.3 us (38%)
  Pallas kernels  7.59 us (12%)
  local copies, waits for them, and re-layouts  1.96 us (3%)
  between operations  0.78 us (1%)
    ppermute x2, waiting for transfers between devices, shards(): zeros.append(lax.ppermute(zeros[-1], ('energy', 'mom'), up_down))  18.7 us
    ppermute x9, starting transfers between devices, exchange(): received.append(lax.ppermute(slot, ('len', 'mom'), pairs))  14.9 us
    ppermute x9, waiting for transfers between devices, exchange(): received.append(lax.ppermute(slot, ('len', 'mom'), pairs))  9.09 us
    ppermute x2, starting transfers between devices, shards(): zeros.append(lax.ppermute(zeros[-1], ('energy', 'mom'), up_down))  7.8 us
    pallas_call x2, Pallas kernels, shards(): pl.pallas_call(functools.partial(mix_kernel, total, group, i == 0, i == l...  3.44 us
    ppermute x2, starting transfers between devices, shards(): ones.append(lax.ppermute(ones[-1], ('energy', 'mom'), down_up))  2.58 us
    pallas_call x1, Pallas kernels, shards(): pl.pallas_call(functools.partial(chain_kernel, layers), out_shape=[part]...  2.22 us
    unnamed x12, local copies, waits for them, and re-layouts  1.96 us
  transfers between devices with their start and end apart: 14, of which 9 were waited for; matrix products, arithmetic and copies ran while one was open for 0% of the time, Pallas kernels for 2%

profile of v1, /device:TPU:0, one launch (start us, length us, event | category | flops | bytes accessed | tf_op | source)
XLA Modules:
  0.0 65.4 jit_solution(4168782823020484584)
XLA Ops:
  0.6 1.0 %copy-done = f32[1,1,4,2,128,128]{5,4,3,2,1,0:T(8,128)S(1)} copy-done((f32[1,1,4,2,128,128]{5,4,3,2,1,0:T(8,128)S(1)}, f32[1,1,4,2,128,128]{5,4,3,2,1,0:T(8,128)}, u32[]{:S(2)}) %copy-start) | copy-done | bytes 524312
  1.7 0.9 %copy-done.1 = f32[1,1,2,128,128]{4,3,2,1,0:T(8,128)S(1)} copy-done((f32[1,1,2,128,128]{4,3,2,1,0:T(8,128)S(1)}, f32[1,1,2,128,128]{4,3,2,1,0:T(8,128)}, u32[]{:S(2)}) %copy-start.1) | copy-done | bytes 131096
  2.6 1.8 %inverse.1 = (f32[1,2,128,128]{3,2,1,0:T(8,128)S(1)}, f32[1,2,128,128]{3,2,1,0:T(8,128)S(1)}, f32[1,2,128,128]{3,2,1,0:T(8,128)S(1)}, f32[1,2,128,128]{3,2,1,0:T(8,128)S(1)}) custom-call(f32[2,128,128]{2,1,0:T(8,128)S(1)} %bitcast.6, f32[4,2,128,128]{3,2,1,0:T(8,128)S(1)} %bitcast.5), custom_call_target="tpu_custom_call" | custom-call | tf_op jit(solution)/shard_map/inverse/pallas_call | solution.py:268
  4.4 3.0 %collective-permute-start = (f32[1,2,128,128]{3,2,1,0:T(8,128)S(1)}, f32[1,2,128,128]{3,2,1,0:T(8,128)S(1)}, u32[]{:S(2)}, u32[]{:S(2)}) collective-permute-start(f32[1,2,128,128]{3,2,1,0:T(8,128)S(1)} %get-tuple-element.17), channel_id=1, source_target_pairs={{0,8},{1,17},{8,0},{9,25},{16,24},{17,1},{24,16},{25,9},{2,10},{3,... | collective-permute-start | bytes 393224 | tf_op jit(solution)/shard_map/ppermute | solution.py:264
  7.4 0.1 collective-permute-start.3
  7.5 2.0 %collective-permute-start.1 = (f32[1,2,128,128]{3,2,1,0:T(8,128)S(1)}, f32[1,2,128,128]{3,2,1,0:T(8,128)S(1)}, u32[]{:S(2)}, u32[]{:S(2)}) collective-permute-start(f32[1,2,128,128]{3,2,1,0:T(8,128)S(1)} %get-tuple-element.18), channel_id=1, source_target_pairs={{0,16},{1,9},{8,24},{9,1},{16,0},{17,25},{24,8},{25,17},{2,18},{3,... | collective-permute-start | bytes 393224 | tf_op jit(solution)/shard_map/ppermute | solution.py:264
  9.5 1.4 %collective-permute-start.2 = (f32[1,2,128,128]{3,2,1,0:T(8,128)S(1)}, f32[1,2,128,128]{3,2,1,0:T(8,128)S(1)}, u32[]{:S(2)}, u32[]{:S(2)}) collective-permute-start(f32[1,2,128,128]{3,2,1,0:T(8,128)S(1)} %get-tuple-element.19), channel_id=1, source_target_pairs={{0,24},{1,25},{8,16},{9,17},{16,8},{17,9},{24,0},{25,1},{2,26},{3,... | collective-permute-start | bytes 393224 | tf_op jit(solution)/shard_map/ppermute | solution.py:264
  10.9 1.5 %collective-permute-start.4 = (f32[128,128]{1,0:T(8,128)S(1)}, f32[128,128]{1,0:T(8,128)S(1)}, u32[]{:S(2)}, u32[]{:S(2)}) collective-permute-start(f32[128,128]{1,0:T(8,128)S(1)} %bitcast.8), channel_id=1, source_target_pairs={{0,16},{1,9},{8,24},{9,1},{16,0},{17,25},{24,8},{25,17},{2,18},{3,... | collective-permute-start | bytes 196616 | tf_op jit(solution)/shard_map/ppermute | solution.py:264
  12.4 0.1 collective-permute-done.3.refs_5_
  12.5 3.3 %collective-permute-start.5 = (f32[128,128]{1,0:T(8,128)S(1)}, f32[128,128]{1,0:T(8,128)S(1)}, u32[]{:S(2)}, u32[]{:S(2)}) collective-permute-start(f32[128,128]{1,0:T(8,128)S(1)} %bitcast.9), channel_id=1, source_target_pairs={{0,24},{1,25},{8,16},{9,17},{16,8},{17,9},{24,0},{25,1},{2,26},{3,... | collective-permute-start | bytes 196616 | tf_op jit(solution)/shard_map/ppermute | solution.py:264
  15.8 1.7 %collective-permute-done.4.refs_6_ = f32[128,128]{1,0:T(8,128)S(1)} collective-permute-done((f32[128,128]{1,0:T(8,128)S(1)}, f32[128,128]{1,0:T(8,128)S(1)}, u32[]{:S(2)}, u32[]{:S(2)}) %collective-permute-start.4) | collective-permute-done | bytes 65568 | tf_op jit(solution)/shard_map/ppermute | solution.py:264
  17.5 1.3 %collective-permute-done.5.refs_7_ = f32[128,128]{1,0:T(8,128)S(1)} collective-permute-done((f32[128,128]{1,0:T(8,128)S(1)}, f32[128,128]{1,0:T(8,128)S(1)}, u32[]{:S(2)}, u32[]{:S(2)}) %collective-permute-start.5) | collective-permute-done | bytes 65568 | tf_op jit(solution)/shard_map/ppermute | solution.py:264
  18.8 2.2 %chains.1 = (f32[1,2,128,128]{3,2,1,0:T(8,128)S(1)}, f32[1,2,128,128]{3,2,1,0:T(8,128)S(1)}, f32[1,2,128,128]{3,2,1,0:T(8,128)S(1)}, f32[1,2,128,128]{3,2,1,0:T(8,128)S(1)}) custom-call(f32[1,2,128,128]{3,2,1,0:T(8,128)S(1)} %get-tuple-element.16.refs_0_, f32[1,2,128,128]{3,2,1,0:T(8,128)S(1)} %collective-permute-done.refs_1_, ...), custom_call_target="tpu_custom_call" | custom-call | tf_op jit(solution)/shard_map/chains/pallas_call | solution.py:276
  21.0 1.6 %collective-permute-start.6 = (f32[1,2,128,128]{3,2,1,0:T(8,128)S(1)}, f32[1,2,128,128]{3,2,1,0:T(8,128)S(1)}, u32[]{:S(2)}, u32[]{:S(2)}) collective-permute-start(f32[1,2,128,128]{3,2,1,0:T(8,128)S(1)} %get-tuple-element.21), channel_id=1, source_target_pairs={{0,8},{1,17},{8,0},{9,25},{16,24},{17,1},{24,16},{25,9},{2,10},{3,... | collective-permute-start | bytes 393224 | tf_op jit(solution)/shard_map/ppermute | solution.py:264
  22.7 1.2 %collective-permute-start.7 = (f32[1,2,128,128]{3,2,1,0:T(8,128)S(1)}, f32[1,2,128,128]{3,2,1,0:T(8,128)S(1)}, u32[]{:S(2)}, u32[]{:S(2)}) collective-permute-start(f32[1,2,128,128]{3,2,1,0:T(8,128)S(1)} %get-tuple-element.22), channel_id=1, source_target_pairs={{0,16},{1,9},{8,24},{9,1},{16,0},{17,25},{24,8},{25,17},{2,18},{3,... | collective-permute-start | bytes 393224 | tf_op jit(solution)/shard_map/ppermute | solution.py:264
  23.8 0.8 %collective-permute-start.8 = (f32[1,2,128,128]{3,2,1,0:T(8,128)S(1)}, f32[1,2,128,128]{3,2,1,0:T(8,128)S(1)}, u32[]{:S(2)}, u32[]{:S(2)}) collective-permute-start(f32[1,2,128,128]{3,2,1,0:T(8,128)S(1)} %get-tuple-element.23), channel_id=1, source_target_pairs={{0,24},{1,25},{8,16},{9,17},{16,8},{17,9},{24,0},{25,1},{2,26},{3,... | collective-permute-start | bytes 393224 | tf_op jit(solution)/shard_map/ppermute | solution.py:264
  24.6 2.8 %collective-permute-done.6.refs_1_ = f32[1,2,128,128]{3,2,1,0:T(8,128)S(1)} collective-permute-done((f32[1,2,128,128]{3,2,1,0:T(8,128)S(1)}, f32[1,2,128,128]{3,2,1,0:T(8,128)S(1)}, u32[]{:S(2)}, u32[]{:S(2)}) %collective-permute-start.6) | collective-permute-done | bytes 131104 | tf_op jit(solution)/shard_map/ppermute | solution.py:264
  27.4 1.7 %collective-permute-done.7.refs_2_ = f32[1,2,128,128]{3,2,1,0:T(8,128)S(1)} collective-permute-done((f32[1,2,128,128]{3,2,1,0:T(8,128)S(1)}, f32[1,2,128,128]{3,2,1,0:T(8,128)S(1)}, u32[]{:S(2)}, u32[]{:S(2)}) %collective-permute-start.7) | collective-permute-done | bytes 131104 | tf_op jit(solution)/shard_map/ppermute | solution.py:264
  29.2 1.5 %collective-permute-done.8.refs_3_ = f32[1,2,128,128]{3,2,1,0:T(8,128)S(1)} collective-permute-done((f32[1,2,128,128]{3,2,1,0:T(8,128)S(1)}, f32[1,2,128,128]{3,2,1,0:T(8,128)S(1)}, u32[]{:S(2)}, u32[]{:S(2)}) %collective-permute-start.8) | collective-permute-done | bytes 131104 | tf_op jit(solution)/shard_map/ppermute | solution.py:264
  30.7 0.1 collective-permute-start.9
  30.8 1.9 %collective-permute-done.9.other_ref = f32[4,2,128,128]{3,2,1,0:T(8,128)S(1)} collective-permute-done((f32[4,2,128,128]{3,2,1,0:T(8,128)S(1)}, f32[4,2,128,128]{3,2,1,0:T(8,128)S(1)}, u32[]{:S(2)}, u32[]{:S(2)}) %collective-permute-start.9) | collective-permute-done | bytes 524320 | tf_op jit(solution)/shard_map/ppermute | solution.py:293
  32.6 0.1 momenta.1
  32.7 0.0 copy-start.4
  32.7 0.0 copy-start.5
  32.8 3.4 %collective-permute-start.10 = (f32[4,2,128,128]{3,2,1,0:T(8,128)S(1)}, f32[4,2,128,128]{3,2,1,0:T(8,128)S(1)}, u32[]{:S(2)}, u32[]{:S(2)}) collective-permute-start(f32[4,2,128,128]{3,2,1,0:T(8,128)S(1)} %get-tuple-element.24.refs_0_), channel_id=1, source_target_pairs={{0,2},{3,1},{2,4},{5,3},{4,6},{7,5},{8,10},{11,9},{10,12},{13,11},... | collective-permute-start | bytes 1572872 | tf_op jit(solution)/shard_map/ppermute | solution.py:313
  36.1 1.3 %collective-permute-start.12 = (f32[4,2,128,128]{3,2,1,0:T(8,128)S(1)}, f32[4,2,128,128]{3,2,1,0:T(8,128)S(1)}, u32[]{:S(2)}, u32[]{:S(2)}) collective-permute-start(f32[4,2,128,128]{3,2,1,0:T(8,128)S(1)} %get-tuple-element.25.refs_2_), channel_id=1, source_target_pairs={{2,0},{1,3},{4,2},{3,5},{6,4},{5,7},{10,8},{9,11},{12,10},{11,13},... | collective-permute-start | bytes 1572872 | tf_op jit(solution)/shard_map/ppermute | solution.py:314
  37.4 9.5 %collective-permute-done.10.refs_1_ = f32[4,2,128,128]{3,2,1,0:T(8,128)S(1)} collective-permute-done((f32[4,2,128,128]{3,2,1,0:T(8,128)S(1)}, f32[4,2,128,128]{3,2,1,0:T(8,128)S(1)}, u32[]{:S(2)}, u32[]{:S(2)}) %collective-permute-start.10) | collective-permute-done | bytes 524320 | tf_op jit(solution)/shard_map/ppermute | solution.py:313
  47.0 4.4 %collective-permute-start.11 = (f32[4,2,128,128]{3,2,1,0:T(8,128)S(1)}, f32[4,2,128,128]{3,2,1,0:T(8,128)S(1)}, u32[]{:S(2)}, u32[]{:S(2)}) collective-permute-start(f32[4,2,128,128]{3,2,1,0:T(8,128)S(1)} %collective-permute-done.10.refs_1_), channel_id=1, source_target_pairs={{0,2},{3,1},{2,4},{5,3},{4,6},{7,5},{8,10},{11,9},{10,12},{13,11},... | collective-permute-start | bytes 1572872 | tf_op jit(solution)/shard_map/ppermute | solution.py:313
  51.4 1.3 %collective-permute-start.13 = (f32[4,2,128,128]{3,2,1,0:T(8,128)S(1)}, f32[4,2,128,128]{3,2,1,0:T(8,128)S(1)}, u32[]{:S(2)}, u32[]{:S(2)}) collective-permute-start(f32[4,2,128,128]{3,2,1,0:T(8,128)S(1)} %collective-permute-done.12.refs_3_), channel_id=1, source_target_pairs={{2,0},{1,3},{4,2},{3,5},{6,4},{5,7},{10,8},{9,11},{12,10},{11,13},... | collective-permute-start | bytes 1572872 | tf_op jit(solution)/shard_map/ppermute | solution.py:314
  52.7 1.5 %mix.2 = (f32[4,2,128,128]{3,2,1,0:T(8,128)S(1)}, f32[4,2,128,128]{3,2,1,0:T(8,128)S(1)}) custom-call(s32[4]{0:T(128)S(1)} %copy-done.4, f32[4]{0:T(128)S(1)} %copy-done.5, f32[4,2,128,128]{3,2,1,0:T(8,128)S(1)} %get-tuple-element.24.refs_0_, f32[4,2,128,128]{3,2,1,0:T(8,128)S(1)} %collective-permute-done.10.refs_1_, ...), custom_call_target="tpu_custom_call" | custom-call | tf_op jit(solution)/shard_map/mix/pallas_call | solution.py:323
  54.2 9.2 %collective-permute-done.11.refs_0_ = f32[4,2,128,128]{3,2,1,0:T(8,128)S(1)} collective-permute-done((f32[4,2,128,128]{3,2,1,0:T(8,128)S(1)}, f32[4,2,128,128]{3,2,1,0:T(8,128)S(1)}, u32[]{:S(2)}, u32[]{:S(2)}) %collective-permute-start.11) | collective-permute-done | bytes 524320 | tf_op jit(solution)/shard_map/ppermute | solution.py:313
  63.4 2.0 %mix.3 = (f32[4,2,128,128]{3,2,1,0:T(8,128)}, f32[4,2,128,128]{3,2,1,0:T(8,128)}) custom-call(s32[4]{0:T(128)S(1)} %copy-done.4, f32[4]{0:T(128)S(1)} %copy-done.5, f32[4,2,128,128]{3,2,1,0:T(8,128)S(1)} %collective-permute-done.11.refs_0_, f32[4,2,128,128]{3,2,1,0:T(8,128)S(1)} %collective-permute-done.13.refs_1_, ...), custom_call_target="tpu_custom_call" | custom-call | tf_op jit(solution)/shard_map/mix/pallas_call | solution.py:323
  (14 shorter events, 0.1 us)
Async XLA Ops:
  0.6 1.0 %copy-start = (f32[1,1,4,2,128,128]{5,4,3,2,1,0:T(8,128)S(1)}, f32[1,1,4,2,128,128]{5,4,3,2,1,0:T(8,128)}, u32[]{:S(2)}) copy-start(f32[1,1,4,2,128,128]{5,4,3,2,1,0:T(8,128)} %param.7) | copy-start | bytes 1572868
  1.7 0.9 %copy-start.1 = (f32[1,1,2,128,128]{4,3,2,1,0:T(8,128)S(1)}, f32[1,1,2,128,128]{4,3,2,1,0:T(8,128)}, u32[]{:S(2)}) copy-start(f32[1,1,2,128,128]{4,3,2,1,0:T(8,128)} %param.6) | copy-start | bytes 393220
  2.6 4.8 %copy-start.2 = (f32[1,128,128]{2,1,0:T(8,128)S(1)}, f32[1,128,128]{2,1,0:T(8,128)}, u32[]{:S(2)}) copy-start(f32[1,128,128]{2,1,0:T(8,128)} %param.8) | copy-start | bytes 196612
  2.6 16.2 %copy-start.3 = (s32[128,128]{1,0:T(8,128)S(1)}, s32[128,128]{1,0:T(8,128)}, u32[]{:S(2)}) copy-start(s32[128,128]{1,0:T(8,128)} %refs_8_.1) | copy-start | bytes 196612
  4.4 14.4 %collective-permute-start = (f32[1,2,128,128]{3,2,1,0:T(8,128)S(1)}, f32[1,2,128,128]{3,2,1,0:T(8,128)S(1)}, u32[]{:S(2)}, u32[]{:S(2)}) collective-permute-start(f32[1,2,128,128]{3,2,1,0:T(8,128)S(1)} %get-tuple-element.17), channel_id=1, source_target_pairs={{0,8},{1,17},{8,0},{9,25},{16,24},{17,1},{24,16},{25,9},{2,10},{3,... | collective-permute-start | bytes 393224 | tf_op jit(solution)/shard_map/ppermute | solution.py:264
  7.4 5.1 %collective-permute-start.3 = (f32[128,128]{1,0:T(8,128)S(1)}, f32[128,128]{1,0:T(8,128)S(1)}, u32[]{:S(2)}, u32[]{:S(2)}) collective-permute-start(f32[128,128]{1,0:T(8,128)S(1)} %bitcast.7), channel_id=1, source_target_pairs={{0,8},{1,17},{8,0},{9,25},{16,24},{17,1},{24,16},{25,9},{2,10},{3,... | collective-permute-start | bytes 196616 | tf_op jit(solution)/shard_map/ppermute | solution.py:264
  7.5 11.3 %collective-permute-start.1 = (f32[1,2,128,128]{3,2,1,0:T(8,128)S(1)}, f32[1,2,128,128]{3,2,1,0:T(8,128)S(1)}, u32[]{:S(2)}, u32[]{:S(2)}) collective-permute-start(f32[1,2,128,128]{3,2,1,0:T(8,128)S(1)} %get-tuple-element.18), channel_id=1, source_target_pairs={{0,16},{1,9},{8,24},{9,1},{16,0},{17,25},{24,8},{25,17},{2,18},{3,... | collective-permute-start | bytes 393224 | tf_op jit(solution)/shard_map/ppermute | solution.py:264
  9.5 9.3 %collective-permute-start.2 = (f32[1,2,128,128]{3,2,1,0:T(8,128)S(1)}, f32[1,2,128,128]{3,2,1,0:T(8,128)S(1)}, u32[]{:S(2)}, u32[]{:S(2)}) collective-permute-start(f32[1,2,128,128]{3,2,1,0:T(8,128)S(1)} %get-tuple-element.19), channel_id=1, source_target_pairs={{0,24},{1,25},{8,16},{9,17},{16,8},{17,9},{24,0},{25,1},{2,26},{3,... | collective-permute-start | bytes 393224 | tf_op jit(solution)/shard_map/ppermute | solution.py:264
  10.9 6.6 %collective-permute-start.4 = (f32[128,128]{1,0:T(8,128)S(1)}, f32[128,128]{1,0:T(8,128)S(1)}, u32[]{:S(2)}, u32[]{:S(2)}) collective-permute-start(f32[128,128]{1,0:T(8,128)S(1)} %bitcast.8), channel_id=1, source_target_pairs={{0,16},{1,9},{8,24},{9,1},{16,0},{17,25},{24,8},{25,17},{2,18},{3,... | collective-permute-start | bytes 196616 | tf_op jit(solution)/shard_map/ppermute | solution.py:264
  12.5 6.3 %collective-permute-start.5 = (f32[128,128]{1,0:T(8,128)S(1)}, f32[128,128]{1,0:T(8,128)S(1)}, u32[]{:S(2)}, u32[]{:S(2)}) collective-permute-start(f32[128,128]{1,0:T(8,128)S(1)} %bitcast.9), channel_id=1, source_target_pairs={{0,24},{1,25},{8,16},{9,17},{16,8},{17,9},{24,0},{25,1},{2,26},{3,... | collective-permute-start | bytes 196616 | tf_op jit(solution)/shard_map/ppermute | solution.py:264
  21.0 6.4 %collective-permute-start.6 = (f32[1,2,128,128]{3,2,1,0:T(8,128)S(1)}, f32[1,2,128,128]{3,2,1,0:T(8,128)S(1)}, u32[]{:S(2)}, u32[]{:S(2)}) collective-permute-start(f32[1,2,128,128]{3,2,1,0:T(8,128)S(1)} %get-tuple-element.21), channel_id=1, source_target_pairs={{0,8},{1,17},{8,0},{9,25},{16,24},{17,1},{24,16},{25,9},{2,10},{3,... | collective-permute-start | bytes 393224 | tf_op jit(solution)/shard_map/ppermute | solution.py:264
  22.7 6.5 %collective-permute-start.7 = (f32[1,2,128,128]{3,2,1,0:T(8,128)S(1)}, f32[1,2,128,128]{3,2,1,0:T(8,128)S(1)}, u32[]{:S(2)}, u32[]{:S(2)}) collective-permute-start(f32[1,2,128,128]{3,2,1,0:T(8,128)S(1)} %get-tuple-element.22), channel_id=1, source_target_pairs={{0,16},{1,9},{8,24},{9,1},{16,0},{17,25},{24,8},{25,17},{2,18},{3,... | collective-permute-start | bytes 393224 | tf_op jit(solution)/shard_map/ppermute | solution.py:264
  23.8 6.8 %collective-permute-start.8 = (f32[1,2,128,128]{3,2,1,0:T(8,128)S(1)}, f32[1,2,128,128]{3,2,1,0:T(8,128)S(1)}, u32[]{:S(2)}, u32[]{:S(2)}) collective-permute-start(f32[1,2,128,128]{3,2,1,0:T(8,128)S(1)} %get-tuple-element.23), channel_id=1, source_target_pairs={{0,24},{1,25},{8,16},{9,17},{16,8},{17,9},{24,0},{25,1},{2,26},{3,... | collective-permute-start | bytes 393224 | tf_op jit(solution)/shard_map/ppermute | solution.py:264
  30.7 2.0 %collective-permute-start.9 = (f32[4,2,128,128]{3,2,1,0:T(8,128)S(1)}, f32[4,2,128,128]{3,2,1,0:T(8,128)S(1)}, u32[]{:S(2)}, u32[]{:S(2)}) collective-permute-start(f32[4,2,128,128]{3,2,1,0:T(8,128)S(1)} %pack.1.own_ref), channel_id=1, source_target_pairs={{0,1},{1,0},{2,3},{3,2},{4,5},{5,4},{6,7},{7,6},{8,9},{9,8},{10,11... | collective-permute-start | bytes 1572872 | tf_op jit(solution)/shard_map/ppermute | solution.py:293
  32.7 20.0 %copy-start.4 = (s32[4]{0:T(128)S(1)}, s32[4]{0:T(128)}, u32[]{:S(2)}) copy-start(s32[4]{0:T(128)} %shift_ref.3) | copy-start | bytes 52
  32.7 20.0 %copy-start.5 = (f32[4]{0:T(128)S(1)}, f32[4]{0:T(128)}, u32[]{:S(2)}) copy-start(f32[4]{0:T(128)} %weight_ref.3) | copy-start | bytes 52
  32.8 14.2 %collective-permute-start.10 = (f32[4,2,128,128]{3,2,1,0:T(8,128)S(1)}, f32[4,2,128,128]{3,2,1,0:T(8,128)S(1)}, u32[]{:S(2)}, u32[]{:S(2)}) collective-permute-start(f32[4,2,128,128]{3,2,1,0:T(8,128)S(1)} %get-tuple-element.24.refs_0_), channel_id=1, source_target_pairs={{0,2},{3,1},{2,4},{5,3},{4,6},{7,5},{8,10},{11,9},{10,12},{13,11},... | collective-permute-start | bytes 1572872 | tf_op jit(solution)/shard_map/ppermute | solution.py:313
  36.1 15.3 %collective-permute-start.12 = (f32[4,2,128,128]{3,2,1,0:T(8,128)S(1)}, f32[4,2,128,128]{3,2,1,0:T(8,128)S(1)}, u32[]{:S(2)}, u32[]{:S(2)}) collective-permute-start(f32[4,2,128,128]{3,2,1,0:T(8,128)S(1)} %get-tuple-element.25.refs_2_), channel_id=1, source_target_pairs={{2,0},{1,3},{4,2},{3,5},{6,4},{5,7},{10,8},{9,11},{12,10},{11,13},... | collective-permute-start | bytes 1572872 | tf_op jit(solution)/shard_map/ppermute | solution.py:314
  47.0 16.4 %collective-permute-start.11 = (f32[4,2,128,128]{3,2,1,0:T(8,128)S(1)}, f32[4,2,128,128]{3,2,1,0:T(8,128)S(1)}, u32[]{:S(2)}, u32[]{:S(2)}) collective-permute-start(f32[4,2,128,128]{3,2,1,0:T(8,128)S(1)} %collective-permute-done.10.refs_1_), channel_id=1, source_target_pairs={{0,2},{3,1},{2,4},{5,3},{4,6},{7,5},{8,10},{11,9},{10,12},{13,11},... | collective-permute-start | bytes 1572872 | tf_op jit(solution)/shard_map/ppermute | solution.py:313
  51.4 12.0 %collective-permute-start.13 = (f32[4,2,128,128]{3,2,1,0:T(8,128)S(1)}, f32[4,2,128,128]{3,2,1,0:T(8,128)S(1)}, u32[]{:S(2)}, u32[]{:S(2)}) collective-permute-start(f32[4,2,128,128]{3,2,1,0:T(8,128)S(1)} %collective-permute-done.12.refs_3_), channel_id=1, source_target_pairs={{2,0},{1,3},{4,2},{3,5},{6,4},{5,7},{10,8},{9,11},{12,10},{11,13},... | collective-permute-start | bytes 1572872 | tf_op jit(solution)/shard_map/ppermute | solution.py:314

commit v2 on v1

--- a/solution.py
+++ b/solution.py
@@ -59,22 +59,33 @@
     return [here] + [here ^ jnp.where(core == 0, a, b) for a, b in zip(first, second)]
 
 
-def inverse_kernel(total, ham_ref, sig_ref, *out_refs):
-    local_e, _, n, _ = sig_ref.shape
-    layers = len(out_refs)
-    per = local_e // layers
-    start = lax.axis_index("energy") * local_e
+def inverse_kernel(total, ham_any, sig_any, coupling_any, pattern_any, *refs):
+    ham_ref, sig_ref, coupling_ref, pattern_ref, sems = refs[-5:]
+    out_refs = refs[:-5]
+    layers, per, _, n, _ = sig_ref.shape
+    slots = list(zip(peers(layers), out_refs))[::-1]
+    copies = [pltpu.make_async_copy(ham_any, ham_ref, sems.at[layers])]
+    for i, (peer, _) in enumerate(slots):
+        copies.append(
+            pltpu.make_async_copy(sig_any.at[pl.ds(peer * per, per)], sig_ref.at[i], sems.at[i])
+        )
+    copies.append(pltpu.make_async_copy(coupling_any, coupling_ref, sems.at[layers + 1]))
+    copies.append(pltpu.make_async_copy(pattern_any, pattern_ref, sems.at[layers + 2]))
+    for copy in copies:
+        copy.start()
+    start = lax.axis_index("energy") * (layers * per)
     eye = identity(n)
-    for out_ref, peer in reversed(list(zip(out_refs, peers(layers)))):
+    copies[0].wait()
+    for i, (peer, out_ref) in enumerate(slots):
+        copies[1 + i].wait()
         for p in range(per):
-            e = peer * per + p
-            pos = jnp.full((1, n), start + e, jnp.int32).astype(F32)
+            pos = jnp.full((1, n), start + peer * per + p, jnp.int32).astype(F32)
             zre = 5.0 + 2.0 * pos / total
             mag = zre * zre + 1.0
             qre = zre / mag
             qim = -1.0 / mag
-            sre = ham_ref[0] + sig_ref[e, 0]
-            sim = ham_ref[1] + sig_ref[e, 1]
+            sre = ham_ref[0] + sig_ref[i, p, 0]
+            sim = ham_ref[1] + sig_ref[i, p, 1]
             a1 = jnp.concatenate([qre * sre - qim * sim, qre * sim + qim * sre], axis=1)
             a1_pair = split(a1)
             a1_right = (right_form(a1_pair[0]), right_form(a1_pair[1]))
@@ -86,20 +97,23 @@
             s = eye + (a1 + (a2 + a3))
             x = s + dot3(split(s), right_pair(a4))
             re, im = x[:, :n], x[:, n:]
-            out_ref[p, 0] = qre * re - qim * im
-            out_ref[p, 1] = qre * im + qim * re
+            out_ref[2 * p] = qre * re - qim * im
+            out_ref[2 * p + 1] = qre * im + qim * re
+    copies[-2].wait()
+    copies[-1].wait()
+    bond = coupling_ref[...] * pattern_ref[...].astype(F32)
+    for _, out_ref in slots:
+        out_ref[2 * per] = bond
 
 
 def chain_kernel(layers, *refs):
-    g_slots, coupling_slots = refs[:layers], refs[layers : 2 * layers]
-    pattern_ref = refs[2 * layers]
-    out_slots = refs[2 * layers + 1 : 3 * layers + 1]
-    g_ref, bond_ref = refs[3 * layers + 1 :]
+    in_slots, out_slots = refs[:layers], refs[layers : 2 * layers]
+    g_ref, bond_ref = refs[2 * layers :]
     _, per, _, n, _ = g_ref.shape
-    mask = pattern_ref[...].astype(F32)
-    for peer, g_slot, coupling_slot in zip(peers(layers), g_slots, coupling_slots):
-        g_ref[peer] = g_slot[...]
-        bond_ref[peer] = coupling_slot[...] * mask
+    for peer, in_slot in zip(peers(layers), in_slots):
+        for p in range(per):
+            g_ref[peer, p] = in_slot[2 * p : 2 * p + 2]
+        bond_ref[peer] = in_slot[2 * per]
     bonds = [None] + [bond_ref[l] for l in range(1, layers)]
     bonds_t = [None] + [b.T for b in bonds[1:]]
     for p in range(per):
@@ -147,35 +161,49 @@
 def pack_kernel(*refs):
     slots, out_ref = refs[:-1], refs[-1]
     per = slots[0].shape[0]
-    for peer, slot in zip(peers(len(slots)), slots):
-        for p in range(per):
-            out_ref[peer * per + p] = slot[p]
-
-
-def momenta_kernel(own_ref, other_ref, zero_ref, one_ref):
+    for i, slot in enumerate(slots):
+        out_ref[i * per : (i + 1) * per] = slot[...]
+
+
+def momenta_kernel(*refs):
+    count = len(refs) // 2 - 1
+    own, other = refs[:count], refs[count : 2 * count]
+    zero_ref, one_ref = refs[2 * count :]
     core = lax.axis_index("mom")
 
     @pl.when(core == 0)
     def _():
-        zero_ref[...] = own_ref[...]
-        one_ref[...] = other_ref[...]
+        pack_kernel(*own, zero_ref)
+        pack_kernel(*other, one_ref)
 
     @pl.when(core != 0)
     def _():
-        zero_ref[...] = other_ref[...]
-        one_ref[...] = own_ref[...]
+        pack_kernel(*other, zero_ref)
+        pack_kernel(*own, one_ref)
 
 
 def occupation(pos, total, n):
     return 1.0 / (1.0 + jnp.exp(8.0 * jnp.full((1, n), pos, jnp.int32).astype(F32) / total - 4.0))
 
 
-def mix_kernel(total, distances, first, last, shift_ref, weight_ref, *refs):
-    count = len(distances)
-    blocks = refs[:count], refs[count : 2 * count]
+def mix_kernel(total, distances, chunks, first, last, shift_ref, weight_ref, *refs):
+    count = len(distances) * chunks
+    blocks = refs[-2:]
     sums_in = (None, None) if first else refs[2 * count : 2 * count + 2]
-    ret_ref, les_ref = refs[-2:]
-    local_e, _, n, _ = blocks[0][0].shape
+    ret_ref, les_ref = refs[-4:-2]
+    _, local_e, _, n, _ = blocks[0].shape
+    layers = lax.axis_size("len")
+    per = local_e // layers
+    here = lax.axis_index("len")
+    each = layers // chunks
+    for momentum, order in enumerate(orders(layers)):
+        masks = [0] + order
+        for i in range(count):
+            source = refs[momentum * count + i]
+            for s in range(each):
+                peer = here ^ masks[i % chunks * each + s]
+                for p in range(per):
+                    blocks[momentum][i // chunks, peer * per + p] = source[s * per + p]
     phonons = shift_ref.shape[0]
     start = lax.axis_index("energy") * local_e
     core = lax.axis_index("mom")
@@ -208,8 +236,8 @@
             for i, d in enumerate(distances):
                 for b in range(local_e):
                     for source, t, occ, factor in (
-                        (own[i], d * local_e + a - b, occ_own[d, b], 1.0),
-                        (other[i], d * local_e + b - a, occ_other[d, b], 0.5),
+                        (own.at[i], d * local_e + a - b, occ_own[d, b], 1.0),
+                        (other.at[i], d * local_e + b - a, occ_other[d, b], 0.5),
                     ):
                         if not 1 <= t <= most:
                             continue
@@ -253,65 +281,113 @@
 
     first, second = orders(layers)
 
-    def exchange(slots):
-        received = [slots[0]]
-        for slot, a, b in zip(slots[1:], first, second):
-            pairs = [
-                (l * moms + k, (l ^ (a if k == 0 else b)) * moms + k)
-                for l in range(layers)
-                for k in range(moms)
-            ]
-            received.append(lax.ppermute(slot, ("len", "mom"), pairs))
-        return received
-
-    couplings = exchange([coupling[0]] * layers)
-    g = pl.pallas_call(
+    def exchange(slots, i):
+        if i == 0:
+            return slots[0]
+        pairs = []
+        for l in range(layers):
+            for k in range(moms):
+                peer = l ^ (first, second)[k][i - 1]
+                pairs.append((l * moms + k, peer * moms + k))
+        return lax.ppermute(slots[i], ("len", "mom"), pairs)
+
+    anywhere = pl.BlockSpec(memory_space=pltpu.HBM)
+    sent = pl.pallas_call(
         functools.partial(inverse_kernel, total),
-        out_shape=[part] * layers,
-        in_specs=whole(2),
+        out_shape=[jax.ShapeDtypeStruct((2 * per + 1, n, n), F32)] * layers,
+        in_specs=[anywhere] * 4,
         out_specs=whole(layers),
+        scratch_shapes=[
+            pltpu.VMEM((2, n, n), F32),
+            pltpu.VMEM((layers, per, 2, n, n), F32),
+            pltpu.VMEM((n, n), F32),
+            pltpu.VMEM((n, n), jnp.int32),
+            pltpu.SemaphoreType.DMA((layers + 3,)),
+        ],
         compiler_params=params(),
         name="inverse",
-    )(hamiltonian[0, 0], sigma_prev[0, 0])
-    y = pl.pallas_call(
+    )(
+        *(
+            pltpu.with_memory_space_constraint(value, pltpu.HBM)
+            for value in (hamiltonian[0, 0], sigma_prev[0, 0], coupling[0], coupling_pattern)
+        )
+    )
+    sent = pl.pallas_call(
         functools.partial(chain_kernel, layers),
         out_shape=[part] * layers,
-        in_specs=whole(2 * layers + 1),
+        in_specs=whole(layers),
         out_specs=whole(layers),
         scratch_shapes=[pltpu.VMEM((layers, per, 2, n, n), F32), pltpu.VMEM((layers, n, n), F32)],
         compiler_params=params(),
         name="chains",
-    )(*exchange(g), *couplings, coupling_pattern)
-    y = pl.pallas_call(
-        pack_kernel,
-        out_shape=block,
-        in_specs=whole(layers),
-        out_specs=whole(1)[0],
-        compiler_params=params(),
-        name="pack",
-    )(*exchange(y))
-    swapped = lax.ppermute(y, "mom", [(k, moms - 1 - k) for k in range(moms)])
-    zero, one = pl.pallas_call(
-        momenta_kernel,
-        out_shape=[block] * 2,
-        in_specs=whole(2),
-        out_specs=whole(2),
-        compiler_params=params(),
-        name="momenta",
-    )(y, swapped)
+    )(*[exchange(sent, i) for i in range(layers)])
+    def swap(value):
+        return lax.ppermute(value, "mom", [(k, moms - 1 - k) for k in range(moms)])
 
     reach = -(-(total // 2) // local_e)
-    up_down = []
-    down_up = []
-    for z in range(count - 1):
-        low, high = z * moms, (z + 1) * moms
-        up_down += [(low, high), (high + 1, low + 1)]
-        down_up += [(high, low), (low + 1, high + 1)]
-    zeros = [zero]
-    ones = [one]
-    for d in range(1, reach + 1):
-        zeros.append(lax.ppermute(zeros[-1], ("energy", "mom"), up_down))
-        ones.append(lax.ppermute(ones[-1], ("energy", "mom"), down_up))
+
+    def hop(value, d, role):
+        pairs = []
+        for z in range(count - 1):
+            low, high = z * moms, (z + 1) * moms
+            if z >= d - 1:
+                pairs.append((low + role, high + role))
+            if z <= count - 1 - d:
+                pairs.append((high + 1 - role, low + 1 - role))
+        return lax.ppermute(value, ("energy", "mom"), pairs)
+
+    chunks = 2
+    each = layers // chunks
+    piece = jax.ShapeDtypeStruct((each * per, 2, n, n), F32)
+    by_chunk = []
+    zeros = [[], []]
+    ones = [[], []]
+    after = swap(sent[0])
+    swapped = [after]
+    for c in range(chunks):
+        now = range(c * each, (c + 1) * each)
+        if c == 0:
+            own = [exchange(sent, i) for i in now]
+            swapped += [swap(value) for value in own[1:]]
+        else:
+            own = [exchange(sent, i) for i in now]
+            own, _ = lax.optimization_barrier((own, by_chunk[-1]))
+            own = [
+                pl.pallas_call(
+                    pack_kernel,
+                    out_shape=piece,
+                    in_specs=whole(each),
+                    out_specs=whole(1)[0],
+                    compiler_params=params(),
+                    name="pack",
+                )(*own)
+            ]
+            swapped = [swap(value) for value in own]
+        by_chunk.append(
+            pl.pallas_call(
+                momenta_kernel,
+                out_shape=[piece] * 2,
+                in_specs=whole(2 * len(own)),
+                out_specs=whole(2),
+                compiler_params=params(),
+                name="momenta",
+            )(*own, *swapped)
+        )
+        zero, one = by_chunk[-1]
+        if c > 0:
+            zero, _ = lax.optimization_barrier((zero, zeros[1][-1]))
+            one, _ = lax.optimization_barrier((one, ones[1][-1]))
+        zeros[0].append(zero)
+        ones[0].append(one)
+        zeros[1].append(hop(zero, 1, 0))
+        ones[1].append(hop(one, 1, 1))
+        if c == 0:
+            later, _ = lax.optimization_barrier((sent[each:], after))
+            sent = list(sent[:each]) + list(later)
+
+    for d in range(2, reach + 1):
+        zeros.append([hop(value, d, 0) for value in zeros[-1]])
+        ones.append([hop(value, d, 1) for value in ones[-1]])
 
     groups = [(0, 1)] + [
         tuple(range(d, min(d + 4, reach + 1))) for d in range(2, reach + 1, 4)
@@ -319,12 +395,13 @@
     smem = pl.BlockSpec(memory_space=pltpu.SMEM)
     sums = []
     for i, group in enumerate(groups):
-        blocks = [zeros[d] for d in group] + [ones[d] for d in group] + list(sums)
+        blocks = sum([zeros[d] for d in group] + [ones[d] for d in group], []) + list(sums)
         sums = pl.pallas_call(
-            functools.partial(mix_kernel, total, group, i == 0, i == len(groups) - 1),
+            functools.partial(mix_kernel, total, group, chunks, i == 0, i == len(groups) - 1),
             out_shape=[block] * 2,
             in_specs=[smem, smem] + whole(len(blocks)),
             out_specs=whole(2),
+            scratch_shapes=[pltpu.VMEM((len(group),) + block.shape, F32)] * 2,
             compiler_params=params(),
             name="mix",
         )(phonon_shift, phonon_weight, *blocks)

time: 65.8 us -> 66.5 us (1.011)
  Pallas kernels: 7.59 us -> 9.99 us
  local copies, waits for them, and re-layouts: 1.96 us -> 0.01 us
    pallas_call x5 -> x6, Pallas kernels: 5.36 us -> 7.77 us  [the longest x1 4.1 us: shards(): pl.pallas_call(functools.partial(inverse_kernel, total), out_shape=[jax.S...]
    unnamed x12 -> x4, local copies, waits for them, and re-layouts: 1.96 us -> 0.01 us
    ppermute x14 -> x17, waiting for transfers between devices: 29.7 us -> 29.8 us  [the longest x6 17.2 us: exchange(): return lax.ppermute(slots[i], ('len', 'mom'), pairs)]
    ppermute x14 -> x17, starting transfers between devices: 25.3 us -> 25.3 us  [the longest x8 15.7 us: hop(): return lax.ppermute(value, ('energy', 'mom'), pairs)]
  transfers between devices with their start and end apart: 14 -> 17, of which waited for: 9 -> 10; matrix products, arithmetic and copies ran while one was open for 0% -> 0% of each run, Pallas kernels for 2% -> 2%
where the time goes in v2:
time: 66.5 us; the launch traced here: 65.9 us
  waiting for transfers between devices  29.8 us (45%)
  starting transfers between devices  25.3 us (38%)
  Pallas kernels  9.99 us (15%)
  between operations  0.79 us (1%)
    ppermute x6, waiting for transfers between devices, exchange(): return lax.ppermute(slots[i], ('len', 'mom'), pairs)  17.2 us
    ppermute x8, starting transfers between devices, hop(): return lax.ppermute(value, ('energy', 'mom'), pairs)  15.7 us
    ppermute x8, waiting for transfers between devices, hop(): return lax.ppermute(value, ('energy', 'mom'), pairs)  12.6 us
    ppermute x6, starting transfers between devices, exchange(): return lax.ppermute(slots[i], ('len', 'mom'), pairs)  9.36 us
    pallas_call x1, Pallas kernels, shards(): pl.pallas_call(functools.partial(inverse_kernel, total), out_shape=[jax.S...  4.1 us
    pallas_call x2, Pallas kernels, shards(): pl.pallas_call(functools.partial(mix_kernel, total, group, chunks, i == 0...  3.57 us
    pallas_call x1, Pallas kernels, shards(): pl.pallas_call(functools.partial(chain_kernel, layers), out_shape=[part]...  2.22 us
  transfers between devices with their start and end apart: 17, of which 10 were waited for; matrix products, arithmetic and copies ran while one was open for 0% of the time, Pallas kernels for 2%

profile of v2, /device:TPU:0, one launch (start us, length us, event | category | flops | bytes accessed | tf_op | source)
XLA Modules:
  0.0 65.9 jit_solution(16963938289887988647)
XLA Ops:
  0.6 4.1 %inverse.1 = (f32[3,128,128]{2,1,0:T(8,128)S(1)}, f32[3,128,128]{2,1,0:T(8,128)S(1)}, f32[3,128,128]{2,1,0:T(8,128)S(1)}, f32[3,128,128]{2,1,0:T(8,128)S(1)}) custom-call(f32[2,128,128]{2,1,0:T(8,128)} %bitcast.6, f32[4,2,128,128]{3,2,1,0:T(8,128)} %bitcast.5, f32[128,128]{1,0:T(8,128)} %bitcast.7, s32[128,128]{1,0:T(8,128)} %pattern_any.1), custom_call_target="tpu_custom_call" | custom-call | tf_op jit(solution)/shard_map/inverse/pallas_call | solution.py:295
  4.7 3.0 %collective-permute-start = (f32[3,128,128]{2,1,0:T(8,128)S(1)}, f32[3,128,128]{2,1,0:T(8,128)S(1)}, u32[]{:S(2)}, u32[]{:S(2)}) collective-permute-start(f32[3,128,128]{2,1,0:T(8,128)S(1)} %get-tuple-element.25), channel_id=1, source_target_pairs={{0,8},{1,17},{8,0},{9,25},{16,24},{17,1},{24,16},{25,9},{2,10},{3,... | collective-permute-start | bytes 589832 | tf_op jit(solution)/shard_map/ppermute | solution.py:292
  7.7 1.5 %collective-permute-start.1 = (f32[3,128,128]{2,1,0:T(8,128)S(1)}, f32[3,128,128]{2,1,0:T(8,128)S(1)}, u32[]{:S(2)}, u32[]{:S(2)}) collective-permute-start(f32[3,128,128]{2,1,0:T(8,128)S(1)} %get-tuple-element.26), channel_id=1, source_target_pairs={{0,16},{1,9},{8,24},{9,1},{16,0},{17,25},{24,8},{25,17},{2,18},{3,... | collective-permute-start | bytes 589832 | tf_op jit(solution)/shard_map/ppermute | solution.py:292
  9.3 0.0 collective-permute-start.2
  9.3 3.6 %collective-permute-done.refs_1_ = f32[3,128,128]{2,1,0:T(8,128)S(1)} collective-permute-done((f32[3,128,128]{2,1,0:T(8,128)S(1)}, f32[3,128,128]{2,1,0:T(8,128)S(1)}, u32[]{:S(2)}, u32[]{:S(2)}) %collective-permute-start) | collective-permute-done | bytes 196640 | tf_op jit(solution)/shard_map/ppermute | solution.py:292
  12.9 1.0 %collective-permute-done.1.refs_2_ = f32[3,128,128]{2,1,0:T(8,128)S(1)} collective-permute-done((f32[3,128,128]{2,1,0:T(8,128)S(1)}, f32[3,128,128]{2,1,0:T(8,128)S(1)}, u32[]{:S(2)}, u32[]{:S(2)}) %collective-permute-start.1) | collective-permute-done | bytes 196640 | tf_op jit(solution)/shard_map/ppermute | solution.py:292
  14.0 4.2 %collective-permute-done.2.refs_3_ = f32[3,128,128]{2,1,0:T(8,128)S(1)} collective-permute-done((f32[3,128,128]{2,1,0:T(8,128)S(1)}, f32[3,128,128]{2,1,0:T(8,128)S(1)}, u32[]{:S(2)}, u32[]{:S(2)}) %collective-permute-start.2) | collective-permute-done | bytes 196640 | tf_op jit(solution)/shard_map/ppermute | solution.py:292
  18.1 2.2 %chains.1 = (f32[1,2,128,128]{3,2,1,0:T(8,128)S(1)}, f32[1,2,128,128]{3,2,1,0:T(8,128)S(1)}, f32[1,2,128,128]{3,2,1,0:T(8,128)S(1)}, f32[1,2,128,128]{3,2,1,0:T(8,128)S(1)}) custom-call(f32[3,128,128]{2,1,0:T(8,128)S(1)} %get-tuple-element.24.refs_0_, f32[3,128,128]{2,1,0:T(8,128)S(1)} %collective-permute-done.refs_1_, ...), custom_call_target="tpu_custom_call" | custom-call | tf_op jit(solution)/shard_map/chains/pallas_call | solution.py:315
  20.4 0.1 collective-permute-start.4
  20.4 1.7 %collective-permute-start.3 = (f32[1,2,128,128]{3,2,1,0:T(8,128)S(1)}, f32[1,2,128,128]{3,2,1,0:T(8,128)S(1)}, u32[]{:S(2)}, u32[]{:S(2)}) collective-permute-start(f32[1,2,128,128]{3,2,1,0:T(8,128)S(1)} %get-tuple-element.29), channel_id=1, source_target_pairs={{0,8},{1,17},{8,0},{9,25},{16,24},{17,1},{24,16},{25,9},{2,10},{3,... | collective-permute-start | bytes 393224 | tf_op jit(solution)/shard_map/ppermute | solution.py:292
  22.2 3.3 %collective-permute-done.3.refs_1_ = f32[1,2,128,128]{3,2,1,0:T(8,128)S(1)} collective-permute-done((f32[1,2,128,128]{3,2,1,0:T(8,128)S(1)}, f32[1,2,128,128]{3,2,1,0:T(8,128)S(1)}, u32[]{:S(2)}, u32[]{:S(2)}) %collective-permute-start.3) | collective-permute-done | bytes 131104 | tf_op jit(solution)/shard_map/ppermute | solution.py:292
  25.5 0.0 collective-permute-start.5
  25.5 1.0 %collective-permute-start.8 = (f32[1,2,128,128]{3,2,1,0:T(8,128)S(1)}, f32[1,2,128,128]{3,2,1,0:T(8,128)S(1)}, u32[]{:S(2)}, u32[]{:S(2)}) collective-permute-start(f32[1,2,128,128]{3,2,1,0:T(8,128)S(1)} %get-tuple-element.33), channel_id=1, source_target_pairs={{0,16},{1,9},{8,24},{9,1},{16,0},{17,25},{24,8},{25,17},{2,18},{3,... | collective-permute-start | bytes 393224 | tf_op jit(solution)/shard_map/ppermute | solution.py:292
  26.4 2.2 %collective-permute-start.9 = (f32[1,2,128,128]{3,2,1,0:T(8,128)S(1)}, f32[1,2,128,128]{3,2,1,0:T(8,128)S(1)}, u32[]{:S(2)}, u32[]{:S(2)}) collective-permute-start(f32[1,2,128,128]{3,2,1,0:T(8,128)S(1)} %get-tuple-element.34), channel_id=1, source_target_pairs={{0,24},{1,25},{8,16},{9,17},{16,8},{17,9},{24,0},{25,1},{2,26},{3,... | collective-permute-start | bytes 393224 | tf_op jit(solution)/shard_map/ppermute | solution.py:292
  28.6 1.8 %collective-permute-done.8.refs_0_ = f32[1,2,128,128]{3,2,1,0:T(8,128)S(1)} collective-permute-done((f32[1,2,128,128]{3,2,1,0:T(8,128)S(1)}, f32[1,2,128,128]{3,2,1,0:T(8,128)S(1)}, u32[]{:S(2)}, u32[]{:S(2)}) %collective-permute-start.8) | collective-permute-done | bytes 131104 | tf_op jit(solution)/shard_map/ppermute | solution.py:292
  30.5 3.2 %collective-permute-done.9.refs_1_ = f32[1,2,128,128]{3,2,1,0:T(8,128)S(1)} collective-permute-done((f32[1,2,128,128]{3,2,1,0:T(8,128)S(1)}, f32[1,2,128,128]{3,2,1,0:T(8,128)S(1)}, u32[]{:S(2)}, u32[]{:S(2)}) %collective-permute-start.9) | collective-permute-done | bytes 131104 | tf_op jit(solution)/shard_map/ppermute | solution.py:292
  33.7 0.1 collective-permute-start.10
  33.8 1.3 %collective-permute-start.13 = (f32[2,2,128,128]{3,2,1,0:T(8,128)S(1)}, f32[2,2,128,128]{3,2,1,0:T(8,128)S(1)}, u32[]{:S(2)}, u32[]{:S(2)}) collective-permute-start(f32[2,2,128,128]{3,2,1,0:T(8,128)S(1)} %get-tuple-element.35.refs_4_), channel_id=1, source_target_pairs={{1,3},{2,0},{3,5},{4,2},{5,7},{6,4},{9,11},{10,8},{11,13},{12,10},... | collective-permute-start | bytes 786440 | tf_op jit(solution)/shard_map/ppermute | solution.py:337
  35.1 4.6 %collective-permute-start.6 = (f32[2,2,128,128]{3,2,1,0:T(8,128)S(1)}, f32[2,2,128,128]{3,2,1,0:T(8,128)S(1)}, u32[]{:S(2)}, u32[]{:S(2)}) collective-permute-start(f32[2,2,128,128]{3,2,1,0:T(8,128)S(1)} %get-tuple-element.30.refs_0_), channel_id=1, source_target_pairs={{0,2},{3,1},{2,4},{5,3},{4,6},{7,5},{8,10},{11,9},{10,12},{13,11},... | collective-permute-start | bytes 786440 | tf_op jit(solution)/shard_map/ppermute | solution.py:337
  39.7 2.3 %collective-permute-done.13.refs_6_ = f32[2,2,128,128]{3,2,1,0:T(8,128)S(1)} collective-permute-done((f32[2,2,128,128]{3,2,1,0:T(8,128)S(1)}, f32[2,2,128,128]{3,2,1,0:T(8,128)S(1)}, u32[]{:S(2)}, u32[]{:S(2)}) %collective-permute-start.13) | collective-permute-done | bytes 262176 | tf_op jit(solution)/shard_map/ppermute | solution.py:337
  42.1 1.4 %collective-permute-start.15 = (f32[2,2,128,128]{3,2,1,0:T(8,128)S(1)}, f32[2,2,128,128]{3,2,1,0:T(8,128)S(1)}, u32[]{:S(2)}, u32[]{:S(2)}) collective-permute-start(f32[2,2,128,128]{3,2,1,0:T(8,128)S(1)} %get-tuple-element.41.refs_5_), channel_id=1, source_target_pairs={{1,3},{2,0},{3,5},{4,2},{5,7},{6,4},{9,11},{10,8},{11,13},{12,10},... | collective-permute-start | bytes 786440 | tf_op jit(solution)/shard_map/ppermute | solution.py:337
  43.5 0.0 collective-permute-done.6.refs_2_
  43.5 4.5 %collective-permute-start.11 = (f32[2,2,128,128]{3,2,1,0:T(8,128)S(1)}, f32[2,2,128,128]{3,2,1,0:T(8,128)S(1)}, u32[]{:S(2)}, u32[]{:S(2)}) collective-permute-start(f32[2,2,128,128]{3,2,1,0:T(8,128)S(1)} %get-tuple-element.39.refs_1_), channel_id=1, source_target_pairs={{0,2},{3,1},{2,4},{5,3},{4,6},{7,5},{8,10},{11,9},{10,12},{13,11},... | collective-permute-start | bytes 786440 | tf_op jit(solution)/shard_map/ppermute | solution.py:337
  48.1 1.3 %collective-permute-start.14 = (f32[2,2,128,128]{3,2,1,0:T(8,128)S(1)}, f32[2,2,128,128]{3,2,1,0:T(8,128)S(1)}, u32[]{:S(2)}, u32[]{:S(2)}) collective-permute-start(f32[2,2,128,128]{3,2,1,0:T(8,128)S(1)} %collective-permute-done.13.refs_6_), channel_id=1, source_target_pairs={{2,0},{3,5},{4,2},{5,7},{10,8},{11,13},{12,10},{13,15},{18,16},{19... | collective-permute-start | bytes 786440 | tf_op jit(solution)/shard_map/ppermute | solution.py:337
  49.4 0.7 %collective-permute-start.7 = (f32[2,2,128,128]{3,2,1,0:T(8,128)S(1)}, f32[2,2,128,128]{3,2,1,0:T(8,128)S(1)}, u32[]{:S(2)}, u32[]{:S(2)}) collective-permute-start(f32[2,2,128,128]{3,2,1,0:T(8,128)S(1)} %collective-permute-done.6.refs_2_), channel_id=1, source_target_pairs={{3,1},{2,4},{5,3},{4,6},{11,9},{10,12},{13,11},{12,14},{19,17},{18... | collective-permute-start | bytes 786440 | tf_op jit(solution)/shard_map/ppermute | solution.py:337
  50.0 1.2 %collective-permute-done.15.refs_7_ = f32[2,2,128,128]{3,2,1,0:T(8,128)S(1)} collective-permute-done((f32[2,2,128,128]{3,2,1,0:T(8,128)S(1)}, f32[2,2,128,128]{3,2,1,0:T(8,128)S(1)}, u32[]{:S(2)}, u32[]{:S(2)}) %collective-permute-start.15) | collective-permute-done | bytes 262176 | tf_op jit(solution)/shard_map/ppermute | solution.py:337
  51.3 1.3 %collective-permute-start.16 = (f32[2,2,128,128]{3,2,1,0:T(8,128)S(1)}, f32[2,2,128,128]{3,2,1,0:T(8,128)S(1)}, u32[]{:S(2)}, u32[]{:S(2)}) collective-permute-start(f32[2,2,128,128]{3,2,1,0:T(8,128)S(1)} %collective-permute-done.15.refs_7_), channel_id=1, source_target_pairs={{2,0},{3,5},{4,2},{5,7},{10,8},{11,13},{12,10},{13,15},{18,16},{19... | collective-permute-start | bytes 786440 | tf_op jit(solution)/shard_map/ppermute | solution.py:337
  52.6 0.7 %collective-permute-start.12 = (f32[2,2,128,128]{3,2,1,0:T(8,128)S(1)}, f32[2,2,128,128]{3,2,1,0:T(8,128)S(1)}, u32[]{:S(2)}, u32[]{:S(2)}) collective-permute-start(f32[2,2,128,128]{3,2,1,0:T(8,128)S(1)} %collective-permute-done.11.refs_3_), channel_id=1, source_target_pairs={{3,1},{2,4},{5,3},{4,6},{11,9},{10,12},{13,11},{12,14},{19,17},{18... | collective-permute-start | bytes 786440 | tf_op jit(solution)/shard_map/ppermute | solution.py:337
  53.3 1.5 %mix.2 = (f32[4,2,128,128]{3,2,1,0:T(8,128)S(1)}, f32[4,2,128,128]{3,2,1,0:T(8,128)S(1)}) custom-call(s32[4]{0:T(128)S(1)} %copy-done, f32[4]{0:T(128)S(1)} %copy-done.1, f32[2,2,128,128]{3,2,1,0:T(8,128)S(1)} %get-tuple-element.30.refs_0_, f32[2,2,128,128]{3,2,1,0:T(8,128)S(1)} %get-tuple-element.39.refs_1_, ...), custom_call_target="tpu_custom_call" | custom-call | tf_op jit(solution)/shard_map/mix/pallas_call | solution.py:399
  54.8 3.1 %collective-permute-done.14.refs_2_ = f32[2,2,128,128]{3,2,1,0:T(8,128)S(1)} collective-permute-done((f32[2,2,128,128]{3,2,1,0:T(8,128)S(1)}, f32[2,2,128,128]{3,2,1,0:T(8,128)S(1)}, u32[]{:S(2)}, u32[]{:S(2)}) %collective-permute-start.14) | collective-permute-done | bytes 262176 | tf_op jit(solution)/shard_map/ppermute | solution.py:337
  57.9 5.9 %collective-permute-done.16.refs_3_ = f32[2,2,128,128]{3,2,1,0:T(8,128)S(1)} collective-permute-done((f32[2,2,128,128]{3,2,1,0:T(8,128)S(1)}, f32[2,2,128,128]{3,2,1,0:T(8,128)S(1)}, u32[]{:S(2)}, u32[]{:S(2)}) %collective-permute-start.16) | collective-permute-done | bytes 262176 | tf_op jit(solution)/shard_map/ppermute | solution.py:337
  63.8 2.0 %mix.3 = (f32[4,2,128,128]{3,2,1,0:T(8,128)}, f32[4,2,128,128]{3,2,1,0:T(8,128)}) custom-call(s32[4]{0:T(128)S(1)} %copy-done, f32[4]{0:T(128)S(1)} %copy-done.1, f32[2,2,128,128]{3,2,1,0:T(8,128)S(1)} %collective-permute-done.7.refs_0_, f32[2,2,128,128]{3,2,1,0:T(8,128)S(1)} %collective-permute-done.12.refs_1_, ...), custom_call_target="tpu_custom_call" | custom-call | tf_op jit(solution)/shard_map/mix/pallas_call | solution.py:399
  (13 shorter events, 0.1 us)
Async XLA Ops:
  4.7 8.2 %collective-permute-start = (f32[3,128,128]{2,1,0:T(8,128)S(1)}, f32[3,128,128]{2,1,0:T(8,128)S(1)}, u32[]{:S(2)}, u32[]{:S(2)}) collective-permute-start(f32[3,128,128]{2,1,0:T(8,128)S(1)} %get-tuple-element.25), channel_id=1, source_target_pairs={{0,8},{1,17},{8,0},{9,25},{16,24},{17,1},{24,16},{25,9},{2,10},{3,... | collective-permute-start | bytes 589832 | tf_op jit(solution)/shard_map/ppermute | solution.py:292
  7.7 6.2 %collective-permute-start.1 = (f32[3,128,128]{2,1,0:T(8,128)S(1)}, f32[3,128,128]{2,1,0:T(8,128)S(1)}, u32[]{:S(2)}, u32[]{:S(2)}) collective-permute-start(f32[3,128,128]{2,1,0:T(8,128)S(1)} %get-tuple-element.26), channel_id=1, source_target_pairs={{0,16},{1,9},{8,24},{9,1},{16,0},{17,25},{24,8},{25,17},{2,18},{3,... | collective-permute-start | bytes 589832 | tf_op jit(solution)/shard_map/ppermute | solution.py:292
  9.3 8.9 %collective-permute-start.2 = (f32[3,128,128]{2,1,0:T(8,128)S(1)}, f32[3,128,128]{2,1,0:T(8,128)S(1)}, u32[]{:S(2)}, u32[]{:S(2)}) collective-permute-start(f32[3,128,128]{2,1,0:T(8,128)S(1)} %get-tuple-element.27), channel_id=1, source_target_pairs={{0,24},{1,25},{8,16},{9,17},{16,8},{17,9},{24,0},{25,1},{2,26},{3,... | collective-permute-start | bytes 589832 | tf_op jit(solution)/shard_map/ppermute | solution.py:292
  20.4 1.8 %collective-permute-start.4 = (f32[1,2,128,128]{3,2,1,0:T(8,128)S(1)}, f32[1,2,128,128]{3,2,1,0:T(8,128)S(1)}, u32[]{:S(2)}, u32[]{:S(2)}) collective-permute-start(f32[1,2,128,128]{3,2,1,0:T(8,128)S(1)} %get-tuple-element.28.refs_0_), channel_id=1, source_target_pairs={{0,1},{1,0},{2,3},{3,2},{4,5},{5,4},{6,7},{7,6},{8,9},{9,8},{10,11... | collective-permute-start | bytes 393224 | tf_op jit(solution)/shard_map/ppermute | solution.py:325
  20.4 5.0 %collective-permute-start.3 = (f32[1,2,128,128]{3,2,1,0:T(8,128)S(1)}, f32[1,2,128,128]{3,2,1,0:T(8,128)S(1)}, u32[]{:S(2)}, u32[]{:S(2)}) collective-permute-start(f32[1,2,128,128]{3,2,1,0:T(8,128)S(1)} %get-tuple-element.29), channel_id=1, source_target_pairs={{0,8},{1,17},{8,0},{9,25},{16,24},{17,1},{24,16},{25,9},{2,10},{3,... | collective-permute-start | bytes 393224 | tf_op jit(solution)/shard_map/ppermute | solution.py:292
  25.5 3.1 %collective-permute-start.5 = (f32[1,2,128,128]{3,2,1,0:T(8,128)S(1)}, f32[1,2,128,128]{3,2,1,0:T(8,128)S(1)}, u32[]{:S(2)}, u32[]{:S(2)}) collective-permute-start(f32[1,2,128,128]{3,2,1,0:T(8,128)S(1)} %collective-permute-done.3.refs_1_), channel_id=1, source_target_pairs={{0,1},{1,0},{2,3},{3,2},{4,5},{5,4},{6,7},{7,6},{8,9},{9,8},{10,11... | collective-permute-start | bytes 393224 | tf_op jit(solution)/shard_map/ppermute | solution.py:325
  25.5 5.0 %collective-permute-start.8 = (f32[1,2,128,128]{3,2,1,0:T(8,128)S(1)}, f32[1,2,128,128]{3,2,1,0:T(8,128)S(1)}, u32[]{:S(2)}, u32[]{:S(2)}) collective-permute-start(f32[1,2,128,128]{3,2,1,0:T(8,128)S(1)} %get-tuple-element.33), channel_id=1, source_target_pairs={{0,16},{1,9},{8,24},{9,1},{16,0},{17,25},{24,8},{25,17},{2,18},{3,... | collective-permute-start | bytes 393224 | tf_op jit(solution)/shard_map/ppermute | solution.py:292
  26.4 7.2 %collective-permute-start.9 = (f32[1,2,128,128]{3,2,1,0:T(8,128)S(1)}, f32[1,2,128,128]{3,2,1,0:T(8,128)S(1)}, u32[]{:S(2)}, u32[]{:S(2)}) collective-permute-start(f32[1,2,128,128]{3,2,1,0:T(8,128)S(1)} %get-tuple-element.34), channel_id=1, source_target_pairs={{0,24},{1,25},{8,16},{9,17},{16,8},{17,9},{24,0},{25,1},{2,26},{3,... | collective-permute-start | bytes 393224 | tf_op jit(solution)/shard_map/ppermute | solution.py:292
  33.7 6.0 %collective-permute-start.10 = (f32[2,2,128,128]{3,2,1,0:T(8,128)S(1)}, f32[2,2,128,128]{3,2,1,0:T(8,128)S(1)}, u32[]{:S(2)}, u32[]{:S(2)}) collective-permute-start(f32[2,2,128,128]{3,2,1,0:T(8,128)S(1)} %pack.1.refs_0_), channel_id=1, source_target_pairs={{0,1},{1,0},{2,3},{3,2},{4,5},{5,4},{6,7},{7,6},{8,9},{9,8},{10,11... | collective-permute-start | bytes 786440 | tf_op jit(solution)/shard_map/ppermute | solution.py:325
  33.8 8.3 %collective-permute-start.13 = (f32[2,2,128,128]{3,2,1,0:T(8,128)S(1)}, f32[2,2,128,128]{3,2,1,0:T(8,128)S(1)}, u32[]{:S(2)}, u32[]{:S(2)}) collective-permute-start(f32[2,2,128,128]{3,2,1,0:T(8,128)S(1)} %get-tuple-element.35.refs_4_), channel_id=1, source_target_pairs={{1,3},{2,0},{3,5},{4,2},{5,7},{6,4},{9,11},{10,8},{11,13},{12,10},... | collective-permute-start | bytes 786440 | tf_op jit(solution)/shard_map/ppermute | solution.py:337
  35.1 8.4 %collective-permute-start.6 = (f32[2,2,128,128]{3,2,1,0:T(8,128)S(1)}, f32[2,2,128,128]{3,2,1,0:T(8,128)S(1)}, u32[]{:S(2)}, u32[]{:S(2)}) collective-permute-start(f32[2,2,128,128]{3,2,1,0:T(8,128)S(1)} %get-tuple-element.30.refs_0_), channel_id=1, source_target_pairs={{0,2},{3,1},{2,4},{5,3},{4,6},{7,5},{8,10},{11,9},{10,12},{13,11},... | collective-permute-start | bytes 786440 | tf_op jit(solution)/shard_map/ppermute | solution.py:337
  42.1 11.2 %copy-start = (s32[4]{0:T(128)S(1)}, s32[4]{0:T(128)}, u32[]{:S(2)}) copy-start(s32[4]{0:T(128)} %shift_ref.3) | copy-start | bytes 52
  42.1 11.2 %copy-start.1 = (f32[4]{0:T(128)S(1)}, f32[4]{0:T(128)}, u32[]{:S(2)}) copy-start(f32[4]{0:T(128)} %weight_ref.3) | copy-start | bytes 52
  42.1 9.2 %collective-permute-start.15 = (f32[2,2,128,128]{3,2,1,0:T(8,128)S(1)}, f32[2,2,128,128]{3,2,1,0:T(8,128)S(1)}, u32[]{:S(2)}, u32[]{:S(2)}) collective-permute-start(f32[2,2,128,128]{3,2,1,0:T(8,128)S(1)} %get-tuple-element.41.refs_5_), channel_id=1, source_target_pairs={{1,3},{2,0},{3,5},{4,2},{5,7},{6,4},{9,11},{10,8},{11,13},{12,10},... | collective-permute-start | bytes 786440 | tf_op jit(solution)/shard_map/ppermute | solution.py:337
  43.5 9.0 %collective-permute-start.11 = (f32[2,2,128,128]{3,2,1,0:T(8,128)S(1)}, f32[2,2,128,128]{3,2,1,0:T(8,128)S(1)}, u32[]{:S(2)}, u32[]{:S(2)}) collective-permute-start(f32[2,2,128,128]{3,2,1,0:T(8,128)S(1)} %get-tuple-element.39.refs_1_), channel_id=1, source_target_pairs={{0,2},{3,1},{2,4},{5,3},{4,6},{7,5},{8,10},{11,9},{10,12},{13,11},... | collective-permute-start | bytes 786440 | tf_op jit(solution)/shard_map/ppermute | solution.py:337
  48.1 9.9 %collective-permute-start.14 = (f32[2,2,128,128]{3,2,1,0:T(8,128)S(1)}, f32[2,2,128,128]{3,2,1,0:T(8,128)S(1)}, u32[]{:S(2)}, u32[]{:S(2)}) collective-permute-start(f32[2,2,128,128]{3,2,1,0:T(8,128)S(1)} %collective-permute-done.13.refs_6_), channel_id=1, source_target_pairs={{2,0},{3,5},{4,2},{5,7},{10,8},{11,13},{12,10},{13,15},{18,16},{19... | collective-permute-start | bytes 786440 | tf_op jit(solution)/shard_map/ppermute | solution.py:337
  49.4 8.6 %collective-permute-start.7 = (f32[2,2,128,128]{3,2,1,0:T(8,128)S(1)}, f32[2,2,128,128]{3,2,1,0:T(8,128)S(1)}, u32[]{:S(2)}, u32[]{:S(2)}) collective-permute-start(f32[2,2,128,128]{3,2,1,0:T(8,128)S(1)} %collective-permute-done.6.refs_2_), channel_id=1, source_target_pairs={{3,1},{2,4},{5,3},{4,6},{11,9},{10,12},{13,11},{12,14},{19,17},{18... | collective-permute-start | bytes 786440 | tf_op jit(solution)/shard_map/ppermute | solution.py:337
  51.3 12.6 %collective-permute-start.16 = (f32[2,2,128,128]{3,2,1,0:T(8,128)S(1)}, f32[2,2,128,128]{3,2,1,0:T(8,128)S(1)}, u32[]{:S(2)}, u32[]{:S(2)}) collective-permute-start(f32[2,2,128,128]{3,2,1,0:T(8,128)S(1)} %collective-permute-done.15.refs_7_), channel_id=1, source_target_pairs={{2,0},{3,5},{4,2},{5,7},{10,8},{11,13},{12,10},{13,15},{18,16},{19... | collective-permute-start | bytes 786440 | tf_op jit(solution)/shard_map/ppermute | solution.py:337
  52.6 11.3 %collective-permute-start.12 = (f32[2,2,128,128]{3,2,1,0:T(8,128)S(1)}, f32[2,2,128,128]{3,2,1,0:T(8,128)S(1)}, u32[]{:S(2)}, u32[]{:S(2)}) collective-permute-start(f32[2,2,128,128]{3,2,1,0:T(8,128)S(1)} %collective-permute-done.11.refs_3_), channel_id=1, source_target_pairs={{3,1},{2,4},{5,3},{4,6},{11,9},{10,12},{13,11},{12,14},{19,17},{18... | collective-permute-start | bytes 786440 | tf_op jit(solution)/shard_map/ppermute | solution.py:337

commit v3 on v1

--- a/solution.py
+++ b/solution.py
@@ -44,30 +44,28 @@
     return (rows == cols).astype(F32)
 
 
-def orders(layers):
-    first = list(range(1, layers))
-    second = list(first)
-    if layers > 2:
-        second[0], second[1] = second[1], second[0]
-    return first, second
-
-
-def peers(layers):
-    here = lax.axis_index("len")
-    core = lax.axis_index("mom")
-    first, second = orders(layers)
-    return [here] + [here ^ jnp.where(core == 0, a, b) for a, b in zip(first, second)]
-
-
-def inverse_kernel(total, ham_ref, sig_ref, *out_refs):
+def inverse_kernel(total, ham_any, sig_any, coupling_any, pattern_any, out_ref, *refs):
+    buffers, sems = refs[:-1], refs[-1]
+    sources = (ham_any, sig_any, coupling_any, pattern_any)
+    copies = [
+        pltpu.make_async_copy(source, buffer, sems.at[i])
+        for i, (source, buffer) in enumerate(zip(sources, buffers))
+    ]
+    for copy in copies:
+        copy.start()
+    for copy in copies:
+        copy.wait()
+    ham_ref, sig_ref, coupling_ref, pattern_ref = buffers
+    layers = out_ref.shape[0]
     local_e, _, n, _ = sig_ref.shape
-    layers = len(out_refs)
     per = local_e // layers
     start = lax.axis_index("energy") * local_e
     eye = identity(n)
-    for out_ref, peer in reversed(list(zip(out_refs, peers(layers)))):
+    bond = coupling_ref[...] * pattern_ref[...].astype(F32)
+    for l in range(layers):
+        out_ref[l, 2 * per] = bond
         for p in range(per):
-            e = peer * per + p
+            e = l * per + p
             pos = jnp.full((1, n), start + e, jnp.int32).astype(F32)
             zre = 5.0 + 2.0 * pos / total
             mag = zre * zre + 1.0
@@ -86,24 +84,20 @@
             s = eye + (a1 + (a2 + a3))
             x = s + dot3(split(s), right_pair(a4))
             re, im = x[:, :n], x[:, n:]
-            out_ref[p, 0] = qre * re - qim * im
-            out_ref[p, 1] = qre * im + qim * re
-
-
-def chain_kernel(layers, *refs):
-    g_slots, coupling_slots = refs[:layers], refs[layers : 2 * layers]
-    pattern_ref = refs[2 * layers]
-    out_slots = refs[2 * layers + 1 : 3 * layers + 1]
-    g_ref, bond_ref = refs[3 * layers + 1 :]
-    _, per, _, n, _ = g_ref.shape
-    mask = pattern_ref[...].astype(F32)
-    for peer, g_slot, coupling_slot in zip(peers(layers), g_slots, coupling_slots):
-        g_ref[peer] = g_slot[...]
-        bond_ref[peer] = coupling_slot[...] * mask
-    bonds = [None] + [bond_ref[l] for l in range(1, layers)]
+            out_ref[l, 2 * p] = qre * re - qim * im
+            out_ref[l, 2 * p + 1] = qre * im + qim * re
+
+
+def chain_kernel(in_ref, out_ref):
+    layers, parts, n, _ = in_ref.shape
+    per = parts // 2
+    bonds = [None] + [in_ref[l, 2 * per] for l in range(1, layers)]
     bonds_t = [None] + [b.T for b in bonds[1:]]
     for p in range(per):
-        g = [jnp.concatenate([g_ref[l, p, 0], g_ref[l, p, 1]], axis=1) for l in range(layers)]
+        g = [
+            jnp.concatenate([in_ref[l, 2 * p], in_ref[l, 2 * p + 1]], axis=1)
+            for l in range(layers)
+        ]
         down = [None] * layers
         up = [None] * layers
         for l in range(layers):
@@ -138,19 +132,8 @@
         for l in range(layers):
             near = [green[m] for m in (l - 1, l + 1) if 0 <= m < layers]
             y = green[l] + 0.5 * sum(near[1:], near[0]) if near else green[l]
-            g_ref[l, p, 0] = y[:, :n]
-            g_ref[l, p, 1] = y[:, n:]
-    for peer, out_slot in zip(peers(layers), out_slots):
-        out_slot[...] = g_ref[peer]
-
-
-def pack_kernel(*refs):
-    slots, out_ref = refs[:-1], refs[-1]
-    per = slots[0].shape[0]
-    for peer, slot in zip(peers(len(slots)), slots):
-        for p in range(per):
-            out_ref[peer * per + p] = slot[p]
-
+            out_ref[l * per + p, 0] = y[:, :n]
+            out_ref[l * per + p, 1] = y[:, n:]
 
 def momenta_kernel(own_ref, other_ref, zero_ref, one_ref):
     core = lax.axis_index("mom")
@@ -173,8 +156,10 @@
 def mix_kernel(total, distances, first, last, shift_ref, weight_ref, *refs):
     count = len(distances)
     blocks = refs[:count], refs[count : 2 * count]
-    sums_in = (None, None) if first else refs[2 * count : 2 * count + 2]
-    ret_ref, les_ref = refs[-2:]
+    inputs = 2 * count + (0 if first else 2)
+    sums_in = refs[2 * count : inputs]
+    results = refs[inputs : inputs + 2]
+    targets = refs[inputs + 2 : inputs + 4] if last else results
     local_e, _, n, _ = blocks[0][0].shape
     phonons = shift_ref.shape[0]
     start = lax.axis_index("energy") * local_e
@@ -188,8 +173,10 @@
             value = value + jnp.where(s == t, w, 0.0)
         return value
 
+    def copy_out(i, a):
+        return pltpu.make_async_copy(targets[i].at[a], results[i].at[a], refs[-1].at[i, a])
+
     def body(own, other):
-        ret_in, les_in = sums_in
         most = total // 2
         coefficients = {}
         for d in distances:
@@ -203,8 +190,12 @@
                 occ_own[d, b] = occupation(start - d * local_e + b, total, n)
                 occ_other[d, b] = occupation(start + d * local_e + b, total, n)
         for a in range(local_e):
-            ret = [jnp.zeros((n, n), F32) if first else ret_in[a, c] for c in range(2)]
-            les = [jnp.zeros((n, n), F32) if first else les_in[a, c] for c in range(2)]
+            if first:
+                ret = [jnp.zeros((n, n), F32)] * 2
+                les = list(ret)
+            else:
+                ret = [sums_in[0][a, c] for c in range(2)]
+                les = [sums_in[1][a, c] for c in range(2)]
             for i, d in enumerate(distances):
                 for b in range(local_e):
                     for source, t, occ, factor in (
@@ -221,8 +212,11 @@
             if last:
                 les = [les[0] - les[0].T, les[1] + les[1].T]
             for c in range(2):
-                ret_ref[a, c] = ret[c]
-                les_ref[a, c] = les[c]
+                targets[0][a, c] = ret[c]
+                targets[1][a, c] = les[c]
+            if last:
+                copy_out(0, a).start()
+                copy_out(1, a).start()
 
     @pl.when(core == 0)
     def _():
@@ -231,6 +225,11 @@
     @pl.when(core != 0)
     def _():
         body(*blocks[::-1])
+
+    if last:
+        for a in range(local_e):
+            copy_out(0, a).wait()
+            copy_out(1, a).wait()
 
 
 def whole(count):
@@ -249,48 +248,28 @@
     total = local_e * count
     per = local_e // layers
     block = jax.ShapeDtypeStruct((local_e, 2, n, n), F32)
-    part = jax.ShapeDtypeStruct((per, 2, n, n), F32)
-
-    first, second = orders(layers)
-
-    def exchange(slots):
-        received = [slots[0]]
-        for slot, a, b in zip(slots[1:], first, second):
-            pairs = [
-                (l * moms + k, (l ^ (a if k == 0 else b)) * moms + k)
-                for l in range(layers)
-                for k in range(moms)
-            ]
-            received.append(lax.ppermute(slot, ("len", "mom"), pairs))
-        return received
-
-    couplings = exchange([coupling[0]] * layers)
-    g = pl.pallas_call(
+    anywhere = pl.BlockSpec(memory_space=pltpu.HBM)
+    inputs = (hamiltonian[0, 0], sigma_prev[0, 0], coupling[0], coupling_pattern)
+    sent = pl.pallas_call(
         functools.partial(inverse_kernel, total),
-        out_shape=[part] * layers,
-        in_specs=whole(2),
-        out_specs=whole(layers),
+        out_shape=jax.ShapeDtypeStruct((layers, 2 * per + 1, n, n), F32),
+        in_specs=[anywhere] * 4,
+        out_specs=whole(1)[0],
+        scratch_shapes=[pltpu.VMEM(value.shape, value.dtype) for value in inputs]
+        + [pltpu.SemaphoreType.DMA((4,))],
         compiler_params=params(),
         name="inverse",
-    )(hamiltonian[0, 0], sigma_prev[0, 0])
-    y = pl.pallas_call(
-        functools.partial(chain_kernel, layers),
-        out_shape=[part] * layers,
-        in_specs=whole(2 * layers + 1),
-        out_specs=whole(layers),
-        scratch_shapes=[pltpu.VMEM((layers, per, 2, n, n), F32), pltpu.VMEM((layers, n, n), F32)],
+    )(*(pltpu.with_memory_space_constraint(value, pltpu.HBM) for value in inputs))
+    sent = pl.pallas_call(
+        chain_kernel,
+        out_shape=block,
+        in_specs=whole(1),
+        out_specs=whole(1)[0],
         compiler_params=params(),
         name="chains",
-    )(*exchange(g), *couplings, coupling_pattern)
-    y = pl.pallas_call(
-        pack_kernel,
-        out_shape=block,
-        in_specs=whole(layers),
-        out_specs=whole(1)[0],
-        compiler_params=params(),
-        name="pack",
-    )(*exchange(y))
-    swapped = lax.ppermute(y, "mom", [(k, moms - 1 - k) for k in range(moms)])
+    )(lax.all_to_all(sent, "len", split_axis=0, concat_axis=0, tiled=True))
+    own = lax.all_to_all(sent, "len", split_axis=0, concat_axis=0, tiled=True)
+
     zero, one = pl.pallas_call(
         momenta_kernel,
         out_shape=[block] * 2,
@@ -298,20 +277,25 @@
         out_specs=whole(2),
         compiler_params=params(),
         name="momenta",
-    )(y, swapped)
+    )(own, lax.ppermute(own, "mom", [(k, moms - 1 - k) for k in range(moms)]))
 
     reach = -(-(total // 2) // local_e)
-    up_down = []
-    down_up = []
-    for z in range(count - 1):
-        low, high = z * moms, (z + 1) * moms
-        up_down += [(low, high), (high + 1, low + 1)]
-        down_up += [(high, low), (low + 1, high + 1)]
+
+    def hop(value, d, role):
+        pairs = []
+        for z in range(count - 1):
+            low, high = z * moms, (z + 1) * moms
+            if z >= d - 1:
+                pairs.append((low + role, high + role))
+            if z <= count - 1 - d:
+                pairs.append((high + 1 - role, low + 1 - role))
+        return lax.ppermute(value, ("energy", "mom"), pairs)
+
     zeros = [zero]
     ones = [one]
     for d in range(1, reach + 1):
-        zeros.append(lax.ppermute(zeros[-1], ("energy", "mom"), up_down))
-        ones.append(lax.ppermute(ones[-1], ("energy", "mom"), down_up))
+        zeros.append(hop(zeros[-1], d, 0))
+        ones.append(hop(ones[-1], d, 1))
 
     groups = [(0, 1)] + [
         tuple(range(d, min(d + 4, reach + 1))) for d in range(2, reach + 1, 4)
@@ -320,11 +304,14 @@
     sums = []
     for i, group in enumerate(groups):
         blocks = [zeros[d] for d in group] + [ones[d] for d in group] + list(sums)
+        last = i == len(groups) - 1
+        scratch = [pltpu.VMEM(block.shape, F32)] * 2 + [pltpu.SemaphoreType.DMA((2, local_e))]
         sums = pl.pallas_call(
-            functools.partial(mix_kernel, total, group, i == 0, i == len(groups) - 1),
+            functools.partial(mix_kernel, total, group, i == 0, last),
             out_shape=[block] * 2,
             in_specs=[smem, smem] + whole(len(blocks)),
-            out_specs=whole(2),
+            out_specs=[pl.BlockSpec(memory_space=pl.ANY)] * 2 if last else whole(2),
+            scratch_shapes=scratch if last else [],
             compiler_params=params(),
             name="mix",
         )(phonon_shift, phonon_weight, *blocks)

time: 65.8 us -> 66.6 us (1.012)
  the two profiles are of different devices: /device:TPU:0 before, /device:TPU:17 now
where the time goes in v3:
time: 66.6 us; the launch traced here: 66.3 us
  blocking collectives  21.7 us (33%)
  waiting for transfers between devices  21.4 us (32%)
  starting transfers between devices  14.1 us (21%)
  Pallas kernels  8.44 us (13%)
  between operations  0.73 us (1%)
    ppermute x4, waiting for transfers between devices, hop(): return lax.ppermute(value, ('energy', 'mom'), pairs)  19.8 us
    all_to_all x1, blocking collectives, shards(): lax.all_to_all(sent, 'len', split_axis=0, concat_axis=0, tiled=True)  13.3 us
    ppermute x4, starting transfers between devices, hop(): return lax.ppermute(value, ('energy', 'mom'), pairs)  10.6 us
    all_to_all x1, blocking collectives, shards(): own = lax.all_to_all(sent, 'len', split_axis=0, concat_axis=0, tiled=True)  8.42 us
    ppermute x1, starting transfers between devices, shards(): lax.ppermute(own, 'mom', [(k, moms - 1 - k) for k in range(moms)])  3.46 us
    pallas_call x2, Pallas kernels, shards(): pl.pallas_call(functools.partial(mix_kernel, total, group, i == 0, last),...  3.32 us
    pallas_call x1, Pallas kernels, shards(): pl.pallas_call(functools.partial(inverse_kernel, total), out_shape=jax.Sh...  2.97 us
    pallas_call x1, Pallas kernels, shards(): pl.pallas_call(chain_kernel, out_shape=block, in_specs=whole(1), out_spec...  2.08 us
  transfers between devices with their start and end apart: 5, of which 4 were waited for; matrix products, arithmetic and copies ran while one was open for 0% of the time, Pallas kernels for 2%

profile of v3, /device:TPU:17, one launch (start us, length us, event | category | flops | bytes accessed | tf_op | source)
XLA Modules:
  0.0 66.3 jit_solution(12664575780188506975)
XLA Ops:
  0.6 3.0 %inverse.1 = f32[4,3,128,128]{3,2,1,0:T(8,128)S(1)} custom-call(f32[2,128,128]{2,1,0:T(8,128)} %bitcast.6, f32[4,2,128,128]{3,2,1,0:T(8,128)} %bitcast.5, f32[128,128]{1,0:T(8,128)} %bitcast.7, s32[128,128]{1,0:T(8,128)} %pattern_any.1), custom_call_target="tpu_custom_call" | custom-call | tf_op jit(solution)/shard_map/inverse/pallas_call | solution.py:253
  3.6 13.3 %all_to_all.10.in_ref = f32[4,3,128,128]{3,2,1,0:T(8,128)S(1)} all-to-all(f32[4,3,128,128]{3,2,1,0:T(8,128)S(1)} %inverse.1), channel_id=1, replica_groups=mesh['len'=4,'energy'=4,'mom'=2] {'len'}, dimensions={0} | all-to-all | bytes 1572864 | tf_op jit(solution)/shard_map/all_to_all | solution.py:270
  16.9 2.1 %chains.1 = f32[4,2,128,128]{3,2,1,0:T(8,128)S(1)} custom-call(f32[4,3,128,128]{3,2,1,0:T(8,128)S(1)} %all_to_all.10.in_ref), custom_call_target="tpu_custom_call" | custom-call | tf_op jit(solution)/shard_map/chains/pallas_call | solution.py:263
  19.0 8.4 %all_to_all.11.own_ref = f32[4,2,128,128]{3,2,1,0:T(8,128)S(1)} all-to-all(f32[4,2,128,128]{3,2,1,0:T(8,128)S(1)} %chains.1), channel_id=1, replica_groups=mesh['len'=4,'energy'=4,'mom'=2] {'len'}, dimensions={0} | all-to-all | bytes 1048576 | tf_op jit(solution)/shard_map/all_to_all | solution.py:271
  27.4 3.5 %collective-permute-start = (f32[4,2,128,128]{3,2,1,0:T(8,128)S(1)}, f32[4,2,128,128]{3,2,1,0:T(8,128)S(1)}, u32[]{:S(2)}, u32[]{:S(2)}) collective-permute-start(f32[4,2,128,128]{3,2,1,0:T(8,128)S(1)} %all_to_all.11.own_ref), channel_id=1, source_target_pairs={{0,1},{1,0},{2,3},{3,2},{4,5},{5,4},{6,7},{7,6},{8,9},{9,8},{10,11... | collective-permute-start | bytes 1572872 | tf_op jit(solution)/shard_map/ppermute | solution.py:280
  30.9 1.5 %collective-permute-done.other_ref = f32[4,2,128,128]{3,2,1,0:T(8,128)S(1)} collective-permute-done((f32[4,2,128,128]{3,2,1,0:T(8,128)S(1)}, f32[4,2,128,128]{3,2,1,0:T(8,128)S(1)}, u32[]{:S(2)}, u32[]{:S(2)}) %collective-permute-start) | collective-permute-done | bytes 524320 | tf_op jit(solution)/shard_map/ppermute | solution.py:280
  32.4 0.1 momenta.1
  32.5 0.0 copy-start
  32.5 0.0 copy-start.1
  32.5 2.1 %collective-permute-start.1 = (f32[4,2,128,128]{3,2,1,0:T(8,128)S(1)}, f32[4,2,128,128]{3,2,1,0:T(8,128)S(1)}, u32[]{:S(2)}, u32[]{:S(2)}) collective-permute-start(f32[4,2,128,128]{3,2,1,0:T(8,128)S(1)} %get-tuple-element.8.refs_0_), channel_id=1, source_target_pairs={{0,2},{3,1},{2,4},{5,3},{4,6},{7,5},{8,10},{11,9},{10,12},{13,11},... | collective-permute-start | bytes 1572872 | tf_op jit(solution)/shard_map/ppermute | solution.py:292
  34.6 3.2 %collective-permute-start.3 = (f32[4,2,128,128]{3,2,1,0:T(8,128)S(1)}, f32[4,2,128,128]{3,2,1,0:T(8,128)S(1)}, u32[]{:S(2)}, u32[]{:S(2)}) collective-permute-start(f32[4,2,128,128]{3,2,1,0:T(8,128)S(1)} %get-tuple-element.9.refs_2_), channel_id=1, source_target_pairs={{1,3},{2,0},{3,5},{4,2},{5,7},{6,4},{9,11},{10,8},{11,13},{12,10},... | collective-permute-start | bytes 1572872 | tf_op jit(solution)/shard_map/ppermute | solution.py:292
  37.8 6.1 %collective-permute-done.1.refs_1_ = f32[4,2,128,128]{3,2,1,0:T(8,128)S(1)} collective-permute-done((f32[4,2,128,128]{3,2,1,0:T(8,128)S(1)}, f32[4,2,128,128]{3,2,1,0:T(8,128)S(1)}, u32[]{:S(2)}, u32[]{:S(2)}) %collective-permute-start.1) | collective-permute-done | bytes 524320 | tf_op jit(solution)/shard_map/ppermute | solution.py:292
  43.9 2.1 %collective-permute-start.2 = (f32[4,2,128,128]{3,2,1,0:T(8,128)S(1)}, f32[4,2,128,128]{3,2,1,0:T(8,128)S(1)}, u32[]{:S(2)}, u32[]{:S(2)}) collective-permute-start(f32[4,2,128,128]{3,2,1,0:T(8,128)S(1)} %collective-permute-done.1.refs_1_), channel_id=1, source_target_pairs={{3,1},{2,4},{5,3},{4,6},{11,9},{10,12},{13,11},{12,14},{19,17},{18... | collective-permute-start | bytes 1572872 | tf_op jit(solution)/shard_map/ppermute | solution.py:292
  46.0 2.9 %collective-permute-done.3.refs_3_ = f32[4,2,128,128]{3,2,1,0:T(8,128)S(1)} collective-permute-done((f32[4,2,128,128]{3,2,1,0:T(8,128)S(1)}, f32[4,2,128,128]{3,2,1,0:T(8,128)S(1)}, u32[]{:S(2)}, u32[]{:S(2)}) %collective-permute-start.3) | collective-permute-done | bytes 524320 | tf_op jit(solution)/shard_map/ppermute | solution.py:292
  48.9 3.2 %collective-permute-start.4 = (f32[4,2,128,128]{3,2,1,0:T(8,128)S(1)}, f32[4,2,128,128]{3,2,1,0:T(8,128)S(1)}, u32[]{:S(2)}, u32[]{:S(2)}) collective-permute-start(f32[4,2,128,128]{3,2,1,0:T(8,128)S(1)} %collective-permute-done.3.refs_3_), channel_id=1, source_target_pairs={{2,0},{3,5},{4,2},{5,7},{10,8},{11,13},{12,10},{13,15},{18,16},{19... | collective-permute-start | bytes 1572872 | tf_op jit(solution)/shard_map/ppermute | solution.py:292
  52.1 0.0 copy-done
  52.1 0.0 copy-done.1
  52.1 1.5 %mix.2 = (f32[4,2,128,128]{3,2,1,0:T(8,128)S(1)}, f32[4,2,128,128]{3,2,1,0:T(8,128)S(1)}) custom-call(s32[4]{0:T(128)S(1)} %copy-done, f32[4]{0:T(128)S(1)} %copy-done.1, f32[4,2,128,128]{3,2,1,0:T(8,128)S(1)} %get-tuple-element.8.refs_0_, f32[4,2,128,128]{3,2,1,0:T(8,128)S(1)} %collective-permute-done.1.refs_1_, ...), custom_call_target="tpu_custom_call" | custom-call | tf_op jit(solution)/shard_map/mix/pallas_call | solution.py:309
  53.6 0.0 collective-permute-done.2.refs_0_
  53.6 10.9 %collective-permute-done.4.refs_1_ = f32[4,2,128,128]{3,2,1,0:T(8,128)S(1)} collective-permute-done((f32[4,2,128,128]{3,2,1,0:T(8,128)S(1)}, f32[4,2,128,128]{3,2,1,0:T(8,128)S(1)}, u32[]{:S(2)}, u32[]{:S(2)}) %collective-permute-start.4) | collective-permute-done | bytes 524320 | tf_op jit(solution)/shard_map/ppermute | solution.py:292
  64.5 1.9 %mix.3 = (f32[4,2,128,128]{3,2,1,0:T(8,128)}, f32[4,2,128,128]{3,2,1,0:T(8,128)}) custom-call(s32[4]{0:T(128)S(1)} %copy-done, f32[4]{0:T(128)S(1)} %copy-done.1, f32[4,2,128,128]{3,2,1,0:T(8,128)S(1)} %collective-permute-done.2.refs_0_, f32[4,2,128,128]{3,2,1,0:T(8,128)S(1)} %collective-permute-done.4.refs_1_, ...), custom_call_target="tpu_custom_call" | custom-call | tf_op jit(solution)/shard_map/mix/pallas_call | solution.py:309
Async XLA Ops:
  27.4 5.0 %collective-permute-start = (f32[4,2,128,128]{3,2,1,0:T(8,128)S(1)}, f32[4,2,128,128]{3,2,1,0:T(8,128)S(1)}, u32[]{:S(2)}, u32[]{:S(2)}) collective-permute-start(f32[4,2,128,128]{3,2,1,0:T(8,128)S(1)} %all_to_all.11.own_ref), channel_id=1, source_target_pairs={{0,1},{1,0},{2,3},{3,2},{4,5},{5,4},{6,7},{7,6},{8,9},{9,8},{10,11... | collective-permute-start | bytes 1572872 | tf_op jit(solution)/shard_map/ppermute | solution.py:280
  32.5 19.6 %copy-start = (s32[4]{0:T(128)S(1)}, s32[4]{0:T(128)}, u32[]{:S(2)}) copy-start(s32[4]{0:T(128)} %shift_ref.3) | copy-start | bytes 52
  32.5 19.6 %copy-start.1 = (f32[4]{0:T(128)S(1)}, f32[4]{0:T(128)}, u32[]{:S(2)}) copy-start(f32[4]{0:T(128)} %weight_ref.3) | copy-start | bytes 52
  32.5 11.4 %collective-permute-start.1 = (f32[4,2,128,128]{3,2,1,0:T(8,128)S(1)}, f32[4,2,128,128]{3,2,1,0:T(8,128)S(1)}, u32[]{:S(2)}, u32[]{:S(2)}) collective-permute-start(f32[4,2,128,128]{3,2,1,0:T(8,128)S(1)} %get-tuple-element.8.refs_0_), channel_id=1, source_target_pairs={{0,2},{3,1},{2,4},{5,3},{4,6},{7,5},{8,10},{11,9},{10,12},{13,11},... | collective-permute-start | bytes 1572872 | tf_op jit(solution)/shard_map/ppermute | solution.py:292
  34.6 14.3 %collective-permute-start.3 = (f32[4,2,128,128]{3,2,1,0:T(8,128)S(1)}, f32[4,2,128,128]{3,2,1,0:T(8,128)S(1)}, u32[]{:S(2)}, u32[]{:S(2)}) collective-permute-start(f32[4,2,128,128]{3,2,1,0:T(8,128)S(1)} %get-tuple-element.9.refs_2_), channel_id=1, source_target_pairs={{1,3},{2,0},{3,5},{4,2},{5,7},{6,4},{9,11},{10,8},{11,13},{12,10},... | collective-permute-start | bytes 1572872 | tf_op jit(solution)/shard_map/ppermute | solution.py:292
  43.9 9.7 %collective-permute-start.2 = (f32[4,2,128,128]{3,2,1,0:T(8,128)S(1)}, f32[4,2,128,128]{3,2,1,0:T(8,128)S(1)}, u32[]{:S(2)}, u32[]{:S(2)}) collective-permute-start(f32[4,2,128,128]{3,2,1,0:T(8,128)S(1)} %collective-permute-done.1.refs_1_), channel_id=1, source_target_pairs={{3,1},{2,4},{5,3},{4,6},{11,9},{10,12},{13,11},{12,14},{19,17},{18... | collective-permute-start | bytes 1572872 | tf_op jit(solution)/shard_map/ppermute | solution.py:292
  48.9 15.6 %collective-permute-start.4 = (f32[4,2,128,128]{3,2,1,0:T(8,128)S(1)}, f32[4,2,128,128]{3,2,1,0:T(8,128)S(1)}, u32[]{:S(2)}, u32[]{:S(2)}) collective-permute-start(f32[4,2,128,128]{3,2,1,0:T(8,128)S(1)} %collective-permute-done.3.refs_3_), channel_id=1, source_target_pairs={{2,0},{3,5},{4,2},{5,7},{10,8},{11,13},{12,10},{13,15},{18,16},{19... | collective-permute-start | bytes 1572872 | tf_op jit(solution)/shard_map/ppermute | solution.py:292

commit v4 on v3

--- a/solution.py
+++ b/solution.py
@@ -44,35 +44,51 @@
     return (rows == cols).astype(F32)
 
 
-def inverse_kernel(total, ham_any, sig_any, coupling_any, pattern_any, out_ref, *refs):
-    buffers, sems = refs[:-1], refs[-1]
-    sources = (ham_any, sig_any, coupling_any, pattern_any)
+def orders(layers):
+    first = list(range(1, layers))
+    second = list(first)
+    if layers > 2:
+        second[0], second[1] = second[1], second[0]
+    return first, second
+
+
+def peers(layers):
+    here = lax.axis_index("len")
+    core = lax.axis_index("mom")
+    first, second = orders(layers)
+    return [here] + [here ^ jnp.where(core == 0, a, b) for a, b in zip(first, second)]
+
+
+def inverse_kernel(total, layers, slots, ham_any, sig_any, coupling_any, pattern_any, *refs):
+    out_refs = refs[: len(slots)]
+    ham_ref, sig_ref, coupling_ref, pattern_ref, sems = refs[len(slots) :]
+    _, per, _, n, _ = sig_ref.shape
+    towards = [peers(layers)[slot] for slot in slots]
     copies = [
-        pltpu.make_async_copy(source, buffer, sems.at[i])
-        for i, (source, buffer) in enumerate(zip(sources, buffers))
+        pltpu.make_async_copy(ham_any, ham_ref, sems.at[0]),
+        pltpu.make_async_copy(coupling_any, coupling_ref, sems.at[1]),
+        pltpu.make_async_copy(pattern_any, pattern_ref, sems.at[2]),
     ]
+    for i, peer in enumerate(towards):
+        group = sig_any.at[pl.ds(peer * per, per)]
+        copies.append(pltpu.make_async_copy(group, sig_ref.at[i], sems.at[3 + i]))
     for copy in copies:
         copy.start()
     for copy in copies:
         copy.wait()
-    ham_ref, sig_ref, coupling_ref, pattern_ref = buffers
-    layers = out_ref.shape[0]
-    local_e, _, n, _ = sig_ref.shape
-    per = local_e // layers
-    start = lax.axis_index("energy") * local_e
+    start = lax.axis_index("energy") * (layers * per)
     eye = identity(n)
     bond = coupling_ref[...] * pattern_ref[...].astype(F32)
-    for l in range(layers):
-        out_ref[l, 2 * per] = bond
+    for i, (peer, out_ref) in enumerate(zip(towards, out_refs)):
+        out_ref[2 * per] = bond
         for p in range(per):
-            e = l * per + p
-            pos = jnp.full((1, n), start + e, jnp.int32).astype(F32)
+            pos = jnp.full((1, n), start + peer * per + p, jnp.int32).astype(F32)
             zre = 5.0 + 2.0 * pos / total
             mag = zre * zre + 1.0
             qre = zre / mag
             qim = -1.0 / mag
-            sre = ham_ref[0] + sig_ref[e, 0]
-            sim = ham_ref[1] + sig_ref[e, 1]
+            sre = ham_ref[0] + sig_ref[i, p, 0]
+            sim = ham_ref[1] + sig_ref[i, p, 1]
             a1 = jnp.concatenate([qre * sre - qim * sim, qre * sim + qim * sre], axis=1)
             a1_pair = split(a1)
             a1_right = (right_form(a1_pair[0]), right_form(a1_pair[1]))
@@ -84,20 +100,22 @@
             s = eye + (a1 + (a2 + a3))
             x = s + dot3(split(s), right_pair(a4))
             re, im = x[:, :n], x[:, n:]
-            out_ref[l, 2 * p] = qre * re - qim * im
-            out_ref[l, 2 * p + 1] = qre * im + qim * re
-
-
-def chain_kernel(in_ref, out_ref):
-    layers, parts, n, _ = in_ref.shape
-    per = parts // 2
-    bonds = [None] + [in_ref[l, 2 * per] for l in range(1, layers)]
+            out_ref[2 * p] = qre * re - qim * im
+            out_ref[2 * p + 1] = qre * im + qim * re
+
+
+def chain_kernel(layers, *refs):
+    in_slots, out_slots = refs[:layers], refs[layers : 2 * layers]
+    g_ref, bond_ref = refs[2 * layers :]
+    _, per, _, n, _ = g_ref.shape
+    for peer, in_slot in zip(peers(layers), in_slots):
+        for p in range(per):
+            g_ref[peer, p] = in_slot[2 * p : 2 * p + 2]
+        bond_ref[peer] = in_slot[2 * per]
+    bonds = [None] + [bond_ref[l] for l in range(1, layers)]
     bonds_t = [None] + [b.T for b in bonds[1:]]
     for p in range(per):
-        g = [
-            jnp.concatenate([in_ref[l, 2 * p], in_ref[l, 2 * p + 1]], axis=1)
-            for l in range(layers)
-        ]
+        g = [jnp.concatenate([g_ref[l, p, 0], g_ref[l, p, 1]], axis=1) for l in range(layers)]
         down = [None] * layers
         up = [None] * layers
         for l in range(layers):
@@ -132,21 +150,34 @@
         for l in range(layers):
             near = [green[m] for m in (l - 1, l + 1) if 0 <= m < layers]
             y = green[l] + 0.5 * sum(near[1:], near[0]) if near else green[l]
-            out_ref[l * per + p, 0] = y[:, :n]
-            out_ref[l * per + p, 1] = y[:, n:]
-
-def momenta_kernel(own_ref, other_ref, zero_ref, one_ref):
+            g_ref[l, p, 0] = y[:, :n]
+            g_ref[l, p, 1] = y[:, n:]
+    for peer, out_slot in zip(peers(layers), out_slots):
+        out_slot[...] = g_ref[peer]
+
+
+def momenta_kernel(layers, *refs):
     core = lax.axis_index("mom")
+    here = lax.axis_index("len")
+    per = refs[0].shape[0]
+    first, second = orders(layers)
+
+    def place(slots, order, out_ref):
+        for mask, slot in zip([0] + order, slots):
+            for p in range(per):
+                out_ref[(here ^ mask) * per + p] = slot[p]
+
+    own, other = refs[:layers], refs[layers : 2 * layers]
 
     @pl.when(core == 0)
     def _():
-        zero_ref[...] = own_ref[...]
-        one_ref[...] = other_ref[...]
+        place(own, first, refs[-2])
+        place(other, second, refs[-1])
 
     @pl.when(core != 0)
     def _():
-        zero_ref[...] = other_ref[...]
-        one_ref[...] = own_ref[...]
+        place(other, first, refs[-2])
+        place(own, second, refs[-1])
 
 
 def occupation(pos, total, n):
@@ -248,36 +279,66 @@
     total = local_e * count
     per = local_e // layers
     block = jax.ShapeDtypeStruct((local_e, 2, n, n), F32)
+    first, second = orders(layers)
+
+    def exchange(slots, i):
+        if i == 0:
+            return slots[0]
+        pairs = []
+        for l in range(layers):
+            for k in range(moms):
+                peer = l ^ (first, second)[k][i - 1]
+                pairs.append((l * moms + k, peer * moms + k))
+        return lax.ppermute(slots[i], ("len", "mom"), pairs)
+
     anywhere = pl.BlockSpec(memory_space=pltpu.HBM)
     inputs = (hamiltonian[0, 0], sigma_prev[0, 0], coupling[0], coupling_pattern)
+    inputs = [pltpu.with_memory_space_constraint(value, pltpu.HBM) for value in inputs]
+
+    def inverse(slots):
+        return pl.pallas_call(
+            functools.partial(inverse_kernel, total, layers, slots),
+            out_shape=[jax.ShapeDtypeStruct((2 * per + 1, n, n), F32)] * len(slots),
+            in_specs=[anywhere] * 4,
+            out_specs=whole(len(slots)),
+            scratch_shapes=[
+                pltpu.VMEM((2, n, n), F32),
+                pltpu.VMEM((len(slots), per, 2, n, n), F32),
+                pltpu.VMEM((n, n), F32),
+                pltpu.VMEM((n, n), jnp.int32),
+                pltpu.SemaphoreType.DMA((3 + len(slots),)),
+            ],
+            compiler_params=params(),
+            cost_estimate=pl.CostEstimate(
+                flops=len(slots) * per * 96 * n**3, bytes_accessed=len(slots) * 8 * n * n, transcendentals=0
+            ),
+            name="inverse",
+        )(*inputs)
+
+    half = (layers + 1) // 2
+    early = tuple(range(1, half + 1))
+    late = tuple(range(half + 1, layers)) + (0,)
+    sent = dict(zip(early, inverse(early))) | dict(zip(late, inverse(late)))
+    part = jax.ShapeDtypeStruct((per, 2, n, n), F32)
     sent = pl.pallas_call(
-        functools.partial(inverse_kernel, total),
-        out_shape=jax.ShapeDtypeStruct((layers, 2 * per + 1, n, n), F32),
-        in_specs=[anywhere] * 4,
-        out_specs=whole(1)[0],
-        scratch_shapes=[pltpu.VMEM(value.shape, value.dtype) for value in inputs]
-        + [pltpu.SemaphoreType.DMA((4,))],
-        compiler_params=params(),
-        name="inverse",
-    )(*(pltpu.with_memory_space_constraint(value, pltpu.HBM) for value in inputs))
-    sent = pl.pallas_call(
-        chain_kernel,
-        out_shape=block,
-        in_specs=whole(1),
-        out_specs=whole(1)[0],
+        functools.partial(chain_kernel, layers),
+        out_shape=[part] * layers,
+        in_specs=whole(layers),
+        out_specs=whole(layers),
+        scratch_shapes=[pltpu.VMEM((layers, per, 2, n, n), F32), pltpu.VMEM((layers, n, n), F32)],
         compiler_params=params(),
         name="chains",
-    )(lax.all_to_all(sent, "len", split_axis=0, concat_axis=0, tiled=True))
-    own = lax.all_to_all(sent, "len", split_axis=0, concat_axis=0, tiled=True)
-
+    )(*[exchange(sent, i) for i in range(layers)])
+    own = [exchange(sent, i) for i in range(layers)]
+    other = [lax.ppermute(v, "mom", [(k, moms - 1 - k) for k in range(moms)]) for v in own]
     zero, one = pl.pallas_call(
-        momenta_kernel,
+        functools.partial(momenta_kernel, layers),
         out_shape=[block] * 2,
-        in_specs=whole(2),
+        in_specs=whole(2 * layers),
         out_specs=whole(2),
         compiler_params=params(),
         name="momenta",
-    )(own, lax.ppermute(own, "mom", [(k, moms - 1 - k) for k in range(moms)]))
+    )(*own, *other)
 
     reach = -(-(total // 2) // local_e)
 

time: 66.6 us -> 62.2 us (0.934)
  blocking collectives: 21.7 us -> 0 us
  starting transfers between devices: 14.1 us -> 24.4 us
  waiting for transfers between devices: 21.4 us -> 26.7 us
  Pallas kernels: 8.44 us -> 10.1 us
    all_to_all x2 -> x0, blocking collectives: 21.7 us -> none  [the longest x1 13.3 us: shards(): lax.all_to_all(sent, 'len', split_axis=0, concat_axis=0, tiled=True)]
    ppermute x1 -> x10, starting transfers between devices: 3.46 us -> 13.8 us  [the longest x4 7.52 us: shards(): lax.ppermute(v, 'mom', [(k, moms - 1 - k) for k in range(moms)])]
    ppermute x1 -> x10, waiting for transfers between devices: 1.54 us -> 7.43 us  [the longest x6 6.1 us: exchange(): return lax.ppermute(slots[i], ('len', 'mom'), pairs)]
    pallas_call x3 -> x4, Pallas kernels: 5.12 us -> 6.81 us  [the longest x2 4.53 us: inverse(): pl.pallas_call(functools.partial(inverse_kernel, total, layers, slots), o...]
  transfers between devices with their start and end apart: 5 -> 14, of which waited for: 4 -> 7; matrix products, arithmetic and copies ran while one was open for 0% -> 0% of each run, Pallas kernels for 2% -> 6%
where the time goes in v4:
time: 62.2 us; the launch traced here: 62 us
  waiting for transfers between devices  26.7 us (43%)
  starting transfers between devices  24.4 us (39%)
  Pallas kernels  10.1 us (16%)
  between operations  0.75 us (1%)
    ppermute x4, waiting for transfers between devices, hop(): return lax.ppermute(value, ('energy', 'mom'), pairs)  19.3 us
    ppermute x4, starting transfers between devices, hop(): return lax.ppermute(value, ('energy', 'mom'), pairs)  10.6 us
    ppermute x4, starting transfers between devices, shards(): lax.ppermute(v, 'mom', [(k, moms - 1 - k) for k in range(moms)])  7.52 us
    ppermute x6, starting transfers between devices, exchange(): return lax.ppermute(slots[i], ('len', 'mom'), pairs)  6.23 us
    ppermute x6, waiting for transfers between devices, exchange(): return lax.ppermute(slots[i], ('len', 'mom'), pairs)  6.1 us
    pallas_call x2, Pallas kernels, inverse(): pl.pallas_call(functools.partial(inverse_kernel, total, layers, slots), o...  4.53 us
    pallas_call x2, Pallas kernels, shards(): pl.pallas_call(functools.partial(mix_kernel, total, group, i == 0, last),...  3.32 us
    pallas_call x1, Pallas kernels, shards(): pl.pallas_call(functools.partial(chain_kernel, layers), out_shape=[part]...  2.22 us
  transfers between devices with their start and end apart: 14, of which 7 were waited for; matrix products, arithmetic and copies ran while one was open for 0% of the time, Pallas kernels for 6%

profile of v4, /device:TPU:17, one launch (start us, length us, event | category | flops | bytes accessed | tf_op | source)
XLA Modules:
  0.0 62.0 jit_solution(11270352765303754929)
XLA Ops:
  0.6 2.3 %inverse.3 = (f32[3,128,128]{2,1,0:T(8,128)S(1)}, f32[3,128,128]{2,1,0:T(8,128)S(1)}) custom-call(f32[2,128,128]{2,1,0:T(8,128)} %bitcast.9, f32[4,2,128,128]{3,2,1,0:T(8,128)} %bitcast.5, f32[128,128]{1,0:T(8,128)} %bitcast.11, s32[128,128]{1,0:T(8,128)} %pattern_any.3), custom_call_target="tpu_custom_call" | custom-call | flops 402653184 | bytes 262144 | tf_op jit(solution)/shard_map/inverse/pallas_call | solution.py:299
  2.9 1.3 %collective-permute-start = (f32[3,128,128]{2,1,0:T(8,128)S(1)}, f32[3,128,128]{2,1,0:T(8,128)S(1)}, u32[]{:S(2)}, u32[]{:S(2)}) collective-permute-start(f32[3,128,128]{2,1,0:T(8,128)S(1)} %get-tuple-element.17), channel_id=1, source_target_pairs={{0,8},{1,17},{8,0},{9,25},{16,24},{17,1},{24,16},{25,9},{2,10},{3,... | collective-permute-start | bytes 589832 | tf_op jit(solution)/shard_map/ppermute | solution.py:292
  4.2 1.2 %collective-permute-start.1 = (f32[3,128,128]{2,1,0:T(8,128)S(1)}, f32[3,128,128]{2,1,0:T(8,128)S(1)}, u32[]{:S(2)}, u32[]{:S(2)}) collective-permute-start(f32[3,128,128]{2,1,0:T(8,128)S(1)} %get-tuple-element.18), channel_id=1, source_target_pairs={{0,16},{1,9},{8,24},{9,1},{16,0},{17,25},{24,8},{25,17},{2,18},{3,... | collective-permute-start | bytes 589832 | tf_op jit(solution)/shard_map/ppermute | solution.py:292
  5.4 2.3 %inverse.2 = (f32[3,128,128]{2,1,0:T(8,128)S(1)}, f32[3,128,128]{2,1,0:T(8,128)S(1)}) custom-call(f32[2,128,128]{2,1,0:T(8,128)} %bitcast.10, f32[4,2,128,128]{3,2,1,0:T(8,128)} %bitcast.6, f32[128,128]{1,0:T(8,128)} %bitcast.12, s32[128,128]{1,0:T(8,128)} %pattern_any.3), custom_call_target="tpu_custom_call" | custom-call | flops 402653184 | bytes 262144 | tf_op jit(solution)/shard_map/inverse/pallas_call | solution.py:299
  7.7 0.3 collective-permute-start.2
  8.0 0.0 collective-permute-done.refs_1_
  8.0 3.0 %collective-permute-done.1.refs_2_ = f32[3,128,128]{2,1,0:T(8,128)S(1)} collective-permute-done((f32[3,128,128]{2,1,0:T(8,128)S(1)}, f32[3,128,128]{2,1,0:T(8,128)S(1)}, u32[]{:S(2)}, u32[]{:S(2)}) %collective-permute-start.1) | collective-permute-done | bytes 196640 | tf_op jit(solution)/shard_map/ppermute | solution.py:292
  10.9 3.1 %collective-permute-done.2.refs_3_ = f32[3,128,128]{2,1,0:T(8,128)S(1)} collective-permute-done((f32[3,128,128]{2,1,0:T(8,128)S(1)}, f32[3,128,128]{2,1,0:T(8,128)S(1)}, u32[]{:S(2)}, u32[]{:S(2)}) %collective-permute-start.2) | collective-permute-done | bytes 196640 | tf_op jit(solution)/shard_map/ppermute | solution.py:292
  14.0 2.2 %chains.1 = (f32[1,2,128,128]{3,2,1,0:T(8,128)S(1)}, f32[1,2,128,128]{3,2,1,0:T(8,128)S(1)}, f32[1,2,128,128]{3,2,1,0:T(8,128)S(1)}, f32[1,2,128,128]{3,2,1,0:T(8,128)S(1)}) custom-call(f32[3,128,128]{2,1,0:T(8,128)S(1)} %get-tuple-element.16.refs_0_, f32[3,128,128]{2,1,0:T(8,128)S(1)} %collective-permute-done.refs_1_, ...), custom_call_target="tpu_custom_call" | custom-call | tf_op jit(solution)/shard_map/chains/pallas_call | solution.py:323
  16.3 1.3 %collective-permute-start.3 = (f32[1,2,128,128]{3,2,1,0:T(8,128)S(1)}, f32[1,2,128,128]{3,2,1,0:T(8,128)S(1)}, u32[]{:S(2)}, u32[]{:S(2)}) collective-permute-start(f32[1,2,128,128]{3,2,1,0:T(8,128)S(1)} %get-tuple-element.21), channel_id=1, source_target_pairs={{0,8},{1,17},{8,0},{9,25},{16,24},{17,1},{24,16},{25,9},{2,10},{3,... | collective-permute-start | bytes 393224 | tf_op jit(solution)/shard_map/ppermute | solution.py:292
  17.6 2.1 %collective-permute-start.4 = (f32[1,2,128,128]{3,2,1,0:T(8,128)S(1)}, f32[1,2,128,128]{3,2,1,0:T(8,128)S(1)}, u32[]{:S(2)}, u32[]{:S(2)}) collective-permute-start(f32[1,2,128,128]{3,2,1,0:T(8,128)S(1)} %get-tuple-element.22), channel_id=1, source_target_pairs={{0,16},{1,9},{8,24},{9,1},{16,0},{17,25},{24,8},{25,17},{2,18},{3,... | collective-permute-start | bytes 393224 | tf_op jit(solution)/shard_map/ppermute | solution.py:292
  19.7 0.0 collective-permute-start.5
  19.7 2.0 %collective-permute-start.6 = (f32[1,2,128,128]{3,2,1,0:T(8,128)S(1)}, f32[1,2,128,128]{3,2,1,0:T(8,128)S(1)}, u32[]{:S(2)}, u32[]{:S(2)}) collective-permute-start(f32[1,2,128,128]{3,2,1,0:T(8,128)S(1)} %get-tuple-element.20.refs_0_), channel_id=1, source_target_pairs={{0,1},{1,0},{2,3},{3,2},{4,5},{5,4},{6,7},{7,6},{8,9},{9,8},{10,11... | collective-permute-start | bytes 393224 | tf_op jit(solution)/shard_map/ppermute | solution.py:333
  21.7 2.8 %collective-permute-start.7 = (f32[1,2,128,128]{3,2,1,0:T(8,128)S(1)}, f32[1,2,128,128]{3,2,1,0:T(8,128)S(1)}, u32[]{:S(2)}, u32[]{:S(2)}) collective-permute-start(f32[1,2,128,128]{3,2,1,0:T(8,128)S(1)} %collective-permute-done.3.refs_1_), channel_id=1, source_target_pairs={{0,1},{1,0},{2,3},{3,2},{4,5},{5,4},{6,7},{7,6},{8,9},{9,8},{10,11... | collective-permute-start | bytes 393224 | tf_op jit(solution)/shard_map/ppermute | solution.py:333
  24.5 0.0 collective-permute-done.4.refs_2_
  24.6 2.7 %collective-permute-start.8 = (f32[1,2,128,128]{3,2,1,0:T(8,128)S(1)}, f32[1,2,128,128]{3,2,1,0:T(8,128)S(1)}, u32[]{:S(2)}, u32[]{:S(2)}) collective-permute-start(f32[1,2,128,128]{3,2,1,0:T(8,128)S(1)} %collective-permute-done.4.refs_2_), channel_id=1, source_target_pairs={{0,1},{1,0},{2,3},{3,2},{4,5},{5,4},{6,7},{7,6},{8,9},{9,8},{10,11... | collective-permute-start | bytes 393224 | tf_op jit(solution)/shard_map/ppermute | solution.py:333
  27.2 0.0 collective-permute-start.9
  27.3 0.0 collective-permute-done.6.refs_4_
  27.3 1.0 %collective-permute-done.8.refs_6_ = f32[1,2,128,128]{3,2,1,0:T(8,128)S(1)} collective-permute-done((f32[1,2,128,128]{3,2,1,0:T(8,128)S(1)}, f32[1,2,128,128]{3,2,1,0:T(8,128)S(1)}, u32[]{:S(2)}, u32[]{:S(2)}) %collective-permute-start.8) | collective-permute-done | bytes 131104 | tf_op jit(solution)/shard_map/ppermute | solution.py:333
  28.2 0.4 collective-permute-done.9.refs_7_
  28.6 0.1 momenta.1
  28.7 0.0 copy-start
  28.7 0.0 copy-start.1
  28.7 2.1 %collective-permute-start.10 = (f32[4,2,128,128]{3,2,1,0:T(8,128)S(1)}, f32[4,2,128,128]{3,2,1,0:T(8,128)S(1)}, u32[]{:S(2)}, u32[]{:S(2)}) collective-permute-start(f32[4,2,128,128]{3,2,1,0:T(8,128)S(1)} %get-tuple-element.24.refs_0_), channel_id=1, source_target_pairs={{0,2},{3,1},{2,4},{5,3},{4,6},{7,5},{8,10},{11,9},{10,12},{13,11},... | collective-permute-start | bytes 1572872 | tf_op jit(solution)/shard_map/ppermute | solution.py:353
  30.8 3.2 %collective-permute-start.12 = (f32[4,2,128,128]{3,2,1,0:T(8,128)S(1)}, f32[4,2,128,128]{3,2,1,0:T(8,128)S(1)}, u32[]{:S(2)}, u32[]{:S(2)}) collective-permute-start(f32[4,2,128,128]{3,2,1,0:T(8,128)S(1)} %get-tuple-element.25.refs_2_), channel_id=1, source_target_pairs={{1,3},{2,0},{3,5},{4,2},{5,7},{6,4},{9,11},{10,8},{11,13},{12,10},... | collective-permute-start | bytes 1572872 | tf_op jit(solution)/shard_map/ppermute | solution.py:353
  34.0 6.3 %collective-permute-done.10.refs_1_ = f32[4,2,128,128]{3,2,1,0:T(8,128)S(1)} collective-permute-done((f32[4,2,128,128]{3,2,1,0:T(8,128)S(1)}, f32[4,2,128,128]{3,2,1,0:T(8,128)S(1)}, u32[]{:S(2)}, u32[]{:S(2)}) %collective-permute-start.10) | collective-permute-done | bytes 524320 | tf_op jit(solution)/shard_map/ppermute | solution.py:353
  40.3 2.1 %collective-permute-start.11 = (f32[4,2,128,128]{3,2,1,0:T(8,128)S(1)}, f32[4,2,128,128]{3,2,1,0:T(8,128)S(1)}, u32[]{:S(2)}, u32[]{:S(2)}) collective-permute-start(f32[4,2,128,128]{3,2,1,0:T(8,128)S(1)} %collective-permute-done.10.refs_1_), channel_id=1, source_target_pairs={{3,1},{2,4},{5,3},{4,6},{11,9},{10,12},{13,11},{12,14},{19,17},{18... | collective-permute-start | bytes 1572872 | tf_op jit(solution)/shard_map/ppermute | solution.py:353
  42.4 2.5 %collective-permute-done.12.refs_3_ = f32[4,2,128,128]{3,2,1,0:T(8,128)S(1)} collective-permute-done((f32[4,2,128,128]{3,2,1,0:T(8,128)S(1)}, f32[4,2,128,128]{3,2,1,0:T(8,128)S(1)}, u32[]{:S(2)}, u32[]{:S(2)}) %collective-permute-start.12) | collective-permute-done | bytes 524320 | tf_op jit(solution)/shard_map/ppermute | solution.py:353
  44.9 3.2 %collective-permute-start.13 = (f32[4,2,128,128]{3,2,1,0:T(8,128)S(1)}, f32[4,2,128,128]{3,2,1,0:T(8,128)S(1)}, u32[]{:S(2)}, u32[]{:S(2)}) collective-permute-start(f32[4,2,128,128]{3,2,1,0:T(8,128)S(1)} %collective-permute-done.12.refs_3_), channel_id=1, source_target_pairs={{2,0},{3,5},{4,2},{5,7},{10,8},{11,13},{12,10},{13,15},{18,16},{19... | collective-permute-start | bytes 1572872 | tf_op jit(solution)/shard_map/ppermute | solution.py:353
  48.1 1.5 %mix.2 = (f32[4,2,128,128]{3,2,1,0:T(8,128)S(1)}, f32[4,2,128,128]{3,2,1,0:T(8,128)S(1)}) custom-call(s32[4]{0:T(128)S(1)} %copy-done, f32[4]{0:T(128)S(1)} %copy-done.1, f32[4,2,128,128]{3,2,1,0:T(8,128)S(1)} %get-tuple-element.24.refs_0_, f32[4,2,128,128]{3,2,1,0:T(8,128)S(1)} %collective-permute-done.10.refs_1_, ...), custom_call_target="tpu_custom_call" | custom-call | tf_op jit(solution)/shard_map/mix/pallas_call | solution.py:370
  49.6 10.5 %collective-permute-done.13.refs_1_ = f32[4,2,128,128]{3,2,1,0:T(8,128)S(1)} collective-permute-done((f32[4,2,128,128]{3,2,1,0:T(8,128)S(1)}, f32[4,2,128,128]{3,2,1,0:T(8,128)S(1)}, u32[]{:S(2)}, u32[]{:S(2)}) %collective-permute-start.13) | collective-permute-done | bytes 524320 | tf_op jit(solution)/shard_map/ppermute | solution.py:353
  60.1 1.9 %mix.3 = (f32[4,2,128,128]{3,2,1,0:T(8,128)}, f32[4,2,128,128]{3,2,1,0:T(8,128)}) custom-call(s32[4]{0:T(128)S(1)} %copy-done, f32[4]{0:T(128)S(1)} %copy-done.1, f32[4,2,128,128]{3,2,1,0:T(8,128)S(1)} %collective-permute-done.11.refs_0_, f32[4,2,128,128]{3,2,1,0:T(8,128)S(1)} %collective-permute-done.13.refs_1_, ...), custom_call_target="tpu_custom_call" | custom-call | tf_op jit(solution)/shard_map/mix/pallas_call | solution.py:370
  (6 shorter events, 0.0 us)
Async XLA Ops:
  2.9 5.0 %collective-permute-start = (f32[3,128,128]{2,1,0:T(8,128)S(1)}, f32[3,128,128]{2,1,0:T(8,128)S(1)}, u32[]{:S(2)}, u32[]{:S(2)}) collective-permute-start(f32[3,128,128]{2,1,0:T(8,128)S(1)} %get-tuple-element.17), channel_id=1, source_target_pairs={{0,8},{1,17},{8,0},{9,25},{16,24},{17,1},{24,16},{25,9},{2,10},{3,... | collective-permute-start | bytes 589832 | tf_op jit(solution)/shard_map/ppermute | solution.py:292
  4.2 6.7 %collective-permute-start.1 = (f32[3,128,128]{2,1,0:T(8,128)S(1)}, f32[3,128,128]{2,1,0:T(8,128)S(1)}, u32[]{:S(2)}, u32[]{:S(2)}) collective-permute-start(f32[3,128,128]{2,1,0:T(8,128)S(1)} %get-tuple-element.18), channel_id=1, source_target_pairs={{0,16},{1,9},{8,24},{9,1},{16,0},{17,25},{24,8},{25,17},{2,18},{3,... | collective-permute-start | bytes 589832 | tf_op jit(solution)/shard_map/ppermute | solution.py:292
  7.7 6.4 %collective-permute-start.2 = (f32[3,128,128]{2,1,0:T(8,128)S(1)}, f32[3,128,128]{2,1,0:T(8,128)S(1)}, u32[]{:S(2)}, u32[]{:S(2)}) collective-permute-start(f32[3,128,128]{2,1,0:T(8,128)S(1)} %get-tuple-element.19), channel_id=1, source_target_pairs={{0,24},{1,25},{8,16},{9,17},{16,8},{17,9},{24,0},{25,1},{2,26},{3,... | collective-permute-start | bytes 589832 | tf_op jit(solution)/shard_map/ppermute | solution.py:292
  16.3 5.5 %collective-permute-start.3 = (f32[1,2,128,128]{3,2,1,0:T(8,128)S(1)}, f32[1,2,128,128]{3,2,1,0:T(8,128)S(1)}, u32[]{:S(2)}, u32[]{:S(2)}) collective-permute-start(f32[1,2,128,128]{3,2,1,0:T(8,128)S(1)} %get-tuple-element.21), channel_id=1, source_target_pairs={{0,8},{1,17},{8,0},{9,25},{16,24},{17,1},{24,16},{25,9},{2,10},{3,... | collective-permute-start | bytes 393224 | tf_op jit(solution)/shard_map/ppermute | solution.py:292
  17.6 7.0 %collective-permute-start.4 = (f32[1,2,128,128]{3,2,1,0:T(8,128)S(1)}, f32[1,2,128,128]{3,2,1,0:T(8,128)S(1)}, u32[]{:S(2)}, u32[]{:S(2)}) collective-permute-start(f32[1,2,128,128]{3,2,1,0:T(8,128)S(1)} %get-tuple-element.22), channel_id=1, source_target_pairs={{0,16},{1,9},{8,24},{9,1},{16,0},{17,25},{24,8},{25,17},{2,18},{3,... | collective-permute-start | bytes 393224 | tf_op jit(solution)/shard_map/ppermute | solution.py:292
  19.7 7.5 %collective-permute-start.5 = (f32[1,2,128,128]{3,2,1,0:T(8,128)S(1)}, f32[1,2,128,128]{3,2,1,0:T(8,128)S(1)}, u32[]{:S(2)}, u32[]{:S(2)}) collective-permute-start(f32[1,2,128,128]{3,2,1,0:T(8,128)S(1)} %get-tuple-element.23), channel_id=1, source_target_pairs={{0,24},{1,25},{8,16},{9,17},{16,8},{17,9},{24,0},{25,1},{2,26},{3,... | collective-permute-start | bytes 393224 | tf_op jit(solution)/shard_map/ppermute | solution.py:292
  19.7 7.5 %collective-permute-start.6 = (f32[1,2,128,128]{3,2,1,0:T(8,128)S(1)}, f32[1,2,128,128]{3,2,1,0:T(8,128)S(1)}, u32[]{:S(2)}, u32[]{:S(2)}) collective-permute-start(f32[1,2,128,128]{3,2,1,0:T(8,128)S(1)} %get-tuple-element.20.refs_0_), channel_id=1, source_target_pairs={{0,1},{1,0},{2,3},{3,2},{4,5},{5,4},{6,7},{7,6},{8,9},{9,8},{10,11... | collective-permute-start | bytes 393224 | tf_op jit(solution)/shard_map/ppermute | solution.py:333
  21.7 5.5 %collective-permute-start.7 = (f32[1,2,128,128]{3,2,1,0:T(8,128)S(1)}, f32[1,2,128,128]{3,2,1,0:T(8,128)S(1)}, u32[]{:S(2)}, u32[]{:S(2)}) collective-permute-start(f32[1,2,128,128]{3,2,1,0:T(8,128)S(1)} %collective-permute-done.3.refs_1_), channel_id=1, source_target_pairs={{0,1},{1,0},{2,3},{3,2},{4,5},{5,4},{6,7},{7,6},{8,9},{9,8},{10,11... | collective-permute-start | bytes 393224 | tf_op jit(solution)/shard_map/ppermute | solution.py:333
  24.6 3.7 %collective-permute-start.8 = (f32[1,2,128,128]{3,2,1,0:T(8,128)S(1)}, f32[1,2,128,128]{3,2,1,0:T(8,128)S(1)}, u32[]{:S(2)}, u32[]{:S(2)}) collective-permute-start(f32[1,2,128,128]{3,2,1,0:T(8,128)S(1)} %collective-permute-done.4.refs_2_), channel_id=1, source_target_pairs={{0,1},{1,0},{2,3},{3,2},{4,5},{5,4},{6,7},{7,6},{8,9},{9,8},{10,11... | collective-permute-start | bytes 393224 | tf_op jit(solution)/shard_map/ppermute | solution.py:333
  27.2 1.3 %collective-permute-start.9 = (f32[1,2,128,128]{3,2,1,0:T(8,128)S(1)}, f32[1,2,128,128]{3,2,1,0:T(8,128)S(1)}, u32[]{:S(2)}, u32[]{:S(2)}) collective-permute-start(f32[1,2,128,128]{3,2,1,0:T(8,128)S(1)} %collective-permute-done.5.refs_3_), channel_id=1, source_target_pairs={{0,1},{1,0},{2,3},{3,2},{4,5},{5,4},{6,7},{7,6},{8,9},{9,8},{10,11... | collective-permute-start | bytes 393224 | tf_op jit(solution)/shard_map/ppermute | solution.py:333
  28.7 19.4 %copy-start = (s32[4]{0:T(128)S(1)}, s32[4]{0:T(128)}, u32[]{:S(2)}) copy-start(s32[4]{0:T(128)} %shift_ref.3) | copy-start | bytes 52
  28.7 19.4 %copy-start.1 = (f32[4]{0:T(128)S(1)}, f32[4]{0:T(128)}, u32[]{:S(2)}) copy-start(f32[4]{0:T(128)} %weight_ref.3) | copy-start | bytes 52
  28.7 11.6 %collective-permute-start.10 = (f32[4,2,128,128]{3,2,1,0:T(8,128)S(1)}, f32[4,2,128,128]{3,2,1,0:T(8,128)S(1)}, u32[]{:S(2)}, u32[]{:S(2)}) collective-permute-start(f32[4,2,128,128]{3,2,1,0:T(8,128)S(1)} %get-tuple-element.24.refs_0_), channel_id=1, source_target_pairs={{0,2},{3,1},{2,4},{5,3},{4,6},{7,5},{8,10},{11,9},{10,12},{13,11},... | collective-permute-start | bytes 1572872 | tf_op jit(solution)/shard_map/ppermute | solution.py:353
  30.8 14.1 %collective-permute-start.12 = (f32[4,2,128,128]{3,2,1,0:T(8,128)S(1)}, f32[4,2,128,128]{3,2,1,0:T(8,128)S(1)}, u32[]{:S(2)}, u32[]{:S(2)}) collective-permute-start(f32[4,2,128,128]{3,2,1,0:T(8,128)S(1)} %get-tuple-element.25.refs_2_), channel_id=1, source_target_pairs={{1,3},{2,0},{3,5},{4,2},{5,7},{6,4},{9,11},{10,8},{11,13},{12,10},... | collective-permute-start | bytes 1572872 | tf_op jit(solution)/shard_map/ppermute | solution.py:353
  40.3 9.3 %collective-permute-start.11 = (f32[4,2,128,128]{3,2,1,0:T(8,128)S(1)}, f32[4,2,128,128]{3,2,1,0:T(8,128)S(1)}, u32[]{:S(2)}, u32[]{:S(2)}) collective-permute-start(f32[4,2,128,128]{3,2,1,0:T(8,128)S(1)} %collective-permute-done.10.refs_1_), channel_id=1, source_target_pairs={{3,1},{2,4},{5,3},{4,6},{11,9},{10,12},{13,11},{12,14},{19,17},{18... | collective-permute-start | bytes 1572872 | tf_op jit(solution)/shard_map/ppermute | solution.py:353
  44.9 15.2 %collective-permute-start.13 = (f32[4,2,128,128]{3,2,1,0:T(8,128)S(1)}, f32[4,2,128,128]{3,2,1,0:T(8,128)S(1)}, u32[]{:S(2)}, u32[]{:S(2)}) collective-permute-start(f32[4,2,128,128]{3,2,1,0:T(8,128)S(1)} %collective-permute-done.12.refs_3_), channel_id=1, source_target_pairs={{2,0},{3,5},{4,2},{5,7},{10,8},{11,13},{12,10},{13,15},{18,16},{19... | collective-permute-start | bytes 1572872 | tf_op jit(solution)/shard_map/ppermute | solution.py:353

commit v5 on v4

--- a/solution.py
+++ b/solution.py
@@ -156,42 +156,38 @@
         out_slot[...] = g_ref[peer]
 
 
-def momenta_kernel(layers, *refs):
+def momentum_kernel(momentum, layers, *refs):
     core = lax.axis_index("mom")
     here = lax.axis_index("len")
+    out_ref = refs[-1]
     per = refs[0].shape[0]
-    first, second = orders(layers)
-
-    def place(slots, order, out_ref):
-        for mask, slot in zip([0] + order, slots):
+    masks = [0] + orders(layers)[momentum]
+
+    def place(slots):
+        for mask, slot in zip(masks, slots):
             for p in range(per):
                 out_ref[(here ^ mask) * per + p] = slot[p]
 
-    own, other = refs[:layers], refs[layers : 2 * layers]
-
-    @pl.when(core == 0)
+    @pl.when(core == momentum)
     def _():
-        place(own, first, refs[-2])
-        place(other, second, refs[-1])
-
-    @pl.when(core != 0)
+        place(refs[:layers])
+
+    @pl.when(core != momentum)
     def _():
-        place(other, first, refs[-2])
-        place(own, second, refs[-1])
+        place(refs[layers : 2 * layers])
 
 
 def occupation(pos, total, n):
     return 1.0 / (1.0 + jnp.exp(8.0 * jnp.full((1, n), pos, jnp.int32).astype(F32) / total - 4.0))
 
 
-def mix_kernel(total, distances, first, last, shift_ref, weight_ref, *refs):
-    count = len(distances)
-    blocks = refs[:count], refs[count : 2 * count]
-    inputs = 2 * count + (0 if first else 2)
-    sums_in = refs[2 * count : inputs]
+def mix_kernel(total, items, first, last, shift_ref, weight_ref, *refs):
+    count = len(items)
+    inputs = count + (0 if first else 2)
+    sums_in = refs[count:inputs]
     results = refs[inputs : inputs + 2]
     targets = refs[inputs + 2 : inputs + 4] if last else results
-    local_e, _, n, _ = blocks[0][0].shape
+    local_e, _, n, _ = refs[0].shape
     phonons = shift_ref.shape[0]
     start = lax.axis_index("energy") * local_e
     core = lax.axis_index("mom")
@@ -207,19 +203,20 @@
     def copy_out(i, a):
         return pltpu.make_async_copy(targets[i].at[a], results[i].at[a], refs[-1].at[i, a])
 
-    def body(own, other):
+    def body(here):
         most = total // 2
         coefficients = {}
-        for d in distances:
-            for t in range(d * local_e - local_e + 1, d * local_e + local_e):
-                if 1 <= t <= most and t not in coefficients:
-                    coefficients[t] = coefficient(t)
-        occ_own = {}
-        occ_other = {}
-        for d in distances:
+        terms = [[] for _ in range(local_e)]
+        for i, (momentum, d) in enumerate(items):
+            sign, factor = (-1, 1.0) if momentum == here else (1, 0.5)
             for b in range(local_e):
-                occ_own[d, b] = occupation(start - d * local_e + b, total, n)
-                occ_other[d, b] = occupation(start + d * local_e + b, total, n)
+                occ = occupation(start + sign * d * local_e + b, total, n)
+                for a in range(local_e):
+                    t = d * local_e + sign * (b - a)
+                    if 1 <= t <= most:
+                        if t not in coefficients:
+                            coefficients[t] = coefficient(t)
+                        terms[a].append((refs[i], b, coefficients[t] * factor, occ))
         for a in range(local_e):
             if first:
                 ret = [jnp.zeros((n, n), F32)] * 2
@@ -227,19 +224,11 @@
             else:
                 ret = [sums_in[0][a, c] for c in range(2)]
                 les = [sums_in[1][a, c] for c in range(2)]
-            for i, d in enumerate(distances):
-                for b in range(local_e):
-                    for source, t, occ, factor in (
-                        (own[i], d * local_e + a - b, occ_own[d, b], 1.0),
-                        (other[i], d * local_e + b - a, occ_other[d, b], 0.5),
-                    ):
-                        if not 1 <= t <= most:
-                            continue
-                        w = coefficients[t] * factor
-                        for c in range(2):
-                            value = w * source[b, c]
-                            ret[c] = ret[c] + value
-                            les[c] = les[c] + occ * value
+            for source, b, w, occ in terms[a]:
+                for c in range(2):
+                    value = w * source[b, c]
+                    ret[c] = ret[c] + value
+                    les[c] = les[c] + occ * value
             if last:
                 les = [les[0] - les[0].T, les[1] + les[1].T]
             for c in range(2):
@@ -251,11 +240,11 @@
 
     @pl.when(core == 0)
     def _():
-        body(*blocks)
+        body(0)
 
     @pl.when(core != 0)
     def _():
-        body(*blocks[::-1])
+        body(1)
 
     if last:
         for a in range(local_e):
@@ -330,15 +319,22 @@
         name="chains",
     )(*[exchange(sent, i) for i in range(layers)])
     own = [exchange(sent, i) for i in range(layers)]
-    other = [lax.ppermute(v, "mom", [(k, moms - 1 - k) for k in range(moms)]) for v in own]
-    zero, one = pl.pallas_call(
-        functools.partial(momenta_kernel, layers),
-        out_shape=[block] * 2,
-        in_specs=whole(2 * layers),
-        out_specs=whole(2),
-        compiler_params=params(),
-        name="momenta",
-    )(*own, *other)
+    both_ways = [(k, moms - 1 - k) for k in range(moms)]
+    other = [lax.ppermute(v, "mom", both_ways) for v in own[:-1]]
+
+    def momentum_blocks(momentum, last_slot):
+        return pl.pallas_call(
+            functools.partial(momentum_kernel, momentum, layers),
+            out_shape=block,
+            in_specs=whole(2 * layers),
+            out_specs=whole(1)[0],
+            compiler_params=params(),
+            name="momentum",
+        )(*own, *other, last_slot)
+
+    zero = momentum_blocks(0, lax.ppermute(own[-1], "mom", both_ways[:1]))
+    held, _ = lax.optimization_barrier((own[-1], zero))
+    one = momentum_blocks(1, lax.ppermute(held, "mom", both_ways[1:]))
 
     reach = -(-(total // 2) // local_e)
 
@@ -352,30 +348,29 @@
                 pairs.append((high + 1 - role, low + 1 - role))
         return lax.ppermute(value, ("energy", "mom"), pairs)
 
-    zeros = [zero]
-    ones = [one]
-    for d in range(1, reach + 1):
-        zeros.append(hop(zeros[-1], d, 0))
-        ones.append(hop(ones[-1], d, 1))
-
-    groups = [(0, 1)] + [
-        tuple(range(d, min(d + 4, reach + 1))) for d in range(2, reach + 1, 4)
-    ]
     smem = pl.BlockSpec(memory_space=pltpu.SMEM)
-    sums = []
-    for i, group in enumerate(groups):
-        blocks = [zeros[d] for d in group] + [ones[d] for d in group] + list(sums)
-        last = i == len(groups) - 1
+
+    def mix(items, blocks, sums, last=False):
         scratch = [pltpu.VMEM(block.shape, F32)] * 2 + [pltpu.SemaphoreType.DMA((2, local_e))]
-        sums = pl.pallas_call(
-            functools.partial(mix_kernel, total, group, i == 0, last),
+        return pl.pallas_call(
+            functools.partial(mix_kernel, total, items, not sums, last),
             out_shape=[block] * 2,
-            in_specs=[smem, smem] + whole(len(blocks)),
+            in_specs=[smem, smem] + whole(len(blocks) + len(sums)),
             out_specs=[pl.BlockSpec(memory_space=pl.ANY)] * 2 if last else whole(2),
             scratch_shapes=scratch if last else [],
             compiler_params=params(),
             name="mix",
-        )(phonon_shift, phonon_weight, *blocks)
+        )(phonon_shift, phonon_weight, *blocks, *sums)
+
+    sums = mix([(0, 0), (1, 0)], [zero, one], [])
+    one, _ = lax.optimization_barrier((one, sums))
+    for d in range(1, reach + 1):
+        zero = hop(zero, d, 0)
+        one = hop(one, d, 1)
+        if d < reach:
+            sums = mix([(0, d), (1, d)], [zero, one], sums)
+    sums = mix([(0, reach)], [zero], sums)
+    sums = mix([(1, reach)], [one], sums, last=True)
     retarded, lesser = sums
     return (retarded[None, None], lesser[None, None])
 

time: 62.2 us -> 63.5 us (1.021)
  the two profiles are of different devices: /device:TPU:17 before, /device:TPU:0 now
where the time goes in v5:
time: 63.5 us; the launch traced here: 62.8 us
  waiting for transfers between devices  32.1 us (51%)
  starting transfers between devices  18.7 us (29%)
  Pallas kernels  11.2 us (18%)
  between operations  0.82 us (1%)
    ppermute x4, waiting for transfers between devices, hop(): return lax.ppermute(value, ('energy', 'mom'), pairs)  18.7 us
    ppermute x6, waiting for transfers between devices, exchange(): return lax.ppermute(slots[i], ('len', 'mom'), pairs)  12.5 us
    ppermute x6, starting transfers between devices, exchange(): return lax.ppermute(slots[i], ('len', 'mom'), pairs)  8.17 us
    ppermute x4, starting transfers between devices, hop(): return lax.ppermute(value, ('energy', 'mom'), pairs)  6.77 us
    pallas_call x2, Pallas kernels, inverse(): pl.pallas_call(functools.partial(inverse_kernel, total, layers, slots), o...  4.51 us
    pallas_call x4, Pallas kernels, mix(): pl.pallas_call(functools.partial(mix_kernel, total, items, not sums, last...  4.42 us
    ppermute x1, starting transfers between devices, shards(): zero = momentum_blocks(0, lax.ppermute(own[-1], 'mom', both_ways[:1]))  2.41 us
    pallas_call x1, Pallas kernels, shards(): pl.pallas_call(functools.partial(chain_kernel, layers), out_shape=[part]...  2.22 us
  transfers between devices with their start and end apart: 15, of which 9 were waited for; matrix products, arithmetic and copies ran while one was open for 0% of the time, Pallas kernels for 8%

profile of v5, /device:TPU:0, one launch (start us, length us, event | category | flops | bytes accessed | tf_op | source)
XLA Modules:
  0.0 62.8 jit_solution(7431784304344826973)
XLA Ops:
  0.6 2.3 %inverse.3 = (f32[3,128,128]{2,1,0:T(8,128)S(1)}, f32[3,128,128]{2,1,0:T(8,128)S(1)}) custom-call(f32[2,128,128]{2,1,0:T(8,128)} %bitcast.9, f32[4,2,128,128]{3,2,1,0:T(8,128)} %bitcast.5, f32[128,128]{1,0:T(8,128)} %bitcast.11, s32[128,128]{1,0:T(8,128)} %pattern_any.3), custom_call_target="tpu_custom_call" | custom-call | flops 402653184 | bytes 262144 | tf_op jit(solution)/shard_map/inverse/pallas_call | solution.py:288
  2.9 3.0 %collective-permute-start = (f32[3,128,128]{2,1,0:T(8,128)S(1)}, f32[3,128,128]{2,1,0:T(8,128)S(1)}, u32[]{:S(2)}, u32[]{:S(2)}) collective-permute-start(f32[3,128,128]{2,1,0:T(8,128)S(1)} %get-tuple-element.21), channel_id=1, source_target_pairs={{0,8},{1,17},{8,0},{9,25},{16,24},{17,1},{24,16},{25,9},{2,10},{3,... | collective-permute-start | bytes 589832 | tf_op jit(solution)/shard_map/ppermute | solution.py:281
  5.9 1.5 %collective-permute-start.1 = (f32[3,128,128]{2,1,0:T(8,128)S(1)}, f32[3,128,128]{2,1,0:T(8,128)S(1)}, u32[]{:S(2)}, u32[]{:S(2)}) collective-permute-start(f32[3,128,128]{2,1,0:T(8,128)S(1)} %get-tuple-element.22), channel_id=1, source_target_pairs={{0,16},{1,9},{8,24},{9,1},{16,0},{17,25},{24,8},{25,17},{2,18},{3,... | collective-permute-start | bytes 589832 | tf_op jit(solution)/shard_map/ppermute | solution.py:281
  7.4 2.2 %inverse.2 = (f32[3,128,128]{2,1,0:T(8,128)S(1)}, f32[3,128,128]{2,1,0:T(8,128)S(1)}) custom-call(f32[2,128,128]{2,1,0:T(8,128)} %bitcast.10, f32[4,2,128,128]{3,2,1,0:T(8,128)} %bitcast.6, f32[128,128]{1,0:T(8,128)} %bitcast.12, s32[128,128]{1,0:T(8,128)} %pattern_any.3), custom_call_target="tpu_custom_call" | custom-call | flops 402653184 | bytes 262144 | tf_op jit(solution)/shard_map/inverse/pallas_call | solution.py:288
  9.7 0.1 collective-permute-start.2
  9.8 1.3 %collective-permute-done.refs_1_ = f32[3,128,128]{2,1,0:T(8,128)S(1)} collective-permute-done((f32[3,128,128]{2,1,0:T(8,128)S(1)}, f32[3,128,128]{2,1,0:T(8,128)S(1)}, u32[]{:S(2)}, u32[]{:S(2)}) %collective-permute-start) | collective-permute-done | bytes 196640 | tf_op jit(solution)/shard_map/ppermute | solution.py:281
  11.1 0.5 collective-permute-done.1.refs_2_
  11.6 5.2 %collective-permute-done.2.refs_3_ = f32[3,128,128]{2,1,0:T(8,128)S(1)} collective-permute-done((f32[3,128,128]{2,1,0:T(8,128)S(1)}, f32[3,128,128]{2,1,0:T(8,128)S(1)}, u32[]{:S(2)}, u32[]{:S(2)}) %collective-permute-start.2) | collective-permute-done | bytes 196640 | tf_op jit(solution)/shard_map/ppermute | solution.py:281
  16.7 2.2 %chains.1 = (f32[1,2,128,128]{3,2,1,0:T(8,128)S(1)}, f32[1,2,128,128]{3,2,1,0:T(8,128)S(1)}, f32[1,2,128,128]{3,2,1,0:T(8,128)S(1)}, f32[1,2,128,128]{3,2,1,0:T(8,128)S(1)}) custom-call(f32[3,128,128]{2,1,0:T(8,128)S(1)} %get-tuple-element.20.refs_0_, f32[3,128,128]{2,1,0:T(8,128)S(1)} %collective-permute-done.refs_1_, ...), custom_call_target="tpu_custom_call" | custom-call | tf_op jit(solution)/shard_map/chains/pallas_call | solution.py:312
  19.0 1.3 %collective-permute-start.3 = (f32[1,2,128,128]{3,2,1,0:T(8,128)S(1)}, f32[1,2,128,128]{3,2,1,0:T(8,128)S(1)}, u32[]{:S(2)}, u32[]{:S(2)}) collective-permute-start(f32[1,2,128,128]{3,2,1,0:T(8,128)S(1)} %get-tuple-element.25), channel_id=1, source_target_pairs={{0,8},{1,17},{8,0},{9,25},{16,24},{17,1},{24,16},{25,9},{2,10},{3,... | collective-permute-start | bytes 393224 | tf_op jit(solution)/shard_map/ppermute | solution.py:281
  20.2 1.3 %collective-permute-start.4 = (f32[1,2,128,128]{3,2,1,0:T(8,128)S(1)}, f32[1,2,128,128]{3,2,1,0:T(8,128)S(1)}, u32[]{:S(2)}, u32[]{:S(2)}) collective-permute-start(f32[1,2,128,128]{3,2,1,0:T(8,128)S(1)} %get-tuple-element.26), channel_id=1, source_target_pairs={{0,16},{1,9},{8,24},{9,1},{16,0},{17,25},{24,8},{25,17},{2,18},{3,... | collective-permute-start | bytes 393224 | tf_op jit(solution)/shard_map/ppermute | solution.py:281
  21.5 1.0 %collective-permute-start.5 = (f32[1,2,128,128]{3,2,1,0:T(8,128)S(1)}, f32[1,2,128,128]{3,2,1,0:T(8,128)S(1)}, u32[]{:S(2)}, u32[]{:S(2)}) collective-permute-start(f32[1,2,128,128]{3,2,1,0:T(8,128)S(1)} %get-tuple-element.27), channel_id=1, source_target_pairs={{0,24},{1,25},{8,16},{9,17},{16,8},{17,9},{24,0},{25,1},{2,26},{3,... | collective-permute-start | bytes 393224 | tf_op jit(solution)/shard_map/ppermute | solution.py:281
  22.5 0.0 collective-permute-start.6
  22.5 2.8 %collective-permute-done.3.refs_1_ = f32[1,2,128,128]{3,2,1,0:T(8,128)S(1)} collective-permute-done((f32[1,2,128,128]{3,2,1,0:T(8,128)S(1)}, f32[1,2,128,128]{3,2,1,0:T(8,128)S(1)}, u32[]{:S(2)}, u32[]{:S(2)}) %collective-permute-start.3) | collective-permute-done | bytes 131104 | tf_op jit(solution)/shard_map/ppermute | solution.py:281
  25.3 2.7 %collective-permute-done.4.refs_2_ = f32[1,2,128,128]{3,2,1,0:T(8,128)S(1)} collective-permute-done((f32[1,2,128,128]{3,2,1,0:T(8,128)S(1)}, f32[1,2,128,128]{3,2,1,0:T(8,128)S(1)}, u32[]{:S(2)}, u32[]{:S(2)}) %collective-permute-start.4) | collective-permute-done | bytes 131104 | tf_op jit(solution)/shard_map/ppermute | solution.py:281
  28.0 2.4 %collective-permute-start.9 = (f32[1,2,128,128]{3,2,1,0:T(8,128)S(1)}, f32[1,2,128,128]{3,2,1,0:T(8,128)S(1)}, u32[]{:S(2)}, u32[]{:S(2)}) collective-permute-start(f32[1,2,128,128]{3,2,1,0:T(8,128)S(1)} %collective-permute-done.5.refs_3_), channel_id=1, source_target_pairs={{0,1},{2,3},{4,5},{6,7},{8,9},{10,11},{12,13},{14,15},{16,17},{18,... | collective-permute-start | bytes 393224 | tf_op jit(solution)/shard_map/ppermute | solution.py:335
  30.5 0.9 %collective-permute-done.9.refs_7_ = f32[1,2,128,128]{3,2,1,0:T(8,128)S(1)} collective-permute-done((f32[1,2,128,128]{3,2,1,0:T(8,128)S(1)}, f32[1,2,128,128]{3,2,1,0:T(8,128)S(1)}, u32[]{:S(2)}, u32[]{:S(2)}) %collective-permute-start.9) | collective-permute-done | bytes 131104 | tf_op jit(solution)/shard_map/ppermute | solution.py:335
  31.4 0.0 copy-start
  31.5 0.0 copy-start.1
  31.5 1.3 %collective-permute-start.10 = (f32[1,2,128,128]{3,2,1,0:T(8,128)S(1)}, f32[1,2,128,128]{3,2,1,0:T(8,128)S(1)}, u32[]{:S(2)}, u32[]{:S(2)}) collective-permute-start(f32[1,2,128,128]{3,2,1,0:T(8,128)S(1)} %collective-permute-done.5.refs_3_), channel_id=1, source_target_pairs={{1,0},{3,2},{5,4},{7,6},{9,8},{11,10},{13,12},{15,14},{17,16},{19,... | collective-permute-start | bytes 393224 | tf_op jit(solution)/shard_map/ppermute | solution.py:337
  32.8 3.5 %collective-permute-start.13 = (f32[4,2,128,128]{3,2,1,0:T(8,128)S(1)}, f32[4,2,128,128]{3,2,1,0:T(8,128)S(1)}, u32[]{:S(2)}, u32[]{:S(2)}) collective-permute-start(f32[4,2,128,128]{3,2,1,0:T(8,128)S(1)} %momentum.2.refs_0_), channel_id=1, source_target_pairs={{0,2},{3,1},{2,4},{5,3},{4,6},{7,5},{8,10},{11,9},{10,12},{13,11},... | collective-permute-start | bytes 1572872 | tf_op jit(solution)/shard_map/ppermute | solution.py:349
  36.3 0.1 momentum.3.refs_1_
  36.4 0.8 %mix.4 = (f32[4,2,128,128]{3,2,1,0:T(8,128)S(1)}, f32[4,2,128,128]{3,2,1,0:T(8,128)S(1)}) custom-call(s32[4]{0:T(128)S(1)} %copy-done, f32[4]{0:T(128)S(1)} %copy-done.1, f32[4,2,128,128]{3,2,1,0:T(8,128)S(1)} %momentum.2.refs_0_, f32[4,2,128,128]{3,2,1,0:T(8,128)S(1)} %momentum.3.refs_1_), custom_call_target="tpu_custom_call" | custom-call | tf_op jit(solution)/shard_map/mix/pallas_call | solution.py:355
  37.2 1.3 %collective-permute-start.11 = (f32[4,2,128,128]{3,2,1,0:T(8,128)S(1)}, f32[4,2,128,128]{3,2,1,0:T(8,128)S(1)}, u32[]{:S(2)}, u32[]{:S(2)}) collective-permute-start(f32[4,2,128,128]{3,2,1,0:T(8,128)S(1)} %momentum.3.refs_1_), channel_id=1, source_target_pairs={{1,3},{2,0},{3,5},{4,2},{5,7},{6,4},{9,11},{10,8},{11,13},{12,10},... | collective-permute-start | bytes 1572872 | tf_op jit(solution)/shard_map/ppermute | solution.py:349
  38.5 6.9 %collective-permute-done.13.refs_0_ = f32[4,2,128,128]{3,2,1,0:T(8,128)S(1)} collective-permute-done((f32[4,2,128,128]{3,2,1,0:T(8,128)S(1)}, f32[4,2,128,128]{3,2,1,0:T(8,128)S(1)}, u32[]{:S(2)}, u32[]{:S(2)}) %collective-permute-start.13) | collective-permute-done | bytes 524320 | tf_op jit(solution)/shard_map/ppermute | solution.py:349
  45.4 0.7 %collective-permute-start.14 = (f32[4,2,128,128]{3,2,1,0:T(8,128)S(1)}, f32[4,2,128,128]{3,2,1,0:T(8,128)S(1)}, u32[]{:S(2)}, u32[]{:S(2)}) collective-permute-start(f32[4,2,128,128]{3,2,1,0:T(8,128)S(1)} %collective-permute-done.13.refs_0_), channel_id=1, source_target_pairs={{3,1},{2,4},{5,3},{4,6},{11,9},{10,12},{13,11},{12,14},{19,17},{18... | collective-permute-start | bytes 1572872 | tf_op jit(solution)/shard_map/ppermute | solution.py:349
  46.1 3.5 %collective-permute-done.11.refs_1_ = f32[4,2,128,128]{3,2,1,0:T(8,128)S(1)} collective-permute-done((f32[4,2,128,128]{3,2,1,0:T(8,128)S(1)}, f32[4,2,128,128]{3,2,1,0:T(8,128)S(1)}, u32[]{:S(2)}, u32[]{:S(2)}) %collective-permute-start.11) | collective-permute-done | bytes 524320 | tf_op jit(solution)/shard_map/ppermute | solution.py:349
  49.6 1.3 %collective-permute-start.12 = (f32[4,2,128,128]{3,2,1,0:T(8,128)S(1)}, f32[4,2,128,128]{3,2,1,0:T(8,128)S(1)}, u32[]{:S(2)}, u32[]{:S(2)}) collective-permute-start(f32[4,2,128,128]{3,2,1,0:T(8,128)S(1)} %collective-permute-done.11.refs_1_), channel_id=1, source_target_pairs={{2,0},{3,5},{4,2},{5,7},{10,8},{11,13},{12,10},{13,15},{18,16},{19... | collective-permute-start | bytes 1572872 | tf_op jit(solution)/shard_map/ppermute | solution.py:349
  50.9 1.2 %mix.5 = (f32[4,2,128,128]{3,2,1,0:T(8,128)S(1)}, f32[4,2,128,128]{3,2,1,0:T(8,128)S(1)}) custom-call(s32[4]{0:T(128)S(1)} %copy-done, f32[4]{0:T(128)S(1)} %copy-done.1, f32[4,2,128,128]{3,2,1,0:T(8,128)S(1)} %collective-permute-done.13.refs_0_, f32[4,2,128,128]{3,2,1,0:T(8,128)S(1)} %collective-permute-done.11.refs_1_, ...), custom_call_target="tpu_custom_call" | custom-call | tf_op jit(solution)/shard_map/mix/pallas_call | solution.py:355
  52.1 0.8 %mix.6 = (f32[4,2,128,128]{3,2,1,0:T(8,128)S(1)}, f32[4,2,128,128]{3,2,1,0:T(8,128)S(1)}) custom-call(s32[4]{0:T(128)S(1)} %copy-done, f32[4]{0:T(128)S(1)} %copy-done.1, f32[4,2,128,128]{3,2,1,0:T(8,128)S(1)} %collective-permute-done.14.refs_0_, f32[4,2,128,128]{3,2,1,0:T(8,128)S(1)} %get-tuple-element.32.refs_1_, ...), custom_call_target="tpu_custom_call" | custom-call | tf_op jit(solution)/shard_map/mix/pallas_call | solution.py:355
  52.9 8.2 %collective-permute-done.12.refs_0_ = f32[4,2,128,128]{3,2,1,0:T(8,128)S(1)} collective-permute-done((f32[4,2,128,128]{3,2,1,0:T(8,128)S(1)}, f32[4,2,128,128]{3,2,1,0:T(8,128)S(1)}, u32[]{:S(2)}, u32[]{:S(2)}) %collective-permute-start.12) | collective-permute-done | bytes 524320 | tf_op jit(solution)/shard_map/ppermute | solution.py:349
  61.1 1.7 %mix.7 = (f32[4,2,128,128]{3,2,1,0:T(8,128)}, f32[4,2,128,128]{3,2,1,0:T(8,128)}) custom-call(s32[4]{0:T(128)S(1)} %copy-done, f32[4]{0:T(128)S(1)} %copy-done.1, f32[4,2,128,128]{3,2,1,0:T(8,128)S(1)} %collective-permute-done.12.refs_0_, f32[4,2,128,128]{3,2,1,0:T(8,128)S(1)} %get-tuple-element.34.refs_1_, f32[4,2,128,128]{3,2,1,0:T(8,128)S(1)} %get-tuple-element.35.refs_2_), custom_call_target="tpu_custom_call" | custom-call | tf_op jit(solution)/shard_map/mix/pallas_call | solution.py:355
  (11 shorter events, 0.1 us)
Async XLA Ops:
  2.9 8.2 %collective-permute-start = (f32[3,128,128]{2,1,0:T(8,128)S(1)}, f32[3,128,128]{2,1,0:T(8,128)S(1)}, u32[]{:S(2)}, u32[]{:S(2)}) collective-permute-start(f32[3,128,128]{2,1,0:T(8,128)S(1)} %get-tuple-element.21), channel_id=1, source_target_pairs={{0,8},{1,17},{8,0},{9,25},{16,24},{17,1},{24,16},{25,9},{2,10},{3,... | collective-permute-start | bytes 589832 | tf_op jit(solution)/shard_map/ppermute | solution.py:281
  5.9 5.7 %collective-permute-start.1 = (f32[3,128,128]{2,1,0:T(8,128)S(1)}, f32[3,128,128]{2,1,0:T(8,128)S(1)}, u32[]{:S(2)}, u32[]{:S(2)}) collective-permute-start(f32[3,128,128]{2,1,0:T(8,128)S(1)} %get-tuple-element.22), channel_id=1, source_target_pairs={{0,16},{1,9},{8,24},{9,1},{16,0},{17,25},{24,8},{25,17},{2,18},{3,... | collective-permute-start | bytes 589832 | tf_op jit(solution)/shard_map/ppermute | solution.py:281
  9.7 7.1 %collective-permute-start.2 = (f32[3,128,128]{2,1,0:T(8,128)S(1)}, f32[3,128,128]{2,1,0:T(8,128)S(1)}, u32[]{:S(2)}, u32[]{:S(2)}) collective-permute-start(f32[3,128,128]{2,1,0:T(8,128)S(1)} %get-tuple-element.23), channel_id=1, source_target_pairs={{0,24},{1,25},{8,16},{9,17},{16,8},{17,9},{24,0},{25,1},{2,26},{3,... | collective-permute-start | bytes 589832 | tf_op jit(solution)/shard_map/ppermute | solution.py:281
  19.0 6.3 %collective-permute-start.3 = (f32[1,2,128,128]{3,2,1,0:T(8,128)S(1)}, f32[1,2,128,128]{3,2,1,0:T(8,128)S(1)}, u32[]{:S(2)}, u32[]{:S(2)}) collective-permute-start(f32[1,2,128,128]{3,2,1,0:T(8,128)S(1)} %get-tuple-element.25), channel_id=1, source_target_pairs={{0,8},{1,17},{8,0},{9,25},{16,24},{17,1},{24,16},{25,9},{2,10},{3,... | collective-permute-start | bytes 393224 | tf_op jit(solution)/shard_map/ppermute | solution.py:281
  20.2 7.8 %collective-permute-start.4 = (f32[1,2,128,128]{3,2,1,0:T(8,128)S(1)}, f32[1,2,128,128]{3,2,1,0:T(8,128)S(1)}, u32[]{:S(2)}, u32[]{:S(2)}) collective-permute-start(f32[1,2,128,128]{3,2,1,0:T(8,128)S(1)} %get-tuple-element.26), channel_id=1, source_target_pairs={{0,16},{1,9},{8,24},{9,1},{16,0},{17,25},{24,8},{25,17},{2,18},{3,... | collective-permute-start | bytes 393224 | tf_op jit(solution)/shard_map/ppermute | solution.py:281
  21.5 6.5 %collective-permute-start.5 = (f32[1,2,128,128]{3,2,1,0:T(8,128)S(1)}, f32[1,2,128,128]{3,2,1,0:T(8,128)S(1)}, u32[]{:S(2)}, u32[]{:S(2)}) collective-permute-start(f32[1,2,128,128]{3,2,1,0:T(8,128)S(1)} %get-tuple-element.27), channel_id=1, source_target_pairs={{0,24},{1,25},{8,16},{9,17},{16,8},{17,9},{24,0},{25,1},{2,26},{3,... | collective-permute-start | bytes 393224 | tf_op jit(solution)/shard_map/ppermute | solution.py:281
  22.5 7.9 %collective-permute-start.6 = (f32[1,2,128,128]{3,2,1,0:T(8,128)S(1)}, f32[1,2,128,128]{3,2,1,0:T(8,128)S(1)}, u32[]{:S(2)}, u32[]{:S(2)}) collective-permute-start(f32[1,2,128,128]{3,2,1,0:T(8,128)S(1)} %get-tuple-element.24.refs_0_), channel_id=1, source_target_pairs={{0,1},{1,0},{2,3},{3,2},{4,5},{5,4},{6,7},{7,6},{8,9},{9,8},{10,11... | collective-permute-start | bytes 393224 | tf_op jit(solution)/shard_map/ppermute | solution.py:323
  25.3 5.1 %collective-permute-start.7 = (f32[1,2,128,128]{3,2,1,0:T(8,128)S(1)}, f32[1,2,128,128]{3,2,1,0:T(8,128)S(1)}, u32[]{:S(2)}, u32[]{:S(2)}) collective-permute-start(f32[1,2,128,128]{3,2,1,0:T(8,128)S(1)} %collective-permute-done.3.refs_1_), channel_id=1, source_target_pairs={{0,1},{1,0},{2,3},{3,2},{4,5},{5,4},{6,7},{7,6},{8,9},{9,8},{10,11... | collective-permute-start | bytes 393224 | tf_op jit(solution)/shard_map/ppermute | solution.py:323
  28.0 2.4 %collective-permute-start.8 = (f32[1,2,128,128]{3,2,1,0:T(8,128)S(1)}, f32[1,2,128,128]{3,2,1,0:T(8,128)S(1)}, u32[]{:S(2)}, u32[]{:S(2)}) collective-permute-start(f32[1,2,128,128]{3,2,1,0:T(8,128)S(1)} %collective-permute-done.4.refs_2_), channel_id=1, source_target_pairs={{0,1},{1,0},{2,3},{3,2},{4,5},{5,4},{6,7},{7,6},{8,9},{9,8},{10,11... | collective-permute-start | bytes 393224 | tf_op jit(solution)/shard_map/ppermute | solution.py:323
  28.0 3.4 %collective-permute-start.9 = (f32[1,2,128,128]{3,2,1,0:T(8,128)S(1)}, f32[1,2,128,128]{3,2,1,0:T(8,128)S(1)}, u32[]{:S(2)}, u32[]{:S(2)}) collective-permute-start(f32[1,2,128,128]{3,2,1,0:T(8,128)S(1)} %collective-permute-done.5.refs_3_), channel_id=1, source_target_pairs={{0,1},{2,3},{4,5},{6,7},{8,9},{10,11},{12,13},{14,15},{16,17},{18,... | collective-permute-start | bytes 393224 | tf_op jit(solution)/shard_map/ppermute | solution.py:335
  31.4 4.9 %copy-start = (s32[4]{0:T(128)S(1)}, s32[4]{0:T(128)}, u32[]{:S(2)}) copy-start(s32[4]{0:T(128)} %shift_ref.7) | copy-start | bytes 52
  31.5 4.9 %copy-start.1 = (f32[4]{0:T(128)S(1)}, f32[4]{0:T(128)}, u32[]{:S(2)}) copy-start(f32[4]{0:T(128)} %weight_ref.7) | copy-start | bytes 52
  31.5 4.8 %collective-permute-start.10 = (f32[1,2,128,128]{3,2,1,0:T(8,128)S(1)}, f32[1,2,128,128]{3,2,1,0:T(8,128)S(1)}, u32[]{:S(2)}, u32[]{:S(2)}) collective-permute-start(f32[1,2,128,128]{3,2,1,0:T(8,128)S(1)} %collective-permute-done.5.refs_3_), channel_id=1, source_target_pairs={{1,0},{3,2},{5,4},{7,6},{9,8},{11,10},{13,12},{15,14},{17,16},{19,... | collective-permute-start | bytes 393224 | tf_op jit(solution)/shard_map/ppermute | solution.py:337
  32.8 12.6 %collective-permute-start.13 = (f32[4,2,128,128]{3,2,1,0:T(8,128)S(1)}, f32[4,2,128,128]{3,2,1,0:T(8,128)S(1)}, u32[]{:S(2)}, u32[]{:S(2)}) collective-permute-start(f32[4,2,128,128]{3,2,1,0:T(8,128)S(1)} %momentum.2.refs_0_), channel_id=1, source_target_pairs={{0,2},{3,1},{2,4},{5,3},{4,6},{7,5},{8,10},{11,9},{10,12},{13,11},... | collective-permute-start | bytes 1572872 | tf_op jit(solution)/shard_map/ppermute | solution.py:349
  37.2 12.5 %collective-permute-start.11 = (f32[4,2,128,128]{3,2,1,0:T(8,128)S(1)}, f32[4,2,128,128]{3,2,1,0:T(8,128)S(1)}, u32[]{:S(2)}, u32[]{:S(2)}) collective-permute-start(f32[4,2,128,128]{3,2,1,0:T(8,128)S(1)} %momentum.3.refs_1_), channel_id=1, source_target_pairs={{1,3},{2,0},{3,5},{4,2},{5,7},{6,4},{9,11},{10,8},{11,13},{12,10},... | collective-permute-start | bytes 1572872 | tf_op jit(solution)/shard_map/ppermute | solution.py:349
  45.4 6.7 %collective-permute-start.14 = (f32[4,2,128,128]{3,2,1,0:T(8,128)S(1)}, f32[4,2,128,128]{3,2,1,0:T(8,128)S(1)}, u32[]{:S(2)}, u32[]{:S(2)}) collective-permute-start(f32[4,2,128,128]{3,2,1,0:T(8,128)S(1)} %collective-permute-done.13.refs_0_), channel_id=1, source_target_pairs={{3,1},{2,4},{5,3},{4,6},{11,9},{10,12},{13,11},{12,14},{19,17},{18... | collective-permute-start | bytes 1572872 | tf_op jit(solution)/shard_map/ppermute | solution.py:349
  49.6 11.5 %collective-permute-start.12 = (f32[4,2,128,128]{3,2,1,0:T(8,128)S(1)}, f32[4,2,128,128]{3,2,1,0:T(8,128)S(1)}, u32[]{:S(2)}, u32[]{:S(2)}) collective-permute-start(f32[4,2,128,128]{3,2,1,0:T(8,128)S(1)} %collective-permute-done.11.refs_1_), channel_id=1, source_target_pairs={{2,0},{3,5},{4,2},{5,7},{10,8},{11,13},{12,10},{13,15},{18,16},{19... | collective-permute-start | bytes 1572872 | tf_op jit(solution)/shard_map/ppermute | solution.py:349

commit v6 on v5

--- a/solution.py
+++ b/solution.py
@@ -45,10 +45,10 @@
 
 
 def orders(layers):
-    first = list(range(1, layers))
+    first = [layers - 1] + list(range(1, layers - 1))
     second = list(first)
-    if layers > 2:
-        second[0], second[1] = second[1], second[0]
+    if layers > 3:
+        second[1], second[2] = second[2], second[1]
     return first, second
 
 
@@ -217,26 +217,18 @@
                         if t not in coefficients:
                             coefficients[t] = coefficient(t)
                         terms[a].append((refs[i], b, coefficients[t] * factor, occ))
-        for a in range(local_e):
-            if first:
-                ret = [jnp.zeros((n, n), F32)] * 2
-                les = list(ret)
-            else:
-                ret = [sums_in[0][a, c] for c in range(2)]
-                les = [sums_in[1][a, c] for c in range(2)]
-            for source, b, w, occ in terms[a]:
+        for i in range(2):
+            for a in range(local_e):
+                sums = [jnp.zeros((n, n), F32) if first else sums_in[i][a, c] for c in range(2)]
+                for source, b, w, occ in terms[a]:
+                    weight = w if i == 0 else w * occ
+                    sums = [sums[c] + weight * source[b, c] for c in range(2)]
+                if last and i == 1:
+                    sums = [sums[0] - sums[0].T, sums[1] + sums[1].T]
                 for c in range(2):
-                    value = w * source[b, c]
-                    ret[c] = ret[c] + value
-                    les[c] = les[c] + occ * value
-            if last:
-                les = [les[0] - les[0].T, les[1] + les[1].T]
-            for c in range(2):
-                targets[0][a, c] = ret[c]
-                targets[1][a, c] = les[c]
-            if last:
-                copy_out(0, a).start()
-                copy_out(1, a).start()
+                    targets[i][a, c] = sums[c]
+                if last:
+                    copy_out(i, a).start()
 
     @pl.when(core == 0)
     def _():
@@ -320,21 +312,18 @@
     )(*[exchange(sent, i) for i in range(layers)])
     own = [exchange(sent, i) for i in range(layers)]
     both_ways = [(k, moms - 1 - k) for k in range(moms)]
-    other = [lax.ppermute(v, "mom", both_ways) for v in own[:-1]]
-
-    def momentum_blocks(momentum, last_slot):
-        return pl.pallas_call(
+    other = [lax.ppermute(v, "mom", both_ways) for v in own]
+    zero, one = (
+        pl.pallas_call(
             functools.partial(momentum_kernel, momentum, layers),
             out_shape=block,
             in_specs=whole(2 * layers),
             out_specs=whole(1)[0],
             compiler_params=params(),
             name="momentum",
-        )(*own, *other, last_slot)
-
-    zero = momentum_blocks(0, lax.ppermute(own[-1], "mom", both_ways[:1]))
-    held, _ = lax.optimization_barrier((own[-1], zero))
-    one = momentum_blocks(1, lax.ppermute(held, "mom", both_ways[1:]))
+        )(*own, *other)
+        for momentum in range(2)
+    )
 
     reach = -(-(total // 2) // local_e)
 

time: 63.5 us -> 60.5 us (0.953)
  the two profiles are of different devices: /device:TPU:0 before, /device:TPU:17 now
where the time goes in v6:
time: 60.5 us; the launch traced here: 60.2 us
  waiting for transfers between devices  26.1 us (43%)
  starting transfers between devices  22.1 us (37%)
  Pallas kernels  11.3 us (19%)
  between operations  0.77 us (1%)
    ppermute x4, waiting for transfers between devices, hop(): return lax.ppermute(value, ('energy', 'mom'), pairs)  17.1 us
    ppermute x4, starting transfers between devices, hop(): return lax.ppermute(value, ('energy', 'mom'), pairs)  10.6 us
    ppermute x6, waiting for transfers between devices, exchange(): return lax.ppermute(slots[i], ('len', 'mom'), pairs)  7.67 us
    ppermute x4, starting transfers between devices, shards(): other = [lax.ppermute(v, 'mom', both_ways) for v in own]  6.03 us
    ppermute x6, starting transfers between devices, exchange(): return lax.ppermute(slots[i], ('len', 'mom'), pairs)  5.49 us
    pallas_call x2, Pallas kernels, inverse(): pl.pallas_call(functools.partial(inverse_kernel, total, layers, slots), o...  4.53 us
    pallas_call x4, Pallas kernels, mix(): pl.pallas_call(functools.partial(mix_kernel, total, items, not sums, last...  4.45 us
    pallas_call x1, Pallas kernels, shards(): pl.pallas_call(functools.partial(chain_kernel, layers), out_shape=[part]...  2.22 us
  transfers between devices with their start and end apart: 14, of which 10 were waited for; matrix products, arithmetic and copies ran while one was open for 0% of the time, Pallas kernels for 8%

profile of v6, /device:TPU:17, one launch (start us, length us, event | category | flops | bytes accessed | tf_op | source)
XLA Modules:
  0.0 60.2 jit_solution(2829758802957657832)
XLA Ops:
  0.6 2.3 %inverse.3 = (f32[3,128,128]{2,1,0:T(8,128)S(1)}, f32[3,128,128]{2,1,0:T(8,128)S(1)}) custom-call(f32[2,128,128]{2,1,0:T(8,128)} %bitcast.9, f32[4,2,128,128]{3,2,1,0:T(8,128)} %bitcast.5, f32[128,128]{1,0:T(8,128)} %bitcast.11, s32[128,128]{1,0:T(8,128)} %pattern_any.3), custom_call_target="tpu_custom_call" | custom-call | flops 402653184 | bytes 262144 | tf_op jit(solution)/shard_map/inverse/pallas_call | solution.py:280
  2.9 2.2 %collective-permute-start = (f32[3,128,128]{2,1,0:T(8,128)S(1)}, f32[3,128,128]{2,1,0:T(8,128)S(1)}, u32[]{:S(2)}, u32[]{:S(2)}) collective-permute-start(f32[3,128,128]{2,1,0:T(8,128)S(1)} %get-tuple-element.20), channel_id=1, source_target_pairs={{0,24},{1,25},{8,16},{9,17},{16,8},{17,9},{24,0},{25,1},{2,26},{3,... | collective-permute-start | bytes 589832 | tf_op jit(solution)/shard_map/ppermute | solution.py:273
  5.1 0.2 collective-permute-start.1
  5.4 2.3 %inverse.2 = (f32[3,128,128]{2,1,0:T(8,128)S(1)}, f32[3,128,128]{2,1,0:T(8,128)S(1)}) custom-call(f32[2,128,128]{2,1,0:T(8,128)} %bitcast.10, f32[4,2,128,128]{3,2,1,0:T(8,128)} %bitcast.6, f32[128,128]{1,0:T(8,128)} %bitcast.12, s32[128,128]{1,0:T(8,128)} %pattern_any.3), custom_call_target="tpu_custom_call" | custom-call | flops 402653184 | bytes 262144 | tf_op jit(solution)/shard_map/inverse/pallas_call | solution.py:280
  7.6 0.3 collective-permute-start.2
  8.0 1.7 %collective-permute-done.refs_1_ = f32[3,128,128]{2,1,0:T(8,128)S(1)} collective-permute-done((f32[3,128,128]{2,1,0:T(8,128)S(1)}, f32[3,128,128]{2,1,0:T(8,128)S(1)}, u32[]{:S(2)}, u32[]{:S(2)}) %collective-permute-start) | collective-permute-done | bytes 196640 | tf_op jit(solution)/shard_map/ppermute | solution.py:273
  9.7 3.9 %collective-permute-done.1.refs_2_ = f32[3,128,128]{2,1,0:T(8,128)S(1)} collective-permute-done((f32[3,128,128]{2,1,0:T(8,128)S(1)}, f32[3,128,128]{2,1,0:T(8,128)S(1)}, u32[]{:S(2)}, u32[]{:S(2)}) %collective-permute-start.1) | collective-permute-done | bytes 196640 | tf_op jit(solution)/shard_map/ppermute | solution.py:273
  13.6 1.1 %collective-permute-done.2.refs_3_ = f32[3,128,128]{2,1,0:T(8,128)S(1)} collective-permute-done((f32[3,128,128]{2,1,0:T(8,128)S(1)}, f32[3,128,128]{2,1,0:T(8,128)S(1)}, u32[]{:S(2)}, u32[]{:S(2)}) %collective-permute-start.2) | collective-permute-done | bytes 196640 | tf_op jit(solution)/shard_map/ppermute | solution.py:273
  14.7 2.2 %chains.1 = (f32[1,2,128,128]{3,2,1,0:T(8,128)S(1)}, f32[1,2,128,128]{3,2,1,0:T(8,128)S(1)}, f32[1,2,128,128]{3,2,1,0:T(8,128)S(1)}, f32[1,2,128,128]{3,2,1,0:T(8,128)S(1)}) custom-call(f32[3,128,128]{2,1,0:T(8,128)S(1)} %get-tuple-element.19.refs_0_, f32[3,128,128]{2,1,0:T(8,128)S(1)} %collective-permute-done.refs_1_, ...), custom_call_target="tpu_custom_call" | custom-call | tf_op jit(solution)/shard_map/chains/pallas_call | solution.py:304
  16.9 1.3 %collective-permute-start.3 = (f32[1,2,128,128]{3,2,1,0:T(8,128)S(1)}, f32[1,2,128,128]{3,2,1,0:T(8,128)S(1)}, u32[]{:S(2)}, u32[]{:S(2)}) collective-permute-start(f32[1,2,128,128]{3,2,1,0:T(8,128)S(1)} %get-tuple-element.24), channel_id=1, source_target_pairs={{0,24},{1,25},{8,16},{9,17},{16,8},{17,9},{24,0},{25,1},{2,26},{3,... | collective-permute-start | bytes 393224 | tf_op jit(solution)/shard_map/ppermute | solution.py:273
  18.2 0.5 collective-permute-start.4
  18.7 0.9 %collective-permute-start.5 = (f32[1,2,128,128]{3,2,1,0:T(8,128)S(1)}, f32[1,2,128,128]{3,2,1,0:T(8,128)S(1)}, u32[]{:S(2)}, u32[]{:S(2)}) collective-permute-start(f32[1,2,128,128]{3,2,1,0:T(8,128)S(1)} %get-tuple-element.26), channel_id=1, source_target_pairs={{0,16},{1,9},{8,24},{9,1},{16,0},{17,25},{24,8},{25,17},{2,18},{3,... | collective-permute-start | bytes 393224 | tf_op jit(solution)/shard_map/ppermute | solution.py:273
  19.6 1.7 %collective-permute-start.6 = (f32[1,2,128,128]{3,2,1,0:T(8,128)S(1)}, f32[1,2,128,128]{3,2,1,0:T(8,128)S(1)}, u32[]{:S(2)}, u32[]{:S(2)}) collective-permute-start(f32[1,2,128,128]{3,2,1,0:T(8,128)S(1)} %get-tuple-element.23.refs_0_), channel_id=1, source_target_pairs={{0,1},{1,0},{2,3},{3,2},{4,5},{5,4},{6,7},{7,6},{8,9},{9,8},{10,11... | collective-permute-start | bytes 393224 | tf_op jit(solution)/shard_map/ppermute | solution.py:315
  21.3 0.8 %collective-permute-done.3.refs_1_ = f32[1,2,128,128]{3,2,1,0:T(8,128)S(1)} collective-permute-done((f32[1,2,128,128]{3,2,1,0:T(8,128)S(1)}, f32[1,2,128,128]{3,2,1,0:T(8,128)S(1)}, u32[]{:S(2)}, u32[]{:S(2)}) %collective-permute-start.3) | collective-permute-done | bytes 131104 | tf_op jit(solution)/shard_map/ppermute | solution.py:273
  22.1 3.0 %collective-permute-start.7 = (f32[1,2,128,128]{3,2,1,0:T(8,128)S(1)}, f32[1,2,128,128]{3,2,1,0:T(8,128)S(1)}, u32[]{:S(2)}, u32[]{:S(2)}) collective-permute-start(f32[1,2,128,128]{3,2,1,0:T(8,128)S(1)} %collective-permute-done.3.refs_1_), channel_id=1, source_target_pairs={{0,1},{1,0},{2,3},{3,2},{4,5},{5,4},{6,7},{7,6},{8,9},{9,8},{10,11... | collective-permute-start | bytes 393224 | tf_op jit(solution)/shard_map/ppermute | solution.py:315
  25.1 0.2 collective-permute-done.4.refs_2_
  25.3 1.3 %collective-permute-start.8 = (f32[1,2,128,128]{3,2,1,0:T(8,128)S(1)}, f32[1,2,128,128]{3,2,1,0:T(8,128)S(1)}, u32[]{:S(2)}, u32[]{:S(2)}) collective-permute-start(f32[1,2,128,128]{3,2,1,0:T(8,128)S(1)} %collective-permute-done.4.refs_2_), channel_id=1, source_target_pairs={{0,1},{1,0},{2,3},{3,2},{4,5},{5,4},{6,7},{7,6},{8,9},{9,8},{10,11... | collective-permute-start | bytes 393224 | tf_op jit(solution)/shard_map/ppermute | solution.py:315
  26.6 0.0 collective-permute-start.9
  26.6 0.9 %collective-permute-done.8.refs_6_ = f32[1,2,128,128]{3,2,1,0:T(8,128)S(1)} collective-permute-done((f32[1,2,128,128]{3,2,1,0:T(8,128)S(1)}, f32[1,2,128,128]{3,2,1,0:T(8,128)S(1)}, u32[]{:S(2)}, u32[]{:S(2)}) %collective-permute-start.8) | collective-permute-done | bytes 131104 | tf_op jit(solution)/shard_map/ppermute | solution.py:315
  27.6 0.4 collective-permute-done.9.refs_7_
  28.0 2.1 %collective-permute-start.12 = (f32[4,2,128,128]{3,2,1,0:T(8,128)S(1)}, f32[4,2,128,128]{3,2,1,0:T(8,128)S(1)}, u32[]{:S(2)}, u32[]{:S(2)}) collective-permute-start(f32[4,2,128,128]{3,2,1,0:T(8,128)S(1)} %momentum.3.refs_0_), channel_id=1, source_target_pairs={{0,2},{3,1},{2,4},{5,3},{4,6},{7,5},{8,10},{11,9},{10,12},{13,11},... | collective-permute-start | bytes 1572872 | tf_op jit(solution)/shard_map/ppermute | solution.py:338
  30.1 0.1 momentum.2.refs_1_
  30.1 0.8 %mix.4 = (f32[4,2,128,128]{3,2,1,0:T(8,128)S(1)}, f32[4,2,128,128]{3,2,1,0:T(8,128)S(1)}) custom-call(s32[4]{0:T(128)S(1)} %copy-done, f32[4]{0:T(128)S(1)} %copy-done.1, f32[4,2,128,128]{3,2,1,0:T(8,128)S(1)} %momentum.3.refs_0_, f32[4,2,128,128]{3,2,1,0:T(8,128)S(1)} %momentum.2.refs_1_), custom_call_target="tpu_custom_call" | custom-call | tf_op jit(solution)/shard_map/mix/pallas_call | solution.py:344
  30.9 3.2 %collective-permute-start.10 = (f32[4,2,128,128]{3,2,1,0:T(8,128)S(1)}, f32[4,2,128,128]{3,2,1,0:T(8,128)S(1)}, u32[]{:S(2)}, u32[]{:S(2)}) collective-permute-start(f32[4,2,128,128]{3,2,1,0:T(8,128)S(1)} %momentum.2.refs_1_), channel_id=1, source_target_pairs={{1,3},{2,0},{3,5},{4,2},{5,7},{6,4},{9,11},{10,8},{11,13},{12,10},... | collective-permute-start | bytes 1572872 | tf_op jit(solution)/shard_map/ppermute | solution.py:338
  34.2 4.6 %collective-permute-done.12.refs_0_ = f32[4,2,128,128]{3,2,1,0:T(8,128)S(1)} collective-permute-done((f32[4,2,128,128]{3,2,1,0:T(8,128)S(1)}, f32[4,2,128,128]{3,2,1,0:T(8,128)S(1)}, u32[]{:S(2)}, u32[]{:S(2)}) %collective-permute-start.12) | collective-permute-done | bytes 524320 | tf_op jit(solution)/shard_map/ppermute | solution.py:338
  38.7 2.1 %collective-permute-start.13 = (f32[4,2,128,128]{3,2,1,0:T(8,128)S(1)}, f32[4,2,128,128]{3,2,1,0:T(8,128)S(1)}, u32[]{:S(2)}, u32[]{:S(2)}) collective-permute-start(f32[4,2,128,128]{3,2,1,0:T(8,128)S(1)} %collective-permute-done.12.refs_0_), channel_id=1, source_target_pairs={{3,1},{2,4},{5,3},{4,6},{11,9},{10,12},{13,11},{12,14},{19,17},{18... | collective-permute-start | bytes 1572872 | tf_op jit(solution)/shard_map/ppermute | solution.py:338
  40.8 3.3 %collective-permute-done.10.refs_1_ = f32[4,2,128,128]{3,2,1,0:T(8,128)S(1)} collective-permute-done((f32[4,2,128,128]{3,2,1,0:T(8,128)S(1)}, f32[4,2,128,128]{3,2,1,0:T(8,128)S(1)}, u32[]{:S(2)}, u32[]{:S(2)}) %collective-permute-start.10) | collective-permute-done | bytes 524320 | tf_op jit(solution)/shard_map/ppermute | solution.py:338
  44.2 3.2 %collective-permute-start.11 = (f32[4,2,128,128]{3,2,1,0:T(8,128)S(1)}, f32[4,2,128,128]{3,2,1,0:T(8,128)S(1)}, u32[]{:S(2)}, u32[]{:S(2)}) collective-permute-start(f32[4,2,128,128]{3,2,1,0:T(8,128)S(1)} %collective-permute-done.10.refs_1_), channel_id=1, source_target_pairs={{2,0},{3,5},{4,2},{5,7},{10,8},{11,13},{12,10},{13,15},{18,16},{19... | collective-permute-start | bytes 1572872 | tf_op jit(solution)/shard_map/ppermute | solution.py:338
  47.4 1.2 %mix.5 = (f32[4,2,128,128]{3,2,1,0:T(8,128)S(1)}, f32[4,2,128,128]{3,2,1,0:T(8,128)S(1)}) custom-call(s32[4]{0:T(128)S(1)} %copy-done, f32[4]{0:T(128)S(1)} %copy-done.1, f32[4,2,128,128]{3,2,1,0:T(8,128)S(1)} %collective-permute-done.12.refs_0_, f32[4,2,128,128]{3,2,1,0:T(8,128)S(1)} %collective-permute-done.10.refs_1_, ...), custom_call_target="tpu_custom_call" | custom-call | tf_op jit(solution)/shard_map/mix/pallas_call | solution.py:344
  48.5 0.8 %mix.6 = (f32[4,2,128,128]{3,2,1,0:T(8,128)S(1)}, f32[4,2,128,128]{3,2,1,0:T(8,128)S(1)}) custom-call(s32[4]{0:T(128)S(1)} %copy-done, f32[4]{0:T(128)S(1)} %copy-done.1, f32[4,2,128,128]{3,2,1,0:T(8,128)S(1)} %collective-permute-done.13.refs_0_, f32[4,2,128,128]{3,2,1,0:T(8,128)S(1)} %get-tuple-element.30.refs_1_, ...), custom_call_target="tpu_custom_call" | custom-call | tf_op jit(solution)/shard_map/mix/pallas_call | solution.py:344
  49.3 9.2 %collective-permute-done.11.refs_0_ = f32[4,2,128,128]{3,2,1,0:T(8,128)S(1)} collective-permute-done((f32[4,2,128,128]{3,2,1,0:T(8,128)S(1)}, f32[4,2,128,128]{3,2,1,0:T(8,128)S(1)}, u32[]{:S(2)}, u32[]{:S(2)}) %collective-permute-start.11) | collective-permute-done | bytes 524320 | tf_op jit(solution)/shard_map/ppermute | solution.py:338
  58.5 1.7 %mix.7 = (f32[4,2,128,128]{3,2,1,0:T(8,128)}, f32[4,2,128,128]{3,2,1,0:T(8,128)}) custom-call(s32[4]{0:T(128)S(1)} %copy-done, f32[4]{0:T(128)S(1)} %copy-done.1, f32[4,2,128,128]{3,2,1,0:T(8,128)S(1)} %collective-permute-done.11.refs_0_, f32[4,2,128,128]{3,2,1,0:T(8,128)S(1)} %get-tuple-element.32.refs_1_, f32[4,2,128,128]{3,2,1,0:T(8,128)S(1)} %get-tuple-element.33.refs_2_), custom_call_target="tpu_custom_call" | custom-call | tf_op jit(solution)/shard_map/mix/pallas_call | solution.py:344
  (9 shorter events, 0.1 us)
Async XLA Ops:
  2.9 6.8 %collective-permute-start = (f32[3,128,128]{2,1,0:T(8,128)S(1)}, f32[3,128,128]{2,1,0:T(8,128)S(1)}, u32[]{:S(2)}, u32[]{:S(2)}) collective-permute-start(f32[3,128,128]{2,1,0:T(8,128)S(1)} %get-tuple-element.20), channel_id=1, source_target_pairs={{0,24},{1,25},{8,16},{9,17},{16,8},{17,9},{24,0},{25,1},{2,26},{3,... | collective-permute-start | bytes 589832 | tf_op jit(solution)/shard_map/ppermute | solution.py:273
  5.1 8.5 %collective-permute-start.1 = (f32[3,128,128]{2,1,0:T(8,128)S(1)}, f32[3,128,128]{2,1,0:T(8,128)S(1)}, u32[]{:S(2)}, u32[]{:S(2)}) collective-permute-start(f32[3,128,128]{2,1,0:T(8,128)S(1)} %get-tuple-element.21), channel_id=1, source_target_pairs={{0,8},{1,17},{8,0},{9,25},{16,24},{17,1},{24,16},{25,9},{2,10},{3,... | collective-permute-start | bytes 589832 | tf_op jit(solution)/shard_map/ppermute | solution.py:273
  7.6 7.1 %collective-permute-start.2 = (f32[3,128,128]{2,1,0:T(8,128)S(1)}, f32[3,128,128]{2,1,0:T(8,128)S(1)}, u32[]{:S(2)}, u32[]{:S(2)}) collective-permute-start(f32[3,128,128]{2,1,0:T(8,128)S(1)} %get-tuple-element.22), channel_id=1, source_target_pairs={{0,16},{1,9},{8,24},{9,1},{16,0},{17,25},{24,8},{25,17},{2,18},{3,... | collective-permute-start | bytes 589832 | tf_op jit(solution)/shard_map/ppermute | solution.py:273
  16.9 5.2 %collective-permute-start.3 = (f32[1,2,128,128]{3,2,1,0:T(8,128)S(1)}, f32[1,2,128,128]{3,2,1,0:T(8,128)S(1)}, u32[]{:S(2)}, u32[]{:S(2)}) collective-permute-start(f32[1,2,128,128]{3,2,1,0:T(8,128)S(1)} %get-tuple-element.24), channel_id=1, source_target_pairs={{0,24},{1,25},{8,16},{9,17},{16,8},{17,9},{24,0},{25,1},{2,26},{3,... | collective-permute-start | bytes 393224 | tf_op jit(solution)/shard_map/ppermute | solution.py:273
  18.2 7.1 %collective-permute-start.4 = (f32[1,2,128,128]{3,2,1,0:T(8,128)S(1)}, f32[1,2,128,128]{3,2,1,0:T(8,128)S(1)}, u32[]{:S(2)}, u32[]{:S(2)}) collective-permute-start(f32[1,2,128,128]{3,2,1,0:T(8,128)S(1)} %get-tuple-element.25), channel_id=1, source_target_pairs={{0,8},{1,17},{8,0},{9,25},{16,24},{17,1},{24,16},{25,9},{2,10},{3,... | collective-permute-start | bytes 393224 | tf_op jit(solution)/shard_map/ppermute | solution.py:273
  18.7 7.9 %collective-permute-start.5 = (f32[1,2,128,128]{3,2,1,0:T(8,128)S(1)}, f32[1,2,128,128]{3,2,1,0:T(8,128)S(1)}, u32[]{:S(2)}, u32[]{:S(2)}) collective-permute-start(f32[1,2,128,128]{3,2,1,0:T(8,128)S(1)} %get-tuple-element.26), channel_id=1, source_target_pairs={{0,16},{1,9},{8,24},{9,1},{16,0},{17,25},{24,8},{25,17},{2,18},{3,... | collective-permute-start | bytes 393224 | tf_op jit(solution)/shard_map/ppermute | solution.py:273
  19.6 7.0 %collective-permute-start.6 = (f32[1,2,128,128]{3,2,1,0:T(8,128)S(1)}, f32[1,2,128,128]{3,2,1,0:T(8,128)S(1)}, u32[]{:S(2)}, u32[]{:S(2)}) collective-permute-start(f32[1,2,128,128]{3,2,1,0:T(8,128)S(1)} %get-tuple-element.23.refs_0_), channel_id=1, source_target_pairs={{0,1},{1,0},{2,3},{3,2},{4,5},{5,4},{6,7},{7,6},{8,9},{9,8},{10,11... | collective-permute-start | bytes 393224 | tf_op jit(solution)/shard_map/ppermute | solution.py:315
  22.1 4.5 %collective-permute-start.7 = (f32[1,2,128,128]{3,2,1,0:T(8,128)S(1)}, f32[1,2,128,128]{3,2,1,0:T(8,128)S(1)}, u32[]{:S(2)}, u32[]{:S(2)}) collective-permute-start(f32[1,2,128,128]{3,2,1,0:T(8,128)S(1)} %collective-permute-done.3.refs_1_), channel_id=1, source_target_pairs={{0,1},{1,0},{2,3},{3,2},{4,5},{5,4},{6,7},{7,6},{8,9},{9,8},{10,11... | collective-permute-start | bytes 393224 | tf_op jit(solution)/shard_map/ppermute | solution.py:315
  25.3 2.3 %collective-permute-start.8 = (f32[1,2,128,128]{3,2,1,0:T(8,128)S(1)}, f32[1,2,128,128]{3,2,1,0:T(8,128)S(1)}, u32[]{:S(2)}, u32[]{:S(2)}) collective-permute-start(f32[1,2,128,128]{3,2,1,0:T(8,128)S(1)} %collective-permute-done.4.refs_2_), channel_id=1, source_target_pairs={{0,1},{1,0},{2,3},{3,2},{4,5},{5,4},{6,7},{7,6},{8,9},{9,8},{10,11... | collective-permute-start | bytes 393224 | tf_op jit(solution)/shard_map/ppermute | solution.py:315
  26.6 1.3 %collective-permute-start.9 = (f32[1,2,128,128]{3,2,1,0:T(8,128)S(1)}, f32[1,2,128,128]{3,2,1,0:T(8,128)S(1)}, u32[]{:S(2)}, u32[]{:S(2)}) collective-permute-start(f32[1,2,128,128]{3,2,1,0:T(8,128)S(1)} %collective-permute-done.5.refs_3_), channel_id=1, source_target_pairs={{0,1},{1,0},{2,3},{3,2},{4,5},{5,4},{6,7},{7,6},{8,9},{9,8},{10,11... | collective-permute-start | bytes 393224 | tf_op jit(solution)/shard_map/ppermute | solution.py:315
  28.0 2.2 %copy-start = (s32[4]{0:T(128)S(1)}, s32[4]{0:T(128)}, u32[]{:S(2)}) copy-start(s32[4]{0:T(128)} %shift_ref.7) | copy-start | bytes 52
  28.0 2.2 %copy-start.1 = (f32[4]{0:T(128)S(1)}, f32[4]{0:T(128)}, u32[]{:S(2)}) copy-start(f32[4]{0:T(128)} %weight_ref.7) | copy-start | bytes 52
  28.0 10.8 %collective-permute-start.12 = (f32[4,2,128,128]{3,2,1,0:T(8,128)S(1)}, f32[4,2,128,128]{3,2,1,0:T(8,128)S(1)}, u32[]{:S(2)}, u32[]{:S(2)}) collective-permute-start(f32[4,2,128,128]{3,2,1,0:T(8,128)S(1)} %momentum.3.refs_0_), channel_id=1, source_target_pairs={{0,2},{3,1},{2,4},{5,3},{4,6},{7,5},{8,10},{11,9},{10,12},{13,11},... | collective-permute-start | bytes 1572872 | tf_op jit(solution)/shard_map/ppermute | solution.py:338
  30.9 13.3 %collective-permute-start.10 = (f32[4,2,128,128]{3,2,1,0:T(8,128)S(1)}, f32[4,2,128,128]{3,2,1,0:T(8,128)S(1)}, u32[]{:S(2)}, u32[]{:S(2)}) collective-permute-start(f32[4,2,128,128]{3,2,1,0:T(8,128)S(1)} %momentum.2.refs_1_), channel_id=1, source_target_pairs={{1,3},{2,0},{3,5},{4,2},{5,7},{6,4},{9,11},{10,8},{11,13},{12,10},... | collective-permute-start | bytes 1572872 | tf_op jit(solution)/shard_map/ppermute | solution.py:338
  38.7 9.8 %collective-permute-start.13 = (f32[4,2,128,128]{3,2,1,0:T(8,128)S(1)}, f32[4,2,128,128]{3,2,1,0:T(8,128)S(1)}, u32[]{:S(2)}, u32[]{:S(2)}) collective-permute-start(f32[4,2,128,128]{3,2,1,0:T(8,128)S(1)} %collective-permute-done.12.refs_0_), channel_id=1, source_target_pairs={{3,1},{2,4},{5,3},{4,6},{11,9},{10,12},{13,11},{12,14},{19,17},{18... | collective-permute-start | bytes 1572872 | tf_op jit(solution)/shard_map/ppermute | solution.py:338
  44.2 14.3 %collective-permute-start.11 = (f32[4,2,128,128]{3,2,1,0:T(8,128)S(1)}, f32[4,2,128,128]{3,2,1,0:T(8,128)S(1)}, u32[]{:S(2)}, u32[]{:S(2)}) collective-permute-start(f32[4,2,128,128]{3,2,1,0:T(8,128)S(1)} %collective-permute-done.10.refs_1_), channel_id=1, source_target_pairs={{2,0},{3,5},{4,2},{5,7},{10,8},{11,13},{12,10},{13,15},{18,16},{19... | collective-permute-start | bytes 1572872 | tf_op jit(solution)/shard_map/ppermute | solution.py:338

commit v7 on v6

--- a/solution.py
+++ b/solution.py
@@ -183,13 +183,14 @@
 
 def mix_kernel(total, items, first, last, shift_ref, weight_ref, *refs):
     count = len(items)
-    inputs = count + (0 if first else 2)
+    inputs = count + (0 if first else 3 if last else 2)
     sums_in = refs[count:inputs]
     results = refs[inputs : inputs + 2]
     targets = refs[inputs + 2 : inputs + 4] if last else results
     local_e, _, n, _ = refs[0].shape
     phonons = shift_ref.shape[0]
-    start = lax.axis_index("energy") * local_e
+    place = lax.axis_index("energy")
+    start = place * local_e
     core = lax.axis_index("mom")
     shifts = [shift_ref[m] for m in range(phonons)]
     weights = [weight_ref[m] for m in range(phonons)]
@@ -203,7 +204,7 @@
     def copy_out(i, a):
         return pltpu.make_async_copy(targets[i].at[a], results[i].at[a], refs[-1].at[i, a])
 
-    def body(here):
+    def body(here, some):
         most = total // 2
         coefficients = {}
         terms = [[] for _ in range(local_e)]
@@ -213,30 +214,40 @@
                 occ = occupation(start + sign * d * local_e + b, total, n)
                 for a in range(local_e):
                     t = d * local_e + sign * (b - a)
-                    if 1 <= t <= most:
+                    if some and 1 <= t <= most:
                         if t not in coefficients:
                             coefficients[t] = coefficient(t)
                         terms[a].append((refs[i], b, coefficients[t] * factor, occ))
         for i in range(2):
             for a in range(local_e):
-                sums = [jnp.zeros((n, n), F32) if first else sums_in[i][a, c] for c in range(2)]
+                if first:
+                    sums = [jnp.zeros((n, n), F32)] * 2
+                else:
+                    sums = [sums_in[i][a, c] for c in range(2)]
                 for source, b, w, occ in terms[a]:
                     weight = w if i == 0 else w * occ
                     sums = [sums[c] + weight * source[b, c] for c in range(2)]
-                if last and i == 1:
+                if (first or last) and i == 1:
                     sums = [sums[0] - sums[0].T, sums[1] + sums[1].T]
+                    if last:
+                        sums = [sums[c] + sums_in[2][a, c] for c in range(2)]
                 for c in range(2):
                     targets[i][a, c] = sums[c]
                 if last:
                     copy_out(i, a).start()
 
-    @pl.when(core == 0)
-    def _():
-        body(0)
-
-    @pl.when(core != 0)
-    def _():
-        body(1)
+    for here in range(2):
+        if len(items) > 1:
+            pl.when(core == here)(functools.partial(body, here, True))
+            continue
+        [(momentum, d)] = items
+        if momentum == here:
+            some = place >= d
+        else:
+            some = place + d < lax.axis_size("energy")
+        pl.when((core == here) & some)(functools.partial(body, here, True))
+        if last:
+            pl.when((core == here) & ~some)(functools.partial(body, here, False))
 
     if last:
         for a in range(local_e):
@@ -339,27 +350,31 @@
 
     smem = pl.BlockSpec(memory_space=pltpu.SMEM)
 
-    def mix(items, blocks, sums, last=False):
+    def mix(items, blocks, sums, first=False, last=False):
         scratch = [pltpu.VMEM(block.shape, F32)] * 2 + [pltpu.SemaphoreType.DMA((2, local_e))]
+        count = 2 + len(blocks)
+        in_place = len(items) == 1 and not last
         return pl.pallas_call(
-            functools.partial(mix_kernel, total, items, not sums, last),
+            functools.partial(mix_kernel, total, items, first, last),
             out_shape=[block] * 2,
             in_specs=[smem, smem] + whole(len(blocks) + len(sums)),
             out_specs=[pl.BlockSpec(memory_space=pl.ANY)] * 2 if last else whole(2),
             scratch_shapes=scratch if last else [],
+            input_output_aliases={count: 0, count + 1: 1} if in_place else {},
             compiler_params=params(),
             name="mix",
         )(phonon_shift, phonon_weight, *blocks, *sums)
 
-    sums = mix([(0, 0), (1, 0)], [zero, one], [])
-    one, _ = lax.optimization_barrier((one, sums))
+    retarded, local_lesser = mix([(0, 0), (1, 0)], [zero, one], [], first=True)
+    one, _ = lax.optimization_barrier((one, local_lesser))
+    sums = [retarded, jnp.zeros_like(local_lesser)]
     for d in range(1, reach + 1):
         zero = hop(zero, d, 0)
         one = hop(one, d, 1)
         if d < reach:
             sums = mix([(0, d), (1, d)], [zero, one], sums)
     sums = mix([(0, reach)], [zero], sums)
-    sums = mix([(1, reach)], [one], sums, last=True)
+    sums = mix([(1, reach)], [one], [*sums, local_lesser], last=True)
     retarded, lesser = sums
     return (retarded[None, None], lesser[None, None])
 

time: 60.5 us -> 60.4 us (level)
  no operation moved by 1% of the time
where the time goes in v7:
time: 60.4 us; the launch traced here: 60.2 us
  waiting for transfers between devices  26.1 us (43%)
  starting transfers between devices  22.1 us (37%)
  Pallas kernels  11.2 us (19%)
  between operations  0.77 us (1%)
    ppermute x4, waiting for transfers between devices, hop(): return lax.ppermute(value, ('energy', 'mom'), pairs)  17.1 us
    ppermute x4, starting transfers between devices, hop(): return lax.ppermute(value, ('energy', 'mom'), pairs)  10.6 us
    ppermute x6, waiting for transfers between devices, exchange(): return lax.ppermute(slots[i], ('len', 'mom'), pairs)  7.67 us
    ppermute x4, starting transfers between devices, shards(): other = [lax.ppermute(v, 'mom', both_ways) for v in own]  6.03 us
    ppermute x6, starting transfers between devices, exchange(): return lax.ppermute(slots[i], ('len', 'mom'), pairs)  5.49 us
    pallas_call x2, Pallas kernels, inverse(): pl.pallas_call(functools.partial(inverse_kernel, total, layers, slots), o...  4.53 us
    pallas_call x4, Pallas kernels, mix(): pl.pallas_call(functools.partial(mix_kernel, total, items, first, last),...  4.34 us
    pallas_call x1, Pallas kernels, shards(): pl.pallas_call(functools.partial(chain_kernel, layers), out_shape=[part]...  2.22 us
  transfers between devices with their start and end apart: 14, of which 10 were waited for; matrix products, arithmetic and copies ran while one was open for 0% of the time, Pallas kernels for 8%

profile of v7, /device:TPU:17, one launch (start us, length us, event | category | flops | bytes accessed | tf_op | source)
XLA Modules:
  0.0 60.2 jit_solution(4185942414144890741)
XLA Ops:
  0.6 2.3 %inverse.3 = (f32[3,128,128]{2,1,0:T(8,128)S(1)}, f32[3,128,128]{2,1,0:T(8,128)S(1)}) custom-call(f32[2,128,128]{2,1,0:T(8,128)} %bitcast.9, f32[4,2,128,128]{3,2,1,0:T(8,128)} %bitcast.5, f32[128,128]{1,0:T(8,128)} %bitcast.11, s32[128,128]{1,0:T(8,128)} %pattern_any.3), custom_call_target="tpu_custom_call" | custom-call | flops 402653184 | bytes 262144 | tf_op jit(solution)/shard_map/inverse/pallas_call | solution.py:291
  2.9 2.2 %collective-permute-start = (f32[3,128,128]{2,1,0:T(8,128)S(1)}, f32[3,128,128]{2,1,0:T(8,128)S(1)}, u32[]{:S(2)}, u32[]{:S(2)}) collective-permute-start(f32[3,128,128]{2,1,0:T(8,128)S(1)} %get-tuple-element.20), channel_id=1, source_target_pairs={{0,24},{1,25},{8,16},{9,17},{16,8},{17,9},{24,0},{25,1},{2,26},{3,... | collective-permute-start | bytes 589832 | tf_op jit(solution)/shard_map/ppermute | solution.py:284
  5.1 0.2 collective-permute-start.1
  5.4 2.3 %inverse.2 = (f32[3,128,128]{2,1,0:T(8,128)S(1)}, f32[3,128,128]{2,1,0:T(8,128)S(1)}) custom-call(f32[2,128,128]{2,1,0:T(8,128)} %bitcast.10, f32[4,2,128,128]{3,2,1,0:T(8,128)} %bitcast.6, f32[128,128]{1,0:T(8,128)} %bitcast.12, s32[128,128]{1,0:T(8,128)} %pattern_any.3), custom_call_target="tpu_custom_call" | custom-call | flops 402653184 | bytes 262144 | tf_op jit(solution)/shard_map/inverse/pallas_call | solution.py:291
  7.6 0.3 collective-permute-start.2
  8.0 1.7 %collective-permute-done.refs_1_ = f32[3,128,128]{2,1,0:T(8,128)S(1)} collective-permute-done((f32[3,128,128]{2,1,0:T(8,128)S(1)}, f32[3,128,128]{2,1,0:T(8,128)S(1)}, u32[]{:S(2)}, u32[]{:S(2)}) %collective-permute-start) | collective-permute-done | bytes 196640 | tf_op jit(solution)/shard_map/ppermute | solution.py:284
  9.7 3.9 %collective-permute-done.1.refs_2_ = f32[3,128,128]{2,1,0:T(8,128)S(1)} collective-permute-done((f32[3,128,128]{2,1,0:T(8,128)S(1)}, f32[3,128,128]{2,1,0:T(8,128)S(1)}, u32[]{:S(2)}, u32[]{:S(2)}) %collective-permute-start.1) | collective-permute-done | bytes 196640 | tf_op jit(solution)/shard_map/ppermute | solution.py:284
  13.6 1.1 %collective-permute-done.2.refs_3_ = f32[3,128,128]{2,1,0:T(8,128)S(1)} collective-permute-done((f32[3,128,128]{2,1,0:T(8,128)S(1)}, f32[3,128,128]{2,1,0:T(8,128)S(1)}, u32[]{:S(2)}, u32[]{:S(2)}) %collective-permute-start.2) | collective-permute-done | bytes 196640 | tf_op jit(solution)/shard_map/ppermute | solution.py:284
  14.7 2.2 %chains.1 = (f32[1,2,128,128]{3,2,1,0:T(8,128)S(1)}, f32[1,2,128,128]{3,2,1,0:T(8,128)S(1)}, f32[1,2,128,128]{3,2,1,0:T(8,128)S(1)}, f32[1,2,128,128]{3,2,1,0:T(8,128)S(1)}) custom-call(f32[3,128,128]{2,1,0:T(8,128)S(1)} %get-tuple-element.19.refs_0_, f32[3,128,128]{2,1,0:T(8,128)S(1)} %collective-permute-done.refs_1_, ...), custom_call_target="tpu_custom_call" | custom-call | tf_op jit(solution)/shard_map/chains/pallas_call | solution.py:315
  16.9 1.3 %collective-permute-start.3 = (f32[1,2,128,128]{3,2,1,0:T(8,128)S(1)}, f32[1,2,128,128]{3,2,1,0:T(8,128)S(1)}, u32[]{:S(2)}, u32[]{:S(2)}) collective-permute-start(f32[1,2,128,128]{3,2,1,0:T(8,128)S(1)} %get-tuple-element.24), channel_id=1, source_target_pairs={{0,24},{1,25},{8,16},{9,17},{16,8},{17,9},{24,0},{25,1},{2,26},{3,... | collective-permute-start | bytes 393224 | tf_op jit(solution)/shard_map/ppermute | solution.py:284
  18.2 0.5 collective-permute-start.4
  18.7 0.9 %collective-permute-start.5 = (f32[1,2,128,128]{3,2,1,0:T(8,128)S(1)}, f32[1,2,128,128]{3,2,1,0:T(8,128)S(1)}, u32[]{:S(2)}, u32[]{:S(2)}) collective-permute-start(f32[1,2,128,128]{3,2,1,0:T(8,128)S(1)} %get-tuple-element.26), channel_id=1, source_target_pairs={{0,16},{1,9},{8,24},{9,1},{16,0},{17,25},{24,8},{25,17},{2,18},{3,... | collective-permute-start | bytes 393224 | tf_op jit(solution)/shard_map/ppermute | solution.py:284
  19.6 1.7 %collective-permute-start.6 = (f32[1,2,128,128]{3,2,1,0:T(8,128)S(1)}, f32[1,2,128,128]{3,2,1,0:T(8,128)S(1)}, u32[]{:S(2)}, u32[]{:S(2)}) collective-permute-start(f32[1,2,128,128]{3,2,1,0:T(8,128)S(1)} %get-tuple-element.23.refs_0_), channel_id=1, source_target_pairs={{0,1},{1,0},{2,3},{3,2},{4,5},{5,4},{6,7},{7,6},{8,9},{9,8},{10,11... | collective-permute-start | bytes 393224 | tf_op jit(solution)/shard_map/ppermute | solution.py:326
  21.3 0.8 %collective-permute-done.3.refs_1_ = f32[1,2,128,128]{3,2,1,0:T(8,128)S(1)} collective-permute-done((f32[1,2,128,128]{3,2,1,0:T(8,128)S(1)}, f32[1,2,128,128]{3,2,1,0:T(8,128)S(1)}, u32[]{:S(2)}, u32[]{:S(2)}) %collective-permute-start.3) | collective-permute-done | bytes 131104 | tf_op jit(solution)/shard_map/ppermute | solution.py:284
  22.1 3.0 %collective-permute-start.7 = (f32[1,2,128,128]{3,2,1,0:T(8,128)S(1)}, f32[1,2,128,128]{3,2,1,0:T(8,128)S(1)}, u32[]{:S(2)}, u32[]{:S(2)}) collective-permute-start(f32[1,2,128,128]{3,2,1,0:T(8,128)S(1)} %collective-permute-done.3.refs_1_), channel_id=1, source_target_pairs={{0,1},{1,0},{2,3},{3,2},{4,5},{5,4},{6,7},{7,6},{8,9},{9,8},{10,11... | collective-permute-start | bytes 393224 | tf_op jit(solution)/shard_map/ppermute | solution.py:326
  25.1 0.2 collective-permute-done.4.refs_2_
  25.3 1.3 %collective-permute-start.8 = (f32[1,2,128,128]{3,2,1,0:T(8,128)S(1)}, f32[1,2,128,128]{3,2,1,0:T(8,128)S(1)}, u32[]{:S(2)}, u32[]{:S(2)}) collective-permute-start(f32[1,2,128,128]{3,2,1,0:T(8,128)S(1)} %collective-permute-done.4.refs_2_), channel_id=1, source_target_pairs={{0,1},{1,0},{2,3},{3,2},{4,5},{5,4},{6,7},{7,6},{8,9},{9,8},{10,11... | collective-permute-start | bytes 393224 | tf_op jit(solution)/shard_map/ppermute | solution.py:326
  26.6 0.0 collective-permute-start.9
  26.6 0.9 %collective-permute-done.8.refs_6_ = f32[1,2,128,128]{3,2,1,0:T(8,128)S(1)} collective-permute-done((f32[1,2,128,128]{3,2,1,0:T(8,128)S(1)}, f32[1,2,128,128]{3,2,1,0:T(8,128)S(1)}, u32[]{:S(2)}, u32[]{:S(2)}) %collective-permute-start.8) | collective-permute-done | bytes 131104 | tf_op jit(solution)/shard_map/ppermute | solution.py:326
  27.6 0.4 collective-permute-done.9.refs_7_
  28.0 2.1 %collective-permute-start.12 = (f32[4,2,128,128]{3,2,1,0:T(8,128)S(1)}, f32[4,2,128,128]{3,2,1,0:T(8,128)S(1)}, u32[]{:S(2)}, u32[]{:S(2)}) collective-permute-start(f32[4,2,128,128]{3,2,1,0:T(8,128)S(1)} %momentum.3.refs_0_), channel_id=1, source_target_pairs={{0,2},{3,1},{2,4},{5,3},{4,6},{7,5},{8,10},{11,9},{10,12},{13,11},... | collective-permute-start | bytes 1572872 | tf_op jit(solution)/shard_map/ppermute | solution.py:349
  30.1 0.1 momentum.2.refs_1_
  30.1 0.9 %mix.4 = (f32[4,2,128,128]{3,2,1,0:T(8,128)S(1)}, f32[4,2,128,128]{3,2,1,0:T(8,128)S(1)}) custom-call(s32[4]{0:T(128)S(1)} %copy-done, f32[4]{0:T(128)S(1)} %copy-done.1, f32[4,2,128,128]{3,2,1,0:T(8,128)S(1)} %momentum.3.refs_0_, f32[4,2,128,128]{3,2,1,0:T(8,128)S(1)} %momentum.2.refs_1_), custom_call_target="tpu_custom_call" | custom-call | tf_op jit(solution)/shard_map/mix/pallas_call | solution.py:357
  31.0 3.2 %collective-permute-start.10 = (f32[4,2,128,128]{3,2,1,0:T(8,128)S(1)}, f32[4,2,128,128]{3,2,1,0:T(8,128)S(1)}, u32[]{:S(2)}, u32[]{:S(2)}) collective-permute-start(f32[4,2,128,128]{3,2,1,0:T(8,128)S(1)} %momentum.2.refs_1_), channel_id=1, source_target_pairs={{1,3},{2,0},{3,5},{4,2},{5,7},{6,4},{9,11},{10,8},{11,13},{12,10},... | collective-permute-start | bytes 1572872 | tf_op jit(solution)/shard_map/ppermute | solution.py:349
  34.2 4.4 %collective-permute-done.12.refs_0_ = f32[4,2,128,128]{3,2,1,0:T(8,128)S(1)} collective-permute-done((f32[4,2,128,128]{3,2,1,0:T(8,128)S(1)}, f32[4,2,128,128]{3,2,1,0:T(8,128)S(1)}, u32[]{:S(2)}, u32[]{:S(2)}) %collective-permute-start.12) | collective-permute-done | bytes 524320 | tf_op jit(solution)/shard_map/ppermute | solution.py:349
  38.7 2.1 %collective-permute-start.13 = (f32[4,2,128,128]{3,2,1,0:T(8,128)S(1)}, f32[4,2,128,128]{3,2,1,0:T(8,128)S(1)}, u32[]{:S(2)}, u32[]{:S(2)}) collective-permute-start(f32[4,2,128,128]{3,2,1,0:T(8,128)S(1)} %collective-permute-done.12.refs_0_), channel_id=1, source_target_pairs={{3,1},{2,4},{5,3},{4,6},{11,9},{10,12},{13,11},{12,14},{19,17},{18... | collective-permute-start | bytes 1572872 | tf_op jit(solution)/shard_map/ppermute | solution.py:349
  40.8 3.4 %collective-permute-done.10.refs_1_ = f32[4,2,128,128]{3,2,1,0:T(8,128)S(1)} collective-permute-done((f32[4,2,128,128]{3,2,1,0:T(8,128)S(1)}, f32[4,2,128,128]{3,2,1,0:T(8,128)S(1)}, u32[]{:S(2)}, u32[]{:S(2)}) %collective-permute-start.10) | collective-permute-done | bytes 524320 | tf_op jit(solution)/shard_map/ppermute | solution.py:349
  44.2 3.2 %collective-permute-start.11 = (f32[4,2,128,128]{3,2,1,0:T(8,128)S(1)}, f32[4,2,128,128]{3,2,1,0:T(8,128)S(1)}, u32[]{:S(2)}, u32[]{:S(2)}) collective-permute-start(f32[4,2,128,128]{3,2,1,0:T(8,128)S(1)} %collective-permute-done.10.refs_1_), channel_id=1, source_target_pairs={{2,0},{3,5},{4,2},{5,7},{10,8},{11,13},{12,10},{13,15},{18,16},{19... | collective-permute-start | bytes 1572872 | tf_op jit(solution)/shard_map/ppermute | solution.py:349
  47.4 1.2 %mix.5 = (f32[4,2,128,128]{3,2,1,0:T(8,128)S(1)}, f32[4,2,128,128]{3,2,1,0:T(8,128)S(1)}) custom-call(s32[4]{0:T(128)S(1)} %copy-done, f32[4]{0:T(128)S(1)} %copy-done.1, f32[4,2,128,128]{3,2,1,0:T(8,128)S(1)} %collective-permute-done.12.refs_0_, f32[4,2,128,128]{3,2,1,0:T(8,128)S(1)} %collective-permute-done.10.refs_1_, ...), custom_call_target="tpu_custom_call" | custom-call | tf_op jit(solution)/shard_map/mix/pallas_call | solution.py:357
  48.6 0.6 mix.6
  49.2 9.3 %collective-permute-done.11.refs_0_ = f32[4,2,128,128]{3,2,1,0:T(8,128)S(1)} collective-permute-done((f32[4,2,128,128]{3,2,1,0:T(8,128)S(1)}, f32[4,2,128,128]{3,2,1,0:T(8,128)S(1)}, u32[]{:S(2)}, u32[]{:S(2)}) %collective-permute-start.11) | collective-permute-done | bytes 524320 | tf_op jit(solution)/shard_map/ppermute | solution.py:349
  58.4 1.8 %mix.7 = (f32[4,2,128,128]{3,2,1,0:T(8,128)}, f32[4,2,128,128]{3,2,1,0:T(8,128)}) custom-call(s32[4]{0:T(128)S(1)} %copy-done, f32[4]{0:T(128)S(1)} %copy-done.1, f32[4,2,128,128]{3,2,1,0:T(8,128)S(1)} %collective-permute-done.11.refs_0_, f32[4,2,128,128]{3,2,1,0:T(8,128)S(1)} %get-tuple-element.32.refs_1_, ...), custom_call_target="tpu_custom_call" | custom-call | tf_op jit(solution)/shard_map/mix/pallas_call | solution.py:357
  (10 shorter events, 0.1 us)
Async XLA Ops:
  2.9 6.8 %collective-permute-start = (f32[3,128,128]{2,1,0:T(8,128)S(1)}, f32[3,128,128]{2,1,0:T(8,128)S(1)}, u32[]{:S(2)}, u32[]{:S(2)}) collective-permute-start(f32[3,128,128]{2,1,0:T(8,128)S(1)} %get-tuple-element.20), channel_id=1, source_target_pairs={{0,24},{1,25},{8,16},{9,17},{16,8},{17,9},{24,0},{25,1},{2,26},{3,... | collective-permute-start | bytes 589832 | tf_op jit(solution)/shard_map/ppermute | solution.py:284
  5.1 8.5 %collective-permute-start.1 = (f32[3,128,128]{2,1,0:T(8,128)S(1)}, f32[3,128,128]{2,1,0:T(8,128)S(1)}, u32[]{:S(2)}, u32[]{:S(2)}) collective-permute-start(f32[3,128,128]{2,1,0:T(8,128)S(1)} %get-tuple-element.21), channel_id=1, source_target_pairs={{0,8},{1,17},{8,0},{9,25},{16,24},{17,1},{24,16},{25,9},{2,10},{3,... | collective-permute-start | bytes 589832 | tf_op jit(solution)/shard_map/ppermute | solution.py:284
  7.6 7.1 %collective-permute-start.2 = (f32[3,128,128]{2,1,0:T(8,128)S(1)}, f32[3,128,128]{2,1,0:T(8,128)S(1)}, u32[]{:S(2)}, u32[]{:S(2)}) collective-permute-start(f32[3,128,128]{2,1,0:T(8,128)S(1)} %get-tuple-element.22), channel_id=1, source_target_pairs={{0,16},{1,9},{8,24},{9,1},{16,0},{17,25},{24,8},{25,17},{2,18},{3,... | collective-permute-start | bytes 589832 | tf_op jit(solution)/shard_map/ppermute | solution.py:284
  16.9 5.2 %collective-permute-start.3 = (f32[1,2,128,128]{3,2,1,0:T(8,128)S(1)}, f32[1,2,128,128]{3,2,1,0:T(8,128)S(1)}, u32[]{:S(2)}, u32[]{:S(2)}) collective-permute-start(f32[1,2,128,128]{3,2,1,0:T(8,128)S(1)} %get-tuple-element.24), channel_id=1, source_target_pairs={{0,24},{1,25},{8,16},{9,17},{16,8},{17,9},{24,0},{25,1},{2,26},{3,... | collective-permute-start | bytes 393224 | tf_op jit(solution)/shard_map/ppermute | solution.py:284
  18.2 7.1 %collective-permute-start.4 = (f32[1,2,128,128]{3,2,1,0:T(8,128)S(1)}, f32[1,2,128,128]{3,2,1,0:T(8,128)S(1)}, u32[]{:S(2)}, u32[]{:S(2)}) collective-permute-start(f32[1,2,128,128]{3,2,1,0:T(8,128)S(1)} %get-tuple-element.25), channel_id=1, source_target_pairs={{0,8},{1,17},{8,0},{9,25},{16,24},{17,1},{24,16},{25,9},{2,10},{3,... | collective-permute-start | bytes 393224 | tf_op jit(solution)/shard_map/ppermute | solution.py:284
  18.7 7.9 %collective-permute-start.5 = (f32[1,2,128,128]{3,2,1,0:T(8,128)S(1)}, f32[1,2,128,128]{3,2,1,0:T(8,128)S(1)}, u32[]{:S(2)}, u32[]{:S(2)}) collective-permute-start(f32[1,2,128,128]{3,2,1,0:T(8,128)S(1)} %get-tuple-element.26), channel_id=1, source_target_pairs={{0,16},{1,9},{8,24},{9,1},{16,0},{17,25},{24,8},{25,17},{2,18},{3,... | collective-permute-start | bytes 393224 | tf_op jit(solution)/shard_map/ppermute | solution.py:284
  19.6 7.0 %collective-permute-start.6 = (f32[1,2,128,128]{3,2,1,0:T(8,128)S(1)}, f32[1,2,128,128]{3,2,1,0:T(8,128)S(1)}, u32[]{:S(2)}, u32[]{:S(2)}) collective-permute-start(f32[1,2,128,128]{3,2,1,0:T(8,128)S(1)} %get-tuple-element.23.refs_0_), channel_id=1, source_target_pairs={{0,1},{1,0},{2,3},{3,2},{4,5},{5,4},{6,7},{7,6},{8,9},{9,8},{10,11... | collective-permute-start | bytes 393224 | tf_op jit(solution)/shard_map/ppermute | solution.py:326
  22.1 4.5 %collective-permute-start.7 = (f32[1,2,128,128]{3,2,1,0:T(8,128)S(1)}, f32[1,2,128,128]{3,2,1,0:T(8,128)S(1)}, u32[]{:S(2)}, u32[]{:S(2)}) collective-permute-start(f32[1,2,128,128]{3,2,1,0:T(8,128)S(1)} %collective-permute-done.3.refs_1_), channel_id=1, source_target_pairs={{0,1},{1,0},{2,3},{3,2},{4,5},{5,4},{6,7},{7,6},{8,9},{9,8},{10,11... | collective-permute-start | bytes 393224 | tf_op jit(solution)/shard_map/ppermute | solution.py:326
  25.3 2.3 %collective-permute-start.8 = (f32[1,2,128,128]{3,2,1,0:T(8,128)S(1)}, f32[1,2,128,128]{3,2,1,0:T(8,128)S(1)}, u32[]{:S(2)}, u32[]{:S(2)}) collective-permute-start(f32[1,2,128,128]{3,2,1,0:T(8,128)S(1)} %collective-permute-done.4.refs_2_), channel_id=1, source_target_pairs={{0,1},{1,0},{2,3},{3,2},{4,5},{5,4},{6,7},{7,6},{8,9},{9,8},{10,11... | collective-permute-start | bytes 393224 | tf_op jit(solution)/shard_map/ppermute | solution.py:326
  26.6 1.3 %collective-permute-start.9 = (f32[1,2,128,128]{3,2,1,0:T(8,128)S(1)}, f32[1,2,128,128]{3,2,1,0:T(8,128)S(1)}, u32[]{:S(2)}, u32[]{:S(2)}) collective-permute-start(f32[1,2,128,128]{3,2,1,0:T(8,128)S(1)} %collective-permute-done.5.refs_3_), channel_id=1, source_target_pairs={{0,1},{1,0},{2,3},{3,2},{4,5},{5,4},{6,7},{7,6},{8,9},{9,8},{10,11... | collective-permute-start | bytes 393224 | tf_op jit(solution)/shard_map/ppermute | solution.py:326
  28.0 2.2 %copy-start = (s32[4]{0:T(128)S(1)}, s32[4]{0:T(128)}, u32[]{:S(2)}) copy-start(s32[4]{0:T(128)} %shift_ref.7) | copy-start | bytes 52
  28.0 2.2 %copy-start.1 = (f32[4]{0:T(128)S(1)}, f32[4]{0:T(128)}, u32[]{:S(2)}) copy-start(f32[4]{0:T(128)} %weight_ref.7) | copy-start | bytes 52
  28.0 10.7 %collective-permute-start.12 = (f32[4,2,128,128]{3,2,1,0:T(8,128)S(1)}, f32[4,2,128,128]{3,2,1,0:T(8,128)S(1)}, u32[]{:S(2)}, u32[]{:S(2)}) collective-permute-start(f32[4,2,128,128]{3,2,1,0:T(8,128)S(1)} %momentum.3.refs_0_), channel_id=1, source_target_pairs={{0,2},{3,1},{2,4},{5,3},{4,6},{7,5},{8,10},{11,9},{10,12},{13,11},... | collective-permute-start | bytes 1572872 | tf_op jit(solution)/shard_map/ppermute | solution.py:349
  31.0 13.2 %collective-permute-start.10 = (f32[4,2,128,128]{3,2,1,0:T(8,128)S(1)}, f32[4,2,128,128]{3,2,1,0:T(8,128)S(1)}, u32[]{:S(2)}, u32[]{:S(2)}) collective-permute-start(f32[4,2,128,128]{3,2,1,0:T(8,128)S(1)} %momentum.2.refs_1_), channel_id=1, source_target_pairs={{1,3},{2,0},{3,5},{4,2},{5,7},{6,4},{9,11},{10,8},{11,13},{12,10},... | collective-permute-start | bytes 1572872 | tf_op jit(solution)/shard_map/ppermute | solution.py:349
  38.7 9.9 %collective-permute-start.13 = (f32[4,2,128,128]{3,2,1,0:T(8,128)S(1)}, f32[4,2,128,128]{3,2,1,0:T(8,128)S(1)}, u32[]{:S(2)}, u32[]{:S(2)}) collective-permute-start(f32[4,2,128,128]{3,2,1,0:T(8,128)S(1)} %collective-permute-done.12.refs_0_), channel_id=1, source_target_pairs={{3,1},{2,4},{5,3},{4,6},{11,9},{10,12},{13,11},{12,14},{19,17},{18... | collective-permute-start | bytes 1572872 | tf_op jit(solution)/shard_map/ppermute | solution.py:349
  44.2 14.2 %collective-permute-start.11 = (f32[4,2,128,128]{3,2,1,0:T(8,128)S(1)}, f32[4,2,128,128]{3,2,1,0:T(8,128)S(1)}, u32[]{:S(2)}, u32[]{:S(2)}) collective-permute-start(f32[4,2,128,128]{3,2,1,0:T(8,128)S(1)} %collective-permute-done.10.refs_1_), channel_id=1, source_target_pairs={{2,0},{3,5},{4,2},{5,7},{10,8},{11,13},{12,10},{13,15},{18,16},{19... | collective-permute-start | bytes 1572872 | tf_op jit(solution)/shard_map/ppermute | solution.py:349

commit v8 on v7

--- a/solution.py
+++ b/solution.py
@@ -181,52 +181,54 @@
     return 1.0 / (1.0 + jnp.exp(8.0 * jnp.full((1, n), pos, jnp.int32).astype(F32) / total - 4.0))
 
 
-def mix_kernel(total, items, first, last, shift_ref, weight_ref, *refs):
+def local_kernel(total, shift_ref, weight_ref, zero_ref, one_ref, ret_ref, les_ref, table_ref):
+    n = table_ref.shape[1]
+    phonons = shift_ref.shape[0]
+    for t in range(1, total // 2 + 1):
+        value = 0.0
+        for m in range(phonons):
+            value = value + jnp.where(shift_ref[m] == t, weight_ref[m], 0.0)
+        table_ref[t : t + 1] = jnp.full((1, n), value, F32)
+    items = [(0, 0), (1, 0)]
+    mix_kernel(total, items, True, False, table_ref, zero_ref, one_ref, ret_ref, les_ref)
+
+
+def mix_kernel(total, items, first, last, table_ref, *refs):
     count = len(items)
     inputs = count + (0 if first else 3 if last else 2)
     sums_in = refs[count:inputs]
     results = refs[inputs : inputs + 2]
     targets = refs[inputs + 2 : inputs + 4] if last else results
     local_e, _, n, _ = refs[0].shape
-    phonons = shift_ref.shape[0]
     place = lax.axis_index("energy")
-    start = place * local_e
+    places = lax.axis_size("energy")
     core = lax.axis_index("mom")
-    shifts = [shift_ref[m] for m in range(phonons)]
-    weights = [weight_ref[m] for m in range(phonons)]
-
-    def coefficient(t):
-        value = 0.0
-        for s, w in zip(shifts, weights):
-            value = value + jnp.where(s == t, w, 0.0)
-        return value
 
     def copy_out(i, a):
         return pltpu.make_async_copy(targets[i].at[a], results[i].at[a], refs[-1].at[i, a])
 
     def body(here, some):
         most = total // 2
-        coefficients = {}
         terms = [[] for _ in range(local_e)]
         for i, (momentum, d) in enumerate(items):
             sign, factor = (-1, 1.0) if momentum == here else (1, 0.5)
+            source = place + sign * d
+            factor = jnp.where((source >= 0) & (source < places), factor, 0.0)
             for b in range(local_e):
-                occ = occupation(start + sign * d * local_e + b, total, n)
+                occ = occupation(source * local_e + b, total, n)
                 for a in range(local_e):
                     t = d * local_e + sign * (b - a)
                     if some and 1 <= t <= most:
-                        if t not in coefficients:
-                            coefficients[t] = coefficient(t)
-                        terms[a].append((refs[i], b, coefficients[t] * factor, occ))
+                        weight = table_ref[t : t + 1] * factor
+                        terms[a].append((refs[i], b, weight, weight * occ))
         for i in range(2):
             for a in range(local_e):
                 if first:
                     sums = [jnp.zeros((n, n), F32)] * 2
                 else:
                     sums = [sums_in[i][a, c] for c in range(2)]
-                for source, b, w, occ in terms[a]:
-                    weight = w if i == 0 else w * occ
-                    sums = [sums[c] + weight * source[b, c] for c in range(2)]
+                for source, b, *weights in terms[a]:
+                    sums = [sums[c] + weights[i] * source[b, c] for c in range(2)]
                 if (first or last) and i == 1:
                     sums = [sums[0] - sums[0].T, sums[1] + sums[1].T]
                     if last:
@@ -241,10 +243,7 @@
             pl.when(core == here)(functools.partial(body, here, True))
             continue
         [(momentum, d)] = items
-        if momentum == here:
-            some = place >= d
-        else:
-            some = place + d < lax.axis_size("energy")
+        some = place >= d if momentum == here else place + d < places
         pl.when((core == here) & some)(functools.partial(body, here, True))
         if last:
             pl.when((core == here) & ~some)(functools.partial(body, here, False))
@@ -338,39 +337,44 @@
 
     reach = -(-(total // 2) // local_e)
 
-    def hop(value, d, role):
-        pairs = []
-        for z in range(count - 1):
-            low, high = z * moms, (z + 1) * moms
-            if z >= d - 1:
-                pairs.append((low + role, high + role))
-            if z <= count - 1 - d:
-                pairs.append((high + 1 - role, low + 1 - role))
-        return lax.ppermute(value, ("energy", "mom"), pairs)
+    ring = [z * moms for z in range(count)] + [z * moms + 1 for z in reversed(range(count))]
+    ring = list(zip(ring, ring[1:] + ring[:1]))
+    ways = ring, [(target, source) for source, target in ring]
+
+    def hop(value, role):
+        return lax.ppermute(value, ("energy", "mom"), ways[role])
 
     smem = pl.BlockSpec(memory_space=pltpu.SMEM)
 
-    def mix(items, blocks, sums, first=False, last=False):
+    retarded, local_lesser, table = pl.pallas_call(
+        functools.partial(local_kernel, total),
+        out_shape=[block] * 2 + [jax.ShapeDtypeStruct((total // 2 + 8, n), F32)],
+        in_specs=[smem, smem] + whole(2),
+        out_specs=whole(3),
+        compiler_params=params(),
+        name="local",
+    )(phonon_shift, phonon_weight, zero, one)
+
+    def mix(items, blocks, sums, last=False):
         scratch = [pltpu.VMEM(block.shape, F32)] * 2 + [pltpu.SemaphoreType.DMA((2, local_e))]
-        count = 2 + len(blocks)
+        count = 1 + len(blocks)
         in_place = len(items) == 1 and not last
         return pl.pallas_call(
-            functools.partial(mix_kernel, total, items, first, last),
+            functools.partial(mix_kernel, total, items, False, last),
             out_shape=[block] * 2,
-            in_specs=[smem, smem] + whole(len(blocks) + len(sums)),
+            in_specs=whole(1 + len(blocks) + len(sums)),
             out_specs=[pl.BlockSpec(memory_space=pl.ANY)] * 2 if last else whole(2),
             scratch_shapes=scratch if last else [],
             input_output_aliases={count: 0, count + 1: 1} if in_place else {},
             compiler_params=params(),
             name="mix",
-        )(phonon_shift, phonon_weight, *blocks, *sums)
-
-    retarded, local_lesser = mix([(0, 0), (1, 0)], [zero, one], [], first=True)
+        )(table, *blocks, *sums)
+
     one, _ = lax.optimization_barrier((one, local_lesser))
     sums = [retarded, jnp.zeros_like(local_lesser)]
     for d in range(1, reach + 1):
-        zero = hop(zero, d, 0)
-        one = hop(one, d, 1)
+        zero = hop(zero, 0)
+        one = hop(one, 1)
         if d < reach:
             sums = mix([(0, d), (1, d)], [zero, one], sums)
     sums = mix([(0, reach)], [zero], sums)

time: 60.4 us -> 58 us (0.960)
  the two profiles are of different devices: /device:TPU:17 before, /device:TPU:0 now
where the time goes in v8:
time: 58 us; the launch traced here: 57.8 us
  waiting for transfers between devices  35 us (60%)
  starting transfers between devices  12.6 us (22%)
  Pallas kernels  9.45 us (16%)
  between operations  0.74 us (1%)
    ppermute x4, waiting for transfers between devices, hop(): return lax.ppermute(value, ('energy', 'mom'), ways[role])  22 us
    ppermute x6, waiting for transfers between devices, exchange(): return lax.ppermute(slots[i], ('len', 'mom'), pairs)  12 us
    ppermute x6, starting transfers between devices, exchange(): return lax.ppermute(slots[i], ('len', 'mom'), pairs)  8.23 us
    pallas_call x2, Pallas kernels, inverse(): pl.pallas_call(functools.partial(inverse_kernel, total, layers, slots), o...  4.51 us
    ppermute x4, starting transfers between devices, hop(): return lax.ppermute(value, ('energy', 'mom'), ways[role])  3.84 us
    pallas_call x1, Pallas kernels, shards(): pl.pallas_call(functools.partial(chain_kernel, layers), out_shape=[part]...  2.22 us
    pallas_call x3, Pallas kernels, mix(): pl.pallas_call(functools.partial(mix_kernel, total, items, False, last),...  1.73 us
  transfers between devices with their start and end apart: 14, of which 8 were waited for; matrix products, arithmetic and copies ran while one was open for 0% of the time, Pallas kernels for 7%

profile of v8, /device:TPU:0, one launch (start us, length us, event | category | flops | bytes accessed | tf_op | source)
XLA Modules:
  0.0 57.8 jit_solution(10155927135137630300)
XLA Ops:
  0.6 2.3 %inverse.3 = (f32[3,128,128]{2,1,0:T(8,128)S(1)}, f32[3,128,128]{2,1,0:T(8,128)S(1)}) custom-call(f32[2,128,128]{2,1,0:T(8,128)} %bitcast.9, f32[4,2,128,128]{3,2,1,0:T(8,128)} %bitcast.5, f32[128,128]{1,0:T(8,128)} %bitcast.11, s32[128,128]{1,0:T(8,128)} %pattern_any.3), custom_call_target="tpu_custom_call" | custom-call | flops 402653184 | bytes 262144 | tf_op jit(solution)/shard_map/inverse/pallas_call | solution.py:290
  2.9 4.0 %collective-permute-start = (f32[3,128,128]{2,1,0:T(8,128)S(1)}, f32[3,128,128]{2,1,0:T(8,128)S(1)}, u32[]{:S(2)}, u32[]{:S(2)}) collective-permute-start(f32[3,128,128]{2,1,0:T(8,128)S(1)} %get-tuple-element.21), channel_id=1, source_target_pairs={{0,24},{1,25},{8,16},{9,17},{16,8},{17,9},{24,0},{25,1},{2,26},{3,... | collective-permute-start | bytes 589832 | tf_op jit(solution)/shard_map/ppermute | solution.py:283
  6.9 0.5 collective-permute-start.1
  7.4 2.2 %inverse.2 = (f32[3,128,128]{2,1,0:T(8,128)S(1)}, f32[3,128,128]{2,1,0:T(8,128)S(1)}) custom-call(f32[2,128,128]{2,1,0:T(8,128)} %bitcast.10, f32[4,2,128,128]{3,2,1,0:T(8,128)} %bitcast.6, f32[128,128]{1,0:T(8,128)} %bitcast.12, s32[128,128]{1,0:T(8,128)} %pattern_any.3), custom_call_target="tpu_custom_call" | custom-call | flops 402653184 | bytes 262144 | tf_op jit(solution)/shard_map/inverse/pallas_call | solution.py:290
  9.6 0.2 collective-permute-start.2
  9.8 2.3 %collective-permute-done.refs_1_ = f32[3,128,128]{2,1,0:T(8,128)S(1)} collective-permute-done((f32[3,128,128]{2,1,0:T(8,128)S(1)}, f32[3,128,128]{2,1,0:T(8,128)S(1)}, u32[]{:S(2)}, u32[]{:S(2)}) %collective-permute-start) | collective-permute-done | bytes 196640 | tf_op jit(solution)/shard_map/ppermute | solution.py:283
  12.2 4.1 %collective-permute-done.1.refs_2_ = f32[3,128,128]{2,1,0:T(8,128)S(1)} collective-permute-done((f32[3,128,128]{2,1,0:T(8,128)S(1)}, f32[3,128,128]{2,1,0:T(8,128)S(1)}, u32[]{:S(2)}, u32[]{:S(2)}) %collective-permute-start.1) | collective-permute-done | bytes 196640 | tf_op jit(solution)/shard_map/ppermute | solution.py:283
  16.3 0.0 collective-permute-done.2.refs_3_
  16.3 2.2 %chains.1 = (f32[1,2,128,128]{3,2,1,0:T(8,128)S(1)}, f32[1,2,128,128]{3,2,1,0:T(8,128)S(1)}, f32[1,2,128,128]{3,2,1,0:T(8,128)S(1)}, f32[1,2,128,128]{3,2,1,0:T(8,128)S(1)}) custom-call(f32[3,128,128]{2,1,0:T(8,128)S(1)} %get-tuple-element.20.refs_0_, f32[3,128,128]{2,1,0:T(8,128)S(1)} %collective-permute-done.refs_1_, ...), custom_call_target="tpu_custom_call" | custom-call | tf_op jit(solution)/shard_map/chains/pallas_call | solution.py:314
  18.5 1.6 %collective-permute-start.3 = (f32[1,2,128,128]{3,2,1,0:T(8,128)S(1)}, f32[1,2,128,128]{3,2,1,0:T(8,128)S(1)}, u32[]{:S(2)}, u32[]{:S(2)}) collective-permute-start(f32[1,2,128,128]{3,2,1,0:T(8,128)S(1)} %get-tuple-element.25), channel_id=1, source_target_pairs={{0,24},{1,25},{8,16},{9,17},{16,8},{17,9},{24,0},{25,1},{2,26},{3,... | collective-permute-start | bytes 393224 | tf_op jit(solution)/shard_map/ppermute | solution.py:283
  20.1 1.4 %collective-permute-start.4 = (f32[1,2,128,128]{3,2,1,0:T(8,128)S(1)}, f32[1,2,128,128]{3,2,1,0:T(8,128)S(1)}, u32[]{:S(2)}, u32[]{:S(2)}) collective-permute-start(f32[1,2,128,128]{3,2,1,0:T(8,128)S(1)} %get-tuple-element.26), channel_id=1, source_target_pairs={{0,8},{1,17},{8,0},{9,25},{16,24},{17,1},{24,16},{25,9},{2,10},{3,... | collective-permute-start | bytes 393224 | tf_op jit(solution)/shard_map/ppermute | solution.py:283
  21.4 0.6 %collective-permute-start.5 = (f32[1,2,128,128]{3,2,1,0:T(8,128)S(1)}, f32[1,2,128,128]{3,2,1,0:T(8,128)S(1)}, u32[]{:S(2)}, u32[]{:S(2)}) collective-permute-start(f32[1,2,128,128]{3,2,1,0:T(8,128)S(1)} %get-tuple-element.27), channel_id=1, source_target_pairs={{0,16},{1,9},{8,24},{9,1},{16,0},{17,25},{24,8},{25,17},{2,18},{3,... | collective-permute-start | bytes 393224 | tf_op jit(solution)/shard_map/ppermute | solution.py:283
  22.1 3.8 %collective-permute-done.3.refs_1_ = f32[1,2,128,128]{3,2,1,0:T(8,128)S(1)} collective-permute-done((f32[1,2,128,128]{3,2,1,0:T(8,128)S(1)}, f32[1,2,128,128]{3,2,1,0:T(8,128)S(1)}, u32[]{:S(2)}, u32[]{:S(2)}) %collective-permute-start.3) | collective-permute-done | bytes 131104 | tf_op jit(solution)/shard_map/ppermute | solution.py:283
  25.8 0.0 collective-permute-start.7
  25.8 1.7 %collective-permute-done.4.refs_2_ = f32[1,2,128,128]{3,2,1,0:T(8,128)S(1)} collective-permute-done((f32[1,2,128,128]{3,2,1,0:T(8,128)S(1)}, f32[1,2,128,128]{3,2,1,0:T(8,128)S(1)}, u32[]{:S(2)}, u32[]{:S(2)}) %collective-permute-start.4) | collective-permute-done | bytes 131104 | tf_op jit(solution)/shard_map/ppermute | solution.py:283
  27.6 0.5 collective-permute-start.9
  28.1 0.0 collective-permute-done.6.refs_4_
  28.1 0.0 collective-permute-done.7.refs_5_
  28.1 0.8 %collective-permute-done.8.refs_6_ = f32[1,2,128,128]{3,2,1,0:T(8,128)S(1)} collective-permute-done((f32[1,2,128,128]{3,2,1,0:T(8,128)S(1)}, f32[1,2,128,128]{3,2,1,0:T(8,128)S(1)}, u32[]{:S(2)}, u32[]{:S(2)}) %collective-permute-start.8) | collective-permute-done | bytes 131104 | tf_op jit(solution)/shard_map/ppermute | solution.py:325
  28.9 0.2 collective-permute-done.9.refs_7_
  29.2 0.0 copy-start
  29.2 0.0 copy-start.1
  29.2 1.3 %collective-permute-start.12 = (f32[4,2,128,128]{3,2,1,0:T(8,128)S(1)}, f32[4,2,128,128]{3,2,1,0:T(8,128)S(1)}, u32[]{:S(2)}, u32[]{:S(2)}) collective-permute-start(f32[4,2,128,128]{3,2,1,0:T(8,128)S(1)} %momentum.2.zero_ref), channel_id=1, source_target_pairs={{0,2},{2,4},{4,6},{6,7},{7,5},{5,3},{3,1},{1,0},{8,10},{10,12},{12... | collective-permute-start | bytes 1572872 | tf_op jit(solution)/shard_map/ppermute | solution.py:345
  30.6 0.9 %local.1 = (f32[4,2,128,128]{3,2,1,0:T(8,128)S(1)}, f32[4,2,128,128]{3,2,1,0:T(8,128)S(1)}, f32[16,128]{1,0:T(8,128)S(1)}) custom-call(s32[4]{0:T(128)S(1)} %copy-done, f32[4]{0:T(128)S(1)} %copy-done.1, f32[4,2,128,128]{3,2,1,0:T(8,128)S(1)} %momentum.2.zero_ref, f32[4,2,128,128]{3,2,1,0:T(8,128)S(1)} %momentum.3.one_ref), custom_call_target="tpu_custom_call" | custom-call | tf_op jit(solution)/shard_map/local/pallas_call | solution.py:349
  31.5 0.0 collective-permute-start.10
  31.6 10.4 %collective-permute-done.12.refs_0_ = f32[4,2,128,128]{3,2,1,0:T(8,128)S(1)} collective-permute-done((f32[4,2,128,128]{3,2,1,0:T(8,128)S(1)}, f32[4,2,128,128]{3,2,1,0:T(8,128)S(1)}, u32[]{:S(2)}, u32[]{:S(2)}) %collective-permute-start.12) | collective-permute-done | bytes 524320 | tf_op jit(solution)/shard_map/ppermute | solution.py:345
  42.0 2.5 %collective-permute-start.13 = (f32[4,2,128,128]{3,2,1,0:T(8,128)S(1)}, f32[4,2,128,128]{3,2,1,0:T(8,128)S(1)}, u32[]{:S(2)}, u32[]{:S(2)}) collective-permute-start(f32[4,2,128,128]{3,2,1,0:T(8,128)S(1)} %collective-permute-done.12.refs_0_), channel_id=1, source_target_pairs={{0,2},{2,4},{4,6},{6,7},{7,5},{5,3},{3,1},{1,0},{8,10},{10,12},{12... | collective-permute-start | bytes 1572872 | tf_op jit(solution)/shard_map/ppermute | solution.py:345
  44.4 0.0 collective-permute-done.10.refs_1_
  44.4 0.0 collective-permute-start.11
  44.5 0.6 %mix.3 = (f32[4,2,128,128]{3,2,1,0:T(8,128)S(1)}, f32[4,2,128,128]{3,2,1,0:T(8,128)S(1)}) custom-call(f32[16,128]{1,0:T(8,128)S(1)} %get-tuple-element.28.table_ref, f32[4,2,128,128]{3,2,1,0:T(8,128)S(1)} %collective-permute-done.12.refs_0_, f32[4,2,128,128]{3,2,1,0:T(8,128)S(1)} %collective-permute-done.10.refs_1_, ...), custom_call_target="tpu_custom_call" | custom-call | tf_op jit(solution)/shard_map/mix/pallas_call | solution.py:362
  45.1 11.6 %collective-permute-done.13.refs_0_ = f32[4,2,128,128]{3,2,1,0:T(8,128)S(1)} collective-permute-done((f32[4,2,128,128]{3,2,1,0:T(8,128)S(1)}, f32[4,2,128,128]{3,2,1,0:T(8,128)S(1)}, u32[]{:S(2)}, u32[]{:S(2)}) %collective-permute-start.13) | collective-permute-done | bytes 524320 | tf_op jit(solution)/shard_map/ppermute | solution.py:345
  56.7 1.1 %mix.5 = (f32[4,2,128,128]{3,2,1,0:T(8,128)}, f32[4,2,128,128]{3,2,1,0:T(8,128)}) custom-call(f32[16,128]{1,0:T(8,128)S(1)} %get-tuple-element.28.table_ref, f32[4,2,128,128]{3,2,1,0:T(8,128)S(1)} %collective-permute-done.11.refs_0_, f32[4,2,128,128]{3,2,1,0:T(8,128)S(1)} %get-tuple-element.34.refs_1_, f32[4,2,128,128]{3,2,1,0:T(8,128)S(1)} %get-tuple-element.35.refs_2_, ...), custom_call_target="tpu_custom_call" | custom-call | tf_op jit(solution)/shard_map/mix/pallas_call | solution.py:362
  (10 shorter events, 0.1 us)
Async XLA Ops:
  2.9 9.3 %collective-permute-start = (f32[3,128,128]{2,1,0:T(8,128)S(1)}, f32[3,128,128]{2,1,0:T(8,128)S(1)}, u32[]{:S(2)}, u32[]{:S(2)}) collective-permute-start(f32[3,128,128]{2,1,0:T(8,128)S(1)} %get-tuple-element.21), channel_id=1, source_target_pairs={{0,24},{1,25},{8,16},{9,17},{16,8},{17,9},{24,0},{25,1},{2,26},{3,... | collective-permute-start | bytes 589832 | tf_op jit(solution)/shard_map/ppermute | solution.py:283
  6.9 9.4 %collective-permute-start.1 = (f32[3,128,128]{2,1,0:T(8,128)S(1)}, f32[3,128,128]{2,1,0:T(8,128)S(1)}, u32[]{:S(2)}, u32[]{:S(2)}) collective-permute-start(f32[3,128,128]{2,1,0:T(8,128)S(1)} %get-tuple-element.22), channel_id=1, source_target_pairs={{0,8},{1,17},{8,0},{9,25},{16,24},{17,1},{24,16},{25,9},{2,10},{3,... | collective-permute-start | bytes 589832 | tf_op jit(solution)/shard_map/ppermute | solution.py:283
  9.6 6.6 %collective-permute-start.2 = (f32[3,128,128]{2,1,0:T(8,128)S(1)}, f32[3,128,128]{2,1,0:T(8,128)S(1)}, u32[]{:S(2)}, u32[]{:S(2)}) collective-permute-start(f32[3,128,128]{2,1,0:T(8,128)S(1)} %get-tuple-element.23), channel_id=1, source_target_pairs={{0,16},{1,9},{8,24},{9,1},{16,0},{17,25},{24,8},{25,17},{2,18},{3,... | collective-permute-start | bytes 589832 | tf_op jit(solution)/shard_map/ppermute | solution.py:283
  18.5 7.3 %collective-permute-start.3 = (f32[1,2,128,128]{3,2,1,0:T(8,128)S(1)}, f32[1,2,128,128]{3,2,1,0:T(8,128)S(1)}, u32[]{:S(2)}, u32[]{:S(2)}) collective-permute-start(f32[1,2,128,128]{3,2,1,0:T(8,128)S(1)} %get-tuple-element.25), channel_id=1, source_target_pairs={{0,24},{1,25},{8,16},{9,17},{16,8},{17,9},{24,0},{25,1},{2,26},{3,... | collective-permute-start | bytes 393224 | tf_op jit(solution)/shard_map/ppermute | solution.py:283
  20.1 7.5 %collective-permute-start.4 = (f32[1,2,128,128]{3,2,1,0:T(8,128)S(1)}, f32[1,2,128,128]{3,2,1,0:T(8,128)S(1)}, u32[]{:S(2)}, u32[]{:S(2)}) collective-permute-start(f32[1,2,128,128]{3,2,1,0:T(8,128)S(1)} %get-tuple-element.26), channel_id=1, source_target_pairs={{0,8},{1,17},{8,0},{9,25},{16,24},{17,1},{24,16},{25,9},{2,10},{3,... | collective-permute-start | bytes 393224 | tf_op jit(solution)/shard_map/ppermute | solution.py:283
  21.4 6.2 %collective-permute-start.5 = (f32[1,2,128,128]{3,2,1,0:T(8,128)S(1)}, f32[1,2,128,128]{3,2,1,0:T(8,128)S(1)}, u32[]{:S(2)}, u32[]{:S(2)}) collective-permute-start(f32[1,2,128,128]{3,2,1,0:T(8,128)S(1)} %get-tuple-element.27), channel_id=1, source_target_pairs={{0,16},{1,9},{8,24},{9,1},{16,0},{17,25},{24,8},{25,17},{2,18},{3,... | collective-permute-start | bytes 393224 | tf_op jit(solution)/shard_map/ppermute | solution.py:283
  22.1 6.1 %collective-permute-start.6 = (f32[1,2,128,128]{3,2,1,0:T(8,128)S(1)}, f32[1,2,128,128]{3,2,1,0:T(8,128)S(1)}, u32[]{:S(2)}, u32[]{:S(2)}) collective-permute-start(f32[1,2,128,128]{3,2,1,0:T(8,128)S(1)} %get-tuple-element.24.refs_0_), channel_id=1, source_target_pairs={{0,1},{1,0},{2,3},{3,2},{4,5},{5,4},{6,7},{7,6},{8,9},{9,8},{10,11... | collective-permute-start | bytes 393224 | tf_op jit(solution)/shard_map/ppermute | solution.py:325
  25.8 2.3 %collective-permute-start.7 = (f32[1,2,128,128]{3,2,1,0:T(8,128)S(1)}, f32[1,2,128,128]{3,2,1,0:T(8,128)S(1)}, u32[]{:S(2)}, u32[]{:S(2)}) collective-permute-start(f32[1,2,128,128]{3,2,1,0:T(8,128)S(1)} %collective-permute-done.3.refs_1_), channel_id=1, source_target_pairs={{0,1},{1,0},{2,3},{3,2},{4,5},{5,4},{6,7},{7,6},{8,9},{9,8},{10,11... | collective-permute-start | bytes 393224 | tf_op jit(solution)/shard_map/ppermute | solution.py:325
  27.6 1.3 %collective-permute-start.8 = (f32[1,2,128,128]{3,2,1,0:T(8,128)S(1)}, f32[1,2,128,128]{3,2,1,0:T(8,128)S(1)}, u32[]{:S(2)}, u32[]{:S(2)}) collective-permute-start(f32[1,2,128,128]{3,2,1,0:T(8,128)S(1)} %collective-permute-done.4.refs_2_), channel_id=1, source_target_pairs={{0,1},{1,0},{2,3},{3,2},{4,5},{5,4},{6,7},{7,6},{8,9},{9,8},{10,11... | collective-permute-start | bytes 393224 | tf_op jit(solution)/shard_map/ppermute | solution.py:325
  27.6 1.5 %collective-permute-start.9 = (f32[1,2,128,128]{3,2,1,0:T(8,128)S(1)}, f32[1,2,128,128]{3,2,1,0:T(8,128)S(1)}, u32[]{:S(2)}, u32[]{:S(2)}) collective-permute-start(f32[1,2,128,128]{3,2,1,0:T(8,128)S(1)} %collective-permute-done.5.refs_3_), channel_id=1, source_target_pairs={{0,1},{1,0},{2,3},{3,2},{4,5},{5,4},{6,7},{7,6},{8,9},{9,8},{10,11... | collective-permute-start | bytes 393224 | tf_op jit(solution)/shard_map/ppermute | solution.py:325
  29.2 1.4 %copy-start = (s32[4]{0:T(128)S(1)}, s32[4]{0:T(128)}, u32[]{:S(2)}) copy-start(s32[4]{0:T(128)} %shift_ref.1) | copy-start | bytes 52
  29.2 1.4 %copy-start.1 = (f32[4]{0:T(128)S(1)}, f32[4]{0:T(128)}, u32[]{:S(2)}) copy-start(f32[4]{0:T(128)} %weight_ref.1) | copy-start | bytes 52
  29.2 12.8 %collective-permute-start.12 = (f32[4,2,128,128]{3,2,1,0:T(8,128)S(1)}, f32[4,2,128,128]{3,2,1,0:T(8,128)S(1)}, u32[]{:S(2)}, u32[]{:S(2)}) collective-permute-start(f32[4,2,128,128]{3,2,1,0:T(8,128)S(1)} %momentum.2.zero_ref), channel_id=1, source_target_pairs={{0,2},{2,4},{4,6},{6,7},{7,5},{5,3},{3,1},{1,0},{8,10},{10,12},{12... | collective-permute-start | bytes 1572872 | tf_op jit(solution)/shard_map/ppermute | solution.py:345
  31.5 12.9 %collective-permute-start.10 = (f32[4,2,128,128]{3,2,1,0:T(8,128)S(1)}, f32[4,2,128,128]{3,2,1,0:T(8,128)S(1)}, u32[]{:S(2)}, u32[]{:S(2)}) collective-permute-start(f32[4,2,128,128]{3,2,1,0:T(8,128)S(1)} %momentum.3.one_ref), channel_id=1, source_target_pairs={{2,0},{4,2},{6,4},{7,6},{5,7},{3,5},{1,3},{0,1},{10,8},{12,10},{14... | collective-permute-start | bytes 1572872 | tf_op jit(solution)/shard_map/ppermute | solution.py:345
  42.0 14.7 %collective-permute-start.13 = (f32[4,2,128,128]{3,2,1,0:T(8,128)S(1)}, f32[4,2,128,128]{3,2,1,0:T(8,128)S(1)}, u32[]{:S(2)}, u32[]{:S(2)}) collective-permute-start(f32[4,2,128,128]{3,2,1,0:T(8,128)S(1)} %collective-permute-done.12.refs_0_), channel_id=1, source_target_pairs={{0,2},{2,4},{4,6},{6,7},{7,5},{5,3},{3,1},{1,0},{8,10},{10,12},{12... | collective-permute-start | bytes 1572872 | tf_op jit(solution)/shard_map/ppermute | solution.py:345
  44.4 12.2 %collective-permute-start.11 = (f32[4,2,128,128]{3,2,1,0:T(8,128)S(1)}, f32[4,2,128,128]{3,2,1,0:T(8,128)S(1)}, u32[]{:S(2)}, u32[]{:S(2)}) collective-permute-start(f32[4,2,128,128]{3,2,1,0:T(8,128)S(1)} %collective-permute-done.10.refs_1_), channel_id=1, source_target_pairs={{2,0},{4,2},{6,4},{7,6},{5,7},{3,5},{1,3},{0,1},{10,8},{12,10},{14... | collective-permute-start | bytes 1572872 | tf_op jit(solution)/shard_map/ppermute | solution.py:345

commit v9 on v8

--- a/solution.py
+++ b/solution.py
@@ -156,25 +156,41 @@
         out_slot[...] = g_ref[peer]
 
 
-def momentum_kernel(momentum, layers, *refs):
+def momentum_kernel(momentum, slots, *refs):
     core = lax.axis_index("mom")
-    here = lax.axis_index("len")
     out_ref = refs[-1]
     per = refs[0].shape[0]
-    masks = [0] + orders(layers)[momentum]
-
-    def place(slots):
-        for mask, slot in zip(masks, slots):
-            for p in range(per):
-                out_ref[(here ^ mask) * per + p] = slot[p]
+
+    def place(blocks):
+        for i, block in enumerate(blocks):
+            out_ref[i * per : (i + 1) * per] = block[...]
 
     @pl.when(core == momentum)
     def _():
-        place(refs[:layers])
+        place(refs[:slots])
 
     @pl.when(core != momentum)
     def _():
-        place(refs[layers : 2 * layers])
+        place(refs[slots : 2 * slots])
+
+
+def join_kernel(*refs):
+    out_ref = refs[-1]
+    start = 0
+    for part in refs[:-1]:
+        out_ref[start : start + part.shape[0]] = part[...]
+        start += part.shape[0]
+
+
+def by_energy_kernel(momentum, layers, order, *refs):
+    here = lax.axis_index("len")
+    parts, out_ref = refs[:-1], refs[-1]
+    per = out_ref.shape[0] // layers
+    masks = [0] + orders(layers)[momentum]
+    slots = [(part, i) for part in parts for i in range(part.shape[0] // per)]
+    for slot, (part, i) in zip(order, slots):
+        for p in range(per):
+            out_ref[(here ^ masks[slot]) * per + p] = part[i * per + p]
 
 
 def occupation(pos, total, n):
@@ -322,18 +338,29 @@
     )(*[exchange(sent, i) for i in range(layers)])
     own = [exchange(sent, i) for i in range(layers)]
     both_ways = [(k, moms - 1 - k) for k in range(moms)]
-    other = [lax.ppermute(v, "mom", both_ways) for v in own]
-    zero, one = (
-        pl.pallas_call(
-            functools.partial(momentum_kernel, momentum, layers),
-            out_shape=block,
-            in_specs=whole(2 * layers),
+    little = pl.CostEstimate(flops=0, bytes_accessed=8 * n, transcendentals=0)
+
+    def call(kernel, shape, *operands, name):
+        return pl.pallas_call(
+            kernel,
+            out_shape=jax.ShapeDtypeStruct((shape, 2, n, n), F32),
+            in_specs=whole(len(operands)),
             out_specs=whole(1)[0],
             compiler_params=params(),
-            name="momentum",
-        )(*own, *other)
-        for momentum in range(2)
-    )
+            cost_estimate=little,
+            name=name,
+        )(*operands)
+
+    def of_momentum(momentum, own, other):
+        kernel = functools.partial(momentum_kernel, momentum, len(own))
+        return call(kernel, len(own) * per, *own, *other, name="momentum")
+
+    def by_energy(momentum, parts):
+        kernel = functools.partial(by_energy_kernel, momentum, layers, sum(chunks, []))
+        return call(kernel, local_e, *parts, name="by_energy")
+
+    def join(parts):
+        return call(join_kernel, sum(p.shape[0] for p in parts), *parts, name="join")
 
     reach = -(-(total // 2) // local_e)
 
@@ -344,8 +371,19 @@
     def hop(value, role):
         return lax.ppermute(value, ("energy", "mom"), ways[role])
 
+    chunks = [[0], [layers - 1], list(range(1, layers - 1))]
+    fields = [[], []]
+    hops = [[], []]
+    for c in chunks:
+        held = [own[i] for i in c]
+        if hops[0]:
+            held, _ = lax.optimization_barrier((held, [steps[0] for steps in hops]))
+        other = [lax.ppermute(v, "mom", both_ways) for v in held]
+        for m in range(2):
+            fields[m].append(of_momentum(m, held, other))
+            hops[m].append(hop(fields[m][-1], m))
+    zero, one = (by_energy(m, fields[m]) for m in range(2))
     smem = pl.BlockSpec(memory_space=pltpu.SMEM)
-
     retarded, local_lesser, table = pl.pallas_call(
         functools.partial(local_kernel, total),
         out_shape=[block] * 2 + [jax.ShapeDtypeStruct((total // 2 + 8, n), F32)],
@@ -370,11 +408,12 @@
             name="mix",
         )(table, *blocks, *sums)
 
-    one, _ = lax.optimization_barrier((one, local_lesser))
     sums = [retarded, jnp.zeros_like(local_lesser)]
     for d in range(1, reach + 1):
-        zero = hop(zero, 0)
-        one = hop(one, 1)
+        fields = hops if d == 1 else [[hop(part, m) for part in fields[m]] for m in range(2)]
+        zero, one = (by_energy(m, fields[m]) for m in range(2))
+        if d == 1:
+            fields = [[join(parts[:-1]), parts[-1]] for parts in fields]
         if d < reach:
             sums = mix([(0, d), (1, d)], [zero, one], sums)
     sums = mix([(0, reach)], [zero], sums)

time: 58 us -> 56.6 us (0.976)
  waiting for transfers between devices: 35 us -> 26.8 us
  starting transfers between devices: 12.6 us -> 18.3 us
  local copies, waits for them, and re-layouts: 0.05 us -> 0.64 us
    ppermute x4 -> x10, waiting for transfers between devices: 22 us -> 15.3 us  [hop(): return lax.ppermute(value, ('energy', 'mom'), ways[role])]
    ppermute x4 -> x10, starting transfers between devices: 3.84 us -> 9.39 us  [hop(): return lax.ppermute(value, ('energy', 'mom'), ways[role])]
    ppermute x6, waiting for transfers between devices: 12 us -> 10.5 us  [exchange(): return lax.ppermute(slots[i], ('len', 'mom'), pairs)]
    unnamed x4, local copies, waits for them, and re-layouts: 0.01 us -> 0.6 us
  transfers between devices with their start and end apart: 14 -> 20, of which waited for: 8 -> 10; matrix products, arithmetic and copies ran while one was open for 0% -> 0% of each run, Pallas kernels for 7% -> 7%
where the time goes in v9:
time: 56.6 us; the launch traced here: 56.4 us
  waiting for transfers between devices  26.8 us (47%)
  starting transfers between devices  18.3 us (32%)
  Pallas kernels  9.81 us (17%)
  between operations  0.88 us (2%)
  local copies, waits for them, and re-layouts  0.64 us (1%)
    ppermute x10, waiting for transfers between devices, hop(): return lax.ppermute(value, ('energy', 'mom'), ways[role])  15.3 us
    ppermute x6, waiting for transfers between devices, exchange(): return lax.ppermute(slots[i], ('len', 'mom'), pairs)  10.5 us
    ppermute x10, starting transfers between devices, hop(): return lax.ppermute(value, ('energy', 'mom'), ways[role])  9.39 us
    ppermute x6, starting transfers between devices, exchange(): return lax.ppermute(slots[i], ('len', 'mom'), pairs)  8.29 us
    pallas_call x2, Pallas kernels, inverse(): pl.pallas_call(functools.partial(inverse_kernel, total, layers, slots), o...  4.51 us
    pallas_call x1, Pallas kernels, shards(): pl.pallas_call(functools.partial(chain_kernel, layers), out_shape=[part]...  2.22 us
    pallas_call x3, Pallas kernels, mix(): pl.pallas_call(functools.partial(mix_kernel, total, items, False, last),...  1.77 us
  transfers between devices with their start and end apart: 20, of which 10 were waited for; matrix products, arithmetic and copies ran while one was open for 0% of the time, Pallas kernels for 7%

profile of v9, /device:TPU:0, one launch (start us, length us, event | category | flops | bytes accessed | tf_op | source)
XLA Modules:
  0.0 56.4 jit_solution(2519377577922671947)
XLA Ops:
  0.6 2.3 %inverse.3 = (f32[3,128,128]{2,1,0:T(8,128)S(1)}, f32[3,128,128]{2,1,0:T(8,128)S(1)}) custom-call(f32[2,128,128]{2,1,0:T(8,128)} %bitcast.9, f32[4,2,128,128]{3,2,1,0:T(8,128)} %bitcast.5, f32[128,128]{1,0:T(8,128)} %bitcast.11, s32[128,128]{1,0:T(8,128)} %pattern_any.3), custom_call_target="tpu_custom_call" | custom-call | flops 402653184 | bytes 262144 | tf_op jit(solution)/shard_map/inverse/pallas_call | solution.py:306
  2.9 4.0 %collective-permute-start = (f32[3,128,128]{2,1,0:T(8,128)S(1)}, f32[3,128,128]{2,1,0:T(8,128)S(1)}, u32[]{:S(2)}, u32[]{:S(2)}) collective-permute-start(f32[3,128,128]{2,1,0:T(8,128)S(1)} %get-tuple-element.23), channel_id=1, source_target_pairs={{0,24},{1,25},{8,16},{9,17},{16,8},{17,9},{24,0},{25,1},{2,26},{3,... | collective-permute-start | bytes 589832 | tf_op jit(solution)/shard_map/ppermute | solution.py:299
  6.9 0.5 collective-permute-start.1
  7.4 2.2 %inverse.2 = (f32[3,128,128]{2,1,0:T(8,128)S(1)}, f32[3,128,128]{2,1,0:T(8,128)S(1)}) custom-call(f32[2,128,128]{2,1,0:T(8,128)} %bitcast.10, f32[4,2,128,128]{3,2,1,0:T(8,128)} %bitcast.6, f32[128,128]{1,0:T(8,128)} %bitcast.12, s32[128,128]{1,0:T(8,128)} %pattern_any.3), custom_call_target="tpu_custom_call" | custom-call | flops 402653184 | bytes 262144 | tf_op jit(solution)/shard_map/inverse/pallas_call | solution.py:306
  9.6 0.2 collective-permute-start.2
  9.8 2.3 %collective-permute-done.refs_1_ = f32[3,128,128]{2,1,0:T(8,128)S(1)} collective-permute-done((f32[3,128,128]{2,1,0:T(8,128)S(1)}, f32[3,128,128]{2,1,0:T(8,128)S(1)}, u32[]{:S(2)}, u32[]{:S(2)}) %collective-permute-start) | collective-permute-done | bytes 196640 | tf_op jit(solution)/shard_map/ppermute | solution.py:299
  12.2 4.1 %collective-permute-done.1.refs_2_ = f32[3,128,128]{2,1,0:T(8,128)S(1)} collective-permute-done((f32[3,128,128]{2,1,0:T(8,128)S(1)}, f32[3,128,128]{2,1,0:T(8,128)S(1)}, u32[]{:S(2)}, u32[]{:S(2)}) %collective-permute-start.1) | collective-permute-done | bytes 196640 | tf_op jit(solution)/shard_map/ppermute | solution.py:299
  16.3 2.2 %chains.1 = (f32[1,2,128,128]{3,2,1,0:T(8,128)S(1)}, f32[1,2,128,128]{3,2,1,0:T(8,128)S(1)}, f32[1,2,128,128]{3,2,1,0:T(8,128)S(1)}, f32[1,2,128,128]{3,2,1,0:T(8,128)S(1)}) custom-call(f32[3,128,128]{2,1,0:T(8,128)S(1)} %get-tuple-element.22.refs_0_, f32[3,128,128]{2,1,0:T(8,128)S(1)} %collective-permute-done.refs_1_, ...), custom_call_target="tpu_custom_call" | custom-call | tf_op jit(solution)/shard_map/chains/pallas_call | solution.py:330
  18.5 0.1 collective-permute-start.3
  18.6 1.6 %collective-permute-start.8 = (f32[1,2,128,128]{3,2,1,0:T(8,128)S(1)}, f32[1,2,128,128]{3,2,1,0:T(8,128)S(1)}, u32[]{:S(2)}, u32[]{:S(2)}) collective-permute-start(f32[1,2,128,128]{3,2,1,0:T(8,128)S(1)} %get-tuple-element.29), channel_id=1, source_target_pairs={{0,24},{1,25},{8,16},{9,17},{16,8},{17,9},{24,0},{25,1},{2,26},{3,... | collective-permute-start | bytes 393224 | tf_op jit(solution)/shard_map/ppermute | solution.py:299
  20.2 1.4 %collective-permute-start.9 = (f32[1,2,128,128]{3,2,1,0:T(8,128)S(1)}, f32[1,2,128,128]{3,2,1,0:T(8,128)S(1)}, u32[]{:S(2)}, u32[]{:S(2)}) collective-permute-start(f32[1,2,128,128]{3,2,1,0:T(8,128)S(1)} %get-tuple-element.30), channel_id=1, source_target_pairs={{0,8},{1,17},{8,0},{9,25},{16,24},{17,1},{24,16},{25,9},{2,10},{3,... | collective-permute-start | bytes 393224 | tf_op jit(solution)/shard_map/ppermute | solution.py:299
  21.5 1.6 %collective-permute-start.5 = (f32[1,2,128,128]{3,2,1,0:T(8,128)S(1)}, f32[1,2,128,128]{3,2,1,0:T(8,128)S(1)}, u32[]{:S(2)}, u32[]{:S(2)}) collective-permute-start(f32[1,2,128,128]{3,2,1,0:T(8,128)S(1)} %momentum.6.refs_0_), channel_id=1, source_target_pairs={{0,2},{2,4},{4,6},{6,7},{7,5},{5,3},{3,1},{1,0},{8,10},{10,12},{12... | collective-permute-start | bytes 393224 | tf_op jit(solution)/shard_map/ppermute | solution.py:372
  23.1 0.0 collective-permute-start.6
  23.2 0.7 %collective-permute-start.4 = (f32[1,2,128,128]{3,2,1,0:T(8,128)S(1)}, f32[1,2,128,128]{3,2,1,0:T(8,128)S(1)}, u32[]{:S(2)}, u32[]{:S(2)}) collective-permute-start(f32[1,2,128,128]{3,2,1,0:T(8,128)S(1)} %get-tuple-element.27), channel_id=1, source_target_pairs={{0,16},{1,9},{8,24},{9,1},{16,0},{17,25},{24,8},{25,17},{2,18},{3,... | collective-permute-start | bytes 393224 | tf_op jit(solution)/shard_map/ppermute | solution.py:299
  23.9 1.6 %collective-permute-done.8.refs_0_ = f32[1,2,128,128]{3,2,1,0:T(8,128)S(1)} collective-permute-done((f32[1,2,128,128]{3,2,1,0:T(8,128)S(1)}, f32[1,2,128,128]{3,2,1,0:T(8,128)S(1)}, u32[]{:S(2)}, u32[]{:S(2)}) %collective-permute-start.8) | collective-permute-done | bytes 131104 | tf_op jit(solution)/shard_map/ppermute | solution.py:299
  25.5 2.4 %collective-permute-done.9.refs_1_ = f32[1,2,128,128]{3,2,1,0:T(8,128)S(1)} collective-permute-done((f32[1,2,128,128]{3,2,1,0:T(8,128)S(1)}, f32[1,2,128,128]{3,2,1,0:T(8,128)S(1)}, u32[]{:S(2)}, u32[]{:S(2)}) %collective-permute-start.9) | collective-permute-done | bytes 131104 | tf_op jit(solution)/shard_map/ppermute | solution.py:299
  27.9 0.2 collective-permute-done.6.refs_0_
  28.1 0.5 collective-permute-start.11
  28.7 0.8 %collective-permute-done.10.refs_2_ = f32[1,2,128,128]{3,2,1,0:T(8,128)S(1)} collective-permute-done((f32[1,2,128,128]{3,2,1,0:T(8,128)S(1)}, f32[1,2,128,128]{3,2,1,0:T(8,128)S(1)}, u32[]{:S(2)}, u32[]{:S(2)}) %collective-permute-start.10) | collective-permute-done | bytes 131104 | tf_op jit(solution)/shard_map/ppermute | solution.py:381
  29.5 0.2 collective-permute-done.11.refs_3_
  29.7 1.6 %collective-permute-start.18 = (f32[2,2,128,128]{3,2,1,0:T(8,128)S(1)}, f32[2,2,128,128]{3,2,1,0:T(8,128)S(1)}, u32[]{:S(2)}, u32[]{:S(2)}) collective-permute-start(f32[2,2,128,128]{3,2,1,0:T(8,128)S(1)} %momentum.9.refs_2_), channel_id=1, source_target_pairs={{0,2},{2,4},{4,6},{6,7},{7,5},{5,3},{3,1},{1,0},{8,10},{10,12},{12... | collective-permute-start | bytes 786440 | tf_op jit(solution)/shard_map/ppermute | solution.py:372
  31.3 0.0 collective-permute-start.14
  31.4 2.0 %collective-permute-start.16 = (f32[1,2,128,128]{3,2,1,0:T(8,128)S(1)}, f32[1,2,128,128]{3,2,1,0:T(8,128)S(1)}, u32[]{:S(2)}, u32[]{:S(2)}) collective-permute-start(f32[1,2,128,128]{3,2,1,0:T(8,128)S(1)} %momentum.8.refs_1_), channel_id=1, source_target_pairs={{0,2},{2,4},{4,6},{6,7},{7,5},{5,3},{3,1},{1,0},{8,10},{10,12},{12... | collective-permute-start | bytes 393224 | tf_op jit(solution)/shard_map/ppermute | solution.py:372
  33.4 6.9 %collective-permute-done.16.refs_1_ = f32[1,2,128,128]{3,2,1,0:T(8,128)S(1)} collective-permute-done((f32[1,2,128,128]{3,2,1,0:T(8,128)S(1)}, f32[1,2,128,128]{3,2,1,0:T(8,128)S(1)}, u32[]{:S(2)}, u32[]{:S(2)}) %collective-permute-start.16) | collective-permute-done | bytes 131104 | tf_op jit(solution)/shard_map/ppermute | solution.py:372
  40.4 2.5 %collective-permute-start.17 = (f32[2,2,128,128]{3,2,1,0:T(8,128)S(1)}, f32[2,2,128,128]{3,2,1,0:T(8,128)S(1)}, u32[]{:S(2)}, u32[]{:S(2)}) collective-permute-start(f32[2,2,128,128]{3,2,1,0:T(8,128)S(1)} %join.3), channel_id=1, source_target_pairs={{0,2},{2,4},{4,6},{6,7},{7,5},{5,3},{3,1},{1,0},{8,10},{10,12},{12... | collective-permute-start | bytes 786440 | tf_op jit(solution)/shard_map/ppermute | solution.py:372
  42.9 1.6 %collective-permute-start.19 = (f32[2,2,128,128]{3,2,1,0:T(8,128)S(1)}, f32[2,2,128,128]{3,2,1,0:T(8,128)S(1)}, u32[]{:S(2)}, u32[]{:S(2)}) collective-permute-start(f32[2,2,128,128]{3,2,1,0:T(8,128)S(1)} %collective-permute-done.18.refs_2_), channel_id=1, source_target_pairs={{0,2},{2,4},{4,6},{6,7},{7,5},{5,3},{3,1},{1,0},{8,10},{10,12},{12... | collective-permute-start | bytes 786440 | tf_op jit(solution)/shard_map/ppermute | solution.py:372
  44.7 0.6 %copy-done = s32[4]{0:T(128)S(1)} copy-done((s32[4]{0:T(128)S(1)}, s32[4]{0:T(128)}, u32[]{:S(2)}) %copy-start) | copy-done | bytes 40
  45.3 0.9 %local.1 = (f32[4,2,128,128]{3,2,1,0:T(8,128)S(1)}, f32[4,2,128,128]{3,2,1,0:T(8,128)S(1)}, f32[16,128]{1,0:T(8,128)S(1)}) custom-call(s32[4]{0:T(128)S(1)} %copy-done, f32[4]{0:T(128)S(1)} %copy-done.1, f32[4,2,128,128]{3,2,1,0:T(8,128)S(1)} %by_energy.6.zero_ref, f32[4,2,128,128]{3,2,1,0:T(8,128)S(1)} %by_energy.7.one_ref), custom_call_target="tpu_custom_call" | custom-call | tf_op jit(solution)/shard_map/local/pallas_call | solution.py:387
  46.4 0.6 %mix.3 = (f32[4,2,128,128]{3,2,1,0:T(8,128)S(1)}, f32[4,2,128,128]{3,2,1,0:T(8,128)S(1)}) custom-call(f32[16,128]{1,0:T(8,128)S(1)} %get-tuple-element.33.table_ref, f32[4,2,128,128]{3,2,1,0:T(8,128)S(1)} %by_energy.10.refs_0_, f32[4,2,128,128]{3,2,1,0:T(8,128)S(1)} %by_energy.11.refs_1_, f32[4,2,128,128]{3,2,1,0:T(8,128)S(1)} %get-tuple-element.34.refs_2_, ...), custom_call_target="tpu_custom_call" | custom-call | tf_op jit(solution)/shard_map/mix/pallas_call | solution.py:400
  47.0 2.6 %collective-permute-done.17.refs_0_ = f32[2,2,128,128]{3,2,1,0:T(8,128)S(1)} collective-permute-done((f32[2,2,128,128]{3,2,1,0:T(8,128)S(1)}, f32[2,2,128,128]{3,2,1,0:T(8,128)S(1)}, u32[]{:S(2)}, u32[]{:S(2)}) %collective-permute-start.17) | collective-permute-done | bytes 262176 | tf_op jit(solution)/shard_map/ppermute | solution.py:372
  49.6 5.5 %collective-permute-done.19.refs_1_ = f32[2,2,128,128]{3,2,1,0:T(8,128)S(1)} collective-permute-done((f32[2,2,128,128]{3,2,1,0:T(8,128)S(1)}, f32[2,2,128,128]{3,2,1,0:T(8,128)S(1)}, u32[]{:S(2)}, u32[]{:S(2)}) %collective-permute-start.19) | collective-permute-done | bytes 262176 | tf_op jit(solution)/shard_map/ppermute | solution.py:372
  55.2 1.2 %mix.5 = (f32[4,2,128,128]{3,2,1,0:T(8,128)}, f32[4,2,128,128]{3,2,1,0:T(8,128)}) custom-call(f32[16,128]{1,0:T(8,128)S(1)} %get-tuple-element.33.table_ref, f32[4,2,128,128]{3,2,1,0:T(8,128)S(1)} %by_energy.8.refs_0_, f32[4,2,128,128]{3,2,1,0:T(8,128)S(1)} %get-tuple-element.37.refs_1_, f32[4,2,128,128]{3,2,1,0:T(8,128)S(1)} %get-tuple-element.38.refs_2_, ...), custom_call_target="tpu_custom_call" | custom-call | tf_op jit(solution)/shard_map/mix/pallas_call | solution.py:400
  (34 shorter events, 0.6 us)
Async XLA Ops:
  2.9 9.3 %collective-permute-start = (f32[3,128,128]{2,1,0:T(8,128)S(1)}, f32[3,128,128]{2,1,0:T(8,128)S(1)}, u32[]{:S(2)}, u32[]{:S(2)}) collective-permute-start(f32[3,128,128]{2,1,0:T(8,128)S(1)} %get-tuple-element.23), channel_id=1, source_target_pairs={{0,24},{1,25},{8,16},{9,17},{16,8},{17,9},{24,0},{25,1},{2,26},{3,... | collective-permute-start | bytes 589832 | tf_op jit(solution)/shard_map/ppermute | solution.py:299
  6.9 9.4 %collective-permute-start.1 = (f32[3,128,128]{2,1,0:T(8,128)S(1)}, f32[3,128,128]{2,1,0:T(8,128)S(1)}, u32[]{:S(2)}, u32[]{:S(2)}) collective-permute-start(f32[3,128,128]{2,1,0:T(8,128)S(1)} %get-tuple-element.24), channel_id=1, source_target_pairs={{0,8},{1,17},{8,0},{9,25},{16,24},{17,1},{24,16},{25,9},{2,10},{3,... | collective-permute-start | bytes 589832 | tf_op jit(solution)/shard_map/ppermute | solution.py:299
  9.6 6.6 %collective-permute-start.2 = (f32[3,128,128]{2,1,0:T(8,128)S(1)}, f32[3,128,128]{2,1,0:T(8,128)S(1)}, u32[]{:S(2)}, u32[]{:S(2)}) collective-permute-start(f32[3,128,128]{2,1,0:T(8,128)S(1)} %get-tuple-element.25), channel_id=1, source_target_pairs={{0,16},{1,9},{8,24},{9,1},{16,0},{17,25},{24,8},{25,17},{2,18},{3,... | collective-permute-start | bytes 589832 | tf_op jit(solution)/shard_map/ppermute | solution.py:299
  18.5 3.0 %collective-permute-start.3 = (f32[1,2,128,128]{3,2,1,0:T(8,128)S(1)}, f32[1,2,128,128]{3,2,1,0:T(8,128)S(1)}, u32[]{:S(2)}, u32[]{:S(2)}) collective-permute-start(f32[1,2,128,128]{3,2,1,0:T(8,128)S(1)} %get-tuple-element.26.refs_0_), channel_id=1, source_target_pairs={{0,1},{1,0},{2,3},{3,2},{4,5},{5,4},{6,7},{7,6},{8,9},{9,8},{10,11... | collective-permute-start | bytes 393224 | tf_op jit(solution)/shard_map/ppermute | solution.py:381
  18.6 6.9 %collective-permute-start.8 = (f32[1,2,128,128]{3,2,1,0:T(8,128)S(1)}, f32[1,2,128,128]{3,2,1,0:T(8,128)S(1)}, u32[]{:S(2)}, u32[]{:S(2)}) collective-permute-start(f32[1,2,128,128]{3,2,1,0:T(8,128)S(1)} %get-tuple-element.29), channel_id=1, source_target_pairs={{0,24},{1,25},{8,16},{9,17},{16,8},{17,9},{24,0},{25,1},{2,26},{3,... | collective-permute-start | bytes 393224 | tf_op jit(solution)/shard_map/ppermute | solution.py:299
  20.2 7.7 %collective-permute-start.9 = (f32[1,2,128,128]{3,2,1,0:T(8,128)S(1)}, f32[1,2,128,128]{3,2,1,0:T(8,128)S(1)}, u32[]{:S(2)}, u32[]{:S(2)}) collective-permute-start(f32[1,2,128,128]{3,2,1,0:T(8,128)S(1)} %get-tuple-element.30), channel_id=1, source_target_pairs={{0,8},{1,17},{8,0},{9,25},{16,24},{17,1},{24,16},{25,9},{2,10},{3,... | collective-permute-start | bytes 393224 | tf_op jit(solution)/shard_map/ppermute | solution.py:299
  21.5 6.4 %collective-permute-start.5 = (f32[1,2,128,128]{3,2,1,0:T(8,128)S(1)}, f32[1,2,128,128]{3,2,1,0:T(8,128)S(1)}, u32[]{:S(2)}, u32[]{:S(2)}) collective-permute-start(f32[1,2,128,128]{3,2,1,0:T(8,128)S(1)} %momentum.6.refs_0_), channel_id=1, source_target_pairs={{0,2},{2,4},{4,6},{6,7},{7,5},{5,3},{3,1},{1,0},{8,10},{10,12},{12... | collective-permute-start | bytes 393224 | tf_op jit(solution)/shard_map/ppermute | solution.py:372
  23.1 5.0 %collective-permute-start.6 = (f32[1,2,128,128]{3,2,1,0:T(8,128)S(1)}, f32[1,2,128,128]{3,2,1,0:T(8,128)S(1)}, u32[]{:S(2)}, u32[]{:S(2)}) collective-permute-start(f32[1,2,128,128]{3,2,1,0:T(8,128)S(1)} %momentum.7.refs_0_), channel_id=1, source_target_pairs={{2,0},{4,2},{6,4},{7,6},{5,7},{3,5},{1,3},{0,1},{10,8},{12,10},{14... | collective-permute-start | bytes 393224 | tf_op jit(solution)/shard_map/ppermute | solution.py:372
  23.2 5.5 %collective-permute-start.4 = (f32[1,2,128,128]{3,2,1,0:T(8,128)S(1)}, f32[1,2,128,128]{3,2,1,0:T(8,128)S(1)}, u32[]{:S(2)}, u32[]{:S(2)}) collective-permute-start(f32[1,2,128,128]{3,2,1,0:T(8,128)S(1)} %get-tuple-element.27), channel_id=1, source_target_pairs={{0,16},{1,9},{8,24},{9,1},{16,0},{17,25},{24,8},{25,17},{2,18},{3,... | collective-permute-start | bytes 393224 | tf_op jit(solution)/shard_map/ppermute | solution.py:299
  28.1 1.3 %collective-permute-start.10 = (f32[1,2,128,128]{3,2,1,0:T(8,128)S(1)}, f32[1,2,128,128]{3,2,1,0:T(8,128)S(1)}, u32[]{:S(2)}, u32[]{:S(2)}) collective-permute-start(f32[1,2,128,128]{3,2,1,0:T(8,128)S(1)} %collective-permute-done.8.refs_0_), channel_id=1, source_target_pairs={{0,1},{1,0},{2,3},{3,2},{4,5},{5,4},{6,7},{7,6},{8,9},{9,8},{10,11... | collective-permute-start | bytes 393224 | tf_op jit(solution)/shard_map/ppermute | solution.py:381
  28.1 1.5 %collective-permute-start.11 = (f32[1,2,128,128]{3,2,1,0:T(8,128)S(1)}, f32[1,2,128,128]{3,2,1,0:T(8,128)S(1)}, u32[]{:S(2)}, u32[]{:S(2)}) collective-permute-start(f32[1,2,128,128]{3,2,1,0:T(8,128)S(1)} %collective-permute-done.9.refs_1_), channel_id=1, source_target_pairs={{0,1},{1,0},{2,3},{3,2},{4,5},{5,4},{6,7},{7,6},{8,9},{9,8},{10,11... | collective-permute-start | bytes 393224 | tf_op jit(solution)/shard_map/ppermute | solution.py:381
  28.6 2.7 %collective-permute-start.7 = (f32[1,2,128,128]{3,2,1,0:T(8,128)S(1)}, f32[1,2,128,128]{3,2,1,0:T(8,128)S(1)}, u32[]{:S(2)}, u32[]{:S(2)}) collective-permute-start(f32[1,2,128,128]{3,2,1,0:T(8,128)S(1)} %collective-permute-done.4.refs_0_), channel_id=1, source_target_pairs={{0,1},{1,0},{2,3},{3,2},{4,5},{5,4},{6,7},{7,6},{8,9},{9,8},{10,11... | collective-permute-start | bytes 393224 | tf_op jit(solution)/shard_map/ppermute | solution.py:381
  29.7 13.2 %collective-permute-start.18 = (f32[2,2,128,128]{3,2,1,0:T(8,128)S(1)}, f32[2,2,128,128]{3,2,1,0:T(8,128)S(1)}, u32[]{:S(2)}, u32[]{:S(2)}) collective-permute-start(f32[2,2,128,128]{3,2,1,0:T(8,128)S(1)} %momentum.9.refs_2_), channel_id=1, source_target_pairs={{0,2},{2,4},{4,6},{6,7},{7,5},{5,3},{3,1},{1,0},{8,10},{10,12},{12... | collective-permute-start | bytes 786440 | tf_op jit(solution)/shard_map/ppermute | solution.py:372
  31.3 13.2 %collective-permute-start.14 = (f32[2,2,128,128]{3,2,1,0:T(8,128)S(1)}, f32[2,2,128,128]{3,2,1,0:T(8,128)S(1)}, u32[]{:S(2)}, u32[]{:S(2)}) collective-permute-start(f32[2,2,128,128]{3,2,1,0:T(8,128)S(1)} %momentum.11.refs_2_), channel_id=1, source_target_pairs={{2,0},{4,2},{6,4},{7,6},{5,7},{3,5},{1,3},{0,1},{10,8},{12,10},{14... | collective-permute-start | bytes 786440 | tf_op jit(solution)/shard_map/ppermute | solution.py:372
  31.4 9.0 %collective-permute-start.16 = (f32[1,2,128,128]{3,2,1,0:T(8,128)S(1)}, f32[1,2,128,128]{3,2,1,0:T(8,128)S(1)}, u32[]{:S(2)}, u32[]{:S(2)}) collective-permute-start(f32[1,2,128,128]{3,2,1,0:T(8,128)S(1)} %momentum.8.refs_1_), channel_id=1, source_target_pairs={{0,2},{2,4},{4,6},{6,7},{7,5},{5,3},{3,1},{1,0},{8,10},{10,12},{12... | collective-permute-start | bytes 393224 | tf_op jit(solution)/shard_map/ppermute | solution.py:372
  33.4 11.1 %collective-permute-start.12 = (f32[1,2,128,128]{3,2,1,0:T(8,128)S(1)}, f32[1,2,128,128]{3,2,1,0:T(8,128)S(1)}, u32[]{:S(2)}, u32[]{:S(2)}) collective-permute-start(f32[1,2,128,128]{3,2,1,0:T(8,128)S(1)} %momentum.10.refs_1_), channel_id=1, source_target_pairs={{2,0},{4,2},{6,4},{7,6},{5,7},{3,5},{1,3},{0,1},{10,8},{12,10},{14... | collective-permute-start | bytes 393224 | tf_op jit(solution)/shard_map/ppermute | solution.py:372
  40.4 9.2 %collective-permute-start.17 = (f32[2,2,128,128]{3,2,1,0:T(8,128)S(1)}, f32[2,2,128,128]{3,2,1,0:T(8,128)S(1)}, u32[]{:S(2)}, u32[]{:S(2)}) collective-permute-start(f32[2,2,128,128]{3,2,1,0:T(8,128)S(1)} %join.3), channel_id=1, source_target_pairs={{0,2},{2,4},{4,6},{6,7},{7,5},{5,3},{3,1},{1,0},{8,10},{10,12},{12... | collective-permute-start | bytes 786440 | tf_op jit(solution)/shard_map/ppermute | solution.py:372
  42.9 12.2 %collective-permute-start.19 = (f32[2,2,128,128]{3,2,1,0:T(8,128)S(1)}, f32[2,2,128,128]{3,2,1,0:T(8,128)S(1)}, u32[]{:S(2)}, u32[]{:S(2)}) collective-permute-start(f32[2,2,128,128]{3,2,1,0:T(8,128)S(1)} %collective-permute-done.18.refs_2_), channel_id=1, source_target_pairs={{0,2},{2,4},{4,6},{6,7},{7,5},{5,3},{3,1},{1,0},{8,10},{10,12},{12... | collective-permute-start | bytes 786440 | tf_op jit(solution)/shard_map/ppermute | solution.py:372
  44.5 10.7 %collective-permute-start.13 = (f32[2,2,128,128]{3,2,1,0:T(8,128)S(1)}, f32[2,2,128,128]{3,2,1,0:T(8,128)S(1)}, u32[]{:S(2)}, u32[]{:S(2)}) collective-permute-start(f32[2,2,128,128]{3,2,1,0:T(8,128)S(1)} %join.2), channel_id=1, source_target_pairs={{2,0},{4,2},{6,4},{7,6},{5,7},{3,5},{1,3},{0,1},{10,8},{12,10},{14... | collective-permute-start | bytes 786440 | tf_op jit(solution)/shard_map/ppermute | solution.py:372
  44.5 10.6 %collective-permute-start.15 = (f32[2,2,128,128]{3,2,1,0:T(8,128)S(1)}, f32[2,2,128,128]{3,2,1,0:T(8,128)S(1)}, u32[]{:S(2)}, u32[]{:S(2)}) collective-permute-start(f32[2,2,128,128]{3,2,1,0:T(8,128)S(1)} %collective-permute-done.14.refs_2_), channel_id=1, source_target_pairs={{2,0},{4,2},{6,4},{7,6},{5,7},{3,5},{1,3},{0,1},{10,8},{12,10},{14... | collective-permute-start | bytes 786440 | tf_op jit(solution)/shard_map/ppermute | solution.py:372
  44.6 0.7 %copy-start = (s32[4]{0:T(128)S(1)}, s32[4]{0:T(128)}, u32[]{:S(2)}) copy-start(s32[4]{0:T(128)} %shift_ref.1) | copy-start | bytes 52
  44.6 0.7 %copy-start.1 = (f32[4]{0:T(128)S(1)}, f32[4]{0:T(128)}, u32[]{:S(2)}) copy-start(f32[4]{0:T(128)} %weight_ref.1) | copy-start | bytes 52

commit v10 on v9

--- a/solution.py
+++ b/solution.py
@@ -174,14 +174,6 @@
         place(refs[slots : 2 * slots])
 
 
-def join_kernel(*refs):
-    out_ref = refs[-1]
-    start = 0
-    for part in refs[:-1]:
-        out_ref[start : start + part.shape[0]] = part[...]
-        start += part.shape[0]
-
-
 def by_energy_kernel(momentum, layers, order, *refs):
     here = lax.axis_index("len")
     parts, out_ref = refs[:-1], refs[-1]
@@ -359,9 +351,6 @@
         kernel = functools.partial(by_energy_kernel, momentum, layers, sum(chunks, []))
         return call(kernel, local_e, *parts, name="by_energy")
 
-    def join(parts):
-        return call(join_kernel, sum(p.shape[0] for p in parts), *parts, name="join")
-
     reach = -(-(total // 2) // local_e)
 
     ring = [z * moms for z in range(count)] + [z * moms + 1 for z in reversed(range(count))]
@@ -371,7 +360,7 @@
     def hop(value, role):
         return lax.ppermute(value, ("energy", "mom"), ways[role])
 
-    chunks = [[0], [layers - 1], list(range(1, layers - 1))]
+    chunks = [[0], list(range(1, layers))]
     fields = [[], []]
     hops = [[], []]
     for c in chunks:
@@ -380,8 +369,12 @@
             held, _ = lax.optimization_barrier((held, [steps[0] for steps in hops]))
         other = [lax.ppermute(v, "mom", both_ways) for v in held]
         for m in range(2):
-            fields[m].append(of_momentum(m, held, other))
-            hops[m].append(hop(fields[m][-1], m))
+            part = of_momentum(m, held, other)
+            fields[m].append(part)
+            if m == 1 and c == chunks[-1]:
+                ahead = [hop(steps[0], k) for k, steps in enumerate(hops)]
+                part, _ = lax.optimization_barrier((part, ahead))
+            hops[m].append(hop(part, m))
     zero, one = (by_energy(m, fields[m]) for m in range(2))
     smem = pl.BlockSpec(memory_space=pltpu.SMEM)
     retarded, local_lesser, table = pl.pallas_call(
@@ -410,10 +403,13 @@
 
     sums = [retarded, jnp.zeros_like(local_lesser)]
     for d in range(1, reach + 1):
-        fields = hops if d == 1 else [[hop(part, m) for part in fields[m]] for m in range(2)]
+        if d == 1:
+            fields = hops
+        elif d == 2:
+            fields = [[ahead[m]] + [hop(part, m) for part in fields[m][1:]] for m in range(2)]
+        else:
+            fields = [[hop(part, m) for part in fields[m]] for m in range(2)]
         zero, one = (by_energy(m, fields[m]) for m in range(2))
-        if d == 1:
-            fields = [[join(parts[:-1]), parts[-1]] for parts in fields]
         if d < reach:
             sums = mix([(0, d), (1, d)], [zero, one], sums)
     sums = mix([(0, reach)], [zero], sums)

time: 56.6 us -> 56.9 us (level)
  waiting for transfers between devices: 26.8 us -> 28.9 us
  starting transfers between devices: 18.3 us -> 16.5 us
    ppermute x10 -> x8, waiting for transfers between devices: 15.3 us -> 18.1 us  [hop(): return lax.ppermute(value, ('energy', 'mom'), ways[role])]
    ppermute x10 -> x8, starting transfers between devices: 9.39 us -> 7.72 us  [hop(): return lax.ppermute(value, ('energy', 'mom'), ways[role])]
    ppermute x4, waiting for transfers between devices: 1.02 us -> 0.01 us  [shards(): other = [lax.ppermute(v, 'mom', both_ways) for v in held]]
  transfers between devices with their start and end apart: 20 -> 18, of which waited for: 10 -> 11; matrix products, arithmetic and copies ran while one was open for 0% -> 0% of each run, Pallas kernels for 7% -> 7%
where the time goes in v10:
time: 56.9 us; the launch traced here: 56.7 us
  waiting for transfers between devices  28.9 us (51%)
  starting transfers between devices  16.5 us (29%)
  Pallas kernels  9.78 us (17%)
  between operations  0.8 us (1%)
  local copies, waits for them, and re-layouts  0.64 us (1%)
    ppermute x8, waiting for transfers between devices, hop(): return lax.ppermute(value, ('energy', 'mom'), ways[role])  18.1 us
    ppermute x6, waiting for transfers between devices, exchange(): return lax.ppermute(slots[i], ('len', 'mom'), pairs)  10.8 us
    ppermute x6, starting transfers between devices, exchange(): return lax.ppermute(slots[i], ('len', 'mom'), pairs)  8.23 us
    ppermute x8, starting transfers between devices, hop(): return lax.ppermute(value, ('energy', 'mom'), ways[role])  7.72 us
    pallas_call x2, Pallas kernels, inverse(): pl.pallas_call(functools.partial(inverse_kernel, total, layers, slots), o...  4.51 us
    pallas_call x1, Pallas kernels, shards(): pl.pallas_call(functools.partial(chain_kernel, layers), out_shape=[part]...  2.22 us
    pallas_call x3, Pallas kernels, mix(): pl.pallas_call(functools.partial(mix_kernel, total, items, False, last),...  1.77 us
  transfers between devices with their start and end apart: 18, of which 11 were waited for; matrix products, arithmetic and copies ran while one was open for 0% of the time, Pallas kernels for 7%

profile of v10, /device:TPU:0, one launch (start us, length us, event | category | flops | bytes accessed | tf_op | source)
XLA Modules:
  0.0 56.7 jit_solution(18065785752666617067)
XLA Ops:
  0.6 2.3 %inverse.3 = (f32[3,128,128]{2,1,0:T(8,128)S(1)}, f32[3,128,128]{2,1,0:T(8,128)S(1)}) custom-call(f32[2,128,128]{2,1,0:T(8,128)} %bitcast.9, f32[4,2,128,128]{3,2,1,0:T(8,128)} %bitcast.5, f32[128,128]{1,0:T(8,128)} %bitcast.11, s32[128,128]{1,0:T(8,128)} %pattern_any.3), custom_call_target="tpu_custom_call" | custom-call | flops 402653184 | bytes 262144 | tf_op jit(solution)/shard_map/inverse/pallas_call | solution.py:298
  2.9 4.0 %collective-permute-start = (f32[3,128,128]{2,1,0:T(8,128)S(1)}, f32[3,128,128]{2,1,0:T(8,128)S(1)}, u32[]{:S(2)}, u32[]{:S(2)}) collective-permute-start(f32[3,128,128]{2,1,0:T(8,128)S(1)} %get-tuple-element.24), channel_id=1, source_target_pairs={{0,24},{1,25},{8,16},{9,17},{16,8},{17,9},{24,0},{25,1},{2,26},{3,... | collective-permute-start | bytes 589832 | tf_op jit(solution)/shard_map/ppermute | solution.py:291
  6.9 0.5 collective-permute-start.1
  7.4 2.2 %inverse.2 = (f32[3,128,128]{2,1,0:T(8,128)S(1)}, f32[3,128,128]{2,1,0:T(8,128)S(1)}) custom-call(f32[2,128,128]{2,1,0:T(8,128)} %bitcast.10, f32[4,2,128,128]{3,2,1,0:T(8,128)} %bitcast.6, f32[128,128]{1,0:T(8,128)} %bitcast.12, s32[128,128]{1,0:T(8,128)} %pattern_any.3), custom_call_target="tpu_custom_call" | custom-call | flops 402653184 | bytes 262144 | tf_op jit(solution)/shard_map/inverse/pallas_call | solution.py:298
  9.6 0.2 collective-permute-start.2
  9.8 2.3 %collective-permute-done.refs_1_ = f32[3,128,128]{2,1,0:T(8,128)S(1)} collective-permute-done((f32[3,128,128]{2,1,0:T(8,128)S(1)}, f32[3,128,128]{2,1,0:T(8,128)S(1)}, u32[]{:S(2)}, u32[]{:S(2)}) %collective-permute-start) | collective-permute-done | bytes 196640 | tf_op jit(solution)/shard_map/ppermute | solution.py:291
  12.2 4.1 %collective-permute-done.1.refs_2_ = f32[3,128,128]{2,1,0:T(8,128)S(1)} collective-permute-done((f32[3,128,128]{2,1,0:T(8,128)S(1)}, f32[3,128,128]{2,1,0:T(8,128)S(1)}, u32[]{:S(2)}, u32[]{:S(2)}) %collective-permute-start.1) | collective-permute-done | bytes 196640 | tf_op jit(solution)/shard_map/ppermute | solution.py:291
  16.3 2.2 %chains.1 = (f32[1,2,128,128]{3,2,1,0:T(8,128)S(1)}, f32[1,2,128,128]{3,2,1,0:T(8,128)S(1)}, f32[1,2,128,128]{3,2,1,0:T(8,128)S(1)}, f32[1,2,128,128]{3,2,1,0:T(8,128)S(1)}) custom-call(f32[3,128,128]{2,1,0:T(8,128)S(1)} %get-tuple-element.23.refs_0_, f32[3,128,128]{2,1,0:T(8,128)S(1)} %collective-permute-done.refs_1_, ...), custom_call_target="tpu_custom_call" | custom-call | tf_op jit(solution)/shard_map/chains/pallas_call | solution.py:322
  18.5 0.1 collective-permute-start.3
  18.6 1.6 %collective-permute-start.4 = (f32[1,2,128,128]{3,2,1,0:T(8,128)S(1)}, f32[1,2,128,128]{3,2,1,0:T(8,128)S(1)}, u32[]{:S(2)}, u32[]{:S(2)}) collective-permute-start(f32[1,2,128,128]{3,2,1,0:T(8,128)S(1)} %get-tuple-element.28), channel_id=1, source_target_pairs={{0,24},{1,25},{8,16},{9,17},{16,8},{17,9},{24,0},{25,1},{2,26},{3,... | collective-permute-start | bytes 393224 | tf_op jit(solution)/shard_map/ppermute | solution.py:291
  20.2 1.4 %collective-permute-start.5 = (f32[1,2,128,128]{3,2,1,0:T(8,128)S(1)}, f32[1,2,128,128]{3,2,1,0:T(8,128)S(1)}, u32[]{:S(2)}, u32[]{:S(2)}) collective-permute-start(f32[1,2,128,128]{3,2,1,0:T(8,128)S(1)} %get-tuple-element.29), channel_id=1, source_target_pairs={{0,8},{1,17},{8,0},{9,25},{16,24},{17,1},{24,16},{25,9},{2,10},{3,... | collective-permute-start | bytes 393224 | tf_op jit(solution)/shard_map/ppermute | solution.py:291
  21.5 0.6 %collective-permute-start.6 = (f32[1,2,128,128]{3,2,1,0:T(8,128)S(1)}, f32[1,2,128,128]{3,2,1,0:T(8,128)S(1)}, u32[]{:S(2)}, u32[]{:S(2)}) collective-permute-start(f32[1,2,128,128]{3,2,1,0:T(8,128)S(1)} %get-tuple-element.30), channel_id=1, source_target_pairs={{0,16},{1,9},{8,24},{9,1},{16,0},{17,25},{24,8},{25,17},{2,18},{3,... | collective-permute-start | bytes 393224 | tf_op jit(solution)/shard_map/ppermute | solution.py:291
  22.2 1.6 %collective-permute-start.7 = (f32[1,2,128,128]{3,2,1,0:T(8,128)S(1)}, f32[1,2,128,128]{3,2,1,0:T(8,128)S(1)}, u32[]{:S(2)}, u32[]{:S(2)}) collective-permute-start(f32[1,2,128,128]{3,2,1,0:T(8,128)S(1)} %momentum.4.refs_0_), channel_id=1, source_target_pairs={{0,2},{2,4},{4,6},{6,7},{7,5},{5,3},{3,1},{1,0},{8,10},{10,12},{12... | collective-permute-start | bytes 393224 | tf_op jit(solution)/shard_map/ppermute | solution.py:361
  23.8 0.0 collective-permute-start.8
  23.8 2.1 %collective-permute-done.4.refs_0_ = f32[1,2,128,128]{3,2,1,0:T(8,128)S(1)} collective-permute-done((f32[1,2,128,128]{3,2,1,0:T(8,128)S(1)}, f32[1,2,128,128]{3,2,1,0:T(8,128)S(1)}, u32[]{:S(2)}, u32[]{:S(2)}) %collective-permute-start.4) | collective-permute-done | bytes 131104 | tf_op jit(solution)/shard_map/ppermute | solution.py:291
  25.9 2.3 %collective-permute-done.5.refs_1_ = f32[1,2,128,128]{3,2,1,0:T(8,128)S(1)} collective-permute-done((f32[1,2,128,128]{3,2,1,0:T(8,128)S(1)}, f32[1,2,128,128]{3,2,1,0:T(8,128)S(1)}, u32[]{:S(2)}, u32[]{:S(2)}) %collective-permute-start.5) | collective-permute-done | bytes 131104 | tf_op jit(solution)/shard_map/ppermute | solution.py:291
  28.2 0.5 collective-permute-done.8.refs_0_
  28.8 0.5 collective-permute-start.10
  29.3 1.6 %collective-permute-start.13 = (f32[1,2,128,128]{3,2,1,0:T(8,128)S(1)}, f32[1,2,128,128]{3,2,1,0:T(8,128)S(1)}, u32[]{:S(2)}, u32[]{:S(2)}) collective-permute-start(f32[1,2,128,128]{3,2,1,0:T(8,128)S(1)} %collective-permute-done.7.refs_0_), channel_id=1, source_target_pairs={{0,2},{2,4},{4,6},{6,7},{7,5},{5,3},{3,1},{1,0},{8,10},{10,12},{12... | collective-permute-start | bytes 393224 | tf_op jit(solution)/shard_map/ppermute | solution.py:361
  30.9 2.0 %collective-permute-start.16 = (f32[3,2,128,128]{3,2,1,0:T(8,128)S(1)}, f32[3,2,128,128]{3,2,1,0:T(8,128)S(1)}, u32[]{:S(2)}, u32[]{:S(2)}) collective-permute-start(f32[3,2,128,128]{3,2,1,0:T(8,128)S(1)} %momentum.6.refs_1_), channel_id=1, source_target_pairs={{0,2},{2,4},{4,6},{6,7},{7,5},{5,3},{3,1},{1,0},{8,10},{10,12},{12... | collective-permute-start | bytes 1179656 | tf_op jit(solution)/shard_map/ppermute | solution.py:361
  33.0 1.5 %collective-permute-done.13.refs_0_ = f32[1,2,128,128]{3,2,1,0:T(8,128)S(1)} collective-permute-done((f32[1,2,128,128]{3,2,1,0:T(8,128)S(1)}, f32[1,2,128,128]{3,2,1,0:T(8,128)S(1)}, u32[]{:S(2)}, u32[]{:S(2)}) %collective-permute-start.13) | collective-permute-done | bytes 131104 | tf_op jit(solution)/shard_map/ppermute | solution.py:361
  34.4 2.7 %collective-permute-done.12.refs_0_ = f32[1,2,128,128]{3,2,1,0:T(8,128)S(1)} collective-permute-done((f32[1,2,128,128]{3,2,1,0:T(8,128)S(1)}, f32[1,2,128,128]{3,2,1,0:T(8,128)S(1)}, u32[]{:S(2)}, u32[]{:S(2)}) %collective-permute-start.12) | collective-permute-done | bytes 131104 | tf_op jit(solution)/shard_map/ppermute | solution.py:361
  37.1 3.2 %collective-permute-done.16.refs_1_ = f32[3,2,128,128]{3,2,1,0:T(8,128)S(1)} collective-permute-done((f32[3,2,128,128]{3,2,1,0:T(8,128)S(1)}, f32[3,2,128,128]{3,2,1,0:T(8,128)S(1)}, u32[]{:S(2)}, u32[]{:S(2)}) %collective-permute-start.16) | collective-permute-done | bytes 393248 | tf_op jit(solution)/shard_map/ppermute | solution.py:361
  40.4 2.5 %collective-permute-start.17 = (f32[3,2,128,128]{3,2,1,0:T(8,128)S(1)}, f32[3,2,128,128]{3,2,1,0:T(8,128)S(1)}, u32[]{:S(2)}, u32[]{:S(2)}) collective-permute-start(f32[3,2,128,128]{3,2,1,0:T(8,128)S(1)} %collective-permute-done.16.refs_1_), channel_id=1, source_target_pairs={{0,2},{2,4},{4,6},{6,7},{7,5},{5,3},{3,1},{1,0},{8,10},{10,12},{12... | collective-permute-start | bytes 1179656 | tf_op jit(solution)/shard_map/ppermute | solution.py:361
  42.9 4.8 %collective-permute-done.14.refs_1_ = f32[3,2,128,128]{3,2,1,0:T(8,128)S(1)} collective-permute-done((f32[3,2,128,128]{3,2,1,0:T(8,128)S(1)}, f32[3,2,128,128]{3,2,1,0:T(8,128)S(1)}, u32[]{:S(2)}, u32[]{:S(2)}) %collective-permute-start.14) | collective-permute-done | bytes 393248 | tf_op jit(solution)/shard_map/ppermute | solution.py:361
  47.8 0.6 %copy-done = s32[4]{0:T(128)S(1)} copy-done((s32[4]{0:T(128)S(1)}, s32[4]{0:T(128)}, u32[]{:S(2)}) %copy-start) | copy-done | bytes 40
  48.4 0.0 copy-done.1
  48.4 0.9 %local.1 = (f32[4,2,128,128]{3,2,1,0:T(8,128)S(1)}, f32[4,2,128,128]{3,2,1,0:T(8,128)S(1)}, f32[16,128]{1,0:T(8,128)S(1)}) custom-call(s32[4]{0:T(128)S(1)} %copy-done, f32[4]{0:T(128)S(1)} %copy-done.1, f32[4,2,128,128]{3,2,1,0:T(8,128)S(1)} %by_energy.6.zero_ref, f32[4,2,128,128]{3,2,1,0:T(8,128)S(1)} %by_energy.7.one_ref), custom_call_target="tpu_custom_call" | custom-call | tf_op jit(solution)/shard_map/local/pallas_call | solution.py:380
  49.5 0.6 %mix.3 = (f32[4,2,128,128]{3,2,1,0:T(8,128)S(1)}, f32[4,2,128,128]{3,2,1,0:T(8,128)S(1)}) custom-call(f32[16,128]{1,0:T(8,128)S(1)} %get-tuple-element.34.table_ref, f32[4,2,128,128]{3,2,1,0:T(8,128)S(1)} %by_energy.10.refs_0_, f32[4,2,128,128]{3,2,1,0:T(8,128)S(1)} %by_energy.11.refs_1_, f32[4,2,128,128]{3,2,1,0:T(8,128)S(1)} %get-tuple-element.36.refs_2_, ...), custom_call_target="tpu_custom_call" | custom-call | tf_op jit(solution)/shard_map/mix/pallas_call | solution.py:393
  50.1 0.6 %collective-permute-done.17.refs_1_ = f32[3,2,128,128]{3,2,1,0:T(8,128)S(1)} collective-permute-done((f32[3,2,128,128]{3,2,1,0:T(8,128)S(1)}, f32[3,2,128,128]{3,2,1,0:T(8,128)S(1)}, u32[]{:S(2)}, u32[]{:S(2)}) %collective-permute-start.17) | collective-permute-done | bytes 393248 | tf_op jit(solution)/shard_map/ppermute | solution.py:361
  50.8 4.7 %collective-permute-done.15.refs_1_ = f32[3,2,128,128]{3,2,1,0:T(8,128)S(1)} collective-permute-done((f32[3,2,128,128]{3,2,1,0:T(8,128)S(1)}, f32[3,2,128,128]{3,2,1,0:T(8,128)S(1)}, u32[]{:S(2)}, u32[]{:S(2)}) %collective-permute-start.15) | collective-permute-done | bytes 393248 | tf_op jit(solution)/shard_map/ppermute | solution.py:361
  55.5 1.2 %mix.5 = (f32[4,2,128,128]{3,2,1,0:T(8,128)}, f32[4,2,128,128]{3,2,1,0:T(8,128)}) custom-call(f32[16,128]{1,0:T(8,128)S(1)} %get-tuple-element.34.table_ref, f32[4,2,128,128]{3,2,1,0:T(8,128)S(1)} %by_energy.8.refs_0_, f32[4,2,128,128]{3,2,1,0:T(8,128)S(1)} %get-tuple-element.39.refs_1_, f32[4,2,128,128]{3,2,1,0:T(8,128)S(1)} %get-tuple-element.40.refs_2_, ...), custom_call_target="tpu_custom_call" | custom-call | tf_op jit(solution)/shard_map/mix/pallas_call | solution.py:393
  (26 shorter events, 0.5 us)
Async XLA Ops:
  2.9 9.3 %collective-permute-start = (f32[3,128,128]{2,1,0:T(8,128)S(1)}, f32[3,128,128]{2,1,0:T(8,128)S(1)}, u32[]{:S(2)}, u32[]{:S(2)}) collective-permute-start(f32[3,128,128]{2,1,0:T(8,128)S(1)} %get-tuple-element.24), channel_id=1, source_target_pairs={{0,24},{1,25},{8,16},{9,17},{16,8},{17,9},{24,0},{25,1},{2,26},{3,... | collective-permute-start | bytes 589832 | tf_op jit(solution)/shard_map/ppermute | solution.py:291
  6.9 9.4 %collective-permute-start.1 = (f32[3,128,128]{2,1,0:T(8,128)S(1)}, f32[3,128,128]{2,1,0:T(8,128)S(1)}, u32[]{:S(2)}, u32[]{:S(2)}) collective-permute-start(f32[3,128,128]{2,1,0:T(8,128)S(1)} %get-tuple-element.25), channel_id=1, source_target_pairs={{0,8},{1,17},{8,0},{9,25},{16,24},{17,1},{24,16},{25,9},{2,10},{3,... | collective-permute-start | bytes 589832 | tf_op jit(solution)/shard_map/ppermute | solution.py:291
  9.6 6.6 %collective-permute-start.2 = (f32[3,128,128]{2,1,0:T(8,128)S(1)}, f32[3,128,128]{2,1,0:T(8,128)S(1)}, u32[]{:S(2)}, u32[]{:S(2)}) collective-permute-start(f32[3,128,128]{2,1,0:T(8,128)S(1)} %get-tuple-element.26), channel_id=1, source_target_pairs={{0,16},{1,9},{8,24},{9,1},{16,0},{17,25},{24,8},{25,17},{2,18},{3,... | collective-permute-start | bytes 589832 | tf_op jit(solution)/shard_map/ppermute | solution.py:291
  18.5 3.6 %collective-permute-start.3 = (f32[1,2,128,128]{3,2,1,0:T(8,128)S(1)}, f32[1,2,128,128]{3,2,1,0:T(8,128)S(1)}, u32[]{:S(2)}, u32[]{:S(2)}) collective-permute-start(f32[1,2,128,128]{3,2,1,0:T(8,128)S(1)} %get-tuple-element.27.refs_0_), channel_id=1, source_target_pairs={{0,1},{1,0},{2,3},{3,2},{4,5},{5,4},{6,7},{7,6},{8,9},{9,8},{10,11... | collective-permute-start | bytes 393224 | tf_op jit(solution)/shard_map/ppermute | solution.py:370
  18.6 7.3 %collective-permute-start.4 = (f32[1,2,128,128]{3,2,1,0:T(8,128)S(1)}, f32[1,2,128,128]{3,2,1,0:T(8,128)S(1)}, u32[]{:S(2)}, u32[]{:S(2)}) collective-permute-start(f32[1,2,128,128]{3,2,1,0:T(8,128)S(1)} %get-tuple-element.28), channel_id=1, source_target_pairs={{0,24},{1,25},{8,16},{9,17},{16,8},{17,9},{24,0},{25,1},{2,26},{3,... | collective-permute-start | bytes 393224 | tf_op jit(solution)/shard_map/ppermute | solution.py:291
  20.2 8.0 %collective-permute-start.5 = (f32[1,2,128,128]{3,2,1,0:T(8,128)S(1)}, f32[1,2,128,128]{3,2,1,0:T(8,128)S(1)}, u32[]{:S(2)}, u32[]{:S(2)}) collective-permute-start(f32[1,2,128,128]{3,2,1,0:T(8,128)S(1)} %get-tuple-element.29), channel_id=1, source_target_pairs={{0,8},{1,17},{8,0},{9,25},{16,24},{17,1},{24,16},{25,9},{2,10},{3,... | collective-permute-start | bytes 393224 | tf_op jit(solution)/shard_map/ppermute | solution.py:291
  21.5 6.7 %collective-permute-start.6 = (f32[1,2,128,128]{3,2,1,0:T(8,128)S(1)}, f32[1,2,128,128]{3,2,1,0:T(8,128)S(1)}, u32[]{:S(2)}, u32[]{:S(2)}) collective-permute-start(f32[1,2,128,128]{3,2,1,0:T(8,128)S(1)} %get-tuple-element.30), channel_id=1, source_target_pairs={{0,16},{1,9},{8,24},{9,1},{16,0},{17,25},{24,8},{25,17},{2,18},{3,... | collective-permute-start | bytes 393224 | tf_op jit(solution)/shard_map/ppermute | solution.py:291
  22.2 6.0 %collective-permute-start.7 = (f32[1,2,128,128]{3,2,1,0:T(8,128)S(1)}, f32[1,2,128,128]{3,2,1,0:T(8,128)S(1)}, u32[]{:S(2)}, u32[]{:S(2)}) collective-permute-start(f32[1,2,128,128]{3,2,1,0:T(8,128)S(1)} %momentum.4.refs_0_), channel_id=1, source_target_pairs={{0,2},{2,4},{4,6},{6,7},{7,5},{5,3},{3,1},{1,0},{8,10},{10,12},{12... | collective-permute-start | bytes 393224 | tf_op jit(solution)/shard_map/ppermute | solution.py:361
  23.8 5.0 %collective-permute-start.8 = (f32[1,2,128,128]{3,2,1,0:T(8,128)S(1)}, f32[1,2,128,128]{3,2,1,0:T(8,128)S(1)}, u32[]{:S(2)}, u32[]{:S(2)}) collective-permute-start(f32[1,2,128,128]{3,2,1,0:T(8,128)S(1)} %momentum.5.refs_0_), channel_id=1, source_target_pairs={{2,0},{4,2},{6,4},{7,6},{5,7},{3,5},{1,3},{0,1},{10,8},{12,10},{14... | collective-permute-start | bytes 393224 | tf_op jit(solution)/shard_map/ppermute | solution.py:361
  28.7 2.1 %collective-permute-start.9 = (f32[1,2,128,128]{3,2,1,0:T(8,128)S(1)}, f32[1,2,128,128]{3,2,1,0:T(8,128)S(1)}, u32[]{:S(2)}, u32[]{:S(2)}) collective-permute-start(f32[1,2,128,128]{3,2,1,0:T(8,128)S(1)} %collective-permute-done.4.refs_0_), channel_id=1, source_target_pairs={{0,1},{1,0},{2,3},{3,2},{4,5},{5,4},{6,7},{7,6},{8,9},{9,8},{10,11... | collective-permute-start | bytes 393224 | tf_op jit(solution)/shard_map/ppermute | solution.py:370
  28.8 2.1 %collective-permute-start.10 = (f32[1,2,128,128]{3,2,1,0:T(8,128)S(1)}, f32[1,2,128,128]{3,2,1,0:T(8,128)S(1)}, u32[]{:S(2)}, u32[]{:S(2)}) collective-permute-start(f32[1,2,128,128]{3,2,1,0:T(8,128)S(1)} %collective-permute-done.5.refs_1_), channel_id=1, source_target_pairs={{0,1},{1,0},{2,3},{3,2},{4,5},{5,4},{6,7},{7,6},{8,9},{9,8},{10,11... | collective-permute-start | bytes 393224 | tf_op jit(solution)/shard_map/ppermute | solution.py:370
  29.3 1.6 %collective-permute-start.11 = (f32[1,2,128,128]{3,2,1,0:T(8,128)S(1)}, f32[1,2,128,128]{3,2,1,0:T(8,128)S(1)}, u32[]{:S(2)}, u32[]{:S(2)}) collective-permute-start(f32[1,2,128,128]{3,2,1,0:T(8,128)S(1)} %collective-permute-done.6.refs_2_), channel_id=1, source_target_pairs={{0,1},{1,0},{2,3},{3,2},{4,5},{5,4},{6,7},{7,6},{8,9},{9,8},{10,11... | collective-permute-start | bytes 393224 | tf_op jit(solution)/shard_map/ppermute | solution.py:370
  29.3 5.2 %collective-permute-start.13 = (f32[1,2,128,128]{3,2,1,0:T(8,128)S(1)}, f32[1,2,128,128]{3,2,1,0:T(8,128)S(1)}, u32[]{:S(2)}, u32[]{:S(2)}) collective-permute-start(f32[1,2,128,128]{3,2,1,0:T(8,128)S(1)} %collective-permute-done.7.refs_0_), channel_id=1, source_target_pairs={{0,2},{2,4},{4,6},{6,7},{7,5},{5,3},{3,1},{1,0},{8,10},{10,12},{12... | collective-permute-start | bytes 393224 | tf_op jit(solution)/shard_map/ppermute | solution.py:361
  30.8 6.3 %collective-permute-start.12 = (f32[1,2,128,128]{3,2,1,0:T(8,128)S(1)}, f32[1,2,128,128]{3,2,1,0:T(8,128)S(1)}, u32[]{:S(2)}, u32[]{:S(2)}) collective-permute-start(f32[1,2,128,128]{3,2,1,0:T(8,128)S(1)} %collective-permute-done.8.refs_0_), channel_id=1, source_target_pairs={{2,0},{4,2},{6,4},{7,6},{5,7},{3,5},{1,3},{0,1},{10,8},{12,10},{14... | collective-permute-start | bytes 393224 | tf_op jit(solution)/shard_map/ppermute | solution.py:361
  30.9 9.5 %collective-permute-start.16 = (f32[3,2,128,128]{3,2,1,0:T(8,128)S(1)}, f32[3,2,128,128]{3,2,1,0:T(8,128)S(1)}, u32[]{:S(2)}, u32[]{:S(2)}) collective-permute-start(f32[3,2,128,128]{3,2,1,0:T(8,128)S(1)} %momentum.6.refs_1_), channel_id=1, source_target_pairs={{0,2},{2,4},{4,6},{6,7},{7,5},{5,3},{3,1},{1,0},{8,10},{10,12},{12... | collective-permute-start | bytes 1179656 | tf_op jit(solution)/shard_map/ppermute | solution.py:361
  37.1 10.6 %collective-permute-start.14 = (f32[3,2,128,128]{3,2,1,0:T(8,128)S(1)}, f32[3,2,128,128]{3,2,1,0:T(8,128)S(1)}, u32[]{:S(2)}, u32[]{:S(2)}) collective-permute-start(f32[3,2,128,128]{3,2,1,0:T(8,128)S(1)} %momentum.7.refs_1_), channel_id=1, source_target_pairs={{2,0},{4,2},{6,4},{7,6},{5,7},{3,5},{1,3},{0,1},{10,8},{12,10},{14... | collective-permute-start | bytes 1179656 | tf_op jit(solution)/shard_map/ppermute | solution.py:361
  40.4 10.3 %collective-permute-start.17 = (f32[3,2,128,128]{3,2,1,0:T(8,128)S(1)}, f32[3,2,128,128]{3,2,1,0:T(8,128)S(1)}, u32[]{:S(2)}, u32[]{:S(2)}) collective-permute-start(f32[3,2,128,128]{3,2,1,0:T(8,128)S(1)} %collective-permute-done.16.refs_1_), channel_id=1, source_target_pairs={{0,2},{2,4},{4,6},{6,7},{7,5},{5,3},{3,1},{1,0},{8,10},{10,12},{12... | collective-permute-start | bytes 1179656 | tf_op jit(solution)/shard_map/ppermute | solution.py:361
  47.7 7.8 %collective-permute-start.15 = (f32[3,2,128,128]{3,2,1,0:T(8,128)S(1)}, f32[3,2,128,128]{3,2,1,0:T(8,128)S(1)}, u32[]{:S(2)}, u32[]{:S(2)}) collective-permute-start(f32[3,2,128,128]{3,2,1,0:T(8,128)S(1)} %collective-permute-done.14.refs_1_), channel_id=1, source_target_pairs={{2,0},{4,2},{6,4},{7,6},{5,7},{3,5},{1,3},{0,1},{10,8},{12,10},{14... | collective-permute-start | bytes 1179656 | tf_op jit(solution)/shard_map/ppermute | solution.py:361
  47.8 0.7 %copy-start = (s32[4]{0:T(128)S(1)}, s32[4]{0:T(128)}, u32[]{:S(2)}) copy-start(s32[4]{0:T(128)} %shift_ref.1) | copy-start | bytes 52
  47.8 0.7 %copy-start.1 = (f32[4]{0:T(128)S(1)}, f32[4]{0:T(128)}, u32[]{:S(2)}) copy-start(f32[4]{0:T(128)} %weight_ref.1) | copy-start | bytes 52

commit v11 on v10

--- a/solution.py
+++ b/solution.py
@@ -360,21 +360,17 @@
     def hop(value, role):
         return lax.ppermute(value, ("energy", "mom"), ways[role])
 
-    chunks = [[0], list(range(1, layers))]
+    chunks = [[0], [layers - 1], list(range(1, layers - 1))]
     fields = [[], []]
     hops = [[], []]
     for c in chunks:
+        if len(hops[0]) == 1:
+            own, _ = lax.optimization_barrier((own, hops))
         held = [own[i] for i in c]
-        if hops[0]:
-            held, _ = lax.optimization_barrier((held, [steps[0] for steps in hops]))
         other = [lax.ppermute(v, "mom", both_ways) for v in held]
         for m in range(2):
-            part = of_momentum(m, held, other)
-            fields[m].append(part)
-            if m == 1 and c == chunks[-1]:
-                ahead = [hop(steps[0], k) for k, steps in enumerate(hops)]
-                part, _ = lax.optimization_barrier((part, ahead))
-            hops[m].append(hop(part, m))
+            fields[m].append(of_momentum(m, held, other))
+            hops[m].append(hop(fields[m][-1], m))
     zero, one = (by_energy(m, fields[m]) for m in range(2))
     smem = pl.BlockSpec(memory_space=pltpu.SMEM)
     retarded, local_lesser, table = pl.pallas_call(
@@ -406,7 +402,10 @@
         if d == 1:
             fields = hops
         elif d == 2:
-            fields = [[ahead[m]] + [hop(part, m) for part in fields[m][1:]] for m in range(2)]
+            ahead = [hop(fields[m][0], m) for m in range(2)]
+            held = [lax.optimization_barrier((fields[m][1], ahead[m]))[0] for m in range(2)]
+            big, _ = lax.optimization_barrier((fields[0][2], fields[1][1]))
+            fields = [[ahead[m], hop(held[m], m), hop([big, fields[1][2]][m], m)] for m in range(2)]
         else:
             fields = [[hop(part, m) for part in fields[m]] for m in range(2)]
         zero, one = (by_energy(m, fields[m]) for m in range(2))

time: 56.9 us -> 56.2 us (0.988)
  waiting for transfers between devices: 28.9 us -> 25 us
  starting transfers between devices: 16.5 us -> 19.7 us
    ppermute x8 -> x12, waiting for transfers between devices: 18.1 us -> 13.2 us  [hop(): return lax.ppermute(value, ('energy', 'mom'), ways[role])]
    ppermute x8 -> x12, starting transfers between devices: 7.72 us -> 10.9 us  [hop(): return lax.ppermute(value, ('energy', 'mom'), ways[role])]
    ppermute x4, waiting for transfers between devices: 0.01 us -> 1.03 us  [shards(): other = [lax.ppermute(v, 'mom', both_ways) for v in held]]
  transfers between devices with their start and end apart: 18 -> 22, of which waited for: 11 -> 11; matrix products, arithmetic and copies ran while one was open for 0% -> 0% of each run, Pallas kernels for 7% -> 7%
where the time goes in v11:
time: 56.2 us; the launch traced here: 56 us
  waiting for transfers between devices  25 us (44%)
  starting transfers between devices  19.7 us (35%)
  Pallas kernels  9.78 us (17%)
  between operations  0.85 us (2%)
  local copies, waits for them, and re-layouts  0.64 us (1%)
    ppermute x12, waiting for transfers between devices, hop(): return lax.ppermute(value, ('energy', 'mom'), ways[role])  13.2 us
    ppermute x12, starting transfers between devices, hop(): return lax.ppermute(value, ('energy', 'mom'), ways[role])  10.9 us
    ppermute x6, waiting for transfers between devices, exchange(): return lax.ppermute(slots[i], ('len', 'mom'), pairs)  10.8 us
    ppermute x6, starting transfers between devices, exchange(): return lax.ppermute(slots[i], ('len', 'mom'), pairs)  8.23 us
    pallas_call x2, Pallas kernels, inverse(): pl.pallas_call(functools.partial(inverse_kernel, total, layers, slots), o...  4.51 us
    pallas_call x1, Pallas kernels, shards(): pl.pallas_call(functools.partial(chain_kernel, layers), out_shape=[part]...  2.22 us
    pallas_call x3, Pallas kernels, mix(): pl.pallas_call(functools.partial(mix_kernel, total, items, False, last),...  1.77 us
  transfers between devices with their start and end apart: 22, of which 11 were waited for; matrix products, arithmetic and copies ran while one was open for 0% of the time, Pallas kernels for 7%

profile of v11, /device:TPU:0, one launch (start us, length us, event | category | flops | bytes accessed | tf_op | source)
XLA Modules:
  0.0 56.0 jit_solution(8022293486153041103)
XLA Ops:
  0.6 2.3 %inverse.3 = (f32[3,128,128]{2,1,0:T(8,128)S(1)}, f32[3,128,128]{2,1,0:T(8,128)S(1)}) custom-call(f32[2,128,128]{2,1,0:T(8,128)} %bitcast.9, f32[4,2,128,128]{3,2,1,0:T(8,128)} %bitcast.5, f32[128,128]{1,0:T(8,128)} %bitcast.11, s32[128,128]{1,0:T(8,128)} %pattern_any.3), custom_call_target="tpu_custom_call" | custom-call | flops 402653184 | bytes 262144 | tf_op jit(solution)/shard_map/inverse/pallas_call | solution.py:298
  2.9 4.0 %collective-permute-start = (f32[3,128,128]{2,1,0:T(8,128)S(1)}, f32[3,128,128]{2,1,0:T(8,128)S(1)}, u32[]{:S(2)}, u32[]{:S(2)}) collective-permute-start(f32[3,128,128]{2,1,0:T(8,128)S(1)} %get-tuple-element.26), channel_id=1, source_target_pairs={{0,24},{1,25},{8,16},{9,17},{16,8},{17,9},{24,0},{25,1},{2,26},{3,... | collective-permute-start | bytes 589832 | tf_op jit(solution)/shard_map/ppermute | solution.py:291
  6.9 0.5 collective-permute-start.1
  7.4 2.2 %inverse.2 = (f32[3,128,128]{2,1,0:T(8,128)S(1)}, f32[3,128,128]{2,1,0:T(8,128)S(1)}) custom-call(f32[2,128,128]{2,1,0:T(8,128)} %bitcast.10, f32[4,2,128,128]{3,2,1,0:T(8,128)} %bitcast.6, f32[128,128]{1,0:T(8,128)} %bitcast.12, s32[128,128]{1,0:T(8,128)} %pattern_any.3), custom_call_target="tpu_custom_call" | custom-call | flops 402653184 | bytes 262144 | tf_op jit(solution)/shard_map/inverse/pallas_call | solution.py:298
  9.6 0.2 collective-permute-start.2
  9.8 2.3 %collective-permute-done.refs_1_ = f32[3,128,128]{2,1,0:T(8,128)S(1)} collective-permute-done((f32[3,128,128]{2,1,0:T(8,128)S(1)}, f32[3,128,128]{2,1,0:T(8,128)S(1)}, u32[]{:S(2)}, u32[]{:S(2)}) %collective-permute-start) | collective-permute-done | bytes 196640 | tf_op jit(solution)/shard_map/ppermute | solution.py:291
  12.2 4.1 %collective-permute-done.1.refs_2_ = f32[3,128,128]{2,1,0:T(8,128)S(1)} collective-permute-done((f32[3,128,128]{2,1,0:T(8,128)S(1)}, f32[3,128,128]{2,1,0:T(8,128)S(1)}, u32[]{:S(2)}, u32[]{:S(2)}) %collective-permute-start.1) | collective-permute-done | bytes 196640 | tf_op jit(solution)/shard_map/ppermute | solution.py:291
  16.3 2.2 %chains.1 = (f32[1,2,128,128]{3,2,1,0:T(8,128)S(1)}, f32[1,2,128,128]{3,2,1,0:T(8,128)S(1)}, f32[1,2,128,128]{3,2,1,0:T(8,128)S(1)}, f32[1,2,128,128]{3,2,1,0:T(8,128)S(1)}) custom-call(f32[3,128,128]{2,1,0:T(8,128)S(1)} %get-tuple-element.25.refs_0_, f32[3,128,128]{2,1,0:T(8,128)S(1)} %collective-permute-done.refs_1_, ...), custom_call_target="tpu_custom_call" | custom-call | tf_op jit(solution)/shard_map/chains/pallas_call | solution.py:322
  18.6 1.6 %collective-permute-start.4 = (f32[1,2,128,128]{3,2,1,0:T(8,128)S(1)}, f32[1,2,128,128]{3,2,1,0:T(8,128)S(1)}, u32[]{:S(2)}, u32[]{:S(2)}) collective-permute-start(f32[1,2,128,128]{3,2,1,0:T(8,128)S(1)} %get-tuple-element.30), channel_id=1, source_target_pairs={{0,24},{1,25},{8,16},{9,17},{16,8},{17,9},{24,0},{25,1},{2,26},{3,... | collective-permute-start | bytes 393224 | tf_op jit(solution)/shard_map/ppermute | solution.py:291
  20.2 1.4 %collective-permute-start.5 = (f32[1,2,128,128]{3,2,1,0:T(8,128)S(1)}, f32[1,2,128,128]{3,2,1,0:T(8,128)S(1)}, u32[]{:S(2)}, u32[]{:S(2)}) collective-permute-start(f32[1,2,128,128]{3,2,1,0:T(8,128)S(1)} %get-tuple-element.31), channel_id=1, source_target_pairs={{0,8},{1,17},{8,0},{9,25},{16,24},{17,1},{24,16},{25,9},{2,10},{3,... | collective-permute-start | bytes 393224 | tf_op jit(solution)/shard_map/ppermute | solution.py:291
  21.5 0.6 %collective-permute-start.6 = (f32[1,2,128,128]{3,2,1,0:T(8,128)S(1)}, f32[1,2,128,128]{3,2,1,0:T(8,128)S(1)}, u32[]{:S(2)}, u32[]{:S(2)}) collective-permute-start(f32[1,2,128,128]{3,2,1,0:T(8,128)S(1)} %get-tuple-element.32), channel_id=1, source_target_pairs={{0,16},{1,9},{8,24},{9,1},{16,0},{17,25},{24,8},{25,17},{2,18},{3,... | collective-permute-start | bytes 393224 | tf_op jit(solution)/shard_map/ppermute | solution.py:291
  22.2 1.6 %collective-permute-start.7 = (f32[1,2,128,128]{3,2,1,0:T(8,128)S(1)}, f32[1,2,128,128]{3,2,1,0:T(8,128)S(1)}, u32[]{:S(2)}, u32[]{:S(2)}) collective-permute-start(f32[1,2,128,128]{3,2,1,0:T(8,128)S(1)} %momentum.6.refs_0_), channel_id=1, source_target_pairs={{0,2},{2,4},{4,6},{6,7},{7,5},{5,3},{3,1},{1,0},{8,10},{10,12},{12... | collective-permute-start | bytes 393224 | tf_op jit(solution)/shard_map/ppermute | solution.py:361
  23.8 2.1 %collective-permute-done.4.refs_0_ = f32[1,2,128,128]{3,2,1,0:T(8,128)S(1)} collective-permute-done((f32[1,2,128,128]{3,2,1,0:T(8,128)S(1)}, f32[1,2,128,128]{3,2,1,0:T(8,128)S(1)}, u32[]{:S(2)}, u32[]{:S(2)}) %collective-permute-start.4) | collective-permute-done | bytes 131104 | tf_op jit(solution)/shard_map/ppermute | solution.py:291
  25.9 2.3 %collective-permute-done.5.refs_1_ = f32[1,2,128,128]{3,2,1,0:T(8,128)S(1)} collective-permute-done((f32[1,2,128,128]{3,2,1,0:T(8,128)S(1)}, f32[1,2,128,128]{3,2,1,0:T(8,128)S(1)}, u32[]{:S(2)}, u32[]{:S(2)}) %collective-permute-start.5) | collective-permute-done | bytes 131104 | tf_op jit(solution)/shard_map/ppermute | solution.py:291
  28.2 0.5 collective-permute-done.8.refs_0_
  28.8 0.5 collective-permute-start.11
  29.3 0.8 %collective-permute-done.10.refs_2_ = f32[1,2,128,128]{3,2,1,0:T(8,128)S(1)} collective-permute-done((f32[1,2,128,128]{3,2,1,0:T(8,128)S(1)}, f32[1,2,128,128]{3,2,1,0:T(8,128)S(1)}, u32[]{:S(2)}, u32[]{:S(2)}) %collective-permute-start.10) | collective-permute-done | bytes 131104 | tf_op jit(solution)/shard_map/ppermute | solution.py:370
  30.1 0.2 collective-permute-done.11.refs_3_
  30.3 1.6 %collective-permute-start.20 = (f32[2,2,128,128]{3,2,1,0:T(8,128)S(1)}, f32[2,2,128,128]{3,2,1,0:T(8,128)S(1)}, u32[]{:S(2)}, u32[]{:S(2)}) collective-permute-start(f32[2,2,128,128]{3,2,1,0:T(8,128)S(1)} %momentum.9.refs_2_), channel_id=1, source_target_pairs={{0,2},{2,4},{4,6},{6,7},{7,5},{5,3},{3,1},{1,0},{8,10},{10,12},{12... | collective-permute-start | bytes 786440 | tf_op jit(solution)/shard_map/ppermute | solution.py:361
  32.0 0.2 collective-permute-start.13
  32.2 1.8 %collective-permute-start.17 = (f32[1,2,128,128]{3,2,1,0:T(8,128)S(1)}, f32[1,2,128,128]{3,2,1,0:T(8,128)S(1)}, u32[]{:S(2)}, u32[]{:S(2)}) collective-permute-start(f32[1,2,128,128]{3,2,1,0:T(8,128)S(1)} %collective-permute-done.7.refs_0_), channel_id=1, source_target_pairs={{0,2},{2,4},{4,6},{6,7},{7,5},{5,3},{3,1},{1,0},{8,10},{10,12},{12... | collective-permute-start | bytes 393224 | tf_op jit(solution)/shard_map/ppermute | solution.py:361
  34.1 2.0 %collective-permute-start.18 = (f32[1,2,128,128]{3,2,1,0:T(8,128)S(1)}, f32[1,2,128,128]{3,2,1,0:T(8,128)S(1)}, u32[]{:S(2)}, u32[]{:S(2)}) collective-permute-start(f32[1,2,128,128]{3,2,1,0:T(8,128)S(1)} %momentum.8.refs_1_), channel_id=1, source_target_pairs={{0,2},{2,4},{4,6},{6,7},{7,5},{5,3},{3,1},{1,0},{8,10},{10,12},{12... | collective-permute-start | bytes 393224 | tf_op jit(solution)/shard_map/ppermute | solution.py:361
  36.1 7.0 %collective-permute-done.13.refs_1_ = f32[1,2,128,128]{3,2,1,0:T(8,128)S(1)} collective-permute-done((f32[1,2,128,128]{3,2,1,0:T(8,128)S(1)}, f32[1,2,128,128]{3,2,1,0:T(8,128)S(1)}, u32[]{:S(2)}, u32[]{:S(2)}) %collective-permute-start.13) | collective-permute-done | bytes 131104 | tf_op jit(solution)/shard_map/ppermute | solution.py:361
  43.1 1.6 %collective-permute-start.21 = (f32[2,2,128,128]{3,2,1,0:T(8,128)S(1)}, f32[2,2,128,128]{3,2,1,0:T(8,128)S(1)}, u32[]{:S(2)}, u32[]{:S(2)}) collective-permute-start(f32[2,2,128,128]{3,2,1,0:T(8,128)S(1)} %collective-permute-done.20.refs_2_), channel_id=1, source_target_pairs={{0,2},{2,4},{4,6},{6,7},{7,5},{5,3},{3,1},{1,0},{8,10},{10,12},{12... | collective-permute-start | bytes 786440 | tf_op jit(solution)/shard_map/ppermute | solution.py:361
  44.7 2.0 %collective-permute-start.19 = (f32[1,2,128,128]{3,2,1,0:T(8,128)S(1)}, f32[1,2,128,128]{3,2,1,0:T(8,128)S(1)}, u32[]{:S(2)}, u32[]{:S(2)}) collective-permute-start(f32[1,2,128,128]{3,2,1,0:T(8,128)S(1)} %collective-permute-done.18.refs_1_), channel_id=1, source_target_pairs={{0,2},{2,4},{4,6},{6,7},{7,5},{5,3},{3,1},{1,0},{8,10},{10,12},{12... | collective-permute-start | bytes 393224 | tf_op jit(solution)/shard_map/ppermute | solution.py:361
  46.7 3.1 %collective-permute-done.12.refs_0_ = f32[1,2,128,128]{3,2,1,0:T(8,128)S(1)} collective-permute-done((f32[1,2,128,128]{3,2,1,0:T(8,128)S(1)}, f32[1,2,128,128]{3,2,1,0:T(8,128)S(1)}, u32[]{:S(2)}, u32[]{:S(2)}) %collective-permute-start.12) | collective-permute-done | bytes 131104 | tf_op jit(solution)/shard_map/ppermute | solution.py:361
  50.0 0.6 %copy-done = s32[4]{0:T(128)S(1)} copy-done((s32[4]{0:T(128)S(1)}, s32[4]{0:T(128)}, u32[]{:S(2)}) %copy-start) | copy-done | bytes 40
  50.6 0.9 %local.1 = (f32[4,2,128,128]{3,2,1,0:T(8,128)S(1)}, f32[4,2,128,128]{3,2,1,0:T(8,128)S(1)}, f32[16,128]{1,0:T(8,128)S(1)}) custom-call(s32[4]{0:T(128)S(1)} %copy-done, f32[4]{0:T(128)S(1)} %copy-done.1, f32[4,2,128,128]{3,2,1,0:T(8,128)S(1)} %by_energy.6.zero_ref, f32[4,2,128,128]{3,2,1,0:T(8,128)S(1)} %by_energy.7.one_ref), custom_call_target="tpu_custom_call" | custom-call | tf_op jit(solution)/shard_map/local/pallas_call | solution.py:376
  51.6 0.6 %mix.3 = (f32[4,2,128,128]{3,2,1,0:T(8,128)S(1)}, f32[4,2,128,128]{3,2,1,0:T(8,128)S(1)}) custom-call(f32[16,128]{1,0:T(8,128)S(1)} %get-tuple-element.36.table_ref, f32[4,2,128,128]{3,2,1,0:T(8,128)S(1)} %by_energy.10.refs_0_, f32[4,2,128,128]{3,2,1,0:T(8,128)S(1)} %by_energy.11.refs_1_, f32[4,2,128,128]{3,2,1,0:T(8,128)S(1)} %get-tuple-element.40.refs_2_, ...), custom_call_target="tpu_custom_call" | custom-call | tf_op jit(solution)/shard_map/mix/pallas_call | solution.py:389
  52.2 1.6 %collective-permute-done.19.refs_1_ = f32[1,2,128,128]{3,2,1,0:T(8,128)S(1)} collective-permute-done((f32[1,2,128,128]{3,2,1,0:T(8,128)S(1)}, f32[1,2,128,128]{3,2,1,0:T(8,128)S(1)}, u32[]{:S(2)}, u32[]{:S(2)}) %collective-permute-start.19) | collective-permute-done | bytes 131104 | tf_op jit(solution)/shard_map/ppermute | solution.py:361
  53.9 0.9 %collective-permute-done.14.refs_1_ = f32[1,2,128,128]{3,2,1,0:T(8,128)S(1)} collective-permute-done((f32[1,2,128,128]{3,2,1,0:T(8,128)S(1)}, f32[1,2,128,128]{3,2,1,0:T(8,128)S(1)}, u32[]{:S(2)}, u32[]{:S(2)}) %collective-permute-start.14) | collective-permute-done | bytes 131104 | tf_op jit(solution)/shard_map/ppermute | solution.py:361
  54.9 1.2 %mix.5 = (f32[4,2,128,128]{3,2,1,0:T(8,128)}, f32[4,2,128,128]{3,2,1,0:T(8,128)}) custom-call(f32[16,128]{1,0:T(8,128)S(1)} %get-tuple-element.36.table_ref, f32[4,2,128,128]{3,2,1,0:T(8,128)S(1)} %by_energy.8.refs_0_, f32[4,2,128,128]{3,2,1,0:T(8,128)S(1)} %get-tuple-element.43.refs_1_, f32[4,2,128,128]{3,2,1,0:T(8,128)S(1)} %get-tuple-element.44.refs_2_, ...), custom_call_target="tpu_custom_call" | custom-call | tf_op jit(solution)/shard_map/mix/pallas_call | solution.py:389
  (36 shorter events, 0.6 us)
Async XLA Ops:
  2.9 9.3 %collective-permute-start = (f32[3,128,128]{2,1,0:T(8,128)S(1)}, f32[3,128,128]{2,1,0:T(8,128)S(1)}, u32[]{:S(2)}, u32[]{:S(2)}) collective-permute-start(f32[3,128,128]{2,1,0:T(8,128)S(1)} %get-tuple-element.26), channel_id=1, source_target_pairs={{0,24},{1,25},{8,16},{9,17},{16,8},{17,9},{24,0},{25,1},{2,26},{3,... | collective-permute-start | bytes 589832 | tf_op jit(solution)/shard_map/ppermute | solution.py:291
  6.9 9.4 %collective-permute-start.1 = (f32[3,128,128]{2,1,0:T(8,128)S(1)}, f32[3,128,128]{2,1,0:T(8,128)S(1)}, u32[]{:S(2)}, u32[]{:S(2)}) collective-permute-start(f32[3,128,128]{2,1,0:T(8,128)S(1)} %get-tuple-element.27), channel_id=1, source_target_pairs={{0,8},{1,17},{8,0},{9,25},{16,24},{17,1},{24,16},{25,9},{2,10},{3,... | collective-permute-start | bytes 589832 | tf_op jit(solution)/shard_map/ppermute | solution.py:291
  9.6 6.6 %collective-permute-start.2 = (f32[3,128,128]{2,1,0:T(8,128)S(1)}, f32[3,128,128]{2,1,0:T(8,128)S(1)}, u32[]{:S(2)}, u32[]{:S(2)}) collective-permute-start(f32[3,128,128]{2,1,0:T(8,128)S(1)} %get-tuple-element.28), channel_id=1, source_target_pairs={{0,16},{1,9},{8,24},{9,1},{16,0},{17,25},{24,8},{25,17},{2,18},{3,... | collective-permute-start | bytes 589832 | tf_op jit(solution)/shard_map/ppermute | solution.py:291
  18.5 3.6 %collective-permute-start.3 = (f32[1,2,128,128]{3,2,1,0:T(8,128)S(1)}, f32[1,2,128,128]{3,2,1,0:T(8,128)S(1)}, u32[]{:S(2)}, u32[]{:S(2)}) collective-permute-start(f32[1,2,128,128]{3,2,1,0:T(8,128)S(1)} %get-tuple-element.29.refs_0_), channel_id=1, source_target_pairs={{0,1},{1,0},{2,3},{3,2},{4,5},{5,4},{6,7},{7,6},{8,9},{9,8},{10,11... | collective-permute-start | bytes 393224 | tf_op jit(solution)/shard_map/ppermute | solution.py:370
  18.6 7.3 %collective-permute-start.4 = (f32[1,2,128,128]{3,2,1,0:T(8,128)S(1)}, f32[1,2,128,128]{3,2,1,0:T(8,128)S(1)}, u32[]{:S(2)}, u32[]{:S(2)}) collective-permute-start(f32[1,2,128,128]{3,2,1,0:T(8,128)S(1)} %get-tuple-element.30), channel_id=1, source_target_pairs={{0,24},{1,25},{8,16},{9,17},{16,8},{17,9},{24,0},{25,1},{2,26},{3,... | collective-permute-start | bytes 393224 | tf_op jit(solution)/shard_map/ppermute | solution.py:291
  20.2 8.0 %collective-permute-start.5 = (f32[1,2,128,128]{3,2,1,0:T(8,128)S(1)}, f32[1,2,128,128]{3,2,1,0:T(8,128)S(1)}, u32[]{:S(2)}, u32[]{:S(2)}) collective-permute-start(f32[1,2,128,128]{3,2,1,0:T(8,128)S(1)} %get-tuple-element.31), channel_id=1, source_target_pairs={{0,8},{1,17},{8,0},{9,25},{16,24},{17,1},{24,16},{25,9},{2,10},{3,... | collective-permute-start | bytes 393224 | tf_op jit(solution)/shard_map/ppermute | solution.py:291
  21.5 6.7 %collective-permute-start.6 = (f32[1,2,128,128]{3,2,1,0:T(8,128)S(1)}, f32[1,2,128,128]{3,2,1,0:T(8,128)S(1)}, u32[]{:S(2)}, u32[]{:S(2)}) collective-permute-start(f32[1,2,128,128]{3,2,1,0:T(8,128)S(1)} %get-tuple-element.32), channel_id=1, source_target_pairs={{0,16},{1,9},{8,24},{9,1},{16,0},{17,25},{24,8},{25,17},{2,18},{3,... | collective-permute-start | bytes 393224 | tf_op jit(solution)/shard_map/ppermute | solution.py:291
  22.2 6.0 %collective-permute-start.7 = (f32[1,2,128,128]{3,2,1,0:T(8,128)S(1)}, f32[1,2,128,128]{3,2,1,0:T(8,128)S(1)}, u32[]{:S(2)}, u32[]{:S(2)}) collective-permute-start(f32[1,2,128,128]{3,2,1,0:T(8,128)S(1)} %momentum.6.refs_0_), channel_id=1, source_target_pairs={{0,2},{2,4},{4,6},{6,7},{7,5},{5,3},{3,1},{1,0},{8,10},{10,12},{12... | collective-permute-start | bytes 393224 | tf_op jit(solution)/shard_map/ppermute | solution.py:361
  23.8 5.0 %collective-permute-start.8 = (f32[1,2,128,128]{3,2,1,0:T(8,128)S(1)}, f32[1,2,128,128]{3,2,1,0:T(8,128)S(1)}, u32[]{:S(2)}, u32[]{:S(2)}) collective-permute-start(f32[1,2,128,128]{3,2,1,0:T(8,128)S(1)} %momentum.7.refs_0_), channel_id=1, source_target_pairs={{2,0},{4,2},{6,4},{7,6},{5,7},{3,5},{1,3},{0,1},{10,8},{12,10},{14... | collective-permute-start | bytes 393224 | tf_op jit(solution)/shard_map/ppermute | solution.py:361
  28.7 1.3 %collective-permute-start.10 = (f32[1,2,128,128]{3,2,1,0:T(8,128)S(1)}, f32[1,2,128,128]{3,2,1,0:T(8,128)S(1)}, u32[]{:S(2)}, u32[]{:S(2)}) collective-permute-start(f32[1,2,128,128]{3,2,1,0:T(8,128)S(1)} %collective-permute-done.4.refs_0_), channel_id=1, source_target_pairs={{0,1},{1,0},{2,3},{3,2},{4,5},{5,4},{6,7},{7,6},{8,9},{9,8},{10,11... | collective-permute-start | bytes 393224 | tf_op jit(solution)/shard_map/ppermute | solution.py:370
  28.8 1.5 %collective-permute-start.11 = (f32[1,2,128,128]{3,2,1,0:T(8,128)S(1)}, f32[1,2,128,128]{3,2,1,0:T(8,128)S(1)}, u32[]{:S(2)}, u32[]{:S(2)}) collective-permute-start(f32[1,2,128,128]{3,2,1,0:T(8,128)S(1)} %collective-permute-done.5.refs_1_), channel_id=1, source_target_pairs={{0,1},{1,0},{2,3},{3,2},{4,5},{5,4},{6,7},{7,6},{8,9},{9,8},{10,11... | collective-permute-start | bytes 393224 | tf_op jit(solution)/shard_map/ppermute | solution.py:370
  29.3 2.7 %collective-permute-start.9 = (f32[1,2,128,128]{3,2,1,0:T(8,128)S(1)}, f32[1,2,128,128]{3,2,1,0:T(8,128)S(1)}, u32[]{:S(2)}, u32[]{:S(2)}) collective-permute-start(f32[1,2,128,128]{3,2,1,0:T(8,128)S(1)} %collective-permute-done.6.refs_0_), channel_id=1, source_target_pairs={{0,1},{1,0},{2,3},{3,2},{4,5},{5,4},{6,7},{7,6},{8,9},{9,8},{10,11... | collective-permute-start | bytes 393224 | tf_op jit(solution)/shard_map/ppermute | solution.py:370
  30.3 12.8 %collective-permute-start.20 = (f32[2,2,128,128]{3,2,1,0:T(8,128)S(1)}, f32[2,2,128,128]{3,2,1,0:T(8,128)S(1)}, u32[]{:S(2)}, u32[]{:S(2)}) collective-permute-start(f32[2,2,128,128]{3,2,1,0:T(8,128)S(1)} %momentum.9.refs_2_), channel_id=1, source_target_pairs={{0,2},{2,4},{4,6},{6,7},{7,5},{5,3},{3,1},{1,0},{8,10},{10,12},{12... | collective-permute-start | bytes 786440 | tf_op jit(solution)/shard_map/ppermute | solution.py:361
  31.9 12.7 %collective-permute-start.15 = (f32[2,2,128,128]{3,2,1,0:T(8,128)S(1)}, f32[2,2,128,128]{3,2,1,0:T(8,128)S(1)}, u32[]{:S(2)}, u32[]{:S(2)}) collective-permute-start(f32[2,2,128,128]{3,2,1,0:T(8,128)S(1)} %momentum.11.refs_2_), channel_id=1, source_target_pairs={{2,0},{4,2},{6,4},{7,6},{5,7},{3,5},{1,3},{0,1},{10,8},{12,10},{14... | collective-permute-start | bytes 786440 | tf_op jit(solution)/shard_map/ppermute | solution.py:361
  32.0 11.1 %collective-permute-start.13 = (f32[1,2,128,128]{3,2,1,0:T(8,128)S(1)}, f32[1,2,128,128]{3,2,1,0:T(8,128)S(1)}, u32[]{:S(2)}, u32[]{:S(2)}) collective-permute-start(f32[1,2,128,128]{3,2,1,0:T(8,128)S(1)} %momentum.10.refs_1_), channel_id=1, source_target_pairs={{2,0},{4,2},{6,4},{7,6},{5,7},{3,5},{1,3},{0,1},{10,8},{12,10},{14... | collective-permute-start | bytes 393224 | tf_op jit(solution)/shard_map/ppermute | solution.py:361
  32.2 12.5 %collective-permute-start.17 = (f32[1,2,128,128]{3,2,1,0:T(8,128)S(1)}, f32[1,2,128,128]{3,2,1,0:T(8,128)S(1)}, u32[]{:S(2)}, u32[]{:S(2)}) collective-permute-start(f32[1,2,128,128]{3,2,1,0:T(8,128)S(1)} %collective-permute-done.7.refs_0_), channel_id=1, source_target_pairs={{0,2},{2,4},{4,6},{6,7},{7,5},{5,3},{3,1},{1,0},{8,10},{10,12},{12... | collective-permute-start | bytes 393224 | tf_op jit(solution)/shard_map/ppermute | solution.py:361
  34.1 10.6 %collective-permute-start.18 = (f32[1,2,128,128]{3,2,1,0:T(8,128)S(1)}, f32[1,2,128,128]{3,2,1,0:T(8,128)S(1)}, u32[]{:S(2)}, u32[]{:S(2)}) collective-permute-start(f32[1,2,128,128]{3,2,1,0:T(8,128)S(1)} %momentum.8.refs_1_), channel_id=1, source_target_pairs={{0,2},{2,4},{4,6},{6,7},{7,5},{5,3},{3,1},{1,0},{8,10},{10,12},{12... | collective-permute-start | bytes 393224 | tf_op jit(solution)/shard_map/ppermute | solution.py:361
  43.1 10.7 %collective-permute-start.21 = (f32[2,2,128,128]{3,2,1,0:T(8,128)S(1)}, f32[2,2,128,128]{3,2,1,0:T(8,128)S(1)}, u32[]{:S(2)}, u32[]{:S(2)}) collective-permute-start(f32[2,2,128,128]{3,2,1,0:T(8,128)S(1)} %collective-permute-done.20.refs_2_), channel_id=1, source_target_pairs={{0,2},{2,4},{4,6},{6,7},{7,5},{5,3},{3,1},{1,0},{8,10},{10,12},{12... | collective-permute-start | bytes 786440 | tf_op jit(solution)/shard_map/ppermute | solution.py:361
  44.7 5.2 %collective-permute-start.12 = (f32[1,2,128,128]{3,2,1,0:T(8,128)S(1)}, f32[1,2,128,128]{3,2,1,0:T(8,128)S(1)}, u32[]{:S(2)}, u32[]{:S(2)}) collective-permute-start(f32[1,2,128,128]{3,2,1,0:T(8,128)S(1)} %collective-permute-done.8.refs_0_), channel_id=1, source_target_pairs={{2,0},{4,2},{6,4},{7,6},{5,7},{3,5},{1,3},{0,1},{10,8},{12,10},{14... | collective-permute-start | bytes 393224 | tf_op jit(solution)/shard_map/ppermute | solution.py:361
  44.7 10.2 %collective-permute-start.16 = (f32[2,2,128,128]{3,2,1,0:T(8,128)S(1)}, f32[2,2,128,128]{3,2,1,0:T(8,128)S(1)}, u32[]{:S(2)}, u32[]{:S(2)}) collective-permute-start(f32[2,2,128,128]{3,2,1,0:T(8,128)S(1)} %collective-permute-done.15.refs_2_), channel_id=1, source_target_pairs={{2,0},{4,2},{6,4},{7,6},{5,7},{3,5},{1,3},{0,1},{10,8},{12,10},{14... | collective-permute-start | bytes 786440 | tf_op jit(solution)/shard_map/ppermute | solution.py:361
  44.7 9.1 %collective-permute-start.19 = (f32[1,2,128,128]{3,2,1,0:T(8,128)S(1)}, f32[1,2,128,128]{3,2,1,0:T(8,128)S(1)}, u32[]{:S(2)}, u32[]{:S(2)}) collective-permute-start(f32[1,2,128,128]{3,2,1,0:T(8,128)S(1)} %collective-permute-done.18.refs_1_), channel_id=1, source_target_pairs={{0,2},{2,4},{4,6},{6,7},{7,5},{5,3},{3,1},{1,0},{8,10},{10,12},{12... | collective-permute-start | bytes 393224 | tf_op jit(solution)/shard_map/ppermute | solution.py:361
  49.8 5.0 %collective-permute-start.14 = (f32[1,2,128,128]{3,2,1,0:T(8,128)S(1)}, f32[1,2,128,128]{3,2,1,0:T(8,128)S(1)}, u32[]{:S(2)}, u32[]{:S(2)}) collective-permute-start(f32[1,2,128,128]{3,2,1,0:T(8,128)S(1)} %collective-permute-done.13.refs_1_), channel_id=1, source_target_pairs={{2,0},{4,2},{6,4},{7,6},{5,7},{3,5},{1,3},{0,1},{10,8},{12,10},{14... | collective-permute-start | bytes 393224 | tf_op jit(solution)/shard_map/ppermute | solution.py:361
  49.9 0.7 %copy-start = (s32[4]{0:T(128)S(1)}, s32[4]{0:T(128)}, u32[]{:S(2)}) copy-start(s32[4]{0:T(128)} %shift_ref.1) | copy-start | bytes 52
  49.9 0.7 %copy-start.1 = (f32[4]{0:T(128)S(1)}, f32[4]{0:T(128)}, u32[]{:S(2)}) copy-start(f32[4]{0:T(128)} %weight_ref.1) | copy-start | bytes 52

commit v12 on v11

--- a/solution.py
+++ b/solution.py
@@ -1,4 +1,5 @@
 import functools
+import itertools
 
 import jax
 import jax.numpy as jnp
@@ -226,7 +227,7 @@
                 occ = occupation(source * local_e + b, total, n)
                 for a in range(local_e):
                     t = d * local_e + sign * (b - a)
-                    if some and 1 <= t <= most:
+                    if some[i] and 1 <= t <= most:
                         weight = table_ref[t : t + 1] * factor
                         terms[a].append((refs[i], b, weight, weight * occ))
         for i in range(2):
@@ -246,15 +247,18 @@
                 if last:
                     copy_out(i, a).start()
 
+    def present(here, momentum, d):
+        return place >= d if momentum == here else place + d < places
+
     for here in range(2):
-        if len(items) > 1:
-            pl.when(core == here)(functools.partial(body, here, True))
+        if not last:
+            pl.when(core == here)(functools.partial(body, here, [True] * count))
             continue
-        [(momentum, d)] = items
-        some = place >= d if momentum == here else place + d < places
-        pl.when((core == here) & some)(functools.partial(body, here, True))
-        if last:
-            pl.when((core == here) & ~some)(functools.partial(body, here, False))
+        for some in itertools.product([False, True], repeat=count):
+            fits = core == here
+            for (momentum, d), there in zip(items, some):
+                fits = fits & (present(here, momentum, d) == there)
+            pl.when(fits)(functools.partial(body, here, some))
 
     if last:
         for a in range(local_e):
@@ -384,15 +388,12 @@
 
     def mix(items, blocks, sums, last=False):
         scratch = [pltpu.VMEM(block.shape, F32)] * 2 + [pltpu.SemaphoreType.DMA((2, local_e))]
-        count = 1 + len(blocks)
-        in_place = len(items) == 1 and not last
         return pl.pallas_call(
             functools.partial(mix_kernel, total, items, False, last),
             out_shape=[block] * 2,
             in_specs=whole(1 + len(blocks) + len(sums)),
             out_specs=[pl.BlockSpec(memory_space=pl.ANY)] * 2 if last else whole(2),
             scratch_shapes=scratch if last else [],
-            input_output_aliases={count: 0, count + 1: 1} if in_place else {},
             compiler_params=params(),
             name="mix",
         )(table, *blocks, *sums)
@@ -411,8 +412,7 @@
         zero, one = (by_energy(m, fields[m]) for m in range(2))
         if d < reach:
             sums = mix([(0, d), (1, d)], [zero, one], sums)
-    sums = mix([(0, reach)], [zero], sums)
-    sums = mix([(1, reach)], [one], [*sums, local_lesser], last=True)
+    sums = mix([(0, reach), (1, reach)], [zero, one], [*sums, local_lesser], last=True)
     retarded, lesser = sums
     return (retarded[None, None], lesser[None, None])
 

time: 56.2 us -> 56.7 us (level)
    pallas_call x3 -> x2, Pallas kernels: 1.77 us -> 1.75 us  [mix(): pl.pallas_call(functools.partial(mix_kernel, total, items, False, last),...]
where the time goes in v12:
time: 56.7 us; the launch traced here: 56.6 us
  waiting for transfers between devices  25.2 us (44%)
  starting transfers between devices  20.1 us (35%)
  Pallas kernels  9.76 us (17%)
  between operations  0.83 us (1%)
  local copies, waits for them, and re-layouts  0.64 us (1%)
    ppermute x12, waiting for transfers between devices, hop(): return lax.ppermute(value, ('energy', 'mom'), ways[role])  13.3 us
    ppermute x12, starting transfers between devices, hop(): return lax.ppermute(value, ('energy', 'mom'), ways[role])  11.3 us
    ppermute x6, waiting for transfers between devices, exchange(): return lax.ppermute(slots[i], ('len', 'mom'), pairs)  10.8 us
    ppermute x6, starting transfers between devices, exchange(): return lax.ppermute(slots[i], ('len', 'mom'), pairs)  8.23 us
    pallas_call x2, Pallas kernels, inverse(): pl.pallas_call(functools.partial(inverse_kernel, total, layers, slots), o...  4.51 us
    pallas_call x1, Pallas kernels, shards(): pl.pallas_call(functools.partial(chain_kernel, layers), out_shape=[part]...  2.22 us
    pallas_call x2, Pallas kernels, mix(): pl.pallas_call(functools.partial(mix_kernel, total, items, False, last),...  1.75 us
  transfers between devices with their start and end apart: 22, of which 11 were waited for; matrix products, arithmetic and copies ran while one was open for 0% of the time, Pallas kernels for 7%

profile of v12, /device:TPU:0, one launch (start us, length us, event | category | flops | bytes accessed | tf_op | source)
XLA Modules:
  0.0 56.6 jit_solution(17482283039548598012)
XLA Ops:
  0.6 2.3 %inverse.3 = (f32[3,128,128]{2,1,0:T(8,128)S(1)}, f32[3,128,128]{2,1,0:T(8,128)S(1)}) custom-call(f32[2,128,128]{2,1,0:T(8,128)} %bitcast.9, f32[4,2,128,128]{3,2,1,0:T(8,128)} %bitcast.5, f32[128,128]{1,0:T(8,128)} %bitcast.11, s32[128,128]{1,0:T(8,128)} %pattern_any.3), custom_call_target="tpu_custom_call" | custom-call | flops 402653184 | bytes 262144 | tf_op jit(solution)/shard_map/inverse/pallas_call | solution.py:302
  2.9 4.0 %collective-permute-start = (f32[3,128,128]{2,1,0:T(8,128)S(1)}, f32[3,128,128]{2,1,0:T(8,128)S(1)}, u32[]{:S(2)}, u32[]{:S(2)}) collective-permute-start(f32[3,128,128]{2,1,0:T(8,128)S(1)} %get-tuple-element.24), channel_id=1, source_target_pairs={{0,24},{1,25},{8,16},{9,17},{16,8},{17,9},{24,0},{25,1},{2,26},{3,... | collective-permute-start | bytes 589832 | tf_op jit(solution)/shard_map/ppermute | solution.py:295
  6.9 0.5 collective-permute-start.1
  7.4 2.2 %inverse.2 = (f32[3,128,128]{2,1,0:T(8,128)S(1)}, f32[3,128,128]{2,1,0:T(8,128)S(1)}) custom-call(f32[2,128,128]{2,1,0:T(8,128)} %bitcast.10, f32[4,2,128,128]{3,2,1,0:T(8,128)} %bitcast.6, f32[128,128]{1,0:T(8,128)} %bitcast.12, s32[128,128]{1,0:T(8,128)} %pattern_any.3), custom_call_target="tpu_custom_call" | custom-call | flops 402653184 | bytes 262144 | tf_op jit(solution)/shard_map/inverse/pallas_call | solution.py:302
  9.6 0.2 collective-permute-start.2
  9.8 2.3 %collective-permute-done.refs_1_ = f32[3,128,128]{2,1,0:T(8,128)S(1)} collective-permute-done((f32[3,128,128]{2,1,0:T(8,128)S(1)}, f32[3,128,128]{2,1,0:T(8,128)S(1)}, u32[]{:S(2)}, u32[]{:S(2)}) %collective-permute-start) | collective-permute-done | bytes 196640 | tf_op jit(solution)/shard_map/ppermute | solution.py:295
  12.2 4.1 %collective-permute-done.1.refs_2_ = f32[3,128,128]{2,1,0:T(8,128)S(1)} collective-permute-done((f32[3,128,128]{2,1,0:T(8,128)S(1)}, f32[3,128,128]{2,1,0:T(8,128)S(1)}, u32[]{:S(2)}, u32[]{:S(2)}) %collective-permute-start.1) | collective-permute-done | bytes 196640 | tf_op jit(solution)/shard_map/ppermute | solution.py:295
  16.3 2.2 %chains.1 = (f32[1,2,128,128]{3,2,1,0:T(8,128)S(1)}, f32[1,2,128,128]{3,2,1,0:T(8,128)S(1)}, f32[1,2,128,128]{3,2,1,0:T(8,128)S(1)}, f32[1,2,128,128]{3,2,1,0:T(8,128)S(1)}) custom-call(f32[3,128,128]{2,1,0:T(8,128)S(1)} %get-tuple-element.23.refs_0_, f32[3,128,128]{2,1,0:T(8,128)S(1)} %collective-permute-done.refs_1_, ...), custom_call_target="tpu_custom_call" | custom-call | tf_op jit(solution)/shard_map/chains/pallas_call | solution.py:326
  18.6 1.6 %collective-permute-start.4 = (f32[1,2,128,128]{3,2,1,0:T(8,128)S(1)}, f32[1,2,128,128]{3,2,1,0:T(8,128)S(1)}, u32[]{:S(2)}, u32[]{:S(2)}) collective-permute-start(f32[1,2,128,128]{3,2,1,0:T(8,128)S(1)} %get-tuple-element.28), channel_id=1, source_target_pairs={{0,24},{1,25},{8,16},{9,17},{16,8},{17,9},{24,0},{25,1},{2,26},{3,... | collective-permute-start | bytes 393224 | tf_op jit(solution)/shard_map/ppermute | solution.py:295
  20.2 1.4 %collective-permute-start.5 = (f32[1,2,128,128]{3,2,1,0:T(8,128)S(1)}, f32[1,2,128,128]{3,2,1,0:T(8,128)S(1)}, u32[]{:S(2)}, u32[]{:S(2)}) collective-permute-start(f32[1,2,128,128]{3,2,1,0:T(8,128)S(1)} %get-tuple-element.29), channel_id=1, source_target_pairs={{0,8},{1,17},{8,0},{9,25},{16,24},{17,1},{24,16},{25,9},{2,10},{3,... | collective-permute-start | bytes 393224 | tf_op jit(solution)/shard_map/ppermute | solution.py:295
  21.5 0.6 %collective-permute-start.6 = (f32[1,2,128,128]{3,2,1,0:T(8,128)S(1)}, f32[1,2,128,128]{3,2,1,0:T(8,128)S(1)}, u32[]{:S(2)}, u32[]{:S(2)}) collective-permute-start(f32[1,2,128,128]{3,2,1,0:T(8,128)S(1)} %get-tuple-element.30), channel_id=1, source_target_pairs={{0,16},{1,9},{8,24},{9,1},{16,0},{17,25},{24,8},{25,17},{2,18},{3,... | collective-permute-start | bytes 393224 | tf_op jit(solution)/shard_map/ppermute | solution.py:295
  22.2 1.6 %collective-permute-start.7 = (f32[1,2,128,128]{3,2,1,0:T(8,128)S(1)}, f32[1,2,128,128]{3,2,1,0:T(8,128)S(1)}, u32[]{:S(2)}, u32[]{:S(2)}) collective-permute-start(f32[1,2,128,128]{3,2,1,0:T(8,128)S(1)} %momentum.6.refs_0_), channel_id=1, source_target_pairs={{0,2},{2,4},{4,6},{6,7},{7,5},{5,3},{3,1},{1,0},{8,10},{10,12},{12... | collective-permute-start | bytes 393224 | tf_op jit(solution)/shard_map/ppermute | solution.py:365
  23.8 2.1 %collective-permute-done.4.refs_0_ = f32[1,2,128,128]{3,2,1,0:T(8,128)S(1)} collective-permute-done((f32[1,2,128,128]{3,2,1,0:T(8,128)S(1)}, f32[1,2,128,128]{3,2,1,0:T(8,128)S(1)}, u32[]{:S(2)}, u32[]{:S(2)}) %collective-permute-start.4) | collective-permute-done | bytes 131104 | tf_op jit(solution)/shard_map/ppermute | solution.py:295
  25.9 2.3 %collective-permute-done.5.refs_1_ = f32[1,2,128,128]{3,2,1,0:T(8,128)S(1)} collective-permute-done((f32[1,2,128,128]{3,2,1,0:T(8,128)S(1)}, f32[1,2,128,128]{3,2,1,0:T(8,128)S(1)}, u32[]{:S(2)}, u32[]{:S(2)}) %collective-permute-start.5) | collective-permute-done | bytes 131104 | tf_op jit(solution)/shard_map/ppermute | solution.py:295
  28.2 0.5 collective-permute-done.8.refs_0_
  28.8 0.5 collective-permute-start.11
  29.3 0.8 %collective-permute-done.10.refs_2_ = f32[1,2,128,128]{3,2,1,0:T(8,128)S(1)} collective-permute-done((f32[1,2,128,128]{3,2,1,0:T(8,128)S(1)}, f32[1,2,128,128]{3,2,1,0:T(8,128)S(1)}, u32[]{:S(2)}, u32[]{:S(2)}) %collective-permute-start.10) | collective-permute-done | bytes 131104 | tf_op jit(solution)/shard_map/ppermute | solution.py:374
  30.1 0.2 collective-permute-done.11.refs_3_
  30.3 1.6 %collective-permute-start.15 = (f32[2,2,128,128]{3,2,1,0:T(8,128)S(1)}, f32[2,2,128,128]{3,2,1,0:T(8,128)S(1)}, u32[]{:S(2)}, u32[]{:S(2)}) collective-permute-start(f32[2,2,128,128]{3,2,1,0:T(8,128)S(1)} %momentum.9.refs_2_), channel_id=1, source_target_pairs={{0,2},{2,4},{4,6},{6,7},{7,5},{5,3},{3,1},{1,0},{8,10},{10,12},{12... | collective-permute-start | bytes 786440 | tf_op jit(solution)/shard_map/ppermute | solution.py:365
  32.0 0.2 collective-permute-start.16
  32.2 1.8 %collective-permute-start.12 = (f32[1,2,128,128]{3,2,1,0:T(8,128)S(1)}, f32[1,2,128,128]{3,2,1,0:T(8,128)S(1)}, u32[]{:S(2)}, u32[]{:S(2)}) collective-permute-start(f32[1,2,128,128]{3,2,1,0:T(8,128)S(1)} %collective-permute-done.7.refs_0_), channel_id=1, source_target_pairs={{0,2},{2,4},{4,6},{6,7},{7,5},{5,3},{3,1},{1,0},{8,10},{10,12},{12... | collective-permute-start | bytes 393224 | tf_op jit(solution)/shard_map/ppermute | solution.py:365
  34.1 2.0 %collective-permute-start.13 = (f32[1,2,128,128]{3,2,1,0:T(8,128)S(1)}, f32[1,2,128,128]{3,2,1,0:T(8,128)S(1)}, u32[]{:S(2)}, u32[]{:S(2)}) collective-permute-start(f32[1,2,128,128]{3,2,1,0:T(8,128)S(1)} %momentum.8.refs_1_), channel_id=1, source_target_pairs={{0,2},{2,4},{4,6},{6,7},{7,5},{5,3},{3,1},{1,0},{8,10},{10,12},{12... | collective-permute-start | bytes 393224 | tf_op jit(solution)/shard_map/ppermute | solution.py:365
  36.1 7.0 %collective-permute-done.16.refs_1_ = f32[1,2,128,128]{3,2,1,0:T(8,128)S(1)} collective-permute-done((f32[1,2,128,128]{3,2,1,0:T(8,128)S(1)}, f32[1,2,128,128]{3,2,1,0:T(8,128)S(1)}, u32[]{:S(2)}, u32[]{:S(2)}) %collective-permute-start.16) | collective-permute-done | bytes 131104 | tf_op jit(solution)/shard_map/ppermute | solution.py:365
  43.1 2.0 %collective-permute-start.17 = (f32[2,2,128,128]{3,2,1,0:T(8,128)S(1)}, f32[2,2,128,128]{3,2,1,0:T(8,128)S(1)}, u32[]{:S(2)}, u32[]{:S(2)}) collective-permute-start(f32[2,2,128,128]{3,2,1,0:T(8,128)S(1)} %collective-permute-done.15.refs_2_), channel_id=1, source_target_pairs={{0,2},{2,4},{4,6},{6,7},{7,5},{5,3},{3,1},{1,0},{8,10},{10,12},{12... | collective-permute-start | bytes 786440 | tf_op jit(solution)/shard_map/ppermute | solution.py:365
  45.1 2.0 %collective-permute-start.14 = (f32[1,2,128,128]{3,2,1,0:T(8,128)S(1)}, f32[1,2,128,128]{3,2,1,0:T(8,128)S(1)}, u32[]{:S(2)}, u32[]{:S(2)}) collective-permute-start(f32[1,2,128,128]{3,2,1,0:T(8,128)S(1)} %collective-permute-done.13.refs_1_), channel_id=1, source_target_pairs={{0,2},{2,4},{4,6},{6,7},{7,5},{5,3},{3,1},{1,0},{8,10},{10,12},{12... | collective-permute-start | bytes 393224 | tf_op jit(solution)/shard_map/ppermute | solution.py:365
  47.1 2.3 %collective-permute-done.18.refs_0_ = f32[1,2,128,128]{3,2,1,0:T(8,128)S(1)} collective-permute-done((f32[1,2,128,128]{3,2,1,0:T(8,128)S(1)}, f32[1,2,128,128]{3,2,1,0:T(8,128)S(1)}, u32[]{:S(2)}, u32[]{:S(2)}) %collective-permute-start.18) | collective-permute-done | bytes 131104 | tf_op jit(solution)/shard_map/ppermute | solution.py:365
  49.6 0.6 %copy-done = s32[4]{0:T(128)S(1)} copy-done((s32[4]{0:T(128)S(1)}, s32[4]{0:T(128)}, u32[]{:S(2)}) %copy-start) | copy-done | bytes 40
  50.2 0.9 %local.1 = (f32[4,2,128,128]{3,2,1,0:T(8,128)S(1)}, f32[4,2,128,128]{3,2,1,0:T(8,128)S(1)}, f32[16,128]{1,0:T(8,128)S(1)}) custom-call(s32[4]{0:T(128)S(1)} %copy-done, f32[4]{0:T(128)S(1)} %copy-done.1, f32[4,2,128,128]{3,2,1,0:T(8,128)S(1)} %by_energy.6.zero_ref, f32[4,2,128,128]{3,2,1,0:T(8,128)S(1)} %by_energy.7.one_ref), custom_call_target="tpu_custom_call" | custom-call | tf_op jit(solution)/shard_map/local/pallas_call | solution.py:380
  51.3 0.6 %mix.2 = (f32[4,2,128,128]{3,2,1,0:T(8,128)S(1)}, f32[4,2,128,128]{3,2,1,0:T(8,128)S(1)}) custom-call(f32[16,128]{1,0:T(8,128)S(1)} %get-tuple-element.34.table_ref, f32[4,2,128,128]{3,2,1,0:T(8,128)S(1)} %by_energy.10.refs_0_, f32[4,2,128,128]{3,2,1,0:T(8,128)S(1)} %by_energy.11.refs_1_, f32[4,2,128,128]{3,2,1,0:T(8,128)S(1)} %get-tuple-element.38.refs_2_, ...), custom_call_target="tpu_custom_call" | custom-call | tf_op jit(solution)/shard_map/mix/pallas_call | solution.py:391
  51.8 1.4 %collective-permute-done.14.refs_1_ = f32[1,2,128,128]{3,2,1,0:T(8,128)S(1)} collective-permute-done((f32[1,2,128,128]{3,2,1,0:T(8,128)S(1)}, f32[1,2,128,128]{3,2,1,0:T(8,128)S(1)}, u32[]{:S(2)}, u32[]{:S(2)}) %collective-permute-start.14) | collective-permute-done | bytes 131104 | tf_op jit(solution)/shard_map/ppermute | solution.py:365
  53.3 2.1 %collective-permute-done.19.refs_1_ = f32[1,2,128,128]{3,2,1,0:T(8,128)S(1)} collective-permute-done((f32[1,2,128,128]{3,2,1,0:T(8,128)S(1)}, f32[1,2,128,128]{3,2,1,0:T(8,128)S(1)}, u32[]{:S(2)}, u32[]{:S(2)}) %collective-permute-start.19) | collective-permute-done | bytes 131104 | tf_op jit(solution)/shard_map/ppermute | solution.py:365
  55.4 1.2 %mix.3 = (f32[4,2,128,128]{3,2,1,0:T(8,128)}, f32[4,2,128,128]{3,2,1,0:T(8,128)}) custom-call(f32[16,128]{1,0:T(8,128)S(1)} %get-tuple-element.34.table_ref, f32[4,2,128,128]{3,2,1,0:T(8,128)S(1)} %by_energy.8.refs_0_, f32[4,2,128,128]{3,2,1,0:T(8,128)S(1)} %by_energy.9.refs_1_, f32[4,2,128,128]{3,2,1,0:T(8,128)S(1)} %get-tuple-element.39.refs_2_, ...), custom_call_target="tpu_custom_call" | custom-call | tf_op jit(solution)/shard_map/mix/pallas_call | solution.py:391
  (35 shorter events, 0.6 us)
Async XLA Ops:
  2.9 9.3 %collective-permute-start = (f32[3,128,128]{2,1,0:T(8,128)S(1)}, f32[3,128,128]{2,1,0:T(8,128)S(1)}, u32[]{:S(2)}, u32[]{:S(2)}) collective-permute-start(f32[3,128,128]{2,1,0:T(8,128)S(1)} %get-tuple-element.24), channel_id=1, source_target_pairs={{0,24},{1,25},{8,16},{9,17},{16,8},{17,9},{24,0},{25,1},{2,26},{3,... | collective-permute-start | bytes 589832 | tf_op jit(solution)/shard_map/ppermute | solution.py:295
  6.9 9.4 %collective-permute-start.1 = (f32[3,128,128]{2,1,0:T(8,128)S(1)}, f32[3,128,128]{2,1,0:T(8,128)S(1)}, u32[]{:S(2)}, u32[]{:S(2)}) collective-permute-start(f32[3,128,128]{2,1,0:T(8,128)S(1)} %get-tuple-element.25), channel_id=1, source_target_pairs={{0,8},{1,17},{8,0},{9,25},{16,24},{17,1},{24,16},{25,9},{2,10},{3,... | collective-permute-start | bytes 589832 | tf_op jit(solution)/shard_map/ppermute | solution.py:295
  9.6 6.6 %collective-permute-start.2 = (f32[3,128,128]{2,1,0:T(8,128)S(1)}, f32[3,128,128]{2,1,0:T(8,128)S(1)}, u32[]{:S(2)}, u32[]{:S(2)}) collective-permute-start(f32[3,128,128]{2,1,0:T(8,128)S(1)} %get-tuple-element.26), channel_id=1, source_target_pairs={{0,16},{1,9},{8,24},{9,1},{16,0},{17,25},{24,8},{25,17},{2,18},{3,... | collective-permute-start | bytes 589832 | tf_op jit(solution)/shard_map/ppermute | solution.py:295
  18.5 3.6 %collective-permute-start.3 = (f32[1,2,128,128]{3,2,1,0:T(8,128)S(1)}, f32[1,2,128,128]{3,2,1,0:T(8,128)S(1)}, u32[]{:S(2)}, u32[]{:S(2)}) collective-permute-start(f32[1,2,128,128]{3,2,1,0:T(8,128)S(1)} %get-tuple-element.27.refs_0_), channel_id=1, source_target_pairs={{0,1},{1,0},{2,3},{3,2},{4,5},{5,4},{6,7},{7,6},{8,9},{9,8},{10,11... | collective-permute-start | bytes 393224 | tf_op jit(solution)/shard_map/ppermute | solution.py:374
  18.6 7.3 %collective-permute-start.4 = (f32[1,2,128,128]{3,2,1,0:T(8,128)S(1)}, f32[1,2,128,128]{3,2,1,0:T(8,128)S(1)}, u32[]{:S(2)}, u32[]{:S(2)}) collective-permute-start(f32[1,2,128,128]{3,2,1,0:T(8,128)S(1)} %get-tuple-element.28), channel_id=1, source_target_pairs={{0,24},{1,25},{8,16},{9,17},{16,8},{17,9},{24,0},{25,1},{2,26},{3,... | collective-permute-start | bytes 393224 | tf_op jit(solution)/shard_map/ppermute | solution.py:295
  20.2 8.0 %collective-permute-start.5 = (f32[1,2,128,128]{3,2,1,0:T(8,128)S(1)}, f32[1,2,128,128]{3,2,1,0:T(8,128)S(1)}, u32[]{:S(2)}, u32[]{:S(2)}) collective-permute-start(f32[1,2,128,128]{3,2,1,0:T(8,128)S(1)} %get-tuple-element.29), channel_id=1, source_target_pairs={{0,8},{1,17},{8,0},{9,25},{16,24},{17,1},{24,16},{25,9},{2,10},{3,... | collective-permute-start | bytes 393224 | tf_op jit(solution)/shard_map/ppermute | solution.py:295
  21.5 6.7 %collective-permute-start.6 = (f32[1,2,128,128]{3,2,1,0:T(8,128)S(1)}, f32[1,2,128,128]{3,2,1,0:T(8,128)S(1)}, u32[]{:S(2)}, u32[]{:S(2)}) collective-permute-start(f32[1,2,128,128]{3,2,1,0:T(8,128)S(1)} %get-tuple-element.30), channel_id=1, source_target_pairs={{0,16},{1,9},{8,24},{9,1},{16,0},{17,25},{24,8},{25,17},{2,18},{3,... | collective-permute-start | bytes 393224 | tf_op jit(solution)/shard_map/ppermute | solution.py:295
  22.2 6.0 %collective-permute-start.7 = (f32[1,2,128,128]{3,2,1,0:T(8,128)S(1)}, f32[1,2,128,128]{3,2,1,0:T(8,128)S(1)}, u32[]{:S(2)}, u32[]{:S(2)}) collective-permute-start(f32[1,2,128,128]{3,2,1,0:T(8,128)S(1)} %momentum.6.refs_0_), channel_id=1, source_target_pairs={{0,2},{2,4},{4,6},{6,7},{7,5},{5,3},{3,1},{1,0},{8,10},{10,12},{12... | collective-permute-start | bytes 393224 | tf_op jit(solution)/shard_map/ppermute | solution.py:365
  23.8 5.0 %collective-permute-start.8 = (f32[1,2,128,128]{3,2,1,0:T(8,128)S(1)}, f32[1,2,128,128]{3,2,1,0:T(8,128)S(1)}, u32[]{:S(2)}, u32[]{:S(2)}) collective-permute-start(f32[1,2,128,128]{3,2,1,0:T(8,128)S(1)} %momentum.7.refs_0_), channel_id=1, source_target_pairs={{2,0},{4,2},{6,4},{7,6},{5,7},{3,5},{1,3},{0,1},{10,8},{12,10},{14... | collective-permute-start | bytes 393224 | tf_op jit(solution)/shard_map/ppermute | solution.py:365
  28.7 1.3 %collective-permute-start.10 = (f32[1,2,128,128]{3,2,1,0:T(8,128)S(1)}, f32[1,2,128,128]{3,2,1,0:T(8,128)S(1)}, u32[]{:S(2)}, u32[]{:S(2)}) collective-permute-start(f32[1,2,128,128]{3,2,1,0:T(8,128)S(1)} %collective-permute-done.4.refs_0_), channel_id=1, source_target_pairs={{0,1},{1,0},{2,3},{3,2},{4,5},{5,4},{6,7},{7,6},{8,9},{9,8},{10,11... | collective-permute-start | bytes 393224 | tf_op jit(solution)/shard_map/ppermute | solution.py:374
  28.8 1.5 %collective-permute-start.11 = (f32[1,2,128,128]{3,2,1,0:T(8,128)S(1)}, f32[1,2,128,128]{3,2,1,0:T(8,128)S(1)}, u32[]{:S(2)}, u32[]{:S(2)}) collective-permute-start(f32[1,2,128,128]{3,2,1,0:T(8,128)S(1)} %collective-permute-done.5.refs_1_), channel_id=1, source_target_pairs={{0,1},{1,0},{2,3},{3,2},{4,5},{5,4},{6,7},{7,6},{8,9},{9,8},{10,11... | collective-permute-start | bytes 393224 | tf_op jit(solution)/shard_map/ppermute | solution.py:374
  29.3 2.7 %collective-permute-start.9 = (f32[1,2,128,128]{3,2,1,0:T(8,128)S(1)}, f32[1,2,128,128]{3,2,1,0:T(8,128)S(1)}, u32[]{:S(2)}, u32[]{:S(2)}) collective-permute-start(f32[1,2,128,128]{3,2,1,0:T(8,128)S(1)} %collective-permute-done.6.refs_0_), channel_id=1, source_target_pairs={{0,1},{1,0},{2,3},{3,2},{4,5},{5,4},{6,7},{7,6},{8,9},{9,8},{10,11... | collective-permute-start | bytes 393224 | tf_op jit(solution)/shard_map/ppermute | solution.py:374
  30.3 12.8 %collective-permute-start.15 = (f32[2,2,128,128]{3,2,1,0:T(8,128)S(1)}, f32[2,2,128,128]{3,2,1,0:T(8,128)S(1)}, u32[]{:S(2)}, u32[]{:S(2)}) collective-permute-start(f32[2,2,128,128]{3,2,1,0:T(8,128)S(1)} %momentum.9.refs_2_), channel_id=1, source_target_pairs={{0,2},{2,4},{4,6},{6,7},{7,5},{5,3},{3,1},{1,0},{8,10},{10,12},{12... | collective-permute-start | bytes 786440 | tf_op jit(solution)/shard_map/ppermute | solution.py:365
  31.9 13.2 %collective-permute-start.20 = (f32[2,2,128,128]{3,2,1,0:T(8,128)S(1)}, f32[2,2,128,128]{3,2,1,0:T(8,128)S(1)}, u32[]{:S(2)}, u32[]{:S(2)}) collective-permute-start(f32[2,2,128,128]{3,2,1,0:T(8,128)S(1)} %momentum.11.refs_2_), channel_id=1, source_target_pairs={{2,0},{4,2},{6,4},{7,6},{5,7},{3,5},{1,3},{0,1},{10,8},{12,10},{14... | collective-permute-start | bytes 786440 | tf_op jit(solution)/shard_map/ppermute | solution.py:365
  32.0 11.1 %collective-permute-start.16 = (f32[1,2,128,128]{3,2,1,0:T(8,128)S(1)}, f32[1,2,128,128]{3,2,1,0:T(8,128)S(1)}, u32[]{:S(2)}, u32[]{:S(2)}) collective-permute-start(f32[1,2,128,128]{3,2,1,0:T(8,128)S(1)} %momentum.10.refs_1_), channel_id=1, source_target_pairs={{2,0},{4,2},{6,4},{7,6},{5,7},{3,5},{1,3},{0,1},{10,8},{12,10},{14... | collective-permute-start | bytes 393224 | tf_op jit(solution)/shard_map/ppermute | solution.py:365
  32.2 12.9 %collective-permute-start.12 = (f32[1,2,128,128]{3,2,1,0:T(8,128)S(1)}, f32[1,2,128,128]{3,2,1,0:T(8,128)S(1)}, u32[]{:S(2)}, u32[]{:S(2)}) collective-permute-start(f32[1,2,128,128]{3,2,1,0:T(8,128)S(1)} %collective-permute-done.7.refs_0_), channel_id=1, source_target_pairs={{0,2},{2,4},{4,6},{6,7},{7,5},{5,3},{3,1},{1,0},{8,10},{10,12},{12... | collective-permute-start | bytes 393224 | tf_op jit(solution)/shard_map/ppermute | solution.py:365
  34.1 11.1 %collective-permute-start.13 = (f32[1,2,128,128]{3,2,1,0:T(8,128)S(1)}, f32[1,2,128,128]{3,2,1,0:T(8,128)S(1)}, u32[]{:S(2)}, u32[]{:S(2)}) collective-permute-start(f32[1,2,128,128]{3,2,1,0:T(8,128)S(1)} %momentum.8.refs_1_), channel_id=1, source_target_pairs={{0,2},{2,4},{4,6},{6,7},{7,5},{5,3},{3,1},{1,0},{8,10},{10,12},{12... | collective-permute-start | bytes 393224 | tf_op jit(solution)/shard_map/ppermute | solution.py:365
  43.1 6.4 %collective-permute-start.18 = (f32[1,2,128,128]{3,2,1,0:T(8,128)S(1)}, f32[1,2,128,128]{3,2,1,0:T(8,128)S(1)}, u32[]{:S(2)}, u32[]{:S(2)}) collective-permute-start(f32[1,2,128,128]{3,2,1,0:T(8,128)S(1)} %collective-permute-done.8.refs_0_), channel_id=1, source_target_pairs={{2,0},{4,2},{6,4},{7,6},{5,7},{3,5},{1,3},{0,1},{10,8},{12,10},{14... | collective-permute-start | bytes 393224 | tf_op jit(solution)/shard_map/ppermute | solution.py:365
  43.1 10.1 %collective-permute-start.17 = (f32[2,2,128,128]{3,2,1,0:T(8,128)S(1)}, f32[2,2,128,128]{3,2,1,0:T(8,128)S(1)}, u32[]{:S(2)}, u32[]{:S(2)}) collective-permute-start(f32[2,2,128,128]{3,2,1,0:T(8,128)S(1)} %collective-permute-done.15.refs_2_), channel_id=1, source_target_pairs={{0,2},{2,4},{4,6},{6,7},{7,5},{5,3},{3,1},{1,0},{8,10},{10,12},{12... | collective-permute-start | bytes 786440 | tf_op jit(solution)/shard_map/ppermute | solution.py:365
  45.1 10.3 %collective-permute-start.21 = (f32[2,2,128,128]{3,2,1,0:T(8,128)S(1)}, f32[2,2,128,128]{3,2,1,0:T(8,128)S(1)}, u32[]{:S(2)}, u32[]{:S(2)}) collective-permute-start(f32[2,2,128,128]{3,2,1,0:T(8,128)S(1)} %collective-permute-done.20.refs_2_), channel_id=1, source_target_pairs={{2,0},{4,2},{6,4},{7,6},{5,7},{3,5},{1,3},{0,1},{10,8},{12,10},{14... | collective-permute-start | bytes 786440 | tf_op jit(solution)/shard_map/ppermute | solution.py:365
  45.1 8.1 %collective-permute-start.14 = (f32[1,2,128,128]{3,2,1,0:T(8,128)S(1)}, f32[1,2,128,128]{3,2,1,0:T(8,128)S(1)}, u32[]{:S(2)}, u32[]{:S(2)}) collective-permute-start(f32[1,2,128,128]{3,2,1,0:T(8,128)S(1)} %collective-permute-done.13.refs_1_), channel_id=1, source_target_pairs={{0,2},{2,4},{4,6},{6,7},{7,5},{5,3},{3,1},{1,0},{8,10},{10,12},{12... | collective-permute-start | bytes 393224 | tf_op jit(solution)/shard_map/ppermute | solution.py:365
  49.4 5.9 %collective-permute-start.19 = (f32[1,2,128,128]{3,2,1,0:T(8,128)S(1)}, f32[1,2,128,128]{3,2,1,0:T(8,128)S(1)}, u32[]{:S(2)}, u32[]{:S(2)}) collective-permute-start(f32[1,2,128,128]{3,2,1,0:T(8,128)S(1)} %collective-permute-done.16.refs_1_), channel_id=1, source_target_pairs={{2,0},{4,2},{6,4},{7,6},{5,7},{3,5},{1,3},{0,1},{10,8},{12,10},{14... | collective-permute-start | bytes 393224 | tf_op jit(solution)/shard_map/ppermute | solution.py:365
  49.5 0.7 %copy-start = (s32[4]{0:T(128)S(1)}, s32[4]{0:T(128)}, u32[]{:S(2)}) copy-start(s32[4]{0:T(128)} %shift_ref.1) | copy-start | bytes 52
  49.5 0.7 %copy-start.1 = (f32[4]{0:T(128)S(1)}, f32[4]{0:T(128)}, u32[]{:S(2)}) copy-start(f32[4]{0:T(128)} %weight_ref.1) | copy-start | bytes 52

commit v13 on v12

--- a/solution.py
+++ b/solution.py
@@ -364,13 +364,16 @@
     def hop(value, role):
         return lax.ppermute(value, ("energy", "mom"), ways[role])
 
-    chunks = [[0], [layers - 1], list(range(1, layers - 1))]
+    chunks = [[0], list(range(1, layers - 1)), [layers - 1]]
     fields = [[], []]
     hops = [[], []]
     for c in chunks:
         if len(hops[0]) == 1:
             own, _ = lax.optimization_barrier((own, hops))
+            ahead = [hop(hops[m][0], m) for m in range(2)]
         held = [own[i] for i in c]
+        if len(hops[0]) == 2:
+            held, _ = lax.optimization_barrier((held, ahead))
         other = [lax.ppermute(v, "mom", both_ways) for v in held]
         for m in range(2):
             fields[m].append(of_momentum(m, held, other))
@@ -403,10 +406,8 @@
         if d == 1:
             fields = hops
         elif d == 2:
-            ahead = [hop(fields[m][0], m) for m in range(2)]
-            held = [lax.optimization_barrier((fields[m][1], ahead[m]))[0] for m in range(2)]
-            big, _ = lax.optimization_barrier((fields[0][2], fields[1][1]))
-            fields = [[ahead[m], hop(held[m], m), hop([big, fields[1][2]][m], m)] for m in range(2)]
+            big, _ = lax.optimization_barrier((fields[0][1], fields[1][2]))
+            fields = [[ahead[m], hop([big, fields[1][1]][m], m), hop(fields[m][2], m)] for m in range(2)]
         else:
             fields = [[hop(part, m) for part in fields[m]] for m in range(2)]
         zero, one = (by_energy(m, fields[m]) for m in range(2))

time: 56.7 us -> 56.3 us (level)
  waiting for transfers between devices: 25.2 us -> 24.4 us
    ppermute x12, waiting for transfers between devices: 13.3 us -> 17.2 us  [hop(): return lax.ppermute(value, ('energy', 'mom'), ways[role])]
    ppermute x6, waiting for transfers between devices: 10.8 us -> 7.24 us  [exchange(): return lax.ppermute(slots[i], ('len', 'mom'), pairs)]
    ppermute x4, waiting for transfers between devices: 1.03 us -> 0.01 us  [shards(): other = [lax.ppermute(v, 'mom', both_ways) for v in held]]
  transfers between devices with their start and end apart: 22 -> 22, of which waited for: 11 -> 9; matrix products, arithmetic and copies ran while one was open for 0% -> 0% of each run, Pallas kernels for 7% -> 7%
where the time goes in v13:
time: 56.3 us; the launch traced here: 56.2 us
  waiting for transfers between devices  24.4 us (43%)
  starting transfers between devices  20.5 us (36%)
  Pallas kernels  9.77 us (17%)
  between operations  0.83 us (1%)
  local copies, waits for them, and re-layouts  0.64 us (1%)
    ppermute x12, waiting for transfers between devices, hop(): return lax.ppermute(value, ('energy', 'mom'), ways[role])  17.2 us
    ppermute x12, starting transfers between devices, hop(): return lax.ppermute(value, ('energy', 'mom'), ways[role])  11.8 us
    ppermute x6, starting transfers between devices, exchange(): return lax.ppermute(slots[i], ('len', 'mom'), pairs)  8.18 us
    ppermute x6, waiting for transfers between devices, exchange(): return lax.ppermute(slots[i], ('len', 'mom'), pairs)  7.24 us
    pallas_call x2, Pallas kernels, inverse(): pl.pallas_call(functools.partial(inverse_kernel, total, layers, slots), o...  4.51 us
    pallas_call x1, Pallas kernels, shards(): pl.pallas_call(functools.partial(chain_kernel, layers), out_shape=[part]...  2.22 us
    pallas_call x2, Pallas kernels, mix(): pl.pallas_call(functools.partial(mix_kernel, total, items, False, last),...  1.75 us
  transfers between devices with their start and end apart: 22, of which 9 were waited for; matrix products, arithmetic and copies ran while one was open for 0% of the time, Pallas kernels for 7%

profile of v13, /device:TPU:0, one launch (start us, length us, event | category | flops | bytes accessed | tf_op | source)
XLA Modules:
  0.0 56.2 jit_solution(17456819067732994032)
XLA Ops:
  0.6 2.3 %inverse.3 = (f32[3,128,128]{2,1,0:T(8,128)S(1)}, f32[3,128,128]{2,1,0:T(8,128)S(1)}) custom-call(f32[2,128,128]{2,1,0:T(8,128)} %bitcast.9, f32[4,2,128,128]{3,2,1,0:T(8,128)} %bitcast.5, f32[128,128]{1,0:T(8,128)} %bitcast.11, s32[128,128]{1,0:T(8,128)} %pattern_any.3), custom_call_target="tpu_custom_call" | custom-call | flops 402653184 | bytes 262144 | tf_op jit(solution)/shard_map/inverse/pallas_call | solution.py:302
  2.9 4.0 %collective-permute-start = (f32[3,128,128]{2,1,0:T(8,128)S(1)}, f32[3,128,128]{2,1,0:T(8,128)S(1)}, u32[]{:S(2)}, u32[]{:S(2)}) collective-permute-start(f32[3,128,128]{2,1,0:T(8,128)S(1)} %get-tuple-element.23), channel_id=1, source_target_pairs={{0,24},{1,25},{8,16},{9,17},{16,8},{17,9},{24,0},{25,1},{2,26},{3,... | collective-permute-start | bytes 589832 | tf_op jit(solution)/shard_map/ppermute | solution.py:295
  6.9 0.5 collective-permute-start.1
  7.4 2.2 %inverse.2 = (f32[3,128,128]{2,1,0:T(8,128)S(1)}, f32[3,128,128]{2,1,0:T(8,128)S(1)}) custom-call(f32[2,128,128]{2,1,0:T(8,128)} %bitcast.10, f32[4,2,128,128]{3,2,1,0:T(8,128)} %bitcast.6, f32[128,128]{1,0:T(8,128)} %bitcast.12, s32[128,128]{1,0:T(8,128)} %pattern_any.3), custom_call_target="tpu_custom_call" | custom-call | flops 402653184 | bytes 262144 | tf_op jit(solution)/shard_map/inverse/pallas_call | solution.py:302
  9.6 0.2 collective-permute-start.2
  9.8 2.3 %collective-permute-done.refs_1_ = f32[3,128,128]{2,1,0:T(8,128)S(1)} collective-permute-done((f32[3,128,128]{2,1,0:T(8,128)S(1)}, f32[3,128,128]{2,1,0:T(8,128)S(1)}, u32[]{:S(2)}, u32[]{:S(2)}) %collective-permute-start) | collective-permute-done | bytes 196640 | tf_op jit(solution)/shard_map/ppermute | solution.py:295
  12.2 4.1 %collective-permute-done.1.refs_2_ = f32[3,128,128]{2,1,0:T(8,128)S(1)} collective-permute-done((f32[3,128,128]{2,1,0:T(8,128)S(1)}, f32[3,128,128]{2,1,0:T(8,128)S(1)}, u32[]{:S(2)}, u32[]{:S(2)}) %collective-permute-start.1) | collective-permute-done | bytes 196640 | tf_op jit(solution)/shard_map/ppermute | solution.py:295
  16.3 2.2 %chains.1 = (f32[1,2,128,128]{3,2,1,0:T(8,128)S(1)}, f32[1,2,128,128]{3,2,1,0:T(8,128)S(1)}, f32[1,2,128,128]{3,2,1,0:T(8,128)S(1)}, f32[1,2,128,128]{3,2,1,0:T(8,128)S(1)}) custom-call(f32[3,128,128]{2,1,0:T(8,128)S(1)} %get-tuple-element.22.refs_0_, f32[3,128,128]{2,1,0:T(8,128)S(1)} %collective-permute-done.refs_1_, ...), custom_call_target="tpu_custom_call" | custom-call | tf_op jit(solution)/shard_map/chains/pallas_call | solution.py:326
  18.5 0.1 collective-permute-start.3
  18.6 1.6 %collective-permute-start.4 = (f32[1,2,128,128]{3,2,1,0:T(8,128)S(1)}, f32[1,2,128,128]{3,2,1,0:T(8,128)S(1)}, u32[]{:S(2)}, u32[]{:S(2)}) collective-permute-start(f32[1,2,128,128]{3,2,1,0:T(8,128)S(1)} %get-tuple-element.27), channel_id=1, source_target_pairs={{0,24},{1,25},{8,16},{9,17},{16,8},{17,9},{24,0},{25,1},{2,26},{3,... | collective-permute-start | bytes 393224 | tf_op jit(solution)/shard_map/ppermute | solution.py:295
  20.2 1.7 %collective-permute-start.7 = (f32[1,2,128,128]{3,2,1,0:T(8,128)S(1)}, f32[1,2,128,128]{3,2,1,0:T(8,128)S(1)}, u32[]{:S(2)}, u32[]{:S(2)}) collective-permute-start(f32[1,2,128,128]{3,2,1,0:T(8,128)S(1)} %momentum.6.refs_0_), channel_id=1, source_target_pairs={{0,2},{2,4},{4,6},{6,7},{7,5},{5,3},{3,1},{1,0},{8,10},{10,12},{12... | collective-permute-start | bytes 393224 | tf_op jit(solution)/shard_map/ppermute | solution.py:365
  21.9 1.3 %collective-permute-start.5 = (f32[1,2,128,128]{3,2,1,0:T(8,128)S(1)}, f32[1,2,128,128]{3,2,1,0:T(8,128)S(1)}, u32[]{:S(2)}, u32[]{:S(2)}) collective-permute-start(f32[1,2,128,128]{3,2,1,0:T(8,128)S(1)} %get-tuple-element.28), channel_id=1, source_target_pairs={{0,8},{1,17},{8,0},{9,25},{16,24},{17,1},{24,16},{25,9},{2,10},{3,... | collective-permute-start | bytes 393224 | tf_op jit(solution)/shard_map/ppermute | solution.py:295
  23.3 0.6 %collective-permute-start.6 = (f32[1,2,128,128]{3,2,1,0:T(8,128)S(1)}, f32[1,2,128,128]{3,2,1,0:T(8,128)S(1)}, u32[]{:S(2)}, u32[]{:S(2)}) collective-permute-start(f32[1,2,128,128]{3,2,1,0:T(8,128)S(1)} %get-tuple-element.29), channel_id=1, source_target_pairs={{0,16},{1,9},{8,24},{9,1},{16,0},{17,25},{24,8},{25,17},{2,18},{3,... | collective-permute-start | bytes 393224 | tf_op jit(solution)/shard_map/ppermute | solution.py:295
  23.9 1.2 %collective-permute-done.7.refs_0_ = f32[1,2,128,128]{3,2,1,0:T(8,128)S(1)} collective-permute-done((f32[1,2,128,128]{3,2,1,0:T(8,128)S(1)}, f32[1,2,128,128]{3,2,1,0:T(8,128)S(1)}, u32[]{:S(2)}, u32[]{:S(2)}) %collective-permute-start.7) | collective-permute-done | bytes 131104 | tf_op jit(solution)/shard_map/ppermute | solution.py:365
  25.1 2.5 %collective-permute-start.11 = (f32[1,2,128,128]{3,2,1,0:T(8,128)S(1)}, f32[1,2,128,128]{3,2,1,0:T(8,128)S(1)}, u32[]{:S(2)}, u32[]{:S(2)}) collective-permute-start(f32[1,2,128,128]{3,2,1,0:T(8,128)S(1)} %collective-permute-done.7.refs_0_), channel_id=1, source_target_pairs={{0,2},{2,4},{4,6},{6,7},{7,5},{5,3},{3,1},{1,0},{8,10},{10,12},{12... | collective-permute-start | bytes 393224 | tf_op jit(solution)/shard_map/ppermute | solution.py:365
  27.6 0.8 %collective-permute-done.5.refs_1_ = f32[1,2,128,128]{3,2,1,0:T(8,128)S(1)} collective-permute-done((f32[1,2,128,128]{3,2,1,0:T(8,128)S(1)}, f32[1,2,128,128]{3,2,1,0:T(8,128)S(1)}, u32[]{:S(2)}, u32[]{:S(2)}) %collective-permute-start.5) | collective-permute-done | bytes 131104 | tf_op jit(solution)/shard_map/ppermute | solution.py:295
  28.3 0.1 collective-permute-start.9
  28.5 0.4 collective-permute-start.10
  28.9 1.2 %collective-permute-done.11.refs_0_ = f32[1,2,128,128]{3,2,1,0:T(8,128)S(1)} collective-permute-done((f32[1,2,128,128]{3,2,1,0:T(8,128)S(1)}, f32[1,2,128,128]{3,2,1,0:T(8,128)S(1)}, u32[]{:S(2)}, u32[]{:S(2)}) %collective-permute-start.11) | collective-permute-done | bytes 131104 | tf_op jit(solution)/shard_map/ppermute | solution.py:365
  30.1 2.4 %collective-permute-done.12.refs_0_ = f32[1,2,128,128]{3,2,1,0:T(8,128)S(1)} collective-permute-done((f32[1,2,128,128]{3,2,1,0:T(8,128)S(1)}, f32[1,2,128,128]{3,2,1,0:T(8,128)S(1)}, u32[]{:S(2)}, u32[]{:S(2)}) %collective-permute-start.12) | collective-permute-done | bytes 131104 | tf_op jit(solution)/shard_map/ppermute | solution.py:365
  32.6 1.7 %collective-permute-start.14 = (f32[2,2,128,128]{3,2,1,0:T(8,128)S(1)}, f32[2,2,128,128]{3,2,1,0:T(8,128)S(1)}, u32[]{:S(2)}, u32[]{:S(2)}) collective-permute-start(f32[2,2,128,128]{3,2,1,0:T(8,128)S(1)} %momentum.8.refs_1_), channel_id=1, source_target_pairs={{0,2},{2,4},{4,6},{6,7},{7,5},{5,3},{3,1},{1,0},{8,10},{10,12},{12... | collective-permute-start | bytes 786440 | tf_op jit(solution)/shard_map/ppermute | solution.py:365
  34.4 0.2 collective-permute-start.15
  34.6 1.8 %collective-permute-start.17 = (f32[1,2,128,128]{3,2,1,0:T(8,128)S(1)}, f32[1,2,128,128]{3,2,1,0:T(8,128)S(1)}, u32[]{:S(2)}, u32[]{:S(2)}) collective-permute-start(f32[1,2,128,128]{3,2,1,0:T(8,128)S(1)} %momentum.9.refs_2_), channel_id=1, source_target_pairs={{0,2},{2,4},{4,6},{6,7},{7,5},{5,3},{3,1},{1,0},{8,10},{10,12},{12... | collective-permute-start | bytes 393224 | tf_op jit(solution)/shard_map/ppermute | solution.py:365
  36.5 7.6 %collective-permute-done.15.refs_2_ = f32[1,2,128,128]{3,2,1,0:T(8,128)S(1)} collective-permute-done((f32[1,2,128,128]{3,2,1,0:T(8,128)S(1)}, f32[1,2,128,128]{3,2,1,0:T(8,128)S(1)}, u32[]{:S(2)}, u32[]{:S(2)}) %collective-permute-start.15) | collective-permute-done | bytes 131104 | tf_op jit(solution)/shard_map/ppermute | solution.py:365
  44.1 1.7 %collective-permute-start.16 = (f32[2,2,128,128]{3,2,1,0:T(8,128)S(1)}, f32[2,2,128,128]{3,2,1,0:T(8,128)S(1)}, u32[]{:S(2)}, u32[]{:S(2)}) collective-permute-start(f32[2,2,128,128]{3,2,1,0:T(8,128)S(1)} %collective-permute-done.14.refs_1_), channel_id=1, source_target_pairs={{0,2},{2,4},{4,6},{6,7},{7,5},{5,3},{3,1},{1,0},{8,10},{10,12},{12... | collective-permute-start | bytes 786440 | tf_op jit(solution)/shard_map/ppermute | solution.py:365
  45.8 2.0 %collective-permute-start.18 = (f32[1,2,128,128]{3,2,1,0:T(8,128)S(1)}, f32[1,2,128,128]{3,2,1,0:T(8,128)S(1)}, u32[]{:S(2)}, u32[]{:S(2)}) collective-permute-start(f32[1,2,128,128]{3,2,1,0:T(8,128)S(1)} %collective-permute-done.17.refs_2_), channel_id=1, source_target_pairs={{0,2},{2,4},{4,6},{6,7},{7,5},{5,3},{3,1},{1,0},{8,10},{10,12},{12... | collective-permute-start | bytes 393224 | tf_op jit(solution)/shard_map/ppermute | solution.py:365
  48.0 0.6 %copy-done = s32[4]{0:T(128)S(1)} copy-done((s32[4]{0:T(128)S(1)}, s32[4]{0:T(128)}, u32[]{:S(2)}) %copy-start) | copy-done | bytes 40
  48.6 0.9 %local.1 = (f32[4,2,128,128]{3,2,1,0:T(8,128)S(1)}, f32[4,2,128,128]{3,2,1,0:T(8,128)S(1)}, f32[16,128]{1,0:T(8,128)S(1)}) custom-call(s32[4]{0:T(128)S(1)} %copy-done, f32[4]{0:T(128)S(1)} %copy-done.1, f32[4,2,128,128]{3,2,1,0:T(8,128)S(1)} %by_energy.6.zero_ref, f32[4,2,128,128]{3,2,1,0:T(8,128)S(1)} %by_energy.7.one_ref), custom_call_target="tpu_custom_call" | custom-call | tf_op jit(solution)/shard_map/local/pallas_call | solution.py:383
  49.6 0.6 %mix.2 = (f32[4,2,128,128]{3,2,1,0:T(8,128)S(1)}, f32[4,2,128,128]{3,2,1,0:T(8,128)S(1)}) custom-call(f32[16,128]{1,0:T(8,128)S(1)} %get-tuple-element.34.table_ref, f32[4,2,128,128]{3,2,1,0:T(8,128)S(1)} %by_energy.10.refs_0_, f32[4,2,128,128]{3,2,1,0:T(8,128)S(1)} %by_energy.11.refs_1_, f32[4,2,128,128]{3,2,1,0:T(8,128)S(1)} %get-tuple-element.36.refs_2_, ...), custom_call_target="tpu_custom_call" | custom-call | tf_op jit(solution)/shard_map/mix/pallas_call | solution.py:394
  50.2 4.0 %collective-permute-done.18.refs_2_ = f32[1,2,128,128]{3,2,1,0:T(8,128)S(1)} collective-permute-done((f32[1,2,128,128]{3,2,1,0:T(8,128)S(1)}, f32[1,2,128,128]{3,2,1,0:T(8,128)S(1)}, u32[]{:S(2)}, u32[]{:S(2)}) %collective-permute-start.18) | collective-permute-done | bytes 131104 | tf_op jit(solution)/shard_map/ppermute | solution.py:365
  54.3 0.7 %collective-permute-done.21.refs_2_ = f32[1,2,128,128]{3,2,1,0:T(8,128)S(1)} collective-permute-done((f32[1,2,128,128]{3,2,1,0:T(8,128)S(1)}, f32[1,2,128,128]{3,2,1,0:T(8,128)S(1)}, u32[]{:S(2)}, u32[]{:S(2)}) %collective-permute-start.21) | collective-permute-done | bytes 131104 | tf_op jit(solution)/shard_map/ppermute | solution.py:365
  55.0 1.2 %mix.3 = (f32[4,2,128,128]{3,2,1,0:T(8,128)}, f32[4,2,128,128]{3,2,1,0:T(8,128)}) custom-call(f32[16,128]{1,0:T(8,128)S(1)} %get-tuple-element.34.table_ref, f32[4,2,128,128]{3,2,1,0:T(8,128)S(1)} %by_energy.8.refs_0_, f32[4,2,128,128]{3,2,1,0:T(8,128)S(1)} %by_energy.9.refs_1_, f32[4,2,128,128]{3,2,1,0:T(8,128)S(1)} %get-tuple-element.37.refs_2_, ...), custom_call_target="tpu_custom_call" | custom-call | tf_op jit(solution)/shard_map/mix/pallas_call | solution.py:394
  (35 shorter events, 0.5 us)
Async XLA Ops:
  2.9 9.3 %collective-permute-start = (f32[3,128,128]{2,1,0:T(8,128)S(1)}, f32[3,128,128]{2,1,0:T(8,128)S(1)}, u32[]{:S(2)}, u32[]{:S(2)}) collective-permute-start(f32[3,128,128]{2,1,0:T(8,128)S(1)} %get-tuple-element.23), channel_id=1, source_target_pairs={{0,24},{1,25},{8,16},{9,17},{16,8},{17,9},{24,0},{25,1},{2,26},{3,... | collective-permute-start | bytes 589832 | tf_op jit(solution)/shard_map/ppermute | solution.py:295
  6.9 9.4 %collective-permute-start.1 = (f32[3,128,128]{2,1,0:T(8,128)S(1)}, f32[3,128,128]{2,1,0:T(8,128)S(1)}, u32[]{:S(2)}, u32[]{:S(2)}) collective-permute-start(f32[3,128,128]{2,1,0:T(8,128)S(1)} %get-tuple-element.24), channel_id=1, source_target_pairs={{0,8},{1,17},{8,0},{9,25},{16,24},{17,1},{24,16},{25,9},{2,10},{3,... | collective-permute-start | bytes 589832 | tf_op jit(solution)/shard_map/ppermute | solution.py:295
  9.6 6.6 %collective-permute-start.2 = (f32[3,128,128]{2,1,0:T(8,128)S(1)}, f32[3,128,128]{2,1,0:T(8,128)S(1)}, u32[]{:S(2)}, u32[]{:S(2)}) collective-permute-start(f32[3,128,128]{2,1,0:T(8,128)S(1)} %get-tuple-element.25), channel_id=1, source_target_pairs={{0,16},{1,9},{8,24},{9,1},{16,0},{17,25},{24,8},{25,17},{2,18},{3,... | collective-permute-start | bytes 589832 | tf_op jit(solution)/shard_map/ppermute | solution.py:295
  18.5 1.7 %collective-permute-start.3 = (f32[1,2,128,128]{3,2,1,0:T(8,128)S(1)}, f32[1,2,128,128]{3,2,1,0:T(8,128)S(1)}, u32[]{:S(2)}, u32[]{:S(2)}) collective-permute-start(f32[1,2,128,128]{3,2,1,0:T(8,128)S(1)} %get-tuple-element.26.refs_0_), channel_id=1, source_target_pairs={{0,1},{1,0},{2,3},{3,2},{4,5},{5,4},{6,7},{7,6},{8,9},{9,8},{10,11... | collective-permute-start | bytes 393224 | tf_op jit(solution)/shard_map/ppermute | solution.py:377
  18.6 9.0 %collective-permute-start.4 = (f32[1,2,128,128]{3,2,1,0:T(8,128)S(1)}, f32[1,2,128,128]{3,2,1,0:T(8,128)S(1)}, u32[]{:S(2)}, u32[]{:S(2)}) collective-permute-start(f32[1,2,128,128]{3,2,1,0:T(8,128)S(1)} %get-tuple-element.27), channel_id=1, source_target_pairs={{0,24},{1,25},{8,16},{9,17},{16,8},{17,9},{24,0},{25,1},{2,26},{3,... | collective-permute-start | bytes 393224 | tf_op jit(solution)/shard_map/ppermute | solution.py:295
  20.2 4.9 %collective-permute-start.7 = (f32[1,2,128,128]{3,2,1,0:T(8,128)S(1)}, f32[1,2,128,128]{3,2,1,0:T(8,128)S(1)}, u32[]{:S(2)}, u32[]{:S(2)}) collective-permute-start(f32[1,2,128,128]{3,2,1,0:T(8,128)S(1)} %momentum.6.refs_0_), channel_id=1, source_target_pairs={{0,2},{2,4},{4,6},{6,7},{7,5},{5,3},{3,1},{1,0},{8,10},{10,12},{12... | collective-permute-start | bytes 393224 | tf_op jit(solution)/shard_map/ppermute | solution.py:365
  21.9 5.6 %collective-permute-start.8 = (f32[1,2,128,128]{3,2,1,0:T(8,128)S(1)}, f32[1,2,128,128]{3,2,1,0:T(8,128)S(1)}, u32[]{:S(2)}, u32[]{:S(2)}) collective-permute-start(f32[1,2,128,128]{3,2,1,0:T(8,128)S(1)} %momentum.7.refs_0_), channel_id=1, source_target_pairs={{2,0},{4,2},{6,4},{7,6},{5,7},{3,5},{1,3},{0,1},{10,8},{12,10},{14... | collective-permute-start | bytes 393224 | tf_op jit(solution)/shard_map/ppermute | solution.py:365
  21.9 6.4 %collective-permute-start.5 = (f32[1,2,128,128]{3,2,1,0:T(8,128)S(1)}, f32[1,2,128,128]{3,2,1,0:T(8,128)S(1)}, u32[]{:S(2)}, u32[]{:S(2)}) collective-permute-start(f32[1,2,128,128]{3,2,1,0:T(8,128)S(1)} %get-tuple-element.28), channel_id=1, source_target_pairs={{0,8},{1,17},{8,0},{9,25},{16,24},{17,1},{24,16},{25,9},{2,10},{3,... | collective-permute-start | bytes 393224 | tf_op jit(solution)/shard_map/ppermute | solution.py:295
  23.3 5.1 %collective-permute-start.6 = (f32[1,2,128,128]{3,2,1,0:T(8,128)S(1)}, f32[1,2,128,128]{3,2,1,0:T(8,128)S(1)}, u32[]{:S(2)}, u32[]{:S(2)}) collective-permute-start(f32[1,2,128,128]{3,2,1,0:T(8,128)S(1)} %get-tuple-element.29), channel_id=1, source_target_pairs={{0,16},{1,9},{8,24},{9,1},{16,0},{17,25},{24,8},{25,17},{2,18},{3,... | collective-permute-start | bytes 393224 | tf_op jit(solution)/shard_map/ppermute | solution.py:295
  25.1 5.0 %collective-permute-start.11 = (f32[1,2,128,128]{3,2,1,0:T(8,128)S(1)}, f32[1,2,128,128]{3,2,1,0:T(8,128)S(1)}, u32[]{:S(2)}, u32[]{:S(2)}) collective-permute-start(f32[1,2,128,128]{3,2,1,0:T(8,128)S(1)} %collective-permute-done.7.refs_0_), channel_id=1, source_target_pairs={{0,2},{2,4},{4,6},{6,7},{7,5},{5,3},{3,1},{1,0},{8,10},{10,12},{12... | collective-permute-start | bytes 393224 | tf_op jit(solution)/shard_map/ppermute | solution.py:365
  27.5 5.0 %collective-permute-start.12 = (f32[1,2,128,128]{3,2,1,0:T(8,128)S(1)}, f32[1,2,128,128]{3,2,1,0:T(8,128)S(1)}, u32[]{:S(2)}, u32[]{:S(2)}) collective-permute-start(f32[1,2,128,128]{3,2,1,0:T(8,128)S(1)} %collective-permute-done.8.refs_0_), channel_id=1, source_target_pairs={{2,0},{4,2},{6,4},{7,6},{5,7},{3,5},{1,3},{0,1},{10,8},{12,10},{14... | collective-permute-start | bytes 393224 | tf_op jit(solution)/shard_map/ppermute | solution.py:365
  28.3 4.2 %collective-permute-start.9 = (f32[1,2,128,128]{3,2,1,0:T(8,128)S(1)}, f32[1,2,128,128]{3,2,1,0:T(8,128)S(1)}, u32[]{:S(2)}, u32[]{:S(2)}) collective-permute-start(f32[1,2,128,128]{3,2,1,0:T(8,128)S(1)} %collective-permute-done.4.refs_0_), channel_id=1, source_target_pairs={{0,1},{1,0},{2,3},{3,2},{4,5},{5,4},{6,7},{7,6},{8,9},{9,8},{10,11... | collective-permute-start | bytes 393224 | tf_op jit(solution)/shard_map/ppermute | solution.py:377
  28.5 4.1 %collective-permute-start.10 = (f32[1,2,128,128]{3,2,1,0:T(8,128)S(1)}, f32[1,2,128,128]{3,2,1,0:T(8,128)S(1)}, u32[]{:S(2)}, u32[]{:S(2)}) collective-permute-start(f32[1,2,128,128]{3,2,1,0:T(8,128)S(1)} %collective-permute-done.5.refs_1_), channel_id=1, source_target_pairs={{0,1},{1,0},{2,3},{3,2},{4,5},{5,4},{6,7},{7,6},{8,9},{9,8},{10,11... | collective-permute-start | bytes 393224 | tf_op jit(solution)/shard_map/ppermute | solution.py:377
  32.5 1.8 %collective-permute-start.13 = (f32[1,2,128,128]{3,2,1,0:T(8,128)S(1)}, f32[1,2,128,128]{3,2,1,0:T(8,128)S(1)}, u32[]{:S(2)}, u32[]{:S(2)}) collective-permute-start(f32[1,2,128,128]{3,2,1,0:T(8,128)S(1)} %collective-permute-done.6.refs_0_), channel_id=1, source_target_pairs={{0,1},{1,0},{2,3},{3,2},{4,5},{5,4},{6,7},{7,6},{8,9},{9,8},{10,11... | collective-permute-start | bytes 393224 | tf_op jit(solution)/shard_map/ppermute | solution.py:377
  32.6 11.5 %collective-permute-start.14 = (f32[2,2,128,128]{3,2,1,0:T(8,128)S(1)}, f32[2,2,128,128]{3,2,1,0:T(8,128)S(1)}, u32[]{:S(2)}, u32[]{:S(2)}) collective-permute-start(f32[2,2,128,128]{3,2,1,0:T(8,128)S(1)} %momentum.8.refs_1_), channel_id=1, source_target_pairs={{0,2},{2,4},{4,6},{6,7},{7,5},{5,3},{3,1},{1,0},{8,10},{10,12},{12... | collective-permute-start | bytes 786440 | tf_op jit(solution)/shard_map/ppermute | solution.py:365
  34.3 11.5 %collective-permute-start.19 = (f32[2,2,128,128]{3,2,1,0:T(8,128)S(1)}, f32[2,2,128,128]{3,2,1,0:T(8,128)S(1)}, u32[]{:S(2)}, u32[]{:S(2)}) collective-permute-start(f32[2,2,128,128]{3,2,1,0:T(8,128)S(1)} %momentum.10.refs_1_), channel_id=1, source_target_pairs={{2,0},{4,2},{6,4},{7,6},{5,7},{3,5},{1,3},{0,1},{10,8},{12,10},{14... | collective-permute-start | bytes 786440 | tf_op jit(solution)/shard_map/ppermute | solution.py:365
  34.4 9.7 %collective-permute-start.15 = (f32[1,2,128,128]{3,2,1,0:T(8,128)S(1)}, f32[1,2,128,128]{3,2,1,0:T(8,128)S(1)}, u32[]{:S(2)}, u32[]{:S(2)}) collective-permute-start(f32[1,2,128,128]{3,2,1,0:T(8,128)S(1)} %momentum.11.refs_2_), channel_id=1, source_target_pairs={{2,0},{4,2},{6,4},{7,6},{5,7},{3,5},{1,3},{0,1},{10,8},{12,10},{14... | collective-permute-start | bytes 393224 | tf_op jit(solution)/shard_map/ppermute | solution.py:365
  34.6 11.2 %collective-permute-start.17 = (f32[1,2,128,128]{3,2,1,0:T(8,128)S(1)}, f32[1,2,128,128]{3,2,1,0:T(8,128)S(1)}, u32[]{:S(2)}, u32[]{:S(2)}) collective-permute-start(f32[1,2,128,128]{3,2,1,0:T(8,128)S(1)} %momentum.9.refs_2_), channel_id=1, source_target_pairs={{0,2},{2,4},{4,6},{6,7},{7,5},{5,3},{3,1},{1,0},{8,10},{10,12},{12... | collective-permute-start | bytes 393224 | tf_op jit(solution)/shard_map/ppermute | solution.py:365
  44.1 10.2 %collective-permute-start.16 = (f32[2,2,128,128]{3,2,1,0:T(8,128)S(1)}, f32[2,2,128,128]{3,2,1,0:T(8,128)S(1)}, u32[]{:S(2)}, u32[]{:S(2)}) collective-permute-start(f32[2,2,128,128]{3,2,1,0:T(8,128)S(1)} %collective-permute-done.14.refs_1_), channel_id=1, source_target_pairs={{0,2},{2,4},{4,6},{6,7},{7,5},{5,3},{3,1},{1,0},{8,10},{10,12},{12... | collective-permute-start | bytes 786440 | tf_op jit(solution)/shard_map/ppermute | solution.py:365
  45.8 9.2 %collective-permute-start.20 = (f32[2,2,128,128]{3,2,1,0:T(8,128)S(1)}, f32[2,2,128,128]{3,2,1,0:T(8,128)S(1)}, u32[]{:S(2)}, u32[]{:S(2)}) collective-permute-start(f32[2,2,128,128]{3,2,1,0:T(8,128)S(1)} %collective-permute-done.19.refs_1_), channel_id=1, source_target_pairs={{2,0},{4,2},{6,4},{7,6},{5,7},{3,5},{1,3},{0,1},{10,8},{12,10},{14... | collective-permute-start | bytes 786440 | tf_op jit(solution)/shard_map/ppermute | solution.py:365
  45.8 8.4 %collective-permute-start.18 = (f32[1,2,128,128]{3,2,1,0:T(8,128)S(1)}, f32[1,2,128,128]{3,2,1,0:T(8,128)S(1)}, u32[]{:S(2)}, u32[]{:S(2)}) collective-permute-start(f32[1,2,128,128]{3,2,1,0:T(8,128)S(1)} %collective-permute-done.17.refs_2_), channel_id=1, source_target_pairs={{0,2},{2,4},{4,6},{6,7},{7,5},{5,3},{3,1},{1,0},{8,10},{10,12},{12... | collective-permute-start | bytes 393224 | tf_op jit(solution)/shard_map/ppermute | solution.py:365
  47.8 7.1 %collective-permute-start.21 = (f32[1,2,128,128]{3,2,1,0:T(8,128)S(1)}, f32[1,2,128,128]{3,2,1,0:T(8,128)S(1)}, u32[]{:S(2)}, u32[]{:S(2)}) collective-permute-start(f32[1,2,128,128]{3,2,1,0:T(8,128)S(1)} %collective-permute-done.15.refs_2_), channel_id=1, source_target_pairs={{2,0},{4,2},{6,4},{7,6},{5,7},{3,5},{1,3},{0,1},{10,8},{12,10},{14... | collective-permute-start | bytes 393224 | tf_op jit(solution)/shard_map/ppermute | solution.py:365
  47.9 0.7 %copy-start = (s32[4]{0:T(128)S(1)}, s32[4]{0:T(128)}, u32[]{:S(2)}) copy-start(s32[4]{0:T(128)} %shift_ref.1) | copy-start | bytes 52
  47.9 0.7 %copy-start.1 = (f32[4]{0:T(128)S(1)}, f32[4]{0:T(128)}, u32[]{:S(2)}) copy-start(f32[4]{0:T(128)} %weight_ref.1) | copy-start | bytes 52

commit v14 on v11

--- a/solution.py
+++ b/solution.py
@@ -174,6 +174,21 @@
         place(refs[slots : 2 * slots])
 
 
+def sender_kernel(momentum, own_ref, passed_ref, out_ref):
+    place = lax.axis_index("energy")
+    places = lax.axis_size("energy")
+    up = lax.axis_index("mom") == momentum
+    own = (up & (place < places // 2)) | (~up & (place >= places - places // 2))
+
+    @pl.when(own)
+    def _():
+        out_ref[...] = own_ref[...]
+
+    @pl.when(~own)
+    def _():
+        out_ref[...] = passed_ref[...]
+
+
 def by_energy_kernel(momentum, layers, order, *refs):
     here = lax.axis_index("len")
     parts, out_ref = refs[:-1], refs[-1]
@@ -360,7 +375,21 @@
     def hop(value, role):
         return lax.ppermute(value, ("energy", "mom"), ways[role])
 
-    chunks = [[0], [layers - 1], list(range(1, layers - 1))]
+    last, middle = count - 1, count // 2
+    up = [(z, z + 2) for z in range(middle - 1)] + [(z, z + 1) for z in range(middle, last)]
+    up += [(middle - 1, 1)]
+    far_ways = []
+    for m in range(2):
+        pairs = [(z * moms + m, target * moms + m) for z, target in up]
+        pairs += [((last - z) * moms + 1 - m, (last - target) * moms + 1 - m) for z, target in up]
+        far_ways.append(pairs + [(last * moms + m, last * moms + 1 - m), (1 - m, m)])
+
+    def second_hop(own, passed, m):
+        kernel = functools.partial(sender_kernel, m)
+        value = call(kernel, own.shape[0], own, passed, name="sender")
+        return lax.ppermute(value, ("energy", "mom"), far_ways[m])
+
+    chunks = [[0], list(range(1, layers))]
     fields = [[], []]
     hops = [[], []]
     for c in chunks:
@@ -400,12 +429,11 @@
     sums = [retarded, jnp.zeros_like(local_lesser)]
     for d in range(1, reach + 1):
         if d == 1:
-            fields = hops
+            starts, fields = fields, hops
         elif d == 2:
-            ahead = [hop(fields[m][0], m) for m in range(2)]
-            held = [lax.optimization_barrier((fields[m][1], ahead[m]))[0] for m in range(2)]
-            big, _ = lax.optimization_barrier((fields[0][2], fields[1][1]))
-            fields = [[ahead[m], hop(held[m], m), hop([big, fields[1][2]][m], m)] for m in range(2)]
+            ahead = [second_hop(starts[m][0], fields[m][0], m) for m in range(2)]
+            held, _ = lax.optimization_barrier((fields[0][1], ahead))
+            fields = [[ahead[m], second_hop(starts[m][1], (held, fields[1][1])[m], m)] for m in range(2)]
         else:
             fields = [[hop(part, m) for part in fields[m]] for m in range(2)]
         zero, one = (by_energy(m, fields[m]) for m in range(2))

time: 56.2 us -> 60.7 us (1.080)
  starting transfers between devices: 19.7 us -> 25.5 us
  waiting for transfers between devices: 25 us -> 23.5 us
    ppermute x0 -> x4, starting transfers between devices: none -> 13.5 us  [second_hop(): return lax.ppermute(value, ('energy', 'mom'), far_ways[m])]
    ppermute x12 -> x4, waiting for transfers between devices: 13.2 us -> 0.55 us  [hop(): return lax.ppermute(value, ('energy', 'mom'), ways[role])]
    ppermute x0 -> x4, waiting for transfers between devices: none -> 10.7 us  [second_hop(): return lax.ppermute(value, ('energy', 'mom'), far_ways[m])]
    ppermute x12 -> x4, starting transfers between devices: 10.9 us -> 3.23 us  [hop(): return lax.ppermute(value, ('energy', 'mom'), ways[role])]
  transfers between devices with their start and end apart: 22 -> 18, of which waited for: 11 -> 12; matrix products, arithmetic and copies ran while one was open for 0% -> 0% of each run, Pallas kernels for 7% -> 7%
where the time goes in v14:
time: 60.7 us; the launch traced here: 60.4 us
  starting transfers between devices  25.5 us (42%)
  waiting for transfers between devices  23.5 us (39%)
  Pallas kernels  9.89 us (16%)
  between operations  0.87 us (1%)
  local copies, waits for them, and re-layouts  0.64 us (1%)
    ppermute x4, starting transfers between devices, second_hop(): return lax.ppermute(value, ('energy', 'mom'), far_ways[m])  13.5 us
    ppermute x6, waiting for transfers between devices, exchange(): return lax.ppermute(slots[i], ('len', 'mom'), pairs)  10.8 us
    ppermute x4, waiting for transfers between devices, second_hop(): return lax.ppermute(value, ('energy', 'mom'), far_ways[m])  10.7 us
    ppermute x6, starting transfers between devices, exchange(): return lax.ppermute(slots[i], ('len', 'mom'), pairs)  8.23 us
    pallas_call x2, Pallas kernels, inverse(): pl.pallas_call(functools.partial(inverse_kernel, total, layers, slots), o...  4.51 us
    ppermute x4, starting transfers between devices, hop(): return lax.ppermute(value, ('energy', 'mom'), ways[role])  3.23 us
    pallas_call x1, Pallas kernels, shards(): pl.pallas_call(functools.partial(chain_kernel, layers), out_shape=[part]...  2.22 us
    pallas_call x3, Pallas kernels, mix(): pl.pallas_call(functools.partial(mix_kernel, total, items, False, last),...  1.77 us
  transfers between devices with their start and end apart: 18, of which 12 were waited for; matrix products, arithmetic and copies ran while one was open for 0% of the time, Pallas kernels for 7%

profile of v14, /device:TPU:0, one launch (start us, length us, event | category | flops | bytes accessed | tf_op | source)
XLA Modules:
  0.0 60.4 jit_solution(1241804152543793589)
XLA Ops:
  0.6 2.3 %inverse.3 = (f32[3,128,128]{2,1,0:T(8,128)S(1)}, f32[3,128,128]{2,1,0:T(8,128)S(1)}) custom-call(f32[2,128,128]{2,1,0:T(8,128)} %bitcast.9, f32[4,2,128,128]{3,2,1,0:T(8,128)} %bitcast.5, f32[128,128]{1,0:T(8,128)} %bitcast.11, s32[128,128]{1,0:T(8,128)} %pattern_any.3), custom_call_target="tpu_custom_call" | custom-call | flops 402653184 | bytes 262144 | tf_op jit(solution)/shard_map/inverse/pallas_call | solution.py:313
  2.9 4.0 %collective-permute-start = (f32[3,128,128]{2,1,0:T(8,128)S(1)}, f32[3,128,128]{2,1,0:T(8,128)S(1)}, u32[]{:S(2)}, u32[]{:S(2)}) collective-permute-start(f32[3,128,128]{2,1,0:T(8,128)S(1)} %get-tuple-element.24), channel_id=1, source_target_pairs={{0,24},{1,25},{8,16},{9,17},{16,8},{17,9},{24,0},{25,1},{2,26},{3,... | collective-permute-start | bytes 589832 | tf_op jit(solution)/shard_map/ppermute | solution.py:306
  6.9 0.5 collective-permute-start.1
  7.4 2.2 %inverse.2 = (f32[3,128,128]{2,1,0:T(8,128)S(1)}, f32[3,128,128]{2,1,0:T(8,128)S(1)}) custom-call(f32[2,128,128]{2,1,0:T(8,128)} %bitcast.10, f32[4,2,128,128]{3,2,1,0:T(8,128)} %bitcast.6, f32[128,128]{1,0:T(8,128)} %bitcast.12, s32[128,128]{1,0:T(8,128)} %pattern_any.3), custom_call_target="tpu_custom_call" | custom-call | flops 402653184 | bytes 262144 | tf_op jit(solution)/shard_map/inverse/pallas_call | solution.py:313
  9.6 0.2 collective-permute-start.2
  9.8 2.3 %collective-permute-done.refs_1_ = f32[3,128,128]{2,1,0:T(8,128)S(1)} collective-permute-done((f32[3,128,128]{2,1,0:T(8,128)S(1)}, f32[3,128,128]{2,1,0:T(8,128)S(1)}, u32[]{:S(2)}, u32[]{:S(2)}) %collective-permute-start) | collective-permute-done | bytes 196640 | tf_op jit(solution)/shard_map/ppermute | solution.py:306
  12.2 4.1 %collective-permute-done.1.refs_2_ = f32[3,128,128]{2,1,0:T(8,128)S(1)} collective-permute-done((f32[3,128,128]{2,1,0:T(8,128)S(1)}, f32[3,128,128]{2,1,0:T(8,128)S(1)}, u32[]{:S(2)}, u32[]{:S(2)}) %collective-permute-start.1) | collective-permute-done | bytes 196640 | tf_op jit(solution)/shard_map/ppermute | solution.py:306
  16.3 2.2 %chains.1 = (f32[1,2,128,128]{3,2,1,0:T(8,128)S(1)}, f32[1,2,128,128]{3,2,1,0:T(8,128)S(1)}, f32[1,2,128,128]{3,2,1,0:T(8,128)S(1)}, f32[1,2,128,128]{3,2,1,0:T(8,128)S(1)}) custom-call(f32[3,128,128]{2,1,0:T(8,128)S(1)} %get-tuple-element.23.refs_0_, f32[3,128,128]{2,1,0:T(8,128)S(1)} %collective-permute-done.refs_1_, ...), custom_call_target="tpu_custom_call" | custom-call | tf_op jit(solution)/shard_map/chains/pallas_call | solution.py:337
  18.6 1.6 %collective-permute-start.4 = (f32[1,2,128,128]{3,2,1,0:T(8,128)S(1)}, f32[1,2,128,128]{3,2,1,0:T(8,128)S(1)}, u32[]{:S(2)}, u32[]{:S(2)}) collective-permute-start(f32[1,2,128,128]{3,2,1,0:T(8,128)S(1)} %get-tuple-element.28), channel_id=1, source_target_pairs={{0,24},{1,25},{8,16},{9,17},{16,8},{17,9},{24,0},{25,1},{2,26},{3,... | collective-permute-start | bytes 393224 | tf_op jit(solution)/shard_map/ppermute | solution.py:306
  20.2 1.4 %collective-permute-start.5 = (f32[1,2,128,128]{3,2,1,0:T(8,128)S(1)}, f32[1,2,128,128]{3,2,1,0:T(8,128)S(1)}, u32[]{:S(2)}, u32[]{:S(2)}) collective-permute-start(f32[1,2,128,128]{3,2,1,0:T(8,128)S(1)} %get-tuple-element.29), channel_id=1, source_target_pairs={{0,8},{1,17},{8,0},{9,25},{16,24},{17,1},{24,16},{25,9},{2,10},{3,... | collective-permute-start | bytes 393224 | tf_op jit(solution)/shard_map/ppermute | solution.py:306
  21.5 0.6 %collective-permute-start.6 = (f32[1,2,128,128]{3,2,1,0:T(8,128)S(1)}, f32[1,2,128,128]{3,2,1,0:T(8,128)S(1)}, u32[]{:S(2)}, u32[]{:S(2)}) collective-permute-start(f32[1,2,128,128]{3,2,1,0:T(8,128)S(1)} %get-tuple-element.30), channel_id=1, source_target_pairs={{0,16},{1,9},{8,24},{9,1},{16,0},{17,25},{24,8},{25,17},{2,18},{3,... | collective-permute-start | bytes 393224 | tf_op jit(solution)/shard_map/ppermute | solution.py:306
  22.2 1.6 %collective-permute-start.7 = (f32[1,2,128,128]{3,2,1,0:T(8,128)S(1)}, f32[1,2,128,128]{3,2,1,0:T(8,128)S(1)}, u32[]{:S(2)}, u32[]{:S(2)}) collective-permute-start(f32[1,2,128,128]{3,2,1,0:T(8,128)S(1)} %momentum.4.refs_0_.own_ref), channel_id=1, source_target_pairs={{0,2},{2,4},{4,6},{6,7},{7,5},{5,3},{3,1},{1,0},{8,10},{10,12},{12... | collective-permute-start | bytes 393224 | tf_op jit(solution)/shard_map/ppermute | solution.py:376
  23.8 2.1 %collective-permute-done.4.refs_0_ = f32[1,2,128,128]{3,2,1,0:T(8,128)S(1)} collective-permute-done((f32[1,2,128,128]{3,2,1,0:T(8,128)S(1)}, f32[1,2,128,128]{3,2,1,0:T(8,128)S(1)}, u32[]{:S(2)}, u32[]{:S(2)}) %collective-permute-start.4) | collective-permute-done | bytes 131104 | tf_op jit(solution)/shard_map/ppermute | solution.py:306
  25.9 2.3 %collective-permute-done.5.refs_1_ = f32[1,2,128,128]{3,2,1,0:T(8,128)S(1)} collective-permute-done((f32[1,2,128,128]{3,2,1,0:T(8,128)S(1)}, f32[1,2,128,128]{3,2,1,0:T(8,128)S(1)}, u32[]{:S(2)}, u32[]{:S(2)}) %collective-permute-start.5) | collective-permute-done | bytes 131104 | tf_op jit(solution)/shard_map/ppermute | solution.py:306
  28.2 0.5 collective-permute-done.8.passed_ref.refs_0_
  28.8 0.5 collective-permute-start.10
  29.3 0.8 %collective-permute-done.9.refs_3_ = f32[1,2,128,128]{3,2,1,0:T(8,128)S(1)} collective-permute-done((f32[1,2,128,128]{3,2,1,0:T(8,128)S(1)}, f32[1,2,128,128]{3,2,1,0:T(8,128)S(1)}, u32[]{:S(2)}, u32[]{:S(2)}) %collective-permute-start.9) | collective-permute-done | bytes 131104 | tf_op jit(solution)/shard_map/ppermute | solution.py:399
  30.1 0.2 collective-permute-done.10.refs_4_
  30.3 0.3 collective-permute-done.11.refs_5_
  30.6 1.6 %collective-permute-start.16 = (f32[3,2,128,128]{3,2,1,0:T(8,128)S(1)}, f32[3,2,128,128]{3,2,1,0:T(8,128)S(1)}, u32[]{:S(2)}, u32[]{:S(2)}) collective-permute-start(f32[3,2,128,128]{3,2,1,0:T(8,128)S(1)} %momentum.6.refs_1_.own_ref), channel_id=1, source_target_pairs={{0,2},{2,4},{4,6},{6,7},{7,5},{5,3},{3,1},{1,0},{8,10},{10,12},{12... | collective-permute-start | bytes 1179656 | tf_op jit(solution)/shard_map/ppermute | solution.py:376
  32.3 4.9 %collective-permute-start.15 = (f32[1,2,128,128]{3,2,1,0:T(8,128)S(1)}, f32[1,2,128,128]{3,2,1,0:T(8,128)S(1)}, u32[]{:S(2)}, u32[]{:S(2)}) collective-permute-start(f32[1,2,128,128]{3,2,1,0:T(8,128)S(1)} %sender.6), channel_id=1, source_target_pairs={{0,4},{4,6},{2,2},{7,3},{3,1},{5,5},{6,7},{1,0},{8,12},{12,14},{10... | collective-permute-start | bytes 393224 | tf_op jit(solution)/shard_map/ppermute | solution.py:390
  37.3 1.9 %collective-permute-start.12 = (f32[1,2,128,128]{3,2,1,0:T(8,128)S(1)}, f32[1,2,128,128]{3,2,1,0:T(8,128)S(1)}, u32[]{:S(2)}, u32[]{:S(2)}) collective-permute-start(f32[1,2,128,128]{3,2,1,0:T(8,128)S(1)} %sender.4), channel_id=1, source_target_pairs={{1,5},{5,7},{3,3},{6,2},{2,0},{4,4},{7,6},{0,1},{9,13},{13,15},{11... | collective-permute-start | bytes 393224 | tf_op jit(solution)/shard_map/ppermute | solution.py:390
  39.2 4.8 %collective-permute-done.15.refs_0_ = f32[1,2,128,128]{3,2,1,0:T(8,128)S(1)} collective-permute-done((f32[1,2,128,128]{3,2,1,0:T(8,128)S(1)}, f32[1,2,128,128]{3,2,1,0:T(8,128)S(1)}, u32[]{:S(2)}, u32[]{:S(2)}) %collective-permute-start.15) | collective-permute-done | bytes 131104 | tf_op jit(solution)/shard_map/ppermute | solution.py:390
  44.1 0.6 %collective-permute-done.12.refs_0_ = f32[1,2,128,128]{3,2,1,0:T(8,128)S(1)} collective-permute-done((f32[1,2,128,128]{3,2,1,0:T(8,128)S(1)}, f32[1,2,128,128]{3,2,1,0:T(8,128)S(1)}, u32[]{:S(2)}, u32[]{:S(2)}) %collective-permute-start.12) | collective-permute-done | bytes 131104 | tf_op jit(solution)/shard_map/ppermute | solution.py:390
  44.7 4.7 %collective-permute-start.17 = (f32[3,2,128,128]{3,2,1,0:T(8,128)S(1)}, f32[3,2,128,128]{3,2,1,0:T(8,128)S(1)}, u32[]{:S(2)}, u32[]{:S(2)}) collective-permute-start(f32[3,2,128,128]{3,2,1,0:T(8,128)S(1)} %sender.7), channel_id=1, source_target_pairs={{0,4},{4,6},{2,2},{7,3},{3,1},{5,5},{6,7},{1,0},{8,12},{12,14},{10... | collective-permute-start | bytes 1179656 | tf_op jit(solution)/shard_map/ppermute | solution.py:390
  49.5 1.9 %collective-permute-start.14 = (f32[3,2,128,128]{3,2,1,0:T(8,128)S(1)}, f32[3,2,128,128]{3,2,1,0:T(8,128)S(1)}, u32[]{:S(2)}, u32[]{:S(2)}) collective-permute-start(f32[3,2,128,128]{3,2,1,0:T(8,128)S(1)} %sender.5), channel_id=1, source_target_pairs={{1,5},{5,7},{3,3},{6,2},{2,0},{4,4},{7,6},{0,1},{9,13},{13,15},{11... | collective-permute-start | bytes 1179656 | tf_op jit(solution)/shard_map/ppermute | solution.py:390
  51.6 0.6 copy-done
  52.2 0.9 %local.1 = (f32[4,2,128,128]{3,2,1,0:T(8,128)S(1)}, f32[4,2,128,128]{3,2,1,0:T(8,128)S(1)}, f32[16,128]{1,0:T(8,128)S(1)}) custom-call(s32[4]{0:T(128)S(1)} %copy-done, f32[4]{0:T(128)S(1)} %copy-done.1, f32[4,2,128,128]{3,2,1,0:T(8,128)S(1)} %by_energy.6.zero_ref, f32[4,2,128,128]{3,2,1,0:T(8,128)S(1)} %by_energy.7.one_ref), custom_call_target="tpu_custom_call" | custom-call | tf_op jit(solution)/shard_map/local/pallas_call | solution.py:405
  53.3 0.6 mix.3
  53.9 4.5 %collective-permute-done.17.refs_1_ = f32[3,2,128,128]{3,2,1,0:T(8,128)S(1)} collective-permute-done((f32[3,2,128,128]{3,2,1,0:T(8,128)S(1)}, f32[3,2,128,128]{3,2,1,0:T(8,128)S(1)}, u32[]{:S(2)}, u32[]{:S(2)}) %collective-permute-start.17) | collective-permute-done | bytes 393248 | tf_op jit(solution)/shard_map/ppermute | solution.py:390
  58.4 0.8 %collective-permute-done.14.refs_1_ = f32[3,2,128,128]{3,2,1,0:T(8,128)S(1)} collective-permute-done((f32[3,2,128,128]{3,2,1,0:T(8,128)S(1)}, f32[3,2,128,128]{3,2,1,0:T(8,128)S(1)}, u32[]{:S(2)}, u32[]{:S(2)}) %collective-permute-start.14) | collective-permute-done | bytes 393248 | tf_op jit(solution)/shard_map/ppermute | solution.py:390
  59.2 1.2 %mix.5 = (f32[4,2,128,128]{3,2,1,0:T(8,128)}, f32[4,2,128,128]{3,2,1,0:T(8,128)}) custom-call(f32[16,128]{1,0:T(8,128)S(1)} %get-tuple-element.34.table_ref, f32[4,2,128,128]{3,2,1,0:T(8,128)S(1)} %by_energy.8.refs_0_, f32[4,2,128,128]{3,2,1,0:T(8,128)S(1)} %get-tuple-element.39.refs_1_, f32[4,2,128,128]{3,2,1,0:T(8,128)S(1)} %get-tuple-element.40.refs_2_, ...), custom_call_target="tpu_custom_call" | custom-call | tf_op jit(solution)/shard_map/mix/pallas_call | solution.py:418
  (30 shorter events, 0.7 us)
Async XLA Ops:
  2.9 9.3 %collective-permute-start = (f32[3,128,128]{2,1,0:T(8,128)S(1)}, f32[3,128,128]{2,1,0:T(8,128)S(1)}, u32[]{:S(2)}, u32[]{:S(2)}) collective-permute-start(f32[3,128,128]{2,1,0:T(8,128)S(1)} %get-tuple-element.24), channel_id=1, source_target_pairs={{0,24},{1,25},{8,16},{9,17},{16,8},{17,9},{24,0},{25,1},{2,26},{3,... | collective-permute-start | bytes 589832 | tf_op jit(solution)/shard_map/ppermute | solution.py:306
  6.9 9.4 %collective-permute-start.1 = (f32[3,128,128]{2,1,0:T(8,128)S(1)}, f32[3,128,128]{2,1,0:T(8,128)S(1)}, u32[]{:S(2)}, u32[]{:S(2)}) collective-permute-start(f32[3,128,128]{2,1,0:T(8,128)S(1)} %get-tuple-element.25), channel_id=1, source_target_pairs={{0,8},{1,17},{8,0},{9,25},{16,24},{17,1},{24,16},{25,9},{2,10},{3,... | collective-permute-start | bytes 589832 | tf_op jit(solution)/shard_map/ppermute | solution.py:306
  9.6 6.6 %collective-permute-start.2 = (f32[3,128,128]{2,1,0:T(8,128)S(1)}, f32[3,128,128]{2,1,0:T(8,128)S(1)}, u32[]{:S(2)}, u32[]{:S(2)}) collective-permute-start(f32[3,128,128]{2,1,0:T(8,128)S(1)} %get-tuple-element.26), channel_id=1, source_target_pairs={{0,16},{1,9},{8,24},{9,1},{16,0},{17,25},{24,8},{25,17},{2,18},{3,... | collective-permute-start | bytes 589832 | tf_op jit(solution)/shard_map/ppermute | solution.py:306
  18.5 3.6 %collective-permute-start.3 = (f32[1,2,128,128]{3,2,1,0:T(8,128)S(1)}, f32[1,2,128,128]{3,2,1,0:T(8,128)S(1)}, u32[]{:S(2)}, u32[]{:S(2)}) collective-permute-start(f32[1,2,128,128]{3,2,1,0:T(8,128)S(1)} %get-tuple-element.27.refs_0_), channel_id=1, source_target_pairs={{0,1},{1,0},{2,3},{3,2},{4,5},{5,4},{6,7},{7,6},{8,9},{9,8},{10,11... | collective-permute-start | bytes 393224 | tf_op jit(solution)/shard_map/ppermute | solution.py:399
  18.6 7.3 %collective-permute-start.4 = (f32[1,2,128,128]{3,2,1,0:T(8,128)S(1)}, f32[1,2,128,128]{3,2,1,0:T(8,128)S(1)}, u32[]{:S(2)}, u32[]{:S(2)}) collective-permute-start(f32[1,2,128,128]{3,2,1,0:T(8,128)S(1)} %get-tuple-element.28), channel_id=1, source_target_pairs={{0,24},{1,25},{8,16},{9,17},{16,8},{17,9},{24,0},{25,1},{2,26},{3,... | collective-permute-start | bytes 393224 | tf_op jit(solution)/shard_map/ppermute | solution.py:306
  20.2 8.0 %collective-permute-start.5 = (f32[1,2,128,128]{3,2,1,0:T(8,128)S(1)}, f32[1,2,128,128]{3,2,1,0:T(8,128)S(1)}, u32[]{:S(2)}, u32[]{:S(2)}) collective-permute-start(f32[1,2,128,128]{3,2,1,0:T(8,128)S(1)} %get-tuple-element.29), channel_id=1, source_target_pairs={{0,8},{1,17},{8,0},{9,25},{16,24},{17,1},{24,16},{25,9},{2,10},{3,... | collective-permute-start | bytes 393224 | tf_op jit(solution)/shard_map/ppermute | solution.py:306
  21.5 6.7 %collective-permute-start.6 = (f32[1,2,128,128]{3,2,1,0:T(8,128)S(1)}, f32[1,2,128,128]{3,2,1,0:T(8,128)S(1)}, u32[]{:S(2)}, u32[]{:S(2)}) collective-permute-start(f32[1,2,128,128]{3,2,1,0:T(8,128)S(1)} %get-tuple-element.30), channel_id=1, source_target_pairs={{0,16},{1,9},{8,24},{9,1},{16,0},{17,25},{24,8},{25,17},{2,18},{3,... | collective-permute-start | bytes 393224 | tf_op jit(solution)/shard_map/ppermute | solution.py:306
  22.2 6.0 %collective-permute-start.7 = (f32[1,2,128,128]{3,2,1,0:T(8,128)S(1)}, f32[1,2,128,128]{3,2,1,0:T(8,128)S(1)}, u32[]{:S(2)}, u32[]{:S(2)}) collective-permute-start(f32[1,2,128,128]{3,2,1,0:T(8,128)S(1)} %momentum.4.refs_0_.own_ref), channel_id=1, source_target_pairs={{0,2},{2,4},{4,6},{6,7},{7,5},{5,3},{3,1},{1,0},{8,10},{10,12},{12... | collective-permute-start | bytes 393224 | tf_op jit(solution)/shard_map/ppermute | solution.py:376
  23.8 5.0 %collective-permute-start.8 = (f32[1,2,128,128]{3,2,1,0:T(8,128)S(1)}, f32[1,2,128,128]{3,2,1,0:T(8,128)S(1)}, u32[]{:S(2)}, u32[]{:S(2)}) collective-permute-start(f32[1,2,128,128]{3,2,1,0:T(8,128)S(1)} %momentum.5.refs_0_.own_ref), channel_id=1, source_target_pairs={{2,0},{4,2},{6,4},{7,6},{5,7},{3,5},{1,3},{0,1},{10,8},{12,10},{14... | collective-permute-start | bytes 393224 | tf_op jit(solution)/shard_map/ppermute | solution.py:376
  28.7 1.3 %collective-permute-start.9 = (f32[1,2,128,128]{3,2,1,0:T(8,128)S(1)}, f32[1,2,128,128]{3,2,1,0:T(8,128)S(1)}, u32[]{:S(2)}, u32[]{:S(2)}) collective-permute-start(f32[1,2,128,128]{3,2,1,0:T(8,128)S(1)} %collective-permute-done.4.refs_0_), channel_id=1, source_target_pairs={{0,1},{1,0},{2,3},{3,2},{4,5},{5,4},{6,7},{7,6},{8,9},{9,8},{10,11... | collective-permute-start | bytes 393224 | tf_op jit(solution)/shard_map/ppermute | solution.py:399
  28.8 1.5 %collective-permute-start.10 = (f32[1,2,128,128]{3,2,1,0:T(8,128)S(1)}, f32[1,2,128,128]{3,2,1,0:T(8,128)S(1)}, u32[]{:S(2)}, u32[]{:S(2)}) collective-permute-start(f32[1,2,128,128]{3,2,1,0:T(8,128)S(1)} %collective-permute-done.5.refs_1_), channel_id=1, source_target_pairs={{0,1},{1,0},{2,3},{3,2},{4,5},{5,4},{6,7},{7,6},{8,9},{9,8},{10,11... | collective-permute-start | bytes 393224 | tf_op jit(solution)/shard_map/ppermute | solution.py:399
  29.3 1.3 %collective-permute-start.11 = (f32[1,2,128,128]{3,2,1,0:T(8,128)S(1)}, f32[1,2,128,128]{3,2,1,0:T(8,128)S(1)}, u32[]{:S(2)}, u32[]{:S(2)}) collective-permute-start(f32[1,2,128,128]{3,2,1,0:T(8,128)S(1)} %collective-permute-done.6.refs_2_), channel_id=1, source_target_pairs={{0,1},{1,0},{2,3},{3,2},{4,5},{5,4},{6,7},{7,6},{8,9},{9,8},{10,11... | collective-permute-start | bytes 393224 | tf_op jit(solution)/shard_map/ppermute | solution.py:399
  30.6 14.0 %collective-permute-start.16 = (f32[3,2,128,128]{3,2,1,0:T(8,128)S(1)}, f32[3,2,128,128]{3,2,1,0:T(8,128)S(1)}, u32[]{:S(2)}, u32[]{:S(2)}) collective-permute-start(f32[3,2,128,128]{3,2,1,0:T(8,128)S(1)} %momentum.6.refs_1_.own_ref), channel_id=1, source_target_pairs={{0,2},{2,4},{4,6},{6,7},{7,5},{5,3},{3,1},{1,0},{8,10},{10,12},{12... | collective-permute-start | bytes 1179656 | tf_op jit(solution)/shard_map/ppermute | solution.py:376
  32.3 17.2 %collective-permute-start.13 = (f32[3,2,128,128]{3,2,1,0:T(8,128)S(1)}, f32[3,2,128,128]{3,2,1,0:T(8,128)S(1)}, u32[]{:S(2)}, u32[]{:S(2)}) collective-permute-start(f32[3,2,128,128]{3,2,1,0:T(8,128)S(1)} %momentum.7.refs_1_.own_ref), channel_id=1, source_target_pairs={{2,0},{4,2},{6,4},{7,6},{5,7},{3,5},{1,3},{0,1},{10,8},{12,10},{14... | collective-permute-start | bytes 1179656 | tf_op jit(solution)/shard_map/ppermute | solution.py:376
  32.3 11.7 %collective-permute-start.15 = (f32[1,2,128,128]{3,2,1,0:T(8,128)S(1)}, f32[1,2,128,128]{3,2,1,0:T(8,128)S(1)}, u32[]{:S(2)}, u32[]{:S(2)}) collective-permute-start(f32[1,2,128,128]{3,2,1,0:T(8,128)S(1)} %sender.6), channel_id=1, source_target_pairs={{0,4},{4,6},{2,2},{7,3},{3,1},{5,5},{6,7},{1,0},{8,12},{12,14},{10... | collective-permute-start | bytes 393224 | tf_op jit(solution)/shard_map/ppermute | solution.py:390
  37.3 7.4 %collective-permute-start.12 = (f32[1,2,128,128]{3,2,1,0:T(8,128)S(1)}, f32[1,2,128,128]{3,2,1,0:T(8,128)S(1)}, u32[]{:S(2)}, u32[]{:S(2)}) collective-permute-start(f32[1,2,128,128]{3,2,1,0:T(8,128)S(1)} %sender.4), channel_id=1, source_target_pairs={{1,5},{5,7},{3,3},{6,2},{2,0},{4,4},{7,6},{0,1},{9,13},{13,15},{11... | collective-permute-start | bytes 393224 | tf_op jit(solution)/shard_map/ppermute | solution.py:390
  44.7 13.6 %collective-permute-start.17 = (f32[3,2,128,128]{3,2,1,0:T(8,128)S(1)}, f32[3,2,128,128]{3,2,1,0:T(8,128)S(1)}, u32[]{:S(2)}, u32[]{:S(2)}) collective-permute-start(f32[3,2,128,128]{3,2,1,0:T(8,128)S(1)} %sender.7), channel_id=1, source_target_pairs={{0,4},{4,6},{2,2},{7,3},{3,1},{5,5},{6,7},{1,0},{8,12},{12,14},{10... | collective-permute-start | bytes 1179656 | tf_op jit(solution)/shard_map/ppermute | solution.py:390
  49.5 9.7 %collective-permute-start.14 = (f32[3,2,128,128]{3,2,1,0:T(8,128)S(1)}, f32[3,2,128,128]{3,2,1,0:T(8,128)S(1)}, u32[]{:S(2)}, u32[]{:S(2)}) collective-permute-start(f32[3,2,128,128]{3,2,1,0:T(8,128)S(1)} %sender.5), channel_id=1, source_target_pairs={{1,5},{5,7},{3,3},{6,2},{2,0},{4,4},{7,6},{0,1},{9,13},{13,15},{11... | collective-permute-start | bytes 1179656 | tf_op jit(solution)/shard_map/ppermute | solution.py:390
  51.5 0.7 %copy-start = (s32[4]{0:T(128)S(1)}, s32[4]{0:T(128)}, u32[]{:S(2)}) copy-start(s32[4]{0:T(128)} %shift_ref.1) | copy-start | bytes 52
  51.5 0.7 %copy-start.1 = (f32[4]{0:T(128)S(1)}, f32[4]{0:T(128)}, u32[]{:S(2)}) copy-start(f32[4]{0:T(128)} %weight_ref.1) | copy-start | bytes 52

commit v15 on v13

--- a/solution.py
+++ b/solution.py
@@ -372,12 +372,14 @@
             own, _ = lax.optimization_barrier((own, hops))
             ahead = [hop(hops[m][0], m) for m in range(2)]
         held = [own[i] for i in c]
+        other = [lax.ppermute(v, "mom", both_ways) for v in held]
+        parts = [of_momentum(m, held, other) for m in range(2)]
+        for m in range(2):
+            fields[m].append(parts[m])
         if len(hops[0]) == 2:
-            held, _ = lax.optimization_barrier((held, ahead))
-        other = [lax.ppermute(v, "mom", both_ways) for v in held]
+            parts, _ = lax.optimization_barrier((parts, ahead))
         for m in range(2):
-            fields[m].append(of_momentum(m, held, other))
-            hops[m].append(hop(fields[m][-1], m))
+            hops[m].append(hop(parts[m], m))
     zero, one = (by_energy(m, fields[m]) for m in range(2))
     smem = pl.BlockSpec(memory_space=pltpu.SMEM)
     retarded, local_lesser, table = pl.pallas_call(

time: 56.3 us -> 55.8 us (level)
  starting transfers between devices: 20.5 us -> 19.7 us
    ppermute x6, waiting for transfers between devices: 7.24 us -> 10.8 us  [exchange(): return lax.ppermute(slots[i], ('len', 'mom'), pairs)]
    ppermute x12, waiting for transfers between devices: 17.2 us -> 13.9 us  [hop(): return lax.ppermute(value, ('energy', 'mom'), ways[role])]
    ppermute x12, starting transfers between devices: 11.8 us -> 10.9 us  [hop(): return lax.ppermute(value, ('energy', 'mom'), ways[role])]
  transfers between devices with their start and end apart: 22 -> 22, of which waited for: 9 -> 10; matrix products, arithmetic and copies ran while one was open for 0% -> 0% of each run, Pallas kernels for 7% -> 7%
where the time goes in v15:
time: 55.8 us; the launch traced here: 55.7 us
  waiting for transfers between devices  24.7 us (44%)
  starting transfers between devices  19.7 us (35%)
  Pallas kernels  9.79 us (18%)
  between operations  0.83 us (1%)
  local copies, waits for them, and re-layouts  0.64 us (1%)
    ppermute x12, waiting for transfers between devices, hop(): return lax.ppermute(value, ('energy', 'mom'), ways[role])  13.9 us
    ppermute x12, starting transfers between devices, hop(): return lax.ppermute(value, ('energy', 'mom'), ways[role])  10.9 us
    ppermute x6, waiting for transfers between devices, exchange(): return lax.ppermute(slots[i], ('len', 'mom'), pairs)  10.8 us
    ppermute x6, starting transfers between devices, exchange(): return lax.ppermute(slots[i], ('len', 'mom'), pairs)  8.23 us
    pallas_call x2, Pallas kernels, inverse(): pl.pallas_call(functools.partial(inverse_kernel, total, layers, slots), o...  4.51 us
    pallas_call x1, Pallas kernels, shards(): pl.pallas_call(functools.partial(chain_kernel, layers), out_shape=[part]...  2.22 us
    pallas_call x2, Pallas kernels, mix(): pl.pallas_call(functools.partial(mix_kernel, total, items, False, last),...  1.75 us
  transfers between devices with their start and end apart: 22, of which 10 were waited for; matrix products, arithmetic and copies ran while one was open for 0% of the time, Pallas kernels for 7%

profile of v15, /device:TPU:0, one launch (start us, length us, event | category | flops | bytes accessed | tf_op | source)
XLA Modules:
  0.0 55.7 jit_solution(15847303383831423126)
XLA Ops:
  0.6 2.3 %inverse.3 = (f32[3,128,128]{2,1,0:T(8,128)S(1)}, f32[3,128,128]{2,1,0:T(8,128)S(1)}) custom-call(f32[2,128,128]{2,1,0:T(8,128)} %bitcast.9, f32[4,2,128,128]{3,2,1,0:T(8,128)} %bitcast.5, f32[128,128]{1,0:T(8,128)} %bitcast.11, s32[128,128]{1,0:T(8,128)} %pattern_any.3), custom_call_target="tpu_custom_call" | custom-call | flops 402653184 | bytes 262144 | tf_op jit(solution)/shard_map/inverse/pallas_call | solution.py:302
  2.9 4.0 %collective-permute-start = (f32[3,128,128]{2,1,0:T(8,128)S(1)}, f32[3,128,128]{2,1,0:T(8,128)S(1)}, u32[]{:S(2)}, u32[]{:S(2)}) collective-permute-start(f32[3,128,128]{2,1,0:T(8,128)S(1)} %get-tuple-element.24), channel_id=1, source_target_pairs={{0,24},{1,25},{8,16},{9,17},{16,8},{17,9},{24,0},{25,1},{2,26},{3,... | collective-permute-start | bytes 589832 | tf_op jit(solution)/shard_map/ppermute | solution.py:295
  6.9 0.5 collective-permute-start.1
  7.4 2.2 %inverse.2 = (f32[3,128,128]{2,1,0:T(8,128)S(1)}, f32[3,128,128]{2,1,0:T(8,128)S(1)}) custom-call(f32[2,128,128]{2,1,0:T(8,128)} %bitcast.10, f32[4,2,128,128]{3,2,1,0:T(8,128)} %bitcast.6, f32[128,128]{1,0:T(8,128)} %bitcast.12, s32[128,128]{1,0:T(8,128)} %pattern_any.3), custom_call_target="tpu_custom_call" | custom-call | flops 402653184 | bytes 262144 | tf_op jit(solution)/shard_map/inverse/pallas_call | solution.py:302
  9.6 0.2 collective-permute-start.2
  9.8 2.3 %collective-permute-done.refs_1_ = f32[3,128,128]{2,1,0:T(8,128)S(1)} collective-permute-done((f32[3,128,128]{2,1,0:T(8,128)S(1)}, f32[3,128,128]{2,1,0:T(8,128)S(1)}, u32[]{:S(2)}, u32[]{:S(2)}) %collective-permute-start) | collective-permute-done | bytes 196640 | tf_op jit(solution)/shard_map/ppermute | solution.py:295
  12.2 4.1 %collective-permute-done.1.refs_2_ = f32[3,128,128]{2,1,0:T(8,128)S(1)} collective-permute-done((f32[3,128,128]{2,1,0:T(8,128)S(1)}, f32[3,128,128]{2,1,0:T(8,128)S(1)}, u32[]{:S(2)}, u32[]{:S(2)}) %collective-permute-start.1) | collective-permute-done | bytes 196640 | tf_op jit(solution)/shard_map/ppermute | solution.py:295
  16.3 2.2 %chains.1 = (f32[1,2,128,128]{3,2,1,0:T(8,128)S(1)}, f32[1,2,128,128]{3,2,1,0:T(8,128)S(1)}, f32[1,2,128,128]{3,2,1,0:T(8,128)S(1)}, f32[1,2,128,128]{3,2,1,0:T(8,128)S(1)}) custom-call(f32[3,128,128]{2,1,0:T(8,128)S(1)} %get-tuple-element.23.refs_0_, f32[3,128,128]{2,1,0:T(8,128)S(1)} %collective-permute-done.refs_1_, ...), custom_call_target="tpu_custom_call" | custom-call | tf_op jit(solution)/shard_map/chains/pallas_call | solution.py:326
  18.5 0.1 collective-permute-start.3
  18.6 1.6 %collective-permute-start.4 = (f32[1,2,128,128]{3,2,1,0:T(8,128)S(1)}, f32[1,2,128,128]{3,2,1,0:T(8,128)S(1)}, u32[]{:S(2)}, u32[]{:S(2)}) collective-permute-start(f32[1,2,128,128]{3,2,1,0:T(8,128)S(1)} %get-tuple-element.28), channel_id=1, source_target_pairs={{0,24},{1,25},{8,16},{9,17},{16,8},{17,9},{24,0},{25,1},{2,26},{3,... | collective-permute-start | bytes 393224 | tf_op jit(solution)/shard_map/ppermute | solution.py:295
  20.2 1.4 %collective-permute-start.5 = (f32[1,2,128,128]{3,2,1,0:T(8,128)S(1)}, f32[1,2,128,128]{3,2,1,0:T(8,128)S(1)}, u32[]{:S(2)}, u32[]{:S(2)}) collective-permute-start(f32[1,2,128,128]{3,2,1,0:T(8,128)S(1)} %get-tuple-element.29), channel_id=1, source_target_pairs={{0,8},{1,17},{8,0},{9,25},{16,24},{17,1},{24,16},{25,9},{2,10},{3,... | collective-permute-start | bytes 393224 | tf_op jit(solution)/shard_map/ppermute | solution.py:295
  21.5 0.6 %collective-permute-start.6 = (f32[1,2,128,128]{3,2,1,0:T(8,128)S(1)}, f32[1,2,128,128]{3,2,1,0:T(8,128)S(1)}, u32[]{:S(2)}, u32[]{:S(2)}) collective-permute-start(f32[1,2,128,128]{3,2,1,0:T(8,128)S(1)} %get-tuple-element.30), channel_id=1, source_target_pairs={{0,16},{1,9},{8,24},{9,1},{16,0},{17,25},{24,8},{25,17},{2,18},{3,... | collective-permute-start | bytes 393224 | tf_op jit(solution)/shard_map/ppermute | solution.py:295
  22.2 1.6 %collective-permute-start.7 = (f32[1,2,128,128]{3,2,1,0:T(8,128)S(1)}, f32[1,2,128,128]{3,2,1,0:T(8,128)S(1)}, u32[]{:S(2)}, u32[]{:S(2)}) collective-permute-start(f32[1,2,128,128]{3,2,1,0:T(8,128)S(1)} %momentum.6.refs_0_), channel_id=1, source_target_pairs={{0,2},{2,4},{4,6},{6,7},{7,5},{5,3},{3,1},{1,0},{8,10},{10,12},{12... | collective-permute-start | bytes 393224 | tf_op jit(solution)/shard_map/ppermute | solution.py:365
  23.8 0.0 collective-permute-start.8
  23.8 2.1 %collective-permute-done.4.refs_0_ = f32[1,2,128,128]{3,2,1,0:T(8,128)S(1)} collective-permute-done((f32[1,2,128,128]{3,2,1,0:T(8,128)S(1)}, f32[1,2,128,128]{3,2,1,0:T(8,128)S(1)}, u32[]{:S(2)}, u32[]{:S(2)}) %collective-permute-start.4) | collective-permute-done | bytes 131104 | tf_op jit(solution)/shard_map/ppermute | solution.py:295
  25.9 2.3 %collective-permute-done.5.refs_1_ = f32[1,2,128,128]{3,2,1,0:T(8,128)S(1)} collective-permute-done((f32[1,2,128,128]{3,2,1,0:T(8,128)S(1)}, f32[1,2,128,128]{3,2,1,0:T(8,128)S(1)}, u32[]{:S(2)}, u32[]{:S(2)}) %collective-permute-start.5) | collective-permute-done | bytes 131104 | tf_op jit(solution)/shard_map/ppermute | solution.py:295
  28.2 0.5 collective-permute-done.8.refs_0_
  28.8 0.5 collective-permute-start.10
  29.3 1.6 %collective-permute-start.12 = (f32[1,2,128,128]{3,2,1,0:T(8,128)S(1)}, f32[1,2,128,128]{3,2,1,0:T(8,128)S(1)}, u32[]{:S(2)}, u32[]{:S(2)}) collective-permute-start(f32[1,2,128,128]{3,2,1,0:T(8,128)S(1)} %collective-permute-done.7.refs_0_), channel_id=1, source_target_pairs={{0,2},{2,4},{4,6},{6,7},{7,5},{5,3},{3,1},{1,0},{8,10},{10,12},{12... | collective-permute-start | bytes 393224 | tf_op jit(solution)/shard_map/ppermute | solution.py:365
  30.9 2.0 %collective-permute-start.13 = (f32[2,2,128,128]{3,2,1,0:T(8,128)S(1)}, f32[2,2,128,128]{3,2,1,0:T(8,128)S(1)}, u32[]{:S(2)}, u32[]{:S(2)}) collective-permute-start(f32[2,2,128,128]{3,2,1,0:T(8,128)S(1)} %momentum.8.refs_1_), channel_id=1, source_target_pairs={{0,2},{2,4},{4,6},{6,7},{7,5},{5,3},{3,1},{1,0},{8,10},{10,12},{12... | collective-permute-start | bytes 786440 | tf_op jit(solution)/shard_map/ppermute | solution.py:365
  33.0 1.7 %collective-permute-done.12.refs_0_ = f32[1,2,128,128]{3,2,1,0:T(8,128)S(1)} collective-permute-done((f32[1,2,128,128]{3,2,1,0:T(8,128)S(1)}, f32[1,2,128,128]{3,2,1,0:T(8,128)S(1)}, u32[]{:S(2)}, u32[]{:S(2)}) %collective-permute-start.12) | collective-permute-done | bytes 131104 | tf_op jit(solution)/shard_map/ppermute | solution.py:365
  34.7 2.4 %collective-permute-done.14.refs_0_ = f32[1,2,128,128]{3,2,1,0:T(8,128)S(1)} collective-permute-done((f32[1,2,128,128]{3,2,1,0:T(8,128)S(1)}, f32[1,2,128,128]{3,2,1,0:T(8,128)S(1)}, u32[]{:S(2)}, u32[]{:S(2)}) %collective-permute-start.14) | collective-permute-done | bytes 131104 | tf_op jit(solution)/shard_map/ppermute | solution.py:365
  37.1 2.0 %collective-permute-start.17 = (f32[1,2,128,128]{3,2,1,0:T(8,128)S(1)}, f32[1,2,128,128]{3,2,1,0:T(8,128)S(1)}, u32[]{:S(2)}, u32[]{:S(2)}) collective-permute-start(f32[1,2,128,128]{3,2,1,0:T(8,128)S(1)} %momentum.9.refs_2_), channel_id=1, source_target_pairs={{0,2},{2,4},{4,6},{6,7},{7,5},{5,3},{3,1},{1,0},{8,10},{10,12},{12... | collective-permute-start | bytes 393224 | tf_op jit(solution)/shard_map/ppermute | solution.py:365
  39.2 4.5 %collective-permute-done.15.refs_2_ = f32[1,2,128,128]{3,2,1,0:T(8,128)S(1)} collective-permute-done((f32[1,2,128,128]{3,2,1,0:T(8,128)S(1)}, f32[1,2,128,128]{3,2,1,0:T(8,128)S(1)}, u32[]{:S(2)}, u32[]{:S(2)}) %collective-permute-start.15) | collective-permute-done | bytes 131104 | tf_op jit(solution)/shard_map/ppermute | solution.py:365
  43.7 1.6 %collective-permute-start.16 = (f32[2,2,128,128]{3,2,1,0:T(8,128)S(1)}, f32[2,2,128,128]{3,2,1,0:T(8,128)S(1)}, u32[]{:S(2)}, u32[]{:S(2)}) collective-permute-start(f32[2,2,128,128]{3,2,1,0:T(8,128)S(1)} %collective-permute-done.13.refs_1_), channel_id=1, source_target_pairs={{0,2},{2,4},{4,6},{6,7},{7,5},{5,3},{3,1},{1,0},{8,10},{10,12},{12... | collective-permute-start | bytes 786440 | tf_op jit(solution)/shard_map/ppermute | solution.py:365
  45.3 2.0 %collective-permute-start.18 = (f32[1,2,128,128]{3,2,1,0:T(8,128)S(1)}, f32[1,2,128,128]{3,2,1,0:T(8,128)S(1)}, u32[]{:S(2)}, u32[]{:S(2)}) collective-permute-start(f32[1,2,128,128]{3,2,1,0:T(8,128)S(1)} %collective-permute-done.17.refs_2_), channel_id=1, source_target_pairs={{0,2},{2,4},{4,6},{6,7},{7,5},{5,3},{3,1},{1,0},{8,10},{10,12},{12... | collective-permute-start | bytes 393224 | tf_op jit(solution)/shard_map/ppermute | solution.py:365
  47.5 0.6 %copy-done = s32[4]{0:T(128)S(1)} copy-done((s32[4]{0:T(128)S(1)}, s32[4]{0:T(128)}, u32[]{:S(2)}) %copy-start) | copy-done | bytes 40
  48.0 0.9 %local.1 = (f32[4,2,128,128]{3,2,1,0:T(8,128)S(1)}, f32[4,2,128,128]{3,2,1,0:T(8,128)S(1)}, f32[16,128]{1,0:T(8,128)S(1)}) custom-call(s32[4]{0:T(128)S(1)} %copy-done, f32[4]{0:T(128)S(1)} %copy-done.1, f32[4,2,128,128]{3,2,1,0:T(8,128)S(1)} %by_energy.6.zero_ref, f32[4,2,128,128]{3,2,1,0:T(8,128)S(1)} %by_energy.7.one_ref), custom_call_target="tpu_custom_call" | custom-call | tf_op jit(solution)/shard_map/local/pallas_call | solution.py:385
  49.1 0.6 %mix.2 = (f32[4,2,128,128]{3,2,1,0:T(8,128)S(1)}, f32[4,2,128,128]{3,2,1,0:T(8,128)S(1)}) custom-call(f32[16,128]{1,0:T(8,128)S(1)} %get-tuple-element.34.table_ref, f32[4,2,128,128]{3,2,1,0:T(8,128)S(1)} %by_energy.10.refs_0_, f32[4,2,128,128]{3,2,1,0:T(8,128)S(1)} %by_energy.11.refs_1_, f32[4,2,128,128]{3,2,1,0:T(8,128)S(1)} %get-tuple-element.38.refs_2_, ...), custom_call_target="tpu_custom_call" | custom-call | tf_op jit(solution)/shard_map/mix/pallas_call | solution.py:396
  49.7 4.0 %collective-permute-done.18.refs_2_ = f32[1,2,128,128]{3,2,1,0:T(8,128)S(1)} collective-permute-done((f32[1,2,128,128]{3,2,1,0:T(8,128)S(1)}, f32[1,2,128,128]{3,2,1,0:T(8,128)S(1)}, u32[]{:S(2)}, u32[]{:S(2)}) %collective-permute-start.18) | collective-permute-done | bytes 131104 | tf_op jit(solution)/shard_map/ppermute | solution.py:365
  53.8 0.7 %collective-permute-done.21.refs_2_ = f32[1,2,128,128]{3,2,1,0:T(8,128)S(1)} collective-permute-done((f32[1,2,128,128]{3,2,1,0:T(8,128)S(1)}, f32[1,2,128,128]{3,2,1,0:T(8,128)S(1)}, u32[]{:S(2)}, u32[]{:S(2)}) %collective-permute-start.21) | collective-permute-done | bytes 131104 | tf_op jit(solution)/shard_map/ppermute | solution.py:365
  54.5 1.2 %mix.3 = (f32[4,2,128,128]{3,2,1,0:T(8,128)}, f32[4,2,128,128]{3,2,1,0:T(8,128)}) custom-call(f32[16,128]{1,0:T(8,128)S(1)} %get-tuple-element.34.table_ref, f32[4,2,128,128]{3,2,1,0:T(8,128)S(1)} %by_energy.8.refs_0_, f32[4,2,128,128]{3,2,1,0:T(8,128)S(1)} %by_energy.9.refs_1_, f32[4,2,128,128]{3,2,1,0:T(8,128)S(1)} %get-tuple-element.39.refs_2_, ...), custom_call_target="tpu_custom_call" | custom-call | tf_op jit(solution)/shard_map/mix/pallas_call | solution.py:396
  (35 shorter events, 0.5 us)
Async XLA Ops:
  2.9 9.3 %collective-permute-start = (f32[3,128,128]{2,1,0:T(8,128)S(1)}, f32[3,128,128]{2,1,0:T(8,128)S(1)}, u32[]{:S(2)}, u32[]{:S(2)}) collective-permute-start(f32[3,128,128]{2,1,0:T(8,128)S(1)} %get-tuple-element.24), channel_id=1, source_target_pairs={{0,24},{1,25},{8,16},{9,17},{16,8},{17,9},{24,0},{25,1},{2,26},{3,... | collective-permute-start | bytes 589832 | tf_op jit(solution)/shard_map/ppermute | solution.py:295
  6.9 9.4 %collective-permute-start.1 = (f32[3,128,128]{2,1,0:T(8,128)S(1)}, f32[3,128,128]{2,1,0:T(8,128)S(1)}, u32[]{:S(2)}, u32[]{:S(2)}) collective-permute-start(f32[3,128,128]{2,1,0:T(8,128)S(1)} %get-tuple-element.25), channel_id=1, source_target_pairs={{0,8},{1,17},{8,0},{9,25},{16,24},{17,1},{24,16},{25,9},{2,10},{3,... | collective-permute-start | bytes 589832 | tf_op jit(solution)/shard_map/ppermute | solution.py:295
  9.6 6.6 %collective-permute-start.2 = (f32[3,128,128]{2,1,0:T(8,128)S(1)}, f32[3,128,128]{2,1,0:T(8,128)S(1)}, u32[]{:S(2)}, u32[]{:S(2)}) collective-permute-start(f32[3,128,128]{2,1,0:T(8,128)S(1)} %get-tuple-element.26), channel_id=1, source_target_pairs={{0,16},{1,9},{8,24},{9,1},{16,0},{17,25},{24,8},{25,17},{2,18},{3,... | collective-permute-start | bytes 589832 | tf_op jit(solution)/shard_map/ppermute | solution.py:295
  18.5 3.6 %collective-permute-start.3 = (f32[1,2,128,128]{3,2,1,0:T(8,128)S(1)}, f32[1,2,128,128]{3,2,1,0:T(8,128)S(1)}, u32[]{:S(2)}, u32[]{:S(2)}) collective-permute-start(f32[1,2,128,128]{3,2,1,0:T(8,128)S(1)} %get-tuple-element.27.refs_0_), channel_id=1, source_target_pairs={{0,1},{1,0},{2,3},{3,2},{4,5},{5,4},{6,7},{7,6},{8,9},{9,8},{10,11... | collective-permute-start | bytes 393224 | tf_op jit(solution)/shard_map/ppermute | solution.py:375
  18.6 7.3 %collective-permute-start.4 = (f32[1,2,128,128]{3,2,1,0:T(8,128)S(1)}, f32[1,2,128,128]{3,2,1,0:T(8,128)S(1)}, u32[]{:S(2)}, u32[]{:S(2)}) collective-permute-start(f32[1,2,128,128]{3,2,1,0:T(8,128)S(1)} %get-tuple-element.28), channel_id=1, source_target_pairs={{0,24},{1,25},{8,16},{9,17},{16,8},{17,9},{24,0},{25,1},{2,26},{3,... | collective-permute-start | bytes 393224 | tf_op jit(solution)/shard_map/ppermute | solution.py:295
  20.2 8.0 %collective-permute-start.5 = (f32[1,2,128,128]{3,2,1,0:T(8,128)S(1)}, f32[1,2,128,128]{3,2,1,0:T(8,128)S(1)}, u32[]{:S(2)}, u32[]{:S(2)}) collective-permute-start(f32[1,2,128,128]{3,2,1,0:T(8,128)S(1)} %get-tuple-element.29), channel_id=1, source_target_pairs={{0,8},{1,17},{8,0},{9,25},{16,24},{17,1},{24,16},{25,9},{2,10},{3,... | collective-permute-start | bytes 393224 | tf_op jit(solution)/shard_map/ppermute | solution.py:295
  21.5 6.7 %collective-permute-start.6 = (f32[1,2,128,128]{3,2,1,0:T(8,128)S(1)}, f32[1,2,128,128]{3,2,1,0:T(8,128)S(1)}, u32[]{:S(2)}, u32[]{:S(2)}) collective-permute-start(f32[1,2,128,128]{3,2,1,0:T(8,128)S(1)} %get-tuple-element.30), channel_id=1, source_target_pairs={{0,16},{1,9},{8,24},{9,1},{16,0},{17,25},{24,8},{25,17},{2,18},{3,... | collective-permute-start | bytes 393224 | tf_op jit(solution)/shard_map/ppermute | solution.py:295
  22.2 6.0 %collective-permute-start.7 = (f32[1,2,128,128]{3,2,1,0:T(8,128)S(1)}, f32[1,2,128,128]{3,2,1,0:T(8,128)S(1)}, u32[]{:S(2)}, u32[]{:S(2)}) collective-permute-start(f32[1,2,128,128]{3,2,1,0:T(8,128)S(1)} %momentum.6.refs_0_), channel_id=1, source_target_pairs={{0,2},{2,4},{4,6},{6,7},{7,5},{5,3},{3,1},{1,0},{8,10},{10,12},{12... | collective-permute-start | bytes 393224 | tf_op jit(solution)/shard_map/ppermute | solution.py:365
  23.8 5.0 %collective-permute-start.8 = (f32[1,2,128,128]{3,2,1,0:T(8,128)S(1)}, f32[1,2,128,128]{3,2,1,0:T(8,128)S(1)}, u32[]{:S(2)}, u32[]{:S(2)}) collective-permute-start(f32[1,2,128,128]{3,2,1,0:T(8,128)S(1)} %momentum.7.refs_0_), channel_id=1, source_target_pairs={{2,0},{4,2},{6,4},{7,6},{5,7},{3,5},{1,3},{0,1},{10,8},{12,10},{14... | collective-permute-start | bytes 393224 | tf_op jit(solution)/shard_map/ppermute | solution.py:365
  28.7 2.1 %collective-permute-start.9 = (f32[1,2,128,128]{3,2,1,0:T(8,128)S(1)}, f32[1,2,128,128]{3,2,1,0:T(8,128)S(1)}, u32[]{:S(2)}, u32[]{:S(2)}) collective-permute-start(f32[1,2,128,128]{3,2,1,0:T(8,128)S(1)} %collective-permute-done.4.refs_0_), channel_id=1, source_target_pairs={{0,1},{1,0},{2,3},{3,2},{4,5},{5,4},{6,7},{7,6},{8,9},{9,8},{10,11... | collective-permute-start | bytes 393224 | tf_op jit(solution)/shard_map/ppermute | solution.py:375
  28.8 2.1 %collective-permute-start.10 = (f32[1,2,128,128]{3,2,1,0:T(8,128)S(1)}, f32[1,2,128,128]{3,2,1,0:T(8,128)S(1)}, u32[]{:S(2)}, u32[]{:S(2)}) collective-permute-start(f32[1,2,128,128]{3,2,1,0:T(8,128)S(1)} %collective-permute-done.5.refs_1_), channel_id=1, source_target_pairs={{0,1},{1,0},{2,3},{3,2},{4,5},{5,4},{6,7},{7,6},{8,9},{9,8},{10,11... | collective-permute-start | bytes 393224 | tf_op jit(solution)/shard_map/ppermute | solution.py:375
  29.3 3.7 %collective-permute-start.11 = (f32[1,2,128,128]{3,2,1,0:T(8,128)S(1)}, f32[1,2,128,128]{3,2,1,0:T(8,128)S(1)}, u32[]{:S(2)}, u32[]{:S(2)}) collective-permute-start(f32[1,2,128,128]{3,2,1,0:T(8,128)S(1)} %collective-permute-done.6.refs_0_), channel_id=1, source_target_pairs={{0,1},{1,0},{2,3},{3,2},{4,5},{5,4},{6,7},{7,6},{8,9},{9,8},{10,11... | collective-permute-start | bytes 393224 | tf_op jit(solution)/shard_map/ppermute | solution.py:375
  29.3 5.5 %collective-permute-start.12 = (f32[1,2,128,128]{3,2,1,0:T(8,128)S(1)}, f32[1,2,128,128]{3,2,1,0:T(8,128)S(1)}, u32[]{:S(2)}, u32[]{:S(2)}) collective-permute-start(f32[1,2,128,128]{3,2,1,0:T(8,128)S(1)} %collective-permute-done.7.refs_0_), channel_id=1, source_target_pairs={{0,2},{2,4},{4,6},{6,7},{7,5},{5,3},{3,1},{1,0},{8,10},{10,12},{12... | collective-permute-start | bytes 393224 | tf_op jit(solution)/shard_map/ppermute | solution.py:365
  30.8 6.3 %collective-permute-start.14 = (f32[1,2,128,128]{3,2,1,0:T(8,128)S(1)}, f32[1,2,128,128]{3,2,1,0:T(8,128)S(1)}, u32[]{:S(2)}, u32[]{:S(2)}) collective-permute-start(f32[1,2,128,128]{3,2,1,0:T(8,128)S(1)} %collective-permute-done.8.refs_0_), channel_id=1, source_target_pairs={{2,0},{4,2},{6,4},{7,6},{5,7},{3,5},{1,3},{0,1},{10,8},{12,10},{14... | collective-permute-start | bytes 393224 | tf_op jit(solution)/shard_map/ppermute | solution.py:365
  30.9 12.8 %collective-permute-start.13 = (f32[2,2,128,128]{3,2,1,0:T(8,128)S(1)}, f32[2,2,128,128]{3,2,1,0:T(8,128)S(1)}, u32[]{:S(2)}, u32[]{:S(2)}) collective-permute-start(f32[2,2,128,128]{3,2,1,0:T(8,128)S(1)} %momentum.8.refs_1_), channel_id=1, source_target_pairs={{0,2},{2,4},{4,6},{6,7},{7,5},{5,3},{3,1},{1,0},{8,10},{10,12},{12... | collective-permute-start | bytes 786440 | tf_op jit(solution)/shard_map/ppermute | solution.py:365
  32.9 12.4 %collective-permute-start.19 = (f32[2,2,128,128]{3,2,1,0:T(8,128)S(1)}, f32[2,2,128,128]{3,2,1,0:T(8,128)S(1)}, u32[]{:S(2)}, u32[]{:S(2)}) collective-permute-start(f32[2,2,128,128]{3,2,1,0:T(8,128)S(1)} %momentum.10.refs_1_), channel_id=1, source_target_pairs={{2,0},{4,2},{6,4},{7,6},{5,7},{3,5},{1,3},{0,1},{10,8},{12,10},{14... | collective-permute-start | bytes 786440 | tf_op jit(solution)/shard_map/ppermute | solution.py:365
  37.1 6.6 %collective-permute-start.15 = (f32[1,2,128,128]{3,2,1,0:T(8,128)S(1)}, f32[1,2,128,128]{3,2,1,0:T(8,128)S(1)}, u32[]{:S(2)}, u32[]{:S(2)}) collective-permute-start(f32[1,2,128,128]{3,2,1,0:T(8,128)S(1)} %momentum.11.refs_2_), channel_id=1, source_target_pairs={{2,0},{4,2},{6,4},{7,6},{5,7},{3,5},{1,3},{0,1},{10,8},{12,10},{14... | collective-permute-start | bytes 393224 | tf_op jit(solution)/shard_map/ppermute | solution.py:365
  37.1 8.2 %collective-permute-start.17 = (f32[1,2,128,128]{3,2,1,0:T(8,128)S(1)}, f32[1,2,128,128]{3,2,1,0:T(8,128)S(1)}, u32[]{:S(2)}, u32[]{:S(2)}) collective-permute-start(f32[1,2,128,128]{3,2,1,0:T(8,128)S(1)} %momentum.9.refs_2_), channel_id=1, source_target_pairs={{0,2},{2,4},{4,6},{6,7},{7,5},{5,3},{3,1},{1,0},{8,10},{10,12},{12... | collective-permute-start | bytes 393224 | tf_op jit(solution)/shard_map/ppermute | solution.py:365
  43.7 10.0 %collective-permute-start.16 = (f32[2,2,128,128]{3,2,1,0:T(8,128)S(1)}, f32[2,2,128,128]{3,2,1,0:T(8,128)S(1)}, u32[]{:S(2)}, u32[]{:S(2)}) collective-permute-start(f32[2,2,128,128]{3,2,1,0:T(8,128)S(1)} %collective-permute-done.13.refs_1_), channel_id=1, source_target_pairs={{0,2},{2,4},{4,6},{6,7},{7,5},{5,3},{3,1},{1,0},{8,10},{10,12},{12... | collective-permute-start | bytes 786440 | tf_op jit(solution)/shard_map/ppermute | solution.py:365
  45.3 9.2 %collective-permute-start.20 = (f32[2,2,128,128]{3,2,1,0:T(8,128)S(1)}, f32[2,2,128,128]{3,2,1,0:T(8,128)S(1)}, u32[]{:S(2)}, u32[]{:S(2)}) collective-permute-start(f32[2,2,128,128]{3,2,1,0:T(8,128)S(1)} %collective-permute-done.19.refs_1_), channel_id=1, source_target_pairs={{2,0},{4,2},{6,4},{7,6},{5,7},{3,5},{1,3},{0,1},{10,8},{12,10},{14... | collective-permute-start | bytes 786440 | tf_op jit(solution)/shard_map/ppermute | solution.py:365
  45.3 8.4 %collective-permute-start.18 = (f32[1,2,128,128]{3,2,1,0:T(8,128)S(1)}, f32[1,2,128,128]{3,2,1,0:T(8,128)S(1)}, u32[]{:S(2)}, u32[]{:S(2)}) collective-permute-start(f32[1,2,128,128]{3,2,1,0:T(8,128)S(1)} %collective-permute-done.17.refs_2_), channel_id=1, source_target_pairs={{0,2},{2,4},{4,6},{6,7},{7,5},{5,3},{3,1},{1,0},{8,10},{10,12},{12... | collective-permute-start | bytes 393224 | tf_op jit(solution)/shard_map/ppermute | solution.py:365
  47.3 7.1 %collective-permute-start.21 = (f32[1,2,128,128]{3,2,1,0:T(8,128)S(1)}, f32[1,2,128,128]{3,2,1,0:T(8,128)S(1)}, u32[]{:S(2)}, u32[]{:S(2)}) collective-permute-start(f32[1,2,128,128]{3,2,1,0:T(8,128)S(1)} %collective-permute-done.15.refs_2_), channel_id=1, source_target_pairs={{2,0},{4,2},{6,4},{7,6},{5,7},{3,5},{1,3},{0,1},{10,8},{12,10},{14... | collective-permute-start | bytes 393224 | tf_op jit(solution)/shard_map/ppermute | solution.py:365
  47.4 0.7 %copy-start = (s32[4]{0:T(128)S(1)}, s32[4]{0:T(128)}, u32[]{:S(2)}) copy-start(s32[4]{0:T(128)} %shift_ref.1) | copy-start | bytes 52
  47.4 0.7 %copy-start.1 = (f32[4]{0:T(128)S(1)}, f32[4]{0:T(128)}, u32[]{:S(2)}) copy-start(f32[4]{0:T(128)} %weight_ref.1) | copy-start | bytes 52

commit v16 on v15

--- a/solution.py
+++ b/solution.py
@@ -369,7 +369,7 @@
     hops = [[], []]
     for c in chunks:
         if len(hops[0]) == 1:
-            own, _ = lax.optimization_barrier((own, hops))
+            own, _ = lax.optimization_barrier((own, hops[0]))
             ahead = [hop(hops[m][0], m) for m in range(2)]
         held = [own[i] for i in c]
         other = [lax.ppermute(v, "mom", both_ways) for v in held]

time: 55.8 us -> 55.2 us (0.989)
  waiting for transfers between devices: 24.7 us -> 24 us
    ppermute x12, waiting for transfers between devices: 13.9 us -> 13.2 us  [hop(): return lax.ppermute(value, ('energy', 'mom'), ways[role])]
  transfers between devices with their start and end apart: 22 -> 22, of which waited for: 10 -> 9; matrix products, arithmetic and copies ran while one was open for 0% -> 0% of each run, Pallas kernels for 7% -> 7%
where the time goes in v16:
time: 55.2 us; the launch traced here: 55.1 us
  waiting for transfers between devices  24 us (43%)
  starting transfers between devices  19.8 us (36%)
  Pallas kernels  9.79 us (18%)
  between operations  0.83 us (2%)
  local copies, waits for them, and re-layouts  0.64 us (1%)
    ppermute x12, waiting for transfers between devices, hop(): return lax.ppermute(value, ('energy', 'mom'), ways[role])  13.2 us
    ppermute x12, starting transfers between devices, hop(): return lax.ppermute(value, ('energy', 'mom'), ways[role])  10.9 us
    ppermute x6, waiting for transfers between devices, exchange(): return lax.ppermute(slots[i], ('len', 'mom'), pairs)  10.8 us
    ppermute x6, starting transfers between devices, exchange(): return lax.ppermute(slots[i], ('len', 'mom'), pairs)  8.23 us
    pallas_call x2, Pallas kernels, inverse(): pl.pallas_call(functools.partial(inverse_kernel, total, layers, slots), o...  4.51 us
    pallas_call x1, Pallas kernels, shards(): pl.pallas_call(functools.partial(chain_kernel, layers), out_shape=[part]...  2.22 us
    pallas_call x2, Pallas kernels, mix(): pl.pallas_call(functools.partial(mix_kernel, total, items, False, last),...  1.75 us
  transfers between devices with their start and end apart: 22, of which 9 were waited for; matrix products, arithmetic and copies ran while one was open for 0% of the time, Pallas kernels for 7%

profile of v16, /device:TPU:0, one launch (start us, length us, event | category | flops | bytes accessed | tf_op | source)
XLA Modules:
  0.0 55.1 jit_solution(14592511711071271135)
XLA Ops:
  0.6 2.3 %inverse.3 = (f32[3,128,128]{2,1,0:T(8,128)S(1)}, f32[3,128,128]{2,1,0:T(8,128)S(1)}) custom-call(f32[2,128,128]{2,1,0:T(8,128)} %bitcast.9, f32[4,2,128,128]{3,2,1,0:T(8,128)} %bitcast.5, f32[128,128]{1,0:T(8,128)} %bitcast.11, s32[128,128]{1,0:T(8,128)} %pattern_any.3), custom_call_target="tpu_custom_call" | custom-call | flops 402653184 | bytes 262144 | tf_op jit(solution)/shard_map/inverse/pallas_call | solution.py:302
  2.9 4.0 %collective-permute-start = (f32[3,128,128]{2,1,0:T(8,128)S(1)}, f32[3,128,128]{2,1,0:T(8,128)S(1)}, u32[]{:S(2)}, u32[]{:S(2)}) collective-permute-start(f32[3,128,128]{2,1,0:T(8,128)S(1)} %get-tuple-element.24), channel_id=1, source_target_pairs={{0,24},{1,25},{8,16},{9,17},{16,8},{17,9},{24,0},{25,1},{2,26},{3,... | collective-permute-start | bytes 589832 | tf_op jit(solution)/shard_map/ppermute | solution.py:295
  6.9 0.5 collective-permute-start.1
  7.4 2.2 %inverse.2 = (f32[3,128,128]{2,1,0:T(8,128)S(1)}, f32[3,128,128]{2,1,0:T(8,128)S(1)}) custom-call(f32[2,128,128]{2,1,0:T(8,128)} %bitcast.10, f32[4,2,128,128]{3,2,1,0:T(8,128)} %bitcast.6, f32[128,128]{1,0:T(8,128)} %bitcast.12, s32[128,128]{1,0:T(8,128)} %pattern_any.3), custom_call_target="tpu_custom_call" | custom-call | flops 402653184 | bytes 262144 | tf_op jit(solution)/shard_map/inverse/pallas_call | solution.py:302
  9.6 0.2 collective-permute-start.2
  9.8 2.3 %collective-permute-done.refs_1_ = f32[3,128,128]{2,1,0:T(8,128)S(1)} collective-permute-done((f32[3,128,128]{2,1,0:T(8,128)S(1)}, f32[3,128,128]{2,1,0:T(8,128)S(1)}, u32[]{:S(2)}, u32[]{:S(2)}) %collective-permute-start) | collective-permute-done | bytes 196640 | tf_op jit(solution)/shard_map/ppermute | solution.py:295
  12.2 4.1 %collective-permute-done.1.refs_2_ = f32[3,128,128]{2,1,0:T(8,128)S(1)} collective-permute-done((f32[3,128,128]{2,1,0:T(8,128)S(1)}, f32[3,128,128]{2,1,0:T(8,128)S(1)}, u32[]{:S(2)}, u32[]{:S(2)}) %collective-permute-start.1) | collective-permute-done | bytes 196640 | tf_op jit(solution)/shard_map/ppermute | solution.py:295
  16.3 2.2 %chains.1 = (f32[1,2,128,128]{3,2,1,0:T(8,128)S(1)}, f32[1,2,128,128]{3,2,1,0:T(8,128)S(1)}, f32[1,2,128,128]{3,2,1,0:T(8,128)S(1)}, f32[1,2,128,128]{3,2,1,0:T(8,128)S(1)}) custom-call(f32[3,128,128]{2,1,0:T(8,128)S(1)} %get-tuple-element.23.refs_0_, f32[3,128,128]{2,1,0:T(8,128)S(1)} %collective-permute-done.refs_1_, ...), custom_call_target="tpu_custom_call" | custom-call | tf_op jit(solution)/shard_map/chains/pallas_call | solution.py:326
  18.5 0.1 collective-permute-start.3
  18.6 1.6 %collective-permute-start.4 = (f32[1,2,128,128]{3,2,1,0:T(8,128)S(1)}, f32[1,2,128,128]{3,2,1,0:T(8,128)S(1)}, u32[]{:S(2)}, u32[]{:S(2)}) collective-permute-start(f32[1,2,128,128]{3,2,1,0:T(8,128)S(1)} %get-tuple-element.28), channel_id=1, source_target_pairs={{0,24},{1,25},{8,16},{9,17},{16,8},{17,9},{24,0},{25,1},{2,26},{3,... | collective-permute-start | bytes 393224 | tf_op jit(solution)/shard_map/ppermute | solution.py:295
  20.2 1.4 %collective-permute-start.5 = (f32[1,2,128,128]{3,2,1,0:T(8,128)S(1)}, f32[1,2,128,128]{3,2,1,0:T(8,128)S(1)}, u32[]{:S(2)}, u32[]{:S(2)}) collective-permute-start(f32[1,2,128,128]{3,2,1,0:T(8,128)S(1)} %get-tuple-element.29), channel_id=1, source_target_pairs={{0,8},{1,17},{8,0},{9,25},{16,24},{17,1},{24,16},{25,9},{2,10},{3,... | collective-permute-start | bytes 393224 | tf_op jit(solution)/shard_map/ppermute | solution.py:295
  21.5 0.6 %collective-permute-start.6 = (f32[1,2,128,128]{3,2,1,0:T(8,128)S(1)}, f32[1,2,128,128]{3,2,1,0:T(8,128)S(1)}, u32[]{:S(2)}, u32[]{:S(2)}) collective-permute-start(f32[1,2,128,128]{3,2,1,0:T(8,128)S(1)} %get-tuple-element.30), channel_id=1, source_target_pairs={{0,16},{1,9},{8,24},{9,1},{16,0},{17,25},{24,8},{25,17},{2,18},{3,... | collective-permute-start | bytes 393224 | tf_op jit(solution)/shard_map/ppermute | solution.py:295
  22.2 1.6 %collective-permute-start.7 = (f32[1,2,128,128]{3,2,1,0:T(8,128)S(1)}, f32[1,2,128,128]{3,2,1,0:T(8,128)S(1)}, u32[]{:S(2)}, u32[]{:S(2)}) collective-permute-start(f32[1,2,128,128]{3,2,1,0:T(8,128)S(1)} %momentum.6.refs_0_), channel_id=1, source_target_pairs={{0,2},{2,4},{4,6},{6,7},{7,5},{5,3},{3,1},{1,0},{8,10},{10,12},{12... | collective-permute-start | bytes 393224 | tf_op jit(solution)/shard_map/ppermute | solution.py:365
  23.8 0.0 collective-permute-start.13
  23.8 2.1 %collective-permute-done.4.refs_0_ = f32[1,2,128,128]{3,2,1,0:T(8,128)S(1)} collective-permute-done((f32[1,2,128,128]{3,2,1,0:T(8,128)S(1)}, f32[1,2,128,128]{3,2,1,0:T(8,128)S(1)}, u32[]{:S(2)}, u32[]{:S(2)}) %collective-permute-start.4) | collective-permute-done | bytes 131104 | tf_op jit(solution)/shard_map/ppermute | solution.py:295
  25.9 2.3 %collective-permute-done.5.refs_1_ = f32[1,2,128,128]{3,2,1,0:T(8,128)S(1)} collective-permute-done((f32[1,2,128,128]{3,2,1,0:T(8,128)S(1)}, f32[1,2,128,128]{3,2,1,0:T(8,128)S(1)}, u32[]{:S(2)}, u32[]{:S(2)}) %collective-permute-start.5) | collective-permute-done | bytes 131104 | tf_op jit(solution)/shard_map/ppermute | solution.py:295
  28.2 0.5 collective-permute-start.9
  28.7 0.1 collective-permute-start.10
  28.8 1.6 %collective-permute-start.11 = (f32[1,2,128,128]{3,2,1,0:T(8,128)S(1)}, f32[1,2,128,128]{3,2,1,0:T(8,128)S(1)}, u32[]{:S(2)}, u32[]{:S(2)}) collective-permute-start(f32[1,2,128,128]{3,2,1,0:T(8,128)S(1)} %collective-permute-done.7.refs_0_), channel_id=1, source_target_pairs={{0,2},{2,4},{4,6},{6,7},{7,5},{5,3},{3,1},{1,0},{8,10},{10,12},{12... | collective-permute-start | bytes 393224 | tf_op jit(solution)/shard_map/ppermute | solution.py:365
  30.4 2.0 %collective-permute-start.12 = (f32[2,2,128,128]{3,2,1,0:T(8,128)S(1)}, f32[2,2,128,128]{3,2,1,0:T(8,128)S(1)}, u32[]{:S(2)}, u32[]{:S(2)}) collective-permute-start(f32[2,2,128,128]{3,2,1,0:T(8,128)S(1)} %momentum.7.refs_1_), channel_id=1, source_target_pairs={{0,2},{2,4},{4,6},{6,7},{7,5},{5,3},{3,1},{1,0},{8,10},{10,12},{12... | collective-permute-start | bytes 786440 | tf_op jit(solution)/shard_map/ppermute | solution.py:365
  32.6 1.6 %collective-permute-done.11.refs_0_ = f32[1,2,128,128]{3,2,1,0:T(8,128)S(1)} collective-permute-done((f32[1,2,128,128]{3,2,1,0:T(8,128)S(1)}, f32[1,2,128,128]{3,2,1,0:T(8,128)S(1)}, u32[]{:S(2)}, u32[]{:S(2)}) %collective-permute-start.11) | collective-permute-done | bytes 131104 | tf_op jit(solution)/shard_map/ppermute | solution.py:365
  34.2 2.5 %collective-permute-done.14.refs_0_ = f32[1,2,128,128]{3,2,1,0:T(8,128)S(1)} collective-permute-done((f32[1,2,128,128]{3,2,1,0:T(8,128)S(1)}, f32[1,2,128,128]{3,2,1,0:T(8,128)S(1)}, u32[]{:S(2)}, u32[]{:S(2)}) %collective-permute-start.14) | collective-permute-done | bytes 131104 | tf_op jit(solution)/shard_map/ppermute | solution.py:365
  36.7 2.0 %collective-permute-start.17 = (f32[1,2,128,128]{3,2,1,0:T(8,128)S(1)}, f32[1,2,128,128]{3,2,1,0:T(8,128)S(1)}, u32[]{:S(2)}, u32[]{:S(2)}) collective-permute-start(f32[1,2,128,128]{3,2,1,0:T(8,128)S(1)} %momentum.8.refs_2_), channel_id=1, source_target_pairs={{0,2},{2,4},{4,6},{6,7},{7,5},{5,3},{3,1},{1,0},{8,10},{10,12},{12... | collective-permute-start | bytes 393224 | tf_op jit(solution)/shard_map/ppermute | solution.py:365
  38.7 4.4 %collective-permute-done.15.refs_2_ = f32[1,2,128,128]{3,2,1,0:T(8,128)S(1)} collective-permute-done((f32[1,2,128,128]{3,2,1,0:T(8,128)S(1)}, f32[1,2,128,128]{3,2,1,0:T(8,128)S(1)}, u32[]{:S(2)}, u32[]{:S(2)}) %collective-permute-start.15) | collective-permute-done | bytes 131104 | tf_op jit(solution)/shard_map/ppermute | solution.py:365
  43.2 1.6 %collective-permute-start.16 = (f32[2,2,128,128]{3,2,1,0:T(8,128)S(1)}, f32[2,2,128,128]{3,2,1,0:T(8,128)S(1)}, u32[]{:S(2)}, u32[]{:S(2)}) collective-permute-start(f32[2,2,128,128]{3,2,1,0:T(8,128)S(1)} %collective-permute-done.12.refs_1_), channel_id=1, source_target_pairs={{0,2},{2,4},{4,6},{6,7},{7,5},{5,3},{3,1},{1,0},{8,10},{10,12},{12... | collective-permute-start | bytes 786440 | tf_op jit(solution)/shard_map/ppermute | solution.py:365
  44.8 2.0 %collective-permute-start.18 = (f32[1,2,128,128]{3,2,1,0:T(8,128)S(1)}, f32[1,2,128,128]{3,2,1,0:T(8,128)S(1)}, u32[]{:S(2)}, u32[]{:S(2)}) collective-permute-start(f32[1,2,128,128]{3,2,1,0:T(8,128)S(1)} %collective-permute-done.17.refs_2_), channel_id=1, source_target_pairs={{0,2},{2,4},{4,6},{6,7},{7,5},{5,3},{3,1},{1,0},{8,10},{10,12},{12... | collective-permute-start | bytes 393224 | tf_op jit(solution)/shard_map/ppermute | solution.py:365
  46.9 0.6 %copy-done = s32[4]{0:T(128)S(1)} copy-done((s32[4]{0:T(128)S(1)}, s32[4]{0:T(128)}, u32[]{:S(2)}) %copy-start) | copy-done | bytes 40
  47.5 0.9 %local.1 = (f32[4,2,128,128]{3,2,1,0:T(8,128)S(1)}, f32[4,2,128,128]{3,2,1,0:T(8,128)S(1)}, f32[16,128]{1,0:T(8,128)S(1)}) custom-call(s32[4]{0:T(128)S(1)} %copy-done, f32[4]{0:T(128)S(1)} %copy-done.1, f32[4,2,128,128]{3,2,1,0:T(8,128)S(1)} %by_energy.6.zero_ref, f32[4,2,128,128]{3,2,1,0:T(8,128)S(1)} %by_energy.7.one_ref), custom_call_target="tpu_custom_call" | custom-call | tf_op jit(solution)/shard_map/local/pallas_call | solution.py:385
  48.6 0.6 %mix.2 = (f32[4,2,128,128]{3,2,1,0:T(8,128)S(1)}, f32[4,2,128,128]{3,2,1,0:T(8,128)S(1)}) custom-call(f32[16,128]{1,0:T(8,128)S(1)} %get-tuple-element.34.table_ref, f32[4,2,128,128]{3,2,1,0:T(8,128)S(1)} %by_energy.10.refs_0_, f32[4,2,128,128]{3,2,1,0:T(8,128)S(1)} %by_energy.11.refs_1_, f32[4,2,128,128]{3,2,1,0:T(8,128)S(1)} %get-tuple-element.38.refs_2_, ...), custom_call_target="tpu_custom_call" | custom-call | tf_op jit(solution)/shard_map/mix/pallas_call | solution.py:396
  49.2 3.9 %collective-permute-done.18.refs_2_ = f32[1,2,128,128]{3,2,1,0:T(8,128)S(1)} collective-permute-done((f32[1,2,128,128]{3,2,1,0:T(8,128)S(1)}, f32[1,2,128,128]{3,2,1,0:T(8,128)S(1)}, u32[]{:S(2)}, u32[]{:S(2)}) %collective-permute-start.18) | collective-permute-done | bytes 131104 | tf_op jit(solution)/shard_map/ppermute | solution.py:365
  53.2 0.7 %collective-permute-done.21.refs_2_ = f32[1,2,128,128]{3,2,1,0:T(8,128)S(1)} collective-permute-done((f32[1,2,128,128]{3,2,1,0:T(8,128)S(1)}, f32[1,2,128,128]{3,2,1,0:T(8,128)S(1)}, u32[]{:S(2)}, u32[]{:S(2)}) %collective-permute-start.21) | collective-permute-done | bytes 131104 | tf_op jit(solution)/shard_map/ppermute | solution.py:365
  53.9 1.2 %mix.3 = (f32[4,2,128,128]{3,2,1,0:T(8,128)}, f32[4,2,128,128]{3,2,1,0:T(8,128)}) custom-call(f32[16,128]{1,0:T(8,128)S(1)} %get-tuple-element.34.table_ref, f32[4,2,128,128]{3,2,1,0:T(8,128)S(1)} %by_energy.8.refs_0_, f32[4,2,128,128]{3,2,1,0:T(8,128)S(1)} %by_energy.9.refs_1_, f32[4,2,128,128]{3,2,1,0:T(8,128)S(1)} %get-tuple-element.39.refs_2_, ...), custom_call_target="tpu_custom_call" | custom-call | tf_op jit(solution)/shard_map/mix/pallas_call | solution.py:396
  (35 shorter events, 0.5 us)
Async XLA Ops:
  2.9 9.3 %collective-permute-start = (f32[3,128,128]{2,1,0:T(8,128)S(1)}, f32[3,128,128]{2,1,0:T(8,128)S(1)}, u32[]{:S(2)}, u32[]{:S(2)}) collective-permute-start(f32[3,128,128]{2,1,0:T(8,128)S(1)} %get-tuple-element.24), channel_id=1, source_target_pairs={{0,24},{1,25},{8,16},{9,17},{16,8},{17,9},{24,0},{25,1},{2,26},{3,... | collective-permute-start | bytes 589832 | tf_op jit(solution)/shard_map/ppermute | solution.py:295
  6.9 9.4 %collective-permute-start.1 = (f32[3,128,128]{2,1,0:T(8,128)S(1)}, f32[3,128,128]{2,1,0:T(8,128)S(1)}, u32[]{:S(2)}, u32[]{:S(2)}) collective-permute-start(f32[3,128,128]{2,1,0:T(8,128)S(1)} %get-tuple-element.25), channel_id=1, source_target_pairs={{0,8},{1,17},{8,0},{9,25},{16,24},{17,1},{24,16},{25,9},{2,10},{3,... | collective-permute-start | bytes 589832 | tf_op jit(solution)/shard_map/ppermute | solution.py:295
  9.6 6.6 %collective-permute-start.2 = (f32[3,128,128]{2,1,0:T(8,128)S(1)}, f32[3,128,128]{2,1,0:T(8,128)S(1)}, u32[]{:S(2)}, u32[]{:S(2)}) collective-permute-start(f32[3,128,128]{2,1,0:T(8,128)S(1)} %get-tuple-element.26), channel_id=1, source_target_pairs={{0,16},{1,9},{8,24},{9,1},{16,0},{17,25},{24,8},{25,17},{2,18},{3,... | collective-permute-start | bytes 589832 | tf_op jit(solution)/shard_map/ppermute | solution.py:295
  18.5 3.6 %collective-permute-start.3 = (f32[1,2,128,128]{3,2,1,0:T(8,128)S(1)}, f32[1,2,128,128]{3,2,1,0:T(8,128)S(1)}, u32[]{:S(2)}, u32[]{:S(2)}) collective-permute-start(f32[1,2,128,128]{3,2,1,0:T(8,128)S(1)} %get-tuple-element.27.refs_0_), channel_id=1, source_target_pairs={{0,1},{1,0},{2,3},{3,2},{4,5},{5,4},{6,7},{7,6},{8,9},{9,8},{10,11... | collective-permute-start | bytes 393224 | tf_op jit(solution)/shard_map/ppermute | solution.py:375
  18.6 7.3 %collective-permute-start.4 = (f32[1,2,128,128]{3,2,1,0:T(8,128)S(1)}, f32[1,2,128,128]{3,2,1,0:T(8,128)S(1)}, u32[]{:S(2)}, u32[]{:S(2)}) collective-permute-start(f32[1,2,128,128]{3,2,1,0:T(8,128)S(1)} %get-tuple-element.28), channel_id=1, source_target_pairs={{0,24},{1,25},{8,16},{9,17},{16,8},{17,9},{24,0},{25,1},{2,26},{3,... | collective-permute-start | bytes 393224 | tf_op jit(solution)/shard_map/ppermute | solution.py:295
  20.2 8.0 %collective-permute-start.5 = (f32[1,2,128,128]{3,2,1,0:T(8,128)S(1)}, f32[1,2,128,128]{3,2,1,0:T(8,128)S(1)}, u32[]{:S(2)}, u32[]{:S(2)}) collective-permute-start(f32[1,2,128,128]{3,2,1,0:T(8,128)S(1)} %get-tuple-element.29), channel_id=1, source_target_pairs={{0,8},{1,17},{8,0},{9,25},{16,24},{17,1},{24,16},{25,9},{2,10},{3,... | collective-permute-start | bytes 393224 | tf_op jit(solution)/shard_map/ppermute | solution.py:295
  21.5 6.7 %collective-permute-start.6 = (f32[1,2,128,128]{3,2,1,0:T(8,128)S(1)}, f32[1,2,128,128]{3,2,1,0:T(8,128)S(1)}, u32[]{:S(2)}, u32[]{:S(2)}) collective-permute-start(f32[1,2,128,128]{3,2,1,0:T(8,128)S(1)} %get-tuple-element.30), channel_id=1, source_target_pairs={{0,16},{1,9},{8,24},{9,1},{16,0},{17,25},{24,8},{25,17},{2,18},{3,... | collective-permute-start | bytes 393224 | tf_op jit(solution)/shard_map/ppermute | solution.py:295
  22.2 6.0 %collective-permute-start.7 = (f32[1,2,128,128]{3,2,1,0:T(8,128)S(1)}, f32[1,2,128,128]{3,2,1,0:T(8,128)S(1)}, u32[]{:S(2)}, u32[]{:S(2)}) collective-permute-start(f32[1,2,128,128]{3,2,1,0:T(8,128)S(1)} %momentum.6.refs_0_), channel_id=1, source_target_pairs={{0,2},{2,4},{4,6},{6,7},{7,5},{5,3},{3,1},{1,0},{8,10},{10,12},{12... | collective-permute-start | bytes 393224 | tf_op jit(solution)/shard_map/ppermute | solution.py:365
  23.8 6.6 %collective-permute-start.13 = (f32[1,2,128,128]{3,2,1,0:T(8,128)S(1)}, f32[1,2,128,128]{3,2,1,0:T(8,128)S(1)}, u32[]{:S(2)}, u32[]{:S(2)}) collective-permute-start(f32[1,2,128,128]{3,2,1,0:T(8,128)S(1)} %momentum.9.refs_0_), channel_id=1, source_target_pairs={{2,0},{4,2},{6,4},{7,6},{5,7},{3,5},{1,3},{0,1},{10,8},{12,10},{14... | collective-permute-start | bytes 393224 | tf_op jit(solution)/shard_map/ppermute | solution.py:365
  28.2 2.2 %collective-permute-start.8 = (f32[1,2,128,128]{3,2,1,0:T(8,128)S(1)}, f32[1,2,128,128]{3,2,1,0:T(8,128)S(1)}, u32[]{:S(2)}, u32[]{:S(2)}) collective-permute-start(f32[1,2,128,128]{3,2,1,0:T(8,128)S(1)} %collective-permute-done.4.refs_0_), channel_id=1, source_target_pairs={{0,1},{1,0},{2,3},{3,2},{4,5},{5,4},{6,7},{7,6},{8,9},{9,8},{10,11... | collective-permute-start | bytes 393224 | tf_op jit(solution)/shard_map/ppermute | solution.py:375
  28.2 2.2 %collective-permute-start.9 = (f32[1,2,128,128]{3,2,1,0:T(8,128)S(1)}, f32[1,2,128,128]{3,2,1,0:T(8,128)S(1)}, u32[]{:S(2)}, u32[]{:S(2)}) collective-permute-start(f32[1,2,128,128]{3,2,1,0:T(8,128)S(1)} %collective-permute-done.5.refs_1_), channel_id=1, source_target_pairs={{0,1},{1,0},{2,3},{3,2},{4,5},{5,4},{6,7},{7,6},{8,9},{9,8},{10,11... | collective-permute-start | bytes 393224 | tf_op jit(solution)/shard_map/ppermute | solution.py:375
  28.7 3.8 %collective-permute-start.10 = (f32[1,2,128,128]{3,2,1,0:T(8,128)S(1)}, f32[1,2,128,128]{3,2,1,0:T(8,128)S(1)}, u32[]{:S(2)}, u32[]{:S(2)}) collective-permute-start(f32[1,2,128,128]{3,2,1,0:T(8,128)S(1)} %collective-permute-done.6.refs_0_), channel_id=1, source_target_pairs={{0,1},{1,0},{2,3},{3,2},{4,5},{5,4},{6,7},{7,6},{8,9},{9,8},{10,11... | collective-permute-start | bytes 393224 | tf_op jit(solution)/shard_map/ppermute | solution.py:375
  28.8 5.4 %collective-permute-start.11 = (f32[1,2,128,128]{3,2,1,0:T(8,128)S(1)}, f32[1,2,128,128]{3,2,1,0:T(8,128)S(1)}, u32[]{:S(2)}, u32[]{:S(2)}) collective-permute-start(f32[1,2,128,128]{3,2,1,0:T(8,128)S(1)} %collective-permute-done.7.refs_0_), channel_id=1, source_target_pairs={{0,2},{2,4},{4,6},{6,7},{7,5},{5,3},{3,1},{1,0},{8,10},{10,12},{12... | collective-permute-start | bytes 393224 | tf_op jit(solution)/shard_map/ppermute | solution.py:365
  30.4 6.3 %collective-permute-start.14 = (f32[1,2,128,128]{3,2,1,0:T(8,128)S(1)}, f32[1,2,128,128]{3,2,1,0:T(8,128)S(1)}, u32[]{:S(2)}, u32[]{:S(2)}) collective-permute-start(f32[1,2,128,128]{3,2,1,0:T(8,128)S(1)} %collective-permute-done.13.refs_0_), channel_id=1, source_target_pairs={{2,0},{4,2},{6,4},{7,6},{5,7},{3,5},{1,3},{0,1},{10,8},{12,10},{14... | collective-permute-start | bytes 393224 | tf_op jit(solution)/shard_map/ppermute | solution.py:365
  30.4 12.7 %collective-permute-start.12 = (f32[2,2,128,128]{3,2,1,0:T(8,128)S(1)}, f32[2,2,128,128]{3,2,1,0:T(8,128)S(1)}, u32[]{:S(2)}, u32[]{:S(2)}) collective-permute-start(f32[2,2,128,128]{3,2,1,0:T(8,128)S(1)} %momentum.7.refs_1_), channel_id=1, source_target_pairs={{0,2},{2,4},{4,6},{6,7},{7,5},{5,3},{3,1},{1,0},{8,10},{10,12},{12... | collective-permute-start | bytes 786440 | tf_op jit(solution)/shard_map/ppermute | solution.py:365
  32.5 12.3 %collective-permute-start.19 = (f32[2,2,128,128]{3,2,1,0:T(8,128)S(1)}, f32[2,2,128,128]{3,2,1,0:T(8,128)S(1)}, u32[]{:S(2)}, u32[]{:S(2)}) collective-permute-start(f32[2,2,128,128]{3,2,1,0:T(8,128)S(1)} %momentum.10.refs_1_), channel_id=1, source_target_pairs={{2,0},{4,2},{6,4},{7,6},{5,7},{3,5},{1,3},{0,1},{10,8},{12,10},{14... | collective-permute-start | bytes 786440 | tf_op jit(solution)/shard_map/ppermute | solution.py:365
  36.7 6.5 %collective-permute-start.15 = (f32[1,2,128,128]{3,2,1,0:T(8,128)S(1)}, f32[1,2,128,128]{3,2,1,0:T(8,128)S(1)}, u32[]{:S(2)}, u32[]{:S(2)}) collective-permute-start(f32[1,2,128,128]{3,2,1,0:T(8,128)S(1)} %momentum.11.refs_2_), channel_id=1, source_target_pairs={{2,0},{4,2},{6,4},{7,6},{5,7},{3,5},{1,3},{0,1},{10,8},{12,10},{14... | collective-permute-start | bytes 393224 | tf_op jit(solution)/shard_map/ppermute | solution.py:365
  36.7 8.1 %collective-permute-start.17 = (f32[1,2,128,128]{3,2,1,0:T(8,128)S(1)}, f32[1,2,128,128]{3,2,1,0:T(8,128)S(1)}, u32[]{:S(2)}, u32[]{:S(2)}) collective-permute-start(f32[1,2,128,128]{3,2,1,0:T(8,128)S(1)} %momentum.8.refs_2_), channel_id=1, source_target_pairs={{0,2},{2,4},{4,6},{6,7},{7,5},{5,3},{3,1},{1,0},{8,10},{10,12},{12... | collective-permute-start | bytes 393224 | tf_op jit(solution)/shard_map/ppermute | solution.py:365
  43.2 10.0 %collective-permute-start.16 = (f32[2,2,128,128]{3,2,1,0:T(8,128)S(1)}, f32[2,2,128,128]{3,2,1,0:T(8,128)S(1)}, u32[]{:S(2)}, u32[]{:S(2)}) collective-permute-start(f32[2,2,128,128]{3,2,1,0:T(8,128)S(1)} %collective-permute-done.12.refs_1_), channel_id=1, source_target_pairs={{0,2},{2,4},{4,6},{6,7},{7,5},{5,3},{3,1},{1,0},{8,10},{10,12},{12... | collective-permute-start | bytes 786440 | tf_op jit(solution)/shard_map/ppermute | solution.py:365
  44.8 9.1 %collective-permute-start.20 = (f32[2,2,128,128]{3,2,1,0:T(8,128)S(1)}, f32[2,2,128,128]{3,2,1,0:T(8,128)S(1)}, u32[]{:S(2)}, u32[]{:S(2)}) collective-permute-start(f32[2,2,128,128]{3,2,1,0:T(8,128)S(1)} %collective-permute-done.19.refs_1_), channel_id=1, source_target_pairs={{2,0},{4,2},{6,4},{7,6},{5,7},{3,5},{1,3},{0,1},{10,8},{12,10},{14... | collective-permute-start | bytes 786440 | tf_op jit(solution)/shard_map/ppermute | solution.py:365
  44.8 8.4 %collective-permute-start.18 = (f32[1,2,128,128]{3,2,1,0:T(8,128)S(1)}, f32[1,2,128,128]{3,2,1,0:T(8,128)S(1)}, u32[]{:S(2)}, u32[]{:S(2)}) collective-permute-start(f32[1,2,128,128]{3,2,1,0:T(8,128)S(1)} %collective-permute-done.17.refs_2_), channel_id=1, source_target_pairs={{0,2},{2,4},{4,6},{6,7},{7,5},{5,3},{3,1},{1,0},{8,10},{10,12},{12... | collective-permute-start | bytes 393224 | tf_op jit(solution)/shard_map/ppermute | solution.py:365
  46.8 7.1 %collective-permute-start.21 = (f32[1,2,128,128]{3,2,1,0:T(8,128)S(1)}, f32[1,2,128,128]{3,2,1,0:T(8,128)S(1)}, u32[]{:S(2)}, u32[]{:S(2)}) collective-permute-start(f32[1,2,128,128]{3,2,1,0:T(8,128)S(1)} %collective-permute-done.15.refs_2_), channel_id=1, source_target_pairs={{2,0},{4,2},{6,4},{7,6},{5,7},{3,5},{1,3},{0,1},{10,8},{12,10},{14... | collective-permute-start | bytes 393224 | tf_op jit(solution)/shard_map/ppermute | solution.py:365
  46.8 0.7 %copy-start = (s32[4]{0:T(128)S(1)}, s32[4]{0:T(128)}, u32[]{:S(2)}) copy-start(s32[4]{0:T(128)} %shift_ref.1) | copy-start | bytes 52
  46.8 0.7 %copy-start.1 = (f32[4]{0:T(128)S(1)}, f32[4]{0:T(128)}, u32[]{:S(2)}) copy-start(f32[4]{0:T(128)} %weight_ref.1) | copy-start | bytes 52

commit v17 on v16

--- a/solution.py
+++ b/solution.py
@@ -377,7 +377,7 @@
         for m in range(2):
             fields[m].append(parts[m])
         if len(hops[0]) == 2:
-            parts, _ = lax.optimization_barrier((parts, ahead))
+            parts = [lax.optimization_barrier((parts[m], ahead[m]))[0] for m in range(2)]
         for m in range(2):
             hops[m].append(hop(parts[m], m))
     zero, one = (by_energy(m, fields[m]) for m in range(2))

time: 55.2 us -> 56 us (1.014)
  starting transfers between devices: 19.8 us -> 21.1 us
    ppermute x12, starting transfers between devices: 10.9 us -> 12.2 us  [hop(): return lax.ppermute(value, ('energy', 'mom'), ways[role])]
    ppermute x12, waiting for transfers between devices: 13.2 us -> 12.2 us  [hop(): return lax.ppermute(value, ('energy', 'mom'), ways[role])]
  transfers between devices with their start and end apart: 22 -> 22, of which waited for: 9 -> 11; matrix products, arithmetic and copies ran while one was open for 0% -> 0% of each run, Pallas kernels for 7% -> 7%
where the time goes in v17:
time: 56 us; the launch traced here: 55.9 us
  waiting for transfers between devices  23.6 us (42%)
  starting transfers between devices  21.1 us (38%)
  Pallas kernels  9.75 us (17%)
  between operations  0.81 us (1%)
  local copies, waits for them, and re-layouts  0.64 us (1%)
    ppermute x12, starting transfers between devices, hop(): return lax.ppermute(value, ('energy', 'mom'), ways[role])  12.2 us
    ppermute x12, waiting for transfers between devices, hop(): return lax.ppermute(value, ('energy', 'mom'), ways[role])  12.2 us
    ppermute x6, waiting for transfers between devices, exchange(): return lax.ppermute(slots[i], ('len', 'mom'), pairs)  10.8 us
    ppermute x6, starting transfers between devices, exchange(): return lax.ppermute(slots[i], ('len', 'mom'), pairs)  8.23 us
    pallas_call x2, Pallas kernels, inverse(): pl.pallas_call(functools.partial(inverse_kernel, total, layers, slots), o...  4.51 us
    pallas_call x1, Pallas kernels, shards(): pl.pallas_call(functools.partial(chain_kernel, layers), out_shape=[part]...  2.22 us
    pallas_call x2, Pallas kernels, mix(): pl.pallas_call(functools.partial(mix_kernel, total, items, False, last),...  1.75 us
  transfers between devices with their start and end apart: 22, of which 11 were waited for; matrix products, arithmetic and copies ran while one was open for 0% of the time, Pallas kernels for 7%

profile of v17, /device:TPU:0, one launch (start us, length us, event | category | flops | bytes accessed | tf_op | source)
XLA Modules:
  0.0 55.9 jit_solution(6809654727547057409)
XLA Ops:
  0.6 2.3 %inverse.3 = (f32[3,128,128]{2,1,0:T(8,128)S(1)}, f32[3,128,128]{2,1,0:T(8,128)S(1)}) custom-call(f32[2,128,128]{2,1,0:T(8,128)} %bitcast.9, f32[4,2,128,128]{3,2,1,0:T(8,128)} %bitcast.5, f32[128,128]{1,0:T(8,128)} %bitcast.11, s32[128,128]{1,0:T(8,128)} %pattern_any.3), custom_call_target="tpu_custom_call" | custom-call | flops 402653184 | bytes 262144 | tf_op jit(solution)/shard_map/inverse/pallas_call | solution.py:302
  2.9 4.0 %collective-permute-start = (f32[3,128,128]{2,1,0:T(8,128)S(1)}, f32[3,128,128]{2,1,0:T(8,128)S(1)}, u32[]{:S(2)}, u32[]{:S(2)}) collective-permute-start(f32[3,128,128]{2,1,0:T(8,128)S(1)} %get-tuple-element.24), channel_id=1, source_target_pairs={{0,24},{1,25},{8,16},{9,17},{16,8},{17,9},{24,0},{25,1},{2,26},{3,... | collective-permute-start | bytes 589832 | tf_op jit(solution)/shard_map/ppermute | solution.py:295
  6.9 0.5 collective-permute-start.1
  7.4 2.2 %inverse.2 = (f32[3,128,128]{2,1,0:T(8,128)S(1)}, f32[3,128,128]{2,1,0:T(8,128)S(1)}) custom-call(f32[2,128,128]{2,1,0:T(8,128)} %bitcast.10, f32[4,2,128,128]{3,2,1,0:T(8,128)} %bitcast.6, f32[128,128]{1,0:T(8,128)} %bitcast.12, s32[128,128]{1,0:T(8,128)} %pattern_any.3), custom_call_target="tpu_custom_call" | custom-call | flops 402653184 | bytes 262144 | tf_op jit(solution)/shard_map/inverse/pallas_call | solution.py:302
  9.6 0.2 collective-permute-start.2
  9.8 2.3 %collective-permute-done.refs_1_ = f32[3,128,128]{2,1,0:T(8,128)S(1)} collective-permute-done((f32[3,128,128]{2,1,0:T(8,128)S(1)}, f32[3,128,128]{2,1,0:T(8,128)S(1)}, u32[]{:S(2)}, u32[]{:S(2)}) %collective-permute-start) | collective-permute-done | bytes 196640 | tf_op jit(solution)/shard_map/ppermute | solution.py:295
  12.2 4.1 %collective-permute-done.1.refs_2_ = f32[3,128,128]{2,1,0:T(8,128)S(1)} collective-permute-done((f32[3,128,128]{2,1,0:T(8,128)S(1)}, f32[3,128,128]{2,1,0:T(8,128)S(1)}, u32[]{:S(2)}, u32[]{:S(2)}) %collective-permute-start.1) | collective-permute-done | bytes 196640 | tf_op jit(solution)/shard_map/ppermute | solution.py:295
  16.3 2.2 %chains.1 = (f32[1,2,128,128]{3,2,1,0:T(8,128)S(1)}, f32[1,2,128,128]{3,2,1,0:T(8,128)S(1)}, f32[1,2,128,128]{3,2,1,0:T(8,128)S(1)}, f32[1,2,128,128]{3,2,1,0:T(8,128)S(1)}) custom-call(f32[3,128,128]{2,1,0:T(8,128)S(1)} %get-tuple-element.23.refs_0_, f32[3,128,128]{2,1,0:T(8,128)S(1)} %collective-permute-done.refs_1_, ...), custom_call_target="tpu_custom_call" | custom-call | tf_op jit(solution)/shard_map/chains/pallas_call | solution.py:326
  18.6 1.6 %collective-permute-start.4 = (f32[1,2,128,128]{3,2,1,0:T(8,128)S(1)}, f32[1,2,128,128]{3,2,1,0:T(8,128)S(1)}, u32[]{:S(2)}, u32[]{:S(2)}) collective-permute-start(f32[1,2,128,128]{3,2,1,0:T(8,128)S(1)} %get-tuple-element.28), channel_id=1, source_target_pairs={{0,24},{1,25},{8,16},{9,17},{16,8},{17,9},{24,0},{25,1},{2,26},{3,... | collective-permute-start | bytes 393224 | tf_op jit(solution)/shard_map/ppermute | solution.py:295
  20.2 1.4 %collective-permute-start.5 = (f32[1,2,128,128]{3,2,1,0:T(8,128)S(1)}, f32[1,2,128,128]{3,2,1,0:T(8,128)S(1)}, u32[]{:S(2)}, u32[]{:S(2)}) collective-permute-start(f32[1,2,128,128]{3,2,1,0:T(8,128)S(1)} %get-tuple-element.29), channel_id=1, source_target_pairs={{0,8},{1,17},{8,0},{9,25},{16,24},{17,1},{24,16},{25,9},{2,10},{3,... | collective-permute-start | bytes 393224 | tf_op jit(solution)/shard_map/ppermute | solution.py:295
  21.5 0.6 %collective-permute-start.6 = (f32[1,2,128,128]{3,2,1,0:T(8,128)S(1)}, f32[1,2,128,128]{3,2,1,0:T(8,128)S(1)}, u32[]{:S(2)}, u32[]{:S(2)}) collective-permute-start(f32[1,2,128,128]{3,2,1,0:T(8,128)S(1)} %get-tuple-element.30), channel_id=1, source_target_pairs={{0,16},{1,9},{8,24},{9,1},{16,0},{17,25},{24,8},{25,17},{2,18},{3,... | collective-permute-start | bytes 393224 | tf_op jit(solution)/shard_map/ppermute | solution.py:295
  22.2 1.6 %collective-permute-start.7 = (f32[1,2,128,128]{3,2,1,0:T(8,128)S(1)}, f32[1,2,128,128]{3,2,1,0:T(8,128)S(1)}, u32[]{:S(2)}, u32[]{:S(2)}) collective-permute-start(f32[1,2,128,128]{3,2,1,0:T(8,128)S(1)} %momentum.6.refs_0_), channel_id=1, source_target_pairs={{0,2},{2,4},{4,6},{6,7},{7,5},{5,3},{3,1},{1,0},{8,10},{10,12},{12... | collective-permute-start | bytes 393224 | tf_op jit(solution)/shard_map/ppermute | solution.py:365
  23.8 2.1 %collective-permute-done.4.refs_0_ = f32[1,2,128,128]{3,2,1,0:T(8,128)S(1)} collective-permute-done((f32[1,2,128,128]{3,2,1,0:T(8,128)S(1)}, f32[1,2,128,128]{3,2,1,0:T(8,128)S(1)}, u32[]{:S(2)}, u32[]{:S(2)}) %collective-permute-start.4) | collective-permute-done | bytes 131104 | tf_op jit(solution)/shard_map/ppermute | solution.py:295
  25.9 2.3 %collective-permute-done.5.refs_1_ = f32[1,2,128,128]{3,2,1,0:T(8,128)S(1)} collective-permute-done((f32[1,2,128,128]{3,2,1,0:T(8,128)S(1)}, f32[1,2,128,128]{3,2,1,0:T(8,128)S(1)}, u32[]{:S(2)}, u32[]{:S(2)}) %collective-permute-start.5) | collective-permute-done | bytes 131104 | tf_op jit(solution)/shard_map/ppermute | solution.py:295
  28.2 0.5 collective-permute-start.9
  28.8 0.4 collective-permute-start.14
  29.2 0.3 collective-permute-done.8.refs_2_
  29.6 0.2 collective-permute-done.9.refs_3_
  29.8 1.6 %collective-permute-start.12 = (f32[2,2,128,128]{3,2,1,0:T(8,128)S(1)}, f32[2,2,128,128]{3,2,1,0:T(8,128)S(1)}, u32[]{:S(2)}, u32[]{:S(2)}) collective-permute-start(f32[2,2,128,128]{3,2,1,0:T(8,128)S(1)} %momentum.7.refs_1_), channel_id=1, source_target_pairs={{0,2},{2,4},{4,6},{6,7},{7,5},{5,3},{3,1},{1,0},{8,10},{10,12},{12... | collective-permute-start | bytes 786440 | tf_op jit(solution)/shard_map/ppermute | solution.py:365
  31.4 2.0 %collective-permute-start.11 = (f32[1,2,128,128]{3,2,1,0:T(8,128)S(1)}, f32[1,2,128,128]{3,2,1,0:T(8,128)S(1)}, u32[]{:S(2)}, u32[]{:S(2)}) collective-permute-start(f32[1,2,128,128]{3,2,1,0:T(8,128)S(1)} %collective-permute-done.7.refs_0_), channel_id=1, source_target_pairs={{0,2},{2,4},{4,6},{6,7},{7,5},{5,3},{3,1},{1,0},{8,10},{10,12},{12... | collective-permute-start | bytes 393224 | tf_op jit(solution)/shard_map/ppermute | solution.py:365
  33.4 0.9 %collective-permute-done.14.refs_0_ = f32[1,2,128,128]{3,2,1,0:T(8,128)S(1)} collective-permute-done((f32[1,2,128,128]{3,2,1,0:T(8,128)S(1)}, f32[1,2,128,128]{3,2,1,0:T(8,128)S(1)}, u32[]{:S(2)}, u32[]{:S(2)}) %collective-permute-start.14) | collective-permute-done | bytes 131104 | tf_op jit(solution)/shard_map/ppermute | solution.py:365
  34.4 6.4 %collective-permute-done.11.refs_0_ = f32[1,2,128,128]{3,2,1,0:T(8,128)S(1)} collective-permute-done((f32[1,2,128,128]{3,2,1,0:T(8,128)S(1)}, f32[1,2,128,128]{3,2,1,0:T(8,128)S(1)}, u32[]{:S(2)}, u32[]{:S(2)}) %collective-permute-start.11) | collective-permute-done | bytes 131104 | tf_op jit(solution)/shard_map/ppermute | solution.py:365
  40.8 2.5 %collective-permute-start.17 = (f32[1,2,128,128]{3,2,1,0:T(8,128)S(1)}, f32[1,2,128,128]{3,2,1,0:T(8,128)S(1)}, u32[]{:S(2)}, u32[]{:S(2)}) collective-permute-start(f32[1,2,128,128]{3,2,1,0:T(8,128)S(1)} %momentum.8.refs_2_), channel_id=1, source_target_pairs={{0,2},{2,4},{4,6},{6,7},{7,5},{5,3},{3,1},{1,0},{8,10},{10,12},{12... | collective-permute-start | bytes 393224 | tf_op jit(solution)/shard_map/ppermute | solution.py:365
  43.3 1.6 %collective-permute-start.16 = (f32[2,2,128,128]{3,2,1,0:T(8,128)S(1)}, f32[2,2,128,128]{3,2,1,0:T(8,128)S(1)}, u32[]{:S(2)}, u32[]{:S(2)}) collective-permute-start(f32[2,2,128,128]{3,2,1,0:T(8,128)S(1)} %collective-permute-done.12.refs_1_), channel_id=1, source_target_pairs={{0,2},{2,4},{4,6},{6,7},{7,5},{5,3},{3,1},{1,0},{8,10},{10,12},{12... | collective-permute-start | bytes 786440 | tf_op jit(solution)/shard_map/ppermute | solution.py:365
  44.9 2.3 %collective-permute-done.17.refs_2_ = f32[1,2,128,128]{3,2,1,0:T(8,128)S(1)} collective-permute-done((f32[1,2,128,128]{3,2,1,0:T(8,128)S(1)}, f32[1,2,128,128]{3,2,1,0:T(8,128)S(1)}, u32[]{:S(2)}, u32[]{:S(2)}) %collective-permute-start.17) | collective-permute-done | bytes 131104 | tf_op jit(solution)/shard_map/ppermute | solution.py:365
  47.2 2.5 %collective-permute-start.18 = (f32[1,2,128,128]{3,2,1,0:T(8,128)S(1)}, f32[1,2,128,128]{3,2,1,0:T(8,128)S(1)}, u32[]{:S(2)}, u32[]{:S(2)}) collective-permute-start(f32[1,2,128,128]{3,2,1,0:T(8,128)S(1)} %collective-permute-done.17.refs_2_), channel_id=1, source_target_pairs={{0,2},{2,4},{4,6},{6,7},{7,5},{5,3},{3,1},{1,0},{8,10},{10,12},{12... | collective-permute-start | bytes 393224 | tf_op jit(solution)/shard_map/ppermute | solution.py:365
  49.8 0.6 %copy-done = s32[4]{0:T(128)S(1)} copy-done((s32[4]{0:T(128)S(1)}, s32[4]{0:T(128)}, u32[]{:S(2)}) %copy-start) | copy-done | bytes 40
  50.4 0.9 %local.1 = (f32[4,2,128,128]{3,2,1,0:T(8,128)S(1)}, f32[4,2,128,128]{3,2,1,0:T(8,128)S(1)}, f32[16,128]{1,0:T(8,128)S(1)}) custom-call(s32[4]{0:T(128)S(1)} %copy-done, f32[4]{0:T(128)S(1)} %copy-done.1, f32[4,2,128,128]{3,2,1,0:T(8,128)S(1)} %by_energy.6.zero_ref, f32[4,2,128,128]{3,2,1,0:T(8,128)S(1)} %by_energy.7.one_ref), custom_call_target="tpu_custom_call" | custom-call | tf_op jit(solution)/shard_map/local/pallas_call | solution.py:385
  51.5 0.6 %mix.2 = (f32[4,2,128,128]{3,2,1,0:T(8,128)S(1)}, f32[4,2,128,128]{3,2,1,0:T(8,128)S(1)}) custom-call(f32[16,128]{1,0:T(8,128)S(1)} %get-tuple-element.34.table_ref, f32[4,2,128,128]{3,2,1,0:T(8,128)S(1)} %by_energy.10.refs_0_, f32[4,2,128,128]{3,2,1,0:T(8,128)S(1)} %by_energy.11.refs_1_, f32[4,2,128,128]{3,2,1,0:T(8,128)S(1)} %get-tuple-element.38.refs_2_, ...), custom_call_target="tpu_custom_call" | custom-call | tf_op jit(solution)/shard_map/mix/pallas_call | solution.py:396
  52.1 2.0 %collective-permute-done.18.refs_2_ = f32[1,2,128,128]{3,2,1,0:T(8,128)S(1)} collective-permute-done((f32[1,2,128,128]{3,2,1,0:T(8,128)S(1)}, f32[1,2,128,128]{3,2,1,0:T(8,128)S(1)}, u32[]{:S(2)}, u32[]{:S(2)}) %collective-permute-start.18) | collective-permute-done | bytes 131104 | tf_op jit(solution)/shard_map/ppermute | solution.py:365
  54.1 0.5 collective-permute-done.21.refs_2_
  54.7 1.2 %mix.3 = (f32[4,2,128,128]{3,2,1,0:T(8,128)}, f32[4,2,128,128]{3,2,1,0:T(8,128)}) custom-call(f32[16,128]{1,0:T(8,128)S(1)} %get-tuple-element.34.table_ref, f32[4,2,128,128]{3,2,1,0:T(8,128)S(1)} %by_energy.8.refs_0_, f32[4,2,128,128]{3,2,1,0:T(8,128)S(1)} %by_energy.9.refs_1_, f32[4,2,128,128]{3,2,1,0:T(8,128)S(1)} %get-tuple-element.39.refs_2_, ...), custom_call_target="tpu_custom_call" | custom-call | tf_op jit(solution)/shard_map/mix/pallas_call | solution.py:396
  (35 shorter events, 0.7 us)
Async XLA Ops:
  2.9 9.3 %collective-permute-start = (f32[3,128,128]{2,1,0:T(8,128)S(1)}, f32[3,128,128]{2,1,0:T(8,128)S(1)}, u32[]{:S(2)}, u32[]{:S(2)}) collective-permute-start(f32[3,128,128]{2,1,0:T(8,128)S(1)} %get-tuple-element.24), channel_id=1, source_target_pairs={{0,24},{1,25},{8,16},{9,17},{16,8},{17,9},{24,0},{25,1},{2,26},{3,... | collective-permute-start | bytes 589832 | tf_op jit(solution)/shard_map/ppermute | solution.py:295
  6.9 9.4 %collective-permute-start.1 = (f32[3,128,128]{2,1,0:T(8,128)S(1)}, f32[3,128,128]{2,1,0:T(8,128)S(1)}, u32[]{:S(2)}, u32[]{:S(2)}) collective-permute-start(f32[3,128,128]{2,1,0:T(8,128)S(1)} %get-tuple-element.25), channel_id=1, source_target_pairs={{0,8},{1,17},{8,0},{9,25},{16,24},{17,1},{24,16},{25,9},{2,10},{3,... | collective-permute-start | bytes 589832 | tf_op jit(solution)/shard_map/ppermute | solution.py:295
  9.6 6.6 %collective-permute-start.2 = (f32[3,128,128]{2,1,0:T(8,128)S(1)}, f32[3,128,128]{2,1,0:T(8,128)S(1)}, u32[]{:S(2)}, u32[]{:S(2)}) collective-permute-start(f32[3,128,128]{2,1,0:T(8,128)S(1)} %get-tuple-element.26), channel_id=1, source_target_pairs={{0,16},{1,9},{8,24},{9,1},{16,0},{17,25},{24,8},{25,17},{2,18},{3,... | collective-permute-start | bytes 589832 | tf_op jit(solution)/shard_map/ppermute | solution.py:295
  18.5 3.6 %collective-permute-start.3 = (f32[1,2,128,128]{3,2,1,0:T(8,128)S(1)}, f32[1,2,128,128]{3,2,1,0:T(8,128)S(1)}, u32[]{:S(2)}, u32[]{:S(2)}) collective-permute-start(f32[1,2,128,128]{3,2,1,0:T(8,128)S(1)} %get-tuple-element.27.refs_0_), channel_id=1, source_target_pairs={{0,1},{1,0},{2,3},{3,2},{4,5},{5,4},{6,7},{7,6},{8,9},{9,8},{10,11... | collective-permute-start | bytes 393224 | tf_op jit(solution)/shard_map/ppermute | solution.py:375
  18.6 7.3 %collective-permute-start.4 = (f32[1,2,128,128]{3,2,1,0:T(8,128)S(1)}, f32[1,2,128,128]{3,2,1,0:T(8,128)S(1)}, u32[]{:S(2)}, u32[]{:S(2)}) collective-permute-start(f32[1,2,128,128]{3,2,1,0:T(8,128)S(1)} %get-tuple-element.28), channel_id=1, source_target_pairs={{0,24},{1,25},{8,16},{9,17},{16,8},{17,9},{24,0},{25,1},{2,26},{3,... | collective-permute-start | bytes 393224 | tf_op jit(solution)/shard_map/ppermute | solution.py:295
  20.2 8.0 %collective-permute-start.5 = (f32[1,2,128,128]{3,2,1,0:T(8,128)S(1)}, f32[1,2,128,128]{3,2,1,0:T(8,128)S(1)}, u32[]{:S(2)}, u32[]{:S(2)}) collective-permute-start(f32[1,2,128,128]{3,2,1,0:T(8,128)S(1)} %get-tuple-element.29), channel_id=1, source_target_pairs={{0,8},{1,17},{8,0},{9,25},{16,24},{17,1},{24,16},{25,9},{2,10},{3,... | collective-permute-start | bytes 393224 | tf_op jit(solution)/shard_map/ppermute | solution.py:295
  21.5 6.7 %collective-permute-start.6 = (f32[1,2,128,128]{3,2,1,0:T(8,128)S(1)}, f32[1,2,128,128]{3,2,1,0:T(8,128)S(1)}, u32[]{:S(2)}, u32[]{:S(2)}) collective-permute-start(f32[1,2,128,128]{3,2,1,0:T(8,128)S(1)} %get-tuple-element.30), channel_id=1, source_target_pairs={{0,16},{1,9},{8,24},{9,1},{16,0},{17,25},{24,8},{25,17},{2,18},{3,... | collective-permute-start | bytes 393224 | tf_op jit(solution)/shard_map/ppermute | solution.py:295
  22.2 6.0 %collective-permute-start.7 = (f32[1,2,128,128]{3,2,1,0:T(8,128)S(1)}, f32[1,2,128,128]{3,2,1,0:T(8,128)S(1)}, u32[]{:S(2)}, u32[]{:S(2)}) collective-permute-start(f32[1,2,128,128]{3,2,1,0:T(8,128)S(1)} %momentum.6.refs_0_), channel_id=1, source_target_pairs={{0,2},{2,4},{4,6},{6,7},{7,5},{5,3},{3,1},{1,0},{8,10},{10,12},{12... | collective-permute-start | bytes 393224 | tf_op jit(solution)/shard_map/ppermute | solution.py:365
  23.8 5.0 %collective-permute-start.13 = (f32[1,2,128,128]{3,2,1,0:T(8,128)S(1)}, f32[1,2,128,128]{3,2,1,0:T(8,128)S(1)}, u32[]{:S(2)}, u32[]{:S(2)}) collective-permute-start(f32[1,2,128,128]{3,2,1,0:T(8,128)S(1)} %momentum.9.refs_0_), channel_id=1, source_target_pairs={{2,0},{4,2},{6,4},{7,6},{5,7},{3,5},{1,3},{0,1},{10,8},{12,10},{14... | collective-permute-start | bytes 393224 | tf_op jit(solution)/shard_map/ppermute | solution.py:365
  28.2 1.3 %collective-permute-start.8 = (f32[1,2,128,128]{3,2,1,0:T(8,128)S(1)}, f32[1,2,128,128]{3,2,1,0:T(8,128)S(1)}, u32[]{:S(2)}, u32[]{:S(2)}) collective-permute-start(f32[1,2,128,128]{3,2,1,0:T(8,128)S(1)} %collective-permute-done.4.refs_0_), channel_id=1, source_target_pairs={{0,1},{1,0},{2,3},{3,2},{4,5},{5,4},{6,7},{7,6},{8,9},{9,8},{10,11... | collective-permute-start | bytes 393224 | tf_op jit(solution)/shard_map/ppermute | solution.py:375
  28.2 1.5 %collective-permute-start.9 = (f32[1,2,128,128]{3,2,1,0:T(8,128)S(1)}, f32[1,2,128,128]{3,2,1,0:T(8,128)S(1)}, u32[]{:S(2)}, u32[]{:S(2)}) collective-permute-start(f32[1,2,128,128]{3,2,1,0:T(8,128)S(1)} %collective-permute-done.5.refs_1_), channel_id=1, source_target_pairs={{0,1},{1,0},{2,3},{3,2},{4,5},{5,4},{6,7},{7,6},{8,9},{9,8},{10,11... | collective-permute-start | bytes 393224 | tf_op jit(solution)/shard_map/ppermute | solution.py:375
  28.7 4.7 %collective-permute-start.10 = (f32[1,2,128,128]{3,2,1,0:T(8,128)S(1)}, f32[1,2,128,128]{3,2,1,0:T(8,128)S(1)}, u32[]{:S(2)}, u32[]{:S(2)}) collective-permute-start(f32[1,2,128,128]{3,2,1,0:T(8,128)S(1)} %collective-permute-done.6.refs_0_), channel_id=1, source_target_pairs={{0,1},{1,0},{2,3},{3,2},{4,5},{5,4},{6,7},{7,6},{8,9},{9,8},{10,11... | collective-permute-start | bytes 393224 | tf_op jit(solution)/shard_map/ppermute | solution.py:375
  28.8 5.6 %collective-permute-start.14 = (f32[1,2,128,128]{3,2,1,0:T(8,128)S(1)}, f32[1,2,128,128]{3,2,1,0:T(8,128)S(1)}, u32[]{:S(2)}, u32[]{:S(2)}) collective-permute-start(f32[1,2,128,128]{3,2,1,0:T(8,128)S(1)} %collective-permute-done.13.refs_0_), channel_id=1, source_target_pairs={{2,0},{4,2},{6,4},{7,6},{5,7},{3,5},{1,3},{0,1},{10,8},{12,10},{14... | collective-permute-start | bytes 393224 | tf_op jit(solution)/shard_map/ppermute | solution.py:365
  29.8 13.6 %collective-permute-start.12 = (f32[2,2,128,128]{3,2,1,0:T(8,128)S(1)}, f32[2,2,128,128]{3,2,1,0:T(8,128)S(1)}, u32[]{:S(2)}, u32[]{:S(2)}) collective-permute-start(f32[2,2,128,128]{3,2,1,0:T(8,128)S(1)} %momentum.7.refs_1_), channel_id=1, source_target_pairs={{0,2},{2,4},{4,6},{6,7},{7,5},{5,3},{3,1},{1,0},{8,10},{10,12},{12... | collective-permute-start | bytes 786440 | tf_op jit(solution)/shard_map/ppermute | solution.py:365
  31.4 13.5 %collective-permute-start.19 = (f32[2,2,128,128]{3,2,1,0:T(8,128)S(1)}, f32[2,2,128,128]{3,2,1,0:T(8,128)S(1)}, u32[]{:S(2)}, u32[]{:S(2)}) collective-permute-start(f32[2,2,128,128]{3,2,1,0:T(8,128)S(1)} %momentum.10.refs_1_), channel_id=1, source_target_pairs={{2,0},{4,2},{6,4},{7,6},{5,7},{3,5},{1,3},{0,1},{10,8},{12,10},{14... | collective-permute-start | bytes 786440 | tf_op jit(solution)/shard_map/ppermute | solution.py:365
  31.4 9.4 %collective-permute-start.11 = (f32[1,2,128,128]{3,2,1,0:T(8,128)S(1)}, f32[1,2,128,128]{3,2,1,0:T(8,128)S(1)}, u32[]{:S(2)}, u32[]{:S(2)}) collective-permute-start(f32[1,2,128,128]{3,2,1,0:T(8,128)S(1)} %collective-permute-done.7.refs_0_), channel_id=1, source_target_pairs={{0,2},{2,4},{4,6},{6,7},{7,5},{5,3},{3,1},{1,0},{8,10},{10,12},{12... | collective-permute-start | bytes 393224 | tf_op jit(solution)/shard_map/ppermute | solution.py:365
  34.4 8.9 %collective-permute-start.15 = (f32[1,2,128,128]{3,2,1,0:T(8,128)S(1)}, f32[1,2,128,128]{3,2,1,0:T(8,128)S(1)}, u32[]{:S(2)}, u32[]{:S(2)}) collective-permute-start(f32[1,2,128,128]{3,2,1,0:T(8,128)S(1)} %momentum.11.refs_2_), channel_id=1, source_target_pairs={{2,0},{4,2},{6,4},{7,6},{5,7},{3,5},{1,3},{0,1},{10,8},{12,10},{14... | collective-permute-start | bytes 393224 | tf_op jit(solution)/shard_map/ppermute | solution.py:365
  40.8 6.4 %collective-permute-start.17 = (f32[1,2,128,128]{3,2,1,0:T(8,128)S(1)}, f32[1,2,128,128]{3,2,1,0:T(8,128)S(1)}, u32[]{:S(2)}, u32[]{:S(2)}) collective-permute-start(f32[1,2,128,128]{3,2,1,0:T(8,128)S(1)} %momentum.8.refs_2_), channel_id=1, source_target_pairs={{0,2},{2,4},{4,6},{6,7},{7,5},{5,3},{3,1},{1,0},{8,10},{10,12},{12... | collective-permute-start | bytes 393224 | tf_op jit(solution)/shard_map/ppermute | solution.py:365
  43.3 10.7 %collective-permute-start.16 = (f32[2,2,128,128]{3,2,1,0:T(8,128)S(1)}, f32[2,2,128,128]{3,2,1,0:T(8,128)S(1)}, u32[]{:S(2)}, u32[]{:S(2)}) collective-permute-start(f32[2,2,128,128]{3,2,1,0:T(8,128)S(1)} %collective-permute-done.12.refs_1_), channel_id=1, source_target_pairs={{0,2},{2,4},{4,6},{6,7},{7,5},{5,3},{3,1},{1,0},{8,10},{10,12},{12... | collective-permute-start | bytes 786440 | tf_op jit(solution)/shard_map/ppermute | solution.py:365
  44.9 9.7 %collective-permute-start.20 = (f32[2,2,128,128]{3,2,1,0:T(8,128)S(1)}, f32[2,2,128,128]{3,2,1,0:T(8,128)S(1)}, u32[]{:S(2)}, u32[]{:S(2)}) collective-permute-start(f32[2,2,128,128]{3,2,1,0:T(8,128)S(1)} %collective-permute-done.19.refs_1_), channel_id=1, source_target_pairs={{2,0},{4,2},{6,4},{7,6},{5,7},{3,5},{1,3},{0,1},{10,8},{12,10},{14... | collective-permute-start | bytes 786440 | tf_op jit(solution)/shard_map/ppermute | solution.py:365
  47.2 6.9 %collective-permute-start.18 = (f32[1,2,128,128]{3,2,1,0:T(8,128)S(1)}, f32[1,2,128,128]{3,2,1,0:T(8,128)S(1)}, u32[]{:S(2)}, u32[]{:S(2)}) collective-permute-start(f32[1,2,128,128]{3,2,1,0:T(8,128)S(1)} %collective-permute-done.17.refs_2_), channel_id=1, source_target_pairs={{0,2},{2,4},{4,6},{6,7},{7,5},{5,3},{3,1},{1,0},{8,10},{10,12},{12... | collective-permute-start | bytes 393224 | tf_op jit(solution)/shard_map/ppermute | solution.py:365
  49.7 5.0 %collective-permute-start.21 = (f32[1,2,128,128]{3,2,1,0:T(8,128)S(1)}, f32[1,2,128,128]{3,2,1,0:T(8,128)S(1)}, u32[]{:S(2)}, u32[]{:S(2)}) collective-permute-start(f32[1,2,128,128]{3,2,1,0:T(8,128)S(1)} %collective-permute-done.15.refs_2_), channel_id=1, source_target_pairs={{2,0},{4,2},{6,4},{7,6},{5,7},{3,5},{1,3},{0,1},{10,8},{12,10},{14... | collective-permute-start | bytes 393224 | tf_op jit(solution)/shard_map/ppermute | solution.py:365
  49.7 0.7 %copy-start = (s32[4]{0:T(128)S(1)}, s32[4]{0:T(128)}, u32[]{:S(2)}) copy-start(s32[4]{0:T(128)} %shift_ref.1) | copy-start | bytes 52
  49.7 0.7 %copy-start.1 = (f32[4]{0:T(128)S(1)}, f32[4]{0:T(128)}, u32[]{:S(2)}) copy-start(f32[4]{0:T(128)} %weight_ref.1) | copy-start | bytes 52

commit v18 on v16

--- a/solution.py
+++ b/solution.py
@@ -318,9 +318,8 @@
             name="inverse",
         )(*inputs)
 
-    half = (layers + 1) // 2
-    early = tuple(range(1, half + 1))
-    late = tuple(range(half + 1, layers)) + (0,)
+    early = (1,)
+    late = tuple(range(2, layers)) + (0,)
     sent = dict(zip(early, inverse(early))) | dict(zip(late, inverse(late)))
     part = jax.ShapeDtypeStruct((per, 2, n, n), F32)
     sent = pl.pallas_call(

time: 55.2 us -> 54.8 us (level)
  transfers between devices with their start and end apart: 22 -> 22, of which waited for: 9 -> 9; matrix products, arithmetic and copies ran while one was open for 0% -> 0% of each run, Pallas kernels for 7% -> 8%
where the time goes in v18:
time: 54.8 us; the launch traced here: 54.7 us
  waiting for transfers between devices  23.7 us (43%)
  starting transfers between devices  19.7 us (36%)
  Pallas kernels  9.79 us (18%)
  between operations  0.84 us (2%)
  local copies, waits for them, and re-layouts  0.64 us (1%)
    ppermute x12, waiting for transfers between devices, hop(): return lax.ppermute(value, ('energy', 'mom'), ways[role])  13.2 us
    ppermute x12, starting transfers between devices, hop(): return lax.ppermute(value, ('energy', 'mom'), ways[role])  10.9 us
    ppermute x6, waiting for transfers between devices, exchange(): return lax.ppermute(slots[i], ('len', 'mom'), pairs)  10.5 us
    ppermute x6, starting transfers between devices, exchange(): return lax.ppermute(slots[i], ('len', 'mom'), pairs)  8.16 us
    pallas_call x2, Pallas kernels, inverse(): pl.pallas_call(functools.partial(inverse_kernel, total, layers, slots), o...  4.51 us
    pallas_call x1, Pallas kernels, shards(): pl.pallas_call(functools.partial(chain_kernel, layers), out_shape=[part]...  2.22 us
    pallas_call x2, Pallas kernels, mix(): pl.pallas_call(functools.partial(mix_kernel, total, items, False, last),...  1.75 us
  transfers between devices with their start and end apart: 22, of which 9 were waited for; matrix products, arithmetic and copies ran while one was open for 0% of the time, Pallas kernels for 8%

profile of v18, /device:TPU:0, one launch (start us, length us, event | category | flops | bytes accessed | tf_op | source)
XLA Modules:
  0.0 54.7 jit_solution(3940071297798440132)
XLA Ops:
  0.6 1.8 %inverse.3 = f32[3,128,128]{2,1,0:T(8,128)S(1)} custom-call(f32[2,128,128]{2,1,0:T(8,128)} %bitcast.7, f32[4,2,128,128]{3,2,1,0:T(8,128)} %bitcast.5, f32[128,128]{1,0:T(8,128)} %bitcast.9, s32[128,128]{1,0:T(8,128)} %pattern_any.3), custom_call_target="tpu_custom_call" | custom-call | flops 201326592 | bytes 131072 | tf_op jit(solution)/shard_map/inverse/pallas_call | solution.py:302
  2.5 4.0 %collective-permute-start = (f32[3,128,128]{2,1,0:T(8,128)S(1)}, f32[3,128,128]{2,1,0:T(8,128)S(1)}, u32[]{:S(2)}, u32[]{:S(2)}) collective-permute-start(f32[3,128,128]{2,1,0:T(8,128)S(1)} %inverse.3), channel_id=1, source_target_pairs={{0,24},{1,25},{8,16},{9,17},{16,8},{17,9},{24,0},{25,1},{2,26},{3,... | collective-permute-start | bytes 589832 | tf_op jit(solution)/shard_map/ppermute | solution.py:295
  6.4 2.7 %inverse.2 = (f32[3,128,128]{2,1,0:T(8,128)S(1)}, f32[3,128,128]{2,1,0:T(8,128)S(1)}, f32[3,128,128]{2,1,0:T(8,128)S(1)}) custom-call(f32[2,128,128]{2,1,0:T(8,128)} %bitcast.8, f32[4,2,128,128]{3,2,1,0:T(8,128)} %bitcast.6, f32[128,128]{1,0:T(8,128)} %bitcast.10, s32[128,128]{1,0:T(8,128)} %pattern_any.3), custom_call_target="tpu_custom_call" | custom-call | flops 603979776 | bytes 393216 | tf_op jit(solution)/shard_map/inverse/pallas_call | solution.py:302
  9.1 0.6 %collective-permute-start.1 = (f32[3,128,128]{2,1,0:T(8,128)S(1)}, f32[3,128,128]{2,1,0:T(8,128)S(1)}, u32[]{:S(2)}, u32[]{:S(2)}) collective-permute-start(f32[3,128,128]{2,1,0:T(8,128)S(1)} %get-tuple-element.23), channel_id=1, source_target_pairs={{0,8},{1,17},{8,0},{9,25},{16,24},{17,1},{24,16},{25,9},{2,10},{3,... | collective-permute-start | bytes 589832 | tf_op jit(solution)/shard_map/ppermute | solution.py:295
  9.7 0.0 collective-permute-start.2
  9.8 1.9 %collective-permute-done.refs_1_ = f32[3,128,128]{2,1,0:T(8,128)S(1)} collective-permute-done((f32[3,128,128]{2,1,0:T(8,128)S(1)}, f32[3,128,128]{2,1,0:T(8,128)S(1)}, u32[]{:S(2)}, u32[]{:S(2)}) %collective-permute-start) | collective-permute-done | bytes 196640 | tf_op jit(solution)/shard_map/ppermute | solution.py:295
  11.7 4.1 %collective-permute-done.1.refs_2_ = f32[3,128,128]{2,1,0:T(8,128)S(1)} collective-permute-done((f32[3,128,128]{2,1,0:T(8,128)S(1)}, f32[3,128,128]{2,1,0:T(8,128)S(1)}, u32[]{:S(2)}, u32[]{:S(2)}) %collective-permute-start.1) | collective-permute-done | bytes 196640 | tf_op jit(solution)/shard_map/ppermute | solution.py:295
  15.8 2.2 %chains.1 = (f32[1,2,128,128]{3,2,1,0:T(8,128)S(1)}, f32[1,2,128,128]{3,2,1,0:T(8,128)S(1)}, f32[1,2,128,128]{3,2,1,0:T(8,128)S(1)}, f32[1,2,128,128]{3,2,1,0:T(8,128)S(1)}) custom-call(f32[3,128,128]{2,1,0:T(8,128)S(1)} %get-tuple-element.22.refs_0_, f32[3,128,128]{2,1,0:T(8,128)S(1)} %collective-permute-done.refs_1_, ...), custom_call_target="tpu_custom_call" | custom-call | tf_op jit(solution)/shard_map/chains/pallas_call | solution.py:325
  18.0 0.1 collective-permute-start.3
  18.1 2.4 %collective-permute-start.4 = (f32[1,2,128,128]{3,2,1,0:T(8,128)S(1)}, f32[1,2,128,128]{3,2,1,0:T(8,128)S(1)}, u32[]{:S(2)}, u32[]{:S(2)}) collective-permute-start(f32[1,2,128,128]{3,2,1,0:T(8,128)S(1)} %get-tuple-element.26), channel_id=1, source_target_pairs={{0,24},{1,25},{8,16},{9,17},{16,8},{17,9},{24,0},{25,1},{2,26},{3,... | collective-permute-start | bytes 393224 | tf_op jit(solution)/shard_map/ppermute | solution.py:295
  20.6 0.6 %collective-permute-start.5 = (f32[1,2,128,128]{3,2,1,0:T(8,128)S(1)}, f32[1,2,128,128]{3,2,1,0:T(8,128)S(1)}, u32[]{:S(2)}, u32[]{:S(2)}) collective-permute-start(f32[1,2,128,128]{3,2,1,0:T(8,128)S(1)} %get-tuple-element.27), channel_id=1, source_target_pairs={{0,8},{1,17},{8,0},{9,25},{16,24},{17,1},{24,16},{25,9},{2,10},{3,... | collective-permute-start | bytes 393224 | tf_op jit(solution)/shard_map/ppermute | solution.py:295
  21.1 0.5 collective-permute-start.6
  21.7 1.6 %collective-permute-start.7 = (f32[1,2,128,128]{3,2,1,0:T(8,128)S(1)}, f32[1,2,128,128]{3,2,1,0:T(8,128)S(1)}, u32[]{:S(2)}, u32[]{:S(2)}) collective-permute-start(f32[1,2,128,128]{3,2,1,0:T(8,128)S(1)} %momentum.6.refs_0_), channel_id=1, source_target_pairs={{0,2},{2,4},{4,6},{6,7},{7,5},{5,3},{3,1},{1,0},{8,10},{10,12},{12... | collective-permute-start | bytes 393224 | tf_op jit(solution)/shard_map/ppermute | solution.py:364
  23.3 0.0 collective-permute-start.13
  23.3 1.9 %collective-permute-done.4.refs_0_ = f32[1,2,128,128]{3,2,1,0:T(8,128)S(1)} collective-permute-done((f32[1,2,128,128]{3,2,1,0:T(8,128)S(1)}, f32[1,2,128,128]{3,2,1,0:T(8,128)S(1)}, u32[]{:S(2)}, u32[]{:S(2)}) %collective-permute-start.4) | collective-permute-done | bytes 131104 | tf_op jit(solution)/shard_map/ppermute | solution.py:295
  25.3 2.5 %collective-permute-done.5.refs_1_ = f32[1,2,128,128]{3,2,1,0:T(8,128)S(1)} collective-permute-done((f32[1,2,128,128]{3,2,1,0:T(8,128)S(1)}, f32[1,2,128,128]{3,2,1,0:T(8,128)S(1)}, u32[]{:S(2)}, u32[]{:S(2)}) %collective-permute-start.5) | collective-permute-done | bytes 131104 | tf_op jit(solution)/shard_map/ppermute | solution.py:295
  27.8 0.5 collective-permute-start.9
  28.3 0.1 collective-permute-start.10
  28.4 1.6 %collective-permute-start.11 = (f32[1,2,128,128]{3,2,1,0:T(8,128)S(1)}, f32[1,2,128,128]{3,2,1,0:T(8,128)S(1)}, u32[]{:S(2)}, u32[]{:S(2)}) collective-permute-start(f32[1,2,128,128]{3,2,1,0:T(8,128)S(1)} %collective-permute-done.7.refs_0_), channel_id=1, source_target_pairs={{0,2},{2,4},{4,6},{6,7},{7,5},{5,3},{3,1},{1,0},{8,10},{10,12},{12... | collective-permute-start | bytes 393224 | tf_op jit(solution)/shard_map/ppermute | solution.py:364
  30.0 2.0 %collective-permute-start.12 = (f32[2,2,128,128]{3,2,1,0:T(8,128)S(1)}, f32[2,2,128,128]{3,2,1,0:T(8,128)S(1)}, u32[]{:S(2)}, u32[]{:S(2)}) collective-permute-start(f32[2,2,128,128]{3,2,1,0:T(8,128)S(1)} %momentum.7.refs_1_), channel_id=1, source_target_pairs={{0,2},{2,4},{4,6},{6,7},{7,5},{5,3},{3,1},{1,0},{8,10},{10,12},{12... | collective-permute-start | bytes 786440 | tf_op jit(solution)/shard_map/ppermute | solution.py:364
  32.2 1.6 %collective-permute-done.11.refs_0_ = f32[1,2,128,128]{3,2,1,0:T(8,128)S(1)} collective-permute-done((f32[1,2,128,128]{3,2,1,0:T(8,128)S(1)}, f32[1,2,128,128]{3,2,1,0:T(8,128)S(1)}, u32[]{:S(2)}, u32[]{:S(2)}) %collective-permute-start.11) | collective-permute-done | bytes 131104 | tf_op jit(solution)/shard_map/ppermute | solution.py:364
  33.8 2.5 %collective-permute-done.14.refs_0_ = f32[1,2,128,128]{3,2,1,0:T(8,128)S(1)} collective-permute-done((f32[1,2,128,128]{3,2,1,0:T(8,128)S(1)}, f32[1,2,128,128]{3,2,1,0:T(8,128)S(1)}, u32[]{:S(2)}, u32[]{:S(2)}) %collective-permute-start.14) | collective-permute-done | bytes 131104 | tf_op jit(solution)/shard_map/ppermute | solution.py:364
  36.3 2.0 %collective-permute-start.17 = (f32[1,2,128,128]{3,2,1,0:T(8,128)S(1)}, f32[1,2,128,128]{3,2,1,0:T(8,128)S(1)}, u32[]{:S(2)}, u32[]{:S(2)}) collective-permute-start(f32[1,2,128,128]{3,2,1,0:T(8,128)S(1)} %momentum.8.refs_2_), channel_id=1, source_target_pairs={{0,2},{2,4},{4,6},{6,7},{7,5},{5,3},{3,1},{1,0},{8,10},{10,12},{12... | collective-permute-start | bytes 393224 | tf_op jit(solution)/shard_map/ppermute | solution.py:364
  38.3 4.4 %collective-permute-done.15.refs_2_ = f32[1,2,128,128]{3,2,1,0:T(8,128)S(1)} collective-permute-done((f32[1,2,128,128]{3,2,1,0:T(8,128)S(1)}, f32[1,2,128,128]{3,2,1,0:T(8,128)S(1)}, u32[]{:S(2)}, u32[]{:S(2)}) %collective-permute-start.15) | collective-permute-done | bytes 131104 | tf_op jit(solution)/shard_map/ppermute | solution.py:364
  42.8 1.6 %collective-permute-start.16 = (f32[2,2,128,128]{3,2,1,0:T(8,128)S(1)}, f32[2,2,128,128]{3,2,1,0:T(8,128)S(1)}, u32[]{:S(2)}, u32[]{:S(2)}) collective-permute-start(f32[2,2,128,128]{3,2,1,0:T(8,128)S(1)} %collective-permute-done.12.refs_1_), channel_id=1, source_target_pairs={{0,2},{2,4},{4,6},{6,7},{7,5},{5,3},{3,1},{1,0},{8,10},{10,12},{12... | collective-permute-start | bytes 786440 | tf_op jit(solution)/shard_map/ppermute | solution.py:364
  44.4 2.0 %collective-permute-start.18 = (f32[1,2,128,128]{3,2,1,0:T(8,128)S(1)}, f32[1,2,128,128]{3,2,1,0:T(8,128)S(1)}, u32[]{:S(2)}, u32[]{:S(2)}) collective-permute-start(f32[1,2,128,128]{3,2,1,0:T(8,128)S(1)} %collective-permute-done.17.refs_2_), channel_id=1, source_target_pairs={{0,2},{2,4},{4,6},{6,7},{7,5},{5,3},{3,1},{1,0},{8,10},{10,12},{12... | collective-permute-start | bytes 393224 | tf_op jit(solution)/shard_map/ppermute | solution.py:364
  46.5 0.6 %copy-done = s32[4]{0:T(128)S(1)} copy-done((s32[4]{0:T(128)S(1)}, s32[4]{0:T(128)}, u32[]{:S(2)}) %copy-start) | copy-done | bytes 40
  47.1 0.9 %local.1 = (f32[4,2,128,128]{3,2,1,0:T(8,128)S(1)}, f32[4,2,128,128]{3,2,1,0:T(8,128)S(1)}, f32[16,128]{1,0:T(8,128)S(1)}) custom-call(s32[4]{0:T(128)S(1)} %copy-done, f32[4]{0:T(128)S(1)} %copy-done.1, f32[4,2,128,128]{3,2,1,0:T(8,128)S(1)} %by_energy.6.zero_ref, f32[4,2,128,128]{3,2,1,0:T(8,128)S(1)} %by_energy.7.one_ref), custom_call_target="tpu_custom_call" | custom-call | tf_op jit(solution)/shard_map/local/pallas_call | solution.py:384
  48.2 0.6 %mix.2 = (f32[4,2,128,128]{3,2,1,0:T(8,128)S(1)}, f32[4,2,128,128]{3,2,1,0:T(8,128)S(1)}) custom-call(f32[16,128]{1,0:T(8,128)S(1)} %get-tuple-element.32.table_ref, f32[4,2,128,128]{3,2,1,0:T(8,128)S(1)} %by_energy.10.refs_0_, f32[4,2,128,128]{3,2,1,0:T(8,128)S(1)} %by_energy.11.refs_1_, f32[4,2,128,128]{3,2,1,0:T(8,128)S(1)} %get-tuple-element.36.refs_2_, ...), custom_call_target="tpu_custom_call" | custom-call | tf_op jit(solution)/shard_map/mix/pallas_call | solution.py:395
  48.8 3.9 %collective-permute-done.18.refs_2_ = f32[1,2,128,128]{3,2,1,0:T(8,128)S(1)} collective-permute-done((f32[1,2,128,128]{3,2,1,0:T(8,128)S(1)}, f32[1,2,128,128]{3,2,1,0:T(8,128)S(1)}, u32[]{:S(2)}, u32[]{:S(2)}) %collective-permute-start.18) | collective-permute-done | bytes 131104 | tf_op jit(solution)/shard_map/ppermute | solution.py:364
  52.8 0.7 %collective-permute-done.21.refs_2_ = f32[1,2,128,128]{3,2,1,0:T(8,128)S(1)} collective-permute-done((f32[1,2,128,128]{3,2,1,0:T(8,128)S(1)}, f32[1,2,128,128]{3,2,1,0:T(8,128)S(1)}, u32[]{:S(2)}, u32[]{:S(2)}) %collective-permute-start.21) | collective-permute-done | bytes 131104 | tf_op jit(solution)/shard_map/ppermute | solution.py:364
  53.5 1.2 %mix.3 = (f32[4,2,128,128]{3,2,1,0:T(8,128)}, f32[4,2,128,128]{3,2,1,0:T(8,128)}) custom-call(f32[16,128]{1,0:T(8,128)S(1)} %get-tuple-element.32.table_ref, f32[4,2,128,128]{3,2,1,0:T(8,128)S(1)} %by_energy.8.refs_0_, f32[4,2,128,128]{3,2,1,0:T(8,128)S(1)} %by_energy.9.refs_1_, f32[4,2,128,128]{3,2,1,0:T(8,128)S(1)} %get-tuple-element.37.refs_2_, ...), custom_call_target="tpu_custom_call" | custom-call | tf_op jit(solution)/shard_map/mix/pallas_call | solution.py:395
  (35 shorter events, 0.5 us)
Async XLA Ops:
  2.5 9.2 %collective-permute-start = (f32[3,128,128]{2,1,0:T(8,128)S(1)}, f32[3,128,128]{2,1,0:T(8,128)S(1)}, u32[]{:S(2)}, u32[]{:S(2)}) collective-permute-start(f32[3,128,128]{2,1,0:T(8,128)S(1)} %inverse.3), channel_id=1, source_target_pairs={{0,24},{1,25},{8,16},{9,17},{16,8},{17,9},{24,0},{25,1},{2,26},{3,... | collective-permute-start | bytes 589832 | tf_op jit(solution)/shard_map/ppermute | solution.py:295
  9.1 6.7 %collective-permute-start.1 = (f32[3,128,128]{2,1,0:T(8,128)S(1)}, f32[3,128,128]{2,1,0:T(8,128)S(1)}, u32[]{:S(2)}, u32[]{:S(2)}) collective-permute-start(f32[3,128,128]{2,1,0:T(8,128)S(1)} %get-tuple-element.23), channel_id=1, source_target_pairs={{0,8},{1,17},{8,0},{9,25},{16,24},{17,1},{24,16},{25,9},{2,10},{3,... | collective-permute-start | bytes 589832 | tf_op jit(solution)/shard_map/ppermute | solution.py:295
  9.7 6.1 %collective-permute-start.2 = (f32[3,128,128]{2,1,0:T(8,128)S(1)}, f32[3,128,128]{2,1,0:T(8,128)S(1)}, u32[]{:S(2)}, u32[]{:S(2)}) collective-permute-start(f32[3,128,128]{2,1,0:T(8,128)S(1)} %get-tuple-element.24), channel_id=1, source_target_pairs={{0,16},{1,9},{8,24},{9,1},{16,0},{17,25},{24,8},{25,17},{2,18},{3,... | collective-permute-start | bytes 589832 | tf_op jit(solution)/shard_map/ppermute | solution.py:295
  18.0 3.6 %collective-permute-start.3 = (f32[1,2,128,128]{3,2,1,0:T(8,128)S(1)}, f32[1,2,128,128]{3,2,1,0:T(8,128)S(1)}, u32[]{:S(2)}, u32[]{:S(2)}) collective-permute-start(f32[1,2,128,128]{3,2,1,0:T(8,128)S(1)} %get-tuple-element.25.refs_0_), channel_id=1, source_target_pairs={{0,1},{1,0},{2,3},{3,2},{4,5},{5,4},{6,7},{7,6},{8,9},{9,8},{10,11... | collective-permute-start | bytes 393224 | tf_op jit(solution)/shard_map/ppermute | solution.py:374
  18.1 7.2 %collective-permute-start.4 = (f32[1,2,128,128]{3,2,1,0:T(8,128)S(1)}, f32[1,2,128,128]{3,2,1,0:T(8,128)S(1)}, u32[]{:S(2)}, u32[]{:S(2)}) collective-permute-start(f32[1,2,128,128]{3,2,1,0:T(8,128)S(1)} %get-tuple-element.26), channel_id=1, source_target_pairs={{0,24},{1,25},{8,16},{9,17},{16,8},{17,9},{24,0},{25,1},{2,26},{3,... | collective-permute-start | bytes 393224 | tf_op jit(solution)/shard_map/ppermute | solution.py:295
  20.6 7.2 %collective-permute-start.5 = (f32[1,2,128,128]{3,2,1,0:T(8,128)S(1)}, f32[1,2,128,128]{3,2,1,0:T(8,128)S(1)}, u32[]{:S(2)}, u32[]{:S(2)}) collective-permute-start(f32[1,2,128,128]{3,2,1,0:T(8,128)S(1)} %get-tuple-element.27), channel_id=1, source_target_pairs={{0,8},{1,17},{8,0},{9,25},{16,24},{17,1},{24,16},{25,9},{2,10},{3,... | collective-permute-start | bytes 393224 | tf_op jit(solution)/shard_map/ppermute | solution.py:295
  21.1 6.7 %collective-permute-start.6 = (f32[1,2,128,128]{3,2,1,0:T(8,128)S(1)}, f32[1,2,128,128]{3,2,1,0:T(8,128)S(1)}, u32[]{:S(2)}, u32[]{:S(2)}) collective-permute-start(f32[1,2,128,128]{3,2,1,0:T(8,128)S(1)} %get-tuple-element.28), channel_id=1, source_target_pairs={{0,16},{1,9},{8,24},{9,1},{16,0},{17,25},{24,8},{25,17},{2,18},{3,... | collective-permute-start | bytes 393224 | tf_op jit(solution)/shard_map/ppermute | solution.py:295
  21.7 6.1 %collective-permute-start.7 = (f32[1,2,128,128]{3,2,1,0:T(8,128)S(1)}, f32[1,2,128,128]{3,2,1,0:T(8,128)S(1)}, u32[]{:S(2)}, u32[]{:S(2)}) collective-permute-start(f32[1,2,128,128]{3,2,1,0:T(8,128)S(1)} %momentum.6.refs_0_), channel_id=1, source_target_pairs={{0,2},{2,4},{4,6},{6,7},{7,5},{5,3},{3,1},{1,0},{8,10},{10,12},{12... | collective-permute-start | bytes 393224 | tf_op jit(solution)/shard_map/ppermute | solution.py:364
  23.3 6.7 %collective-permute-start.13 = (f32[1,2,128,128]{3,2,1,0:T(8,128)S(1)}, f32[1,2,128,128]{3,2,1,0:T(8,128)S(1)}, u32[]{:S(2)}, u32[]{:S(2)}) collective-permute-start(f32[1,2,128,128]{3,2,1,0:T(8,128)S(1)} %momentum.9.refs_0_), channel_id=1, source_target_pairs={{2,0},{4,2},{6,4},{7,6},{5,7},{3,5},{1,3},{0,1},{10,8},{12,10},{14... | collective-permute-start | bytes 393224 | tf_op jit(solution)/shard_map/ppermute | solution.py:364
  27.8 2.2 %collective-permute-start.8 = (f32[1,2,128,128]{3,2,1,0:T(8,128)S(1)}, f32[1,2,128,128]{3,2,1,0:T(8,128)S(1)}, u32[]{:S(2)}, u32[]{:S(2)}) collective-permute-start(f32[1,2,128,128]{3,2,1,0:T(8,128)S(1)} %collective-permute-done.4.refs_0_), channel_id=1, source_target_pairs={{0,1},{1,0},{2,3},{3,2},{4,5},{5,4},{6,7},{7,6},{8,9},{9,8},{10,11... | collective-permute-start | bytes 393224 | tf_op jit(solution)/shard_map/ppermute | solution.py:374
  27.8 2.2 %collective-permute-start.9 = (f32[1,2,128,128]{3,2,1,0:T(8,128)S(1)}, f32[1,2,128,128]{3,2,1,0:T(8,128)S(1)}, u32[]{:S(2)}, u32[]{:S(2)}) collective-permute-start(f32[1,2,128,128]{3,2,1,0:T(8,128)S(1)} %collective-permute-done.5.refs_1_), channel_id=1, source_target_pairs={{0,1},{1,0},{2,3},{3,2},{4,5},{5,4},{6,7},{7,6},{8,9},{9,8},{10,11... | collective-permute-start | bytes 393224 | tf_op jit(solution)/shard_map/ppermute | solution.py:374
  28.3 3.8 %collective-permute-start.10 = (f32[1,2,128,128]{3,2,1,0:T(8,128)S(1)}, f32[1,2,128,128]{3,2,1,0:T(8,128)S(1)}, u32[]{:S(2)}, u32[]{:S(2)}) collective-permute-start(f32[1,2,128,128]{3,2,1,0:T(8,128)S(1)} %collective-permute-done.6.refs_0_), channel_id=1, source_target_pairs={{0,1},{1,0},{2,3},{3,2},{4,5},{5,4},{6,7},{7,6},{8,9},{9,8},{10,11... | collective-permute-start | bytes 393224 | tf_op jit(solution)/shard_map/ppermute | solution.py:374
  28.4 5.4 %collective-permute-start.11 = (f32[1,2,128,128]{3,2,1,0:T(8,128)S(1)}, f32[1,2,128,128]{3,2,1,0:T(8,128)S(1)}, u32[]{:S(2)}, u32[]{:S(2)}) collective-permute-start(f32[1,2,128,128]{3,2,1,0:T(8,128)S(1)} %collective-permute-done.7.refs_0_), channel_id=1, source_target_pairs={{0,2},{2,4},{4,6},{6,7},{7,5},{5,3},{3,1},{1,0},{8,10},{10,12},{12... | collective-permute-start | bytes 393224 | tf_op jit(solution)/shard_map/ppermute | solution.py:364
  30.0 6.3 %collective-permute-start.14 = (f32[1,2,128,128]{3,2,1,0:T(8,128)S(1)}, f32[1,2,128,128]{3,2,1,0:T(8,128)S(1)}, u32[]{:S(2)}, u32[]{:S(2)}) collective-permute-start(f32[1,2,128,128]{3,2,1,0:T(8,128)S(1)} %collective-permute-done.13.refs_0_), channel_id=1, source_target_pairs={{2,0},{4,2},{6,4},{7,6},{5,7},{3,5},{1,3},{0,1},{10,8},{12,10},{14... | collective-permute-start | bytes 393224 | tf_op jit(solution)/shard_map/ppermute | solution.py:364
  30.0 12.7 %collective-permute-start.12 = (f32[2,2,128,128]{3,2,1,0:T(8,128)S(1)}, f32[2,2,128,128]{3,2,1,0:T(8,128)S(1)}, u32[]{:S(2)}, u32[]{:S(2)}) collective-permute-start(f32[2,2,128,128]{3,2,1,0:T(8,128)S(1)} %momentum.7.refs_1_), channel_id=1, source_target_pairs={{0,2},{2,4},{4,6},{6,7},{7,5},{5,3},{3,1},{1,0},{8,10},{10,12},{12... | collective-permute-start | bytes 786440 | tf_op jit(solution)/shard_map/ppermute | solution.py:364
  32.1 12.3 %collective-permute-start.19 = (f32[2,2,128,128]{3,2,1,0:T(8,128)S(1)}, f32[2,2,128,128]{3,2,1,0:T(8,128)S(1)}, u32[]{:S(2)}, u32[]{:S(2)}) collective-permute-start(f32[2,2,128,128]{3,2,1,0:T(8,128)S(1)} %momentum.10.refs_1_), channel_id=1, source_target_pairs={{2,0},{4,2},{6,4},{7,6},{5,7},{3,5},{1,3},{0,1},{10,8},{12,10},{14... | collective-permute-start | bytes 786440 | tf_op jit(solution)/shard_map/ppermute | solution.py:364
  36.3 6.5 %collective-permute-start.15 = (f32[1,2,128,128]{3,2,1,0:T(8,128)S(1)}, f32[1,2,128,128]{3,2,1,0:T(8,128)S(1)}, u32[]{:S(2)}, u32[]{:S(2)}) collective-permute-start(f32[1,2,128,128]{3,2,1,0:T(8,128)S(1)} %momentum.11.refs_2_), channel_id=1, source_target_pairs={{2,0},{4,2},{6,4},{7,6},{5,7},{3,5},{1,3},{0,1},{10,8},{12,10},{14... | collective-permute-start | bytes 393224 | tf_op jit(solution)/shard_map/ppermute | solution.py:364
  36.3 8.1 %collective-permute-start.17 = (f32[1,2,128,128]{3,2,1,0:T(8,128)S(1)}, f32[1,2,128,128]{3,2,1,0:T(8,128)S(1)}, u32[]{:S(2)}, u32[]{:S(2)}) collective-permute-start(f32[1,2,128,128]{3,2,1,0:T(8,128)S(1)} %momentum.8.refs_2_), channel_id=1, source_target_pairs={{0,2},{2,4},{4,6},{6,7},{7,5},{5,3},{3,1},{1,0},{8,10},{10,12},{12... | collective-permute-start | bytes 393224 | tf_op jit(solution)/shard_map/ppermute | solution.py:364
  42.8 10.0 %collective-permute-start.16 = (f32[2,2,128,128]{3,2,1,0:T(8,128)S(1)}, f32[2,2,128,128]{3,2,1,0:T(8,128)S(1)}, u32[]{:S(2)}, u32[]{:S(2)}) collective-permute-start(f32[2,2,128,128]{3,2,1,0:T(8,128)S(1)} %collective-permute-done.12.refs_1_), channel_id=1, source_target_pairs={{0,2},{2,4},{4,6},{6,7},{7,5},{5,3},{3,1},{1,0},{8,10},{10,12},{12... | collective-permute-start | bytes 786440 | tf_op jit(solution)/shard_map/ppermute | solution.py:364
  44.4 9.1 %collective-permute-start.20 = (f32[2,2,128,128]{3,2,1,0:T(8,128)S(1)}, f32[2,2,128,128]{3,2,1,0:T(8,128)S(1)}, u32[]{:S(2)}, u32[]{:S(2)}) collective-permute-start(f32[2,2,128,128]{3,2,1,0:T(8,128)S(1)} %collective-permute-done.19.refs_1_), channel_id=1, source_target_pairs={{2,0},{4,2},{6,4},{7,6},{5,7},{3,5},{1,3},{0,1},{10,8},{12,10},{14... | collective-permute-start | bytes 786440 | tf_op jit(solution)/shard_map/ppermute | solution.py:364
  44.4 8.4 %collective-permute-start.18 = (f32[1,2,128,128]{3,2,1,0:T(8,128)S(1)}, f32[1,2,128,128]{3,2,1,0:T(8,128)S(1)}, u32[]{:S(2)}, u32[]{:S(2)}) collective-permute-start(f32[1,2,128,128]{3,2,1,0:T(8,128)S(1)} %collective-permute-done.17.refs_2_), channel_id=1, source_target_pairs={{0,2},{2,4},{4,6},{6,7},{7,5},{5,3},{3,1},{1,0},{8,10},{10,12},{12... | collective-permute-start | bytes 393224 | tf_op jit(solution)/shard_map/ppermute | solution.py:364
  46.4 7.1 %collective-permute-start.21 = (f32[1,2,128,128]{3,2,1,0:T(8,128)S(1)}, f32[1,2,128,128]{3,2,1,0:T(8,128)S(1)}, u32[]{:S(2)}, u32[]{:S(2)}) collective-permute-start(f32[1,2,128,128]{3,2,1,0:T(8,128)S(1)} %collective-permute-done.15.refs_2_), channel_id=1, source_target_pairs={{2,0},{4,2},{6,4},{7,6},{5,7},{3,5},{1,3},{0,1},{10,8},{12,10},{14... | collective-permute-start | bytes 393224 | tf_op jit(solution)/shard_map/ppermute | solution.py:364
  46.4 0.7 %copy-start = (s32[4]{0:T(128)S(1)}, s32[4]{0:T(128)}, u32[]{:S(2)}) copy-start(s32[4]{0:T(128)} %shift_ref.1) | copy-start | bytes 52
  46.4 0.7 %copy-start.1 = (f32[4]{0:T(128)S(1)}, f32[4]{0:T(128)}, u32[]{:S(2)}) copy-start(f32[4]{0:T(128)} %weight_ref.1) | copy-start | bytes 52

commit v19 on v18

--- a/solution.py
+++ b/solution.py
@@ -319,8 +319,8 @@
         )(*inputs)
 
     early = (1,)
-    late = tuple(range(2, layers)) + (0,)
-    sent = dict(zip(early, inverse(early))) | dict(zip(late, inverse(late)))
+    late = tuple(range(2, layers))
+    sent = {i: v for c in (early, late, (0,)) for i, v in zip(c, inverse(c))}
     part = jax.ShapeDtypeStruct((per, 2, n, n), F32)
     sent = pl.pallas_call(
         functools.partial(chain_kernel, layers),

time: 54.8 us -> 54.8 us (level)
  waiting for transfers between devices: 23.7 us -> 22.2 us
  Pallas kernels: 9.79 us -> 11.2 us
    ppermute x6, waiting for transfers between devices: 10.5 us -> 9.06 us  [exchange(): return lax.ppermute(slots[i], ('len', 'mom'), pairs)]
    pallas_call x2 -> x3, Pallas kernels: 4.51 us -> 5.91 us  [inverse(): pl.pallas_call(functools.partial(inverse_kernel, total, layers, slots), o...]
  transfers between devices with their start and end apart: 22 -> 22, of which waited for: 9 -> 9; matrix products, arithmetic and copies ran while one was open for 0% -> 0% of each run, Pallas kernels for 8% -> 11%
where the time goes in v19:
time: 54.8 us; the launch traced here: 54.6 us
  waiting for transfers between devices  22.2 us (41%)
  starting transfers between devices  19.7 us (36%)
  Pallas kernels  11.2 us (20%)
  between operations  0.85 us (2%)
  local copies, waits for them, and re-layouts  0.64 us (1%)
    ppermute x12, waiting for transfers between devices, hop(): return lax.ppermute(value, ('energy', 'mom'), ways[role])  13.2 us
    ppermute x12, starting transfers between devices, hop(): return lax.ppermute(value, ('energy', 'mom'), ways[role])  10.9 us
    ppermute x6, waiting for transfers between devices, exchange(): return lax.ppermute(slots[i], ('len', 'mom'), pairs)  9.06 us
    ppermute x6, starting transfers between devices, exchange(): return lax.ppermute(slots[i], ('len', 'mom'), pairs)  8.18 us
    pallas_call x3, Pallas kernels, inverse(): pl.pallas_call(functools.partial(inverse_kernel, total, layers, slots), o...  5.91 us
    pallas_call x1, Pallas kernels, shards(): pl.pallas_call(functools.partial(chain_kernel, layers), out_shape=[part]...  2.22 us
    pallas_call x2, Pallas kernels, mix(): pl.pallas_call(functools.partial(mix_kernel, total, items, False, last),...  1.75 us
  transfers between devices with their start and end apart: 22, of which 9 were waited for; matrix products, arithmetic and copies ran while one was open for 0% of the time, Pallas kernels for 11%

profile of v19, /device:TPU:0, one launch (start us, length us, event | category | flops | bytes accessed | tf_op | source)
XLA Modules:
  0.0 54.6 jit_solution(12312048963507854085)
XLA Ops:
  0.6 1.8 %inverse.4 = f32[3,128,128]{2,1,0:T(8,128)S(1)} custom-call(f32[2,128,128]{2,1,0:T(8,128)} %bitcast.8, f32[4,2,128,128]{3,2,1,0:T(8,128)} %bitcast.5, f32[128,128]{1,0:T(8,128)} %bitcast.11, s32[128,128]{1,0:T(8,128)} %pattern_any.5), custom_call_target="tpu_custom_call" | custom-call | flops 201326592 | bytes 131072 | tf_op jit(solution)/shard_map/inverse/pallas_call | solution.py:302
  2.5 4.0 %collective-permute-start = (f32[3,128,128]{2,1,0:T(8,128)S(1)}, f32[3,128,128]{2,1,0:T(8,128)S(1)}, u32[]{:S(2)}, u32[]{:S(2)}) collective-permute-start(f32[3,128,128]{2,1,0:T(8,128)S(1)} %inverse.4), channel_id=1, source_target_pairs={{0,24},{1,25},{8,16},{9,17},{16,8},{17,9},{24,0},{25,1},{2,26},{3,... | collective-permute-start | bytes 589832 | tf_op jit(solution)/shard_map/ppermute | solution.py:295
  6.4 2.2 %inverse.5 = (f32[3,128,128]{2,1,0:T(8,128)S(1)}, f32[3,128,128]{2,1,0:T(8,128)S(1)}) custom-call(f32[2,128,128]{2,1,0:T(8,128)} %bitcast.9, f32[4,2,128,128]{3,2,1,0:T(8,128)} %bitcast.6, f32[128,128]{1,0:T(8,128)} %bitcast.12, s32[128,128]{1,0:T(8,128)} %pattern_any.5), custom_call_target="tpu_custom_call" | custom-call | flops 402653184 | bytes 262144 | tf_op jit(solution)/shard_map/inverse/pallas_call | solution.py:302
  8.7 0.6 %collective-permute-start.1 = (f32[3,128,128]{2,1,0:T(8,128)S(1)}, f32[3,128,128]{2,1,0:T(8,128)S(1)}, u32[]{:S(2)}, u32[]{:S(2)}) collective-permute-start(f32[3,128,128]{2,1,0:T(8,128)S(1)} %get-tuple-element.21), channel_id=1, source_target_pairs={{0,8},{1,17},{8,0},{9,25},{16,24},{17,1},{24,16},{25,9},{2,10},{3,... | collective-permute-start | bytes 589832 | tf_op jit(solution)/shard_map/ppermute | solution.py:295
  9.3 0.1 collective-permute-start.2
  9.4 1.8 %inverse.3.refs_0_ = f32[3,128,128]{2,1,0:T(8,128)S(1)} custom-call(f32[2,128,128]{2,1,0:T(8,128)} %bitcast.10, f32[4,2,128,128]{3,2,1,0:T(8,128)} %bitcast.7, f32[128,128]{1,0:T(8,128)} %bitcast.13, s32[128,128]{1,0:T(8,128)} %pattern_any.5), custom_call_target="tpu_custom_call" | custom-call | flops 201326592 | bytes 131072 | tf_op jit(solution)/shard_map/inverse/pallas_call | solution.py:302
  11.2 0.6 %collective-permute-done.refs_1_ = f32[3,128,128]{2,1,0:T(8,128)S(1)} collective-permute-done((f32[3,128,128]{2,1,0:T(8,128)S(1)}, f32[3,128,128]{2,1,0:T(8,128)S(1)}, u32[]{:S(2)}, u32[]{:S(2)}) %collective-permute-start) | collective-permute-done | bytes 196640 | tf_op jit(solution)/shard_map/ppermute | solution.py:295
  11.8 4.0 %collective-permute-done.1.refs_2_ = f32[3,128,128]{2,1,0:T(8,128)S(1)} collective-permute-done((f32[3,128,128]{2,1,0:T(8,128)S(1)}, f32[3,128,128]{2,1,0:T(8,128)S(1)}, u32[]{:S(2)}, u32[]{:S(2)}) %collective-permute-start.1) | collective-permute-done | bytes 196640 | tf_op jit(solution)/shard_map/ppermute | solution.py:295
  15.8 2.2 %chains.1 = (f32[1,2,128,128]{3,2,1,0:T(8,128)S(1)}, f32[1,2,128,128]{3,2,1,0:T(8,128)S(1)}, f32[1,2,128,128]{3,2,1,0:T(8,128)S(1)}, f32[1,2,128,128]{3,2,1,0:T(8,128)S(1)}) custom-call(f32[3,128,128]{2,1,0:T(8,128)S(1)} %inverse.3.refs_0_, f32[3,128,128]{2,1,0:T(8,128)S(1)} %collective-permute-done.refs_1_, ...), custom_call_target="tpu_custom_call" | custom-call | tf_op jit(solution)/shard_map/chains/pallas_call | solution.py:325
  18.0 0.1 collective-permute-start.3
  18.1 2.4 %collective-permute-start.4 = (f32[1,2,128,128]{3,2,1,0:T(8,128)S(1)}, f32[1,2,128,128]{3,2,1,0:T(8,128)S(1)}, u32[]{:S(2)}, u32[]{:S(2)}) collective-permute-start(f32[1,2,128,128]{3,2,1,0:T(8,128)S(1)} %get-tuple-element.24), channel_id=1, source_target_pairs={{0,24},{1,25},{8,16},{9,17},{16,8},{17,9},{24,0},{25,1},{2,26},{3,... | collective-permute-start | bytes 393224 | tf_op jit(solution)/shard_map/ppermute | solution.py:295
  20.6 0.5 collective-permute-start.5
  21.1 0.6 %collective-permute-start.6 = (f32[1,2,128,128]{3,2,1,0:T(8,128)S(1)}, f32[1,2,128,128]{3,2,1,0:T(8,128)S(1)}, u32[]{:S(2)}, u32[]{:S(2)}) collective-permute-start(f32[1,2,128,128]{3,2,1,0:T(8,128)S(1)} %get-tuple-element.26), channel_id=1, source_target_pairs={{0,16},{1,9},{8,24},{9,1},{16,0},{17,25},{24,8},{25,17},{2,18},{3,... | collective-permute-start | bytes 393224 | tf_op jit(solution)/shard_map/ppermute | solution.py:295
  21.7 1.6 %collective-permute-start.7 = (f32[1,2,128,128]{3,2,1,0:T(8,128)S(1)}, f32[1,2,128,128]{3,2,1,0:T(8,128)S(1)}, u32[]{:S(2)}, u32[]{:S(2)}) collective-permute-start(f32[1,2,128,128]{3,2,1,0:T(8,128)S(1)} %momentum.6.refs_0_), channel_id=1, source_target_pairs={{0,2},{2,4},{4,6},{6,7},{7,5},{5,3},{3,1},{1,0},{8,10},{10,12},{12... | collective-permute-start | bytes 393224 | tf_op jit(solution)/shard_map/ppermute | solution.py:364
  23.3 1.9 %collective-permute-done.4.refs_0_ = f32[1,2,128,128]{3,2,1,0:T(8,128)S(1)} collective-permute-done((f32[1,2,128,128]{3,2,1,0:T(8,128)S(1)}, f32[1,2,128,128]{3,2,1,0:T(8,128)S(1)}, u32[]{:S(2)}, u32[]{:S(2)}) %collective-permute-start.4) | collective-permute-done | bytes 131104 | tf_op jit(solution)/shard_map/ppermute | solution.py:295
  25.3 2.5 %collective-permute-done.5.refs_1_ = f32[1,2,128,128]{3,2,1,0:T(8,128)S(1)} collective-permute-done((f32[1,2,128,128]{3,2,1,0:T(8,128)S(1)}, f32[1,2,128,128]{3,2,1,0:T(8,128)S(1)}, u32[]{:S(2)}, u32[]{:S(2)}) %collective-permute-start.5) | collective-permute-done | bytes 131104 | tf_op jit(solution)/shard_map/ppermute | solution.py:295
  27.8 0.5 collective-permute-start.9
  28.3 0.1 collective-permute-start.10
  28.4 1.6 %collective-permute-start.11 = (f32[1,2,128,128]{3,2,1,0:T(8,128)S(1)}, f32[1,2,128,128]{3,2,1,0:T(8,128)S(1)}, u32[]{:S(2)}, u32[]{:S(2)}) collective-permute-start(f32[1,2,128,128]{3,2,1,0:T(8,128)S(1)} %collective-permute-done.7.refs_0_), channel_id=1, source_target_pairs={{0,2},{2,4},{4,6},{6,7},{7,5},{5,3},{3,1},{1,0},{8,10},{10,12},{12... | collective-permute-start | bytes 393224 | tf_op jit(solution)/shard_map/ppermute | solution.py:364
  30.0 2.0 %collective-permute-start.12 = (f32[2,2,128,128]{3,2,1,0:T(8,128)S(1)}, f32[2,2,128,128]{3,2,1,0:T(8,128)S(1)}, u32[]{:S(2)}, u32[]{:S(2)}) collective-permute-start(f32[2,2,128,128]{3,2,1,0:T(8,128)S(1)} %momentum.7.refs_1_), channel_id=1, source_target_pairs={{0,2},{2,4},{4,6},{6,7},{7,5},{5,3},{3,1},{1,0},{8,10},{10,12},{12... | collective-permute-start | bytes 786440 | tf_op jit(solution)/shard_map/ppermute | solution.py:364
  32.2 1.6 %collective-permute-done.11.refs_0_ = f32[1,2,128,128]{3,2,1,0:T(8,128)S(1)} collective-permute-done((f32[1,2,128,128]{3,2,1,0:T(8,128)S(1)}, f32[1,2,128,128]{3,2,1,0:T(8,128)S(1)}, u32[]{:S(2)}, u32[]{:S(2)}) %collective-permute-start.11) | collective-permute-done | bytes 131104 | tf_op jit(solution)/shard_map/ppermute | solution.py:364
  33.7 2.5 %collective-permute-done.14.refs_0_ = f32[1,2,128,128]{3,2,1,0:T(8,128)S(1)} collective-permute-done((f32[1,2,128,128]{3,2,1,0:T(8,128)S(1)}, f32[1,2,128,128]{3,2,1,0:T(8,128)S(1)}, u32[]{:S(2)}, u32[]{:S(2)}) %collective-permute-start.14) | collective-permute-done | bytes 131104 | tf_op jit(solution)/shard_map/ppermute | solution.py:364
  36.3 2.0 %collective-permute-start.17 = (f32[1,2,128,128]{3,2,1,0:T(8,128)S(1)}, f32[1,2,128,128]{3,2,1,0:T(8,128)S(1)}, u32[]{:S(2)}, u32[]{:S(2)}) collective-permute-start(f32[1,2,128,128]{3,2,1,0:T(8,128)S(1)} %momentum.8.refs_2_), channel_id=1, source_target_pairs={{0,2},{2,4},{4,6},{6,7},{7,5},{5,3},{3,1},{1,0},{8,10},{10,12},{12... | collective-permute-start | bytes 393224 | tf_op jit(solution)/shard_map/ppermute | solution.py:364
  38.3 4.4 %collective-permute-done.15.refs_2_ = f32[1,2,128,128]{3,2,1,0:T(8,128)S(1)} collective-permute-done((f32[1,2,128,128]{3,2,1,0:T(8,128)S(1)}, f32[1,2,128,128]{3,2,1,0:T(8,128)S(1)}, u32[]{:S(2)}, u32[]{:S(2)}) %collective-permute-start.15) | collective-permute-done | bytes 131104 | tf_op jit(solution)/shard_map/ppermute | solution.py:364
  42.7 1.6 %collective-permute-start.16 = (f32[2,2,128,128]{3,2,1,0:T(8,128)S(1)}, f32[2,2,128,128]{3,2,1,0:T(8,128)S(1)}, u32[]{:S(2)}, u32[]{:S(2)}) collective-permute-start(f32[2,2,128,128]{3,2,1,0:T(8,128)S(1)} %collective-permute-done.12.refs_1_), channel_id=1, source_target_pairs={{0,2},{2,4},{4,6},{6,7},{7,5},{5,3},{3,1},{1,0},{8,10},{10,12},{12... | collective-permute-start | bytes 786440 | tf_op jit(solution)/shard_map/ppermute | solution.py:364
  44.3 2.0 %collective-permute-start.18 = (f32[1,2,128,128]{3,2,1,0:T(8,128)S(1)}, f32[1,2,128,128]{3,2,1,0:T(8,128)S(1)}, u32[]{:S(2)}, u32[]{:S(2)}) collective-permute-start(f32[1,2,128,128]{3,2,1,0:T(8,128)S(1)} %collective-permute-done.17.refs_2_), channel_id=1, source_target_pairs={{0,2},{2,4},{4,6},{6,7},{7,5},{5,3},{3,1},{1,0},{8,10},{10,12},{12... | collective-permute-start | bytes 393224 | tf_op jit(solution)/shard_map/ppermute | solution.py:364
  46.5 0.6 %copy-done = s32[4]{0:T(128)S(1)} copy-done((s32[4]{0:T(128)S(1)}, s32[4]{0:T(128)}, u32[]{:S(2)}) %copy-start) | copy-done | bytes 40
  47.1 0.9 %local.1 = (f32[4,2,128,128]{3,2,1,0:T(8,128)S(1)}, f32[4,2,128,128]{3,2,1,0:T(8,128)S(1)}, f32[16,128]{1,0:T(8,128)S(1)}) custom-call(s32[4]{0:T(128)S(1)} %copy-done, f32[4]{0:T(128)S(1)} %copy-done.1, f32[4,2,128,128]{3,2,1,0:T(8,128)S(1)} %by_energy.6.zero_ref, f32[4,2,128,128]{3,2,1,0:T(8,128)S(1)} %by_energy.7.one_ref), custom_call_target="tpu_custom_call" | custom-call | tf_op jit(solution)/shard_map/local/pallas_call | solution.py:384
  48.2 0.6 %mix.2 = (f32[4,2,128,128]{3,2,1,0:T(8,128)S(1)}, f32[4,2,128,128]{3,2,1,0:T(8,128)S(1)}) custom-call(f32[16,128]{1,0:T(8,128)S(1)} %get-tuple-element.30.table_ref, f32[4,2,128,128]{3,2,1,0:T(8,128)S(1)} %by_energy.10.refs_0_, f32[4,2,128,128]{3,2,1,0:T(8,128)S(1)} %by_energy.11.refs_1_, f32[4,2,128,128]{3,2,1,0:T(8,128)S(1)} %get-tuple-element.34.refs_2_, ...), custom_call_target="tpu_custom_call" | custom-call | tf_op jit(solution)/shard_map/mix/pallas_call | solution.py:395
  48.8 3.9 %collective-permute-done.18.refs_2_ = f32[1,2,128,128]{3,2,1,0:T(8,128)S(1)} collective-permute-done((f32[1,2,128,128]{3,2,1,0:T(8,128)S(1)}, f32[1,2,128,128]{3,2,1,0:T(8,128)S(1)}, u32[]{:S(2)}, u32[]{:S(2)}) %collective-permute-start.18) | collective-permute-done | bytes 131104 | tf_op jit(solution)/shard_map/ppermute | solution.py:364
  52.7 0.7 %collective-permute-done.21.refs_2_ = f32[1,2,128,128]{3,2,1,0:T(8,128)S(1)} collective-permute-done((f32[1,2,128,128]{3,2,1,0:T(8,128)S(1)}, f32[1,2,128,128]{3,2,1,0:T(8,128)S(1)}, u32[]{:S(2)}, u32[]{:S(2)}) %collective-permute-start.21) | collective-permute-done | bytes 131104 | tf_op jit(solution)/shard_map/ppermute | solution.py:364
  53.5 1.2 %mix.3 = (f32[4,2,128,128]{3,2,1,0:T(8,128)}, f32[4,2,128,128]{3,2,1,0:T(8,128)}) custom-call(f32[16,128]{1,0:T(8,128)S(1)} %get-tuple-element.30.table_ref, f32[4,2,128,128]{3,2,1,0:T(8,128)S(1)} %by_energy.8.refs_0_, f32[4,2,128,128]{3,2,1,0:T(8,128)S(1)} %by_energy.9.refs_1_, f32[4,2,128,128]{3,2,1,0:T(8,128)S(1)} %get-tuple-element.35.refs_2_, ...), custom_call_target="tpu_custom_call" | custom-call | tf_op jit(solution)/shard_map/mix/pallas_call | solution.py:395
  (36 shorter events, 0.5 us)
Async XLA Ops:
  2.5 9.3 %collective-permute-start = (f32[3,128,128]{2,1,0:T(8,128)S(1)}, f32[3,128,128]{2,1,0:T(8,128)S(1)}, u32[]{:S(2)}, u32[]{:S(2)}) collective-permute-start(f32[3,128,128]{2,1,0:T(8,128)S(1)} %inverse.4), channel_id=1, source_target_pairs={{0,24},{1,25},{8,16},{9,17},{16,8},{17,9},{24,0},{25,1},{2,26},{3,... | collective-permute-start | bytes 589832 | tf_op jit(solution)/shard_map/ppermute | solution.py:295
  8.7 7.1 %collective-permute-start.1 = (f32[3,128,128]{2,1,0:T(8,128)S(1)}, f32[3,128,128]{2,1,0:T(8,128)S(1)}, u32[]{:S(2)}, u32[]{:S(2)}) collective-permute-start(f32[3,128,128]{2,1,0:T(8,128)S(1)} %get-tuple-element.21), channel_id=1, source_target_pairs={{0,8},{1,17},{8,0},{9,25},{16,24},{17,1},{24,16},{25,9},{2,10},{3,... | collective-permute-start | bytes 589832 | tf_op jit(solution)/shard_map/ppermute | solution.py:295
  9.3 6.5 %collective-permute-start.2 = (f32[3,128,128]{2,1,0:T(8,128)S(1)}, f32[3,128,128]{2,1,0:T(8,128)S(1)}, u32[]{:S(2)}, u32[]{:S(2)}) collective-permute-start(f32[3,128,128]{2,1,0:T(8,128)S(1)} %get-tuple-element.22), channel_id=1, source_target_pairs={{0,16},{1,9},{8,24},{9,1},{16,0},{17,25},{24,8},{25,17},{2,18},{3,... | collective-permute-start | bytes 589832 | tf_op jit(solution)/shard_map/ppermute | solution.py:295
  18.0 3.6 %collective-permute-start.3 = (f32[1,2,128,128]{3,2,1,0:T(8,128)S(1)}, f32[1,2,128,128]{3,2,1,0:T(8,128)S(1)}, u32[]{:S(2)}, u32[]{:S(2)}) collective-permute-start(f32[1,2,128,128]{3,2,1,0:T(8,128)S(1)} %get-tuple-element.23.refs_0_), channel_id=1, source_target_pairs={{0,1},{1,0},{2,3},{3,2},{4,5},{5,4},{6,7},{7,6},{8,9},{9,8},{10,11... | collective-permute-start | bytes 393224 | tf_op jit(solution)/shard_map/ppermute | solution.py:374
  18.1 7.2 %collective-permute-start.4 = (f32[1,2,128,128]{3,2,1,0:T(8,128)S(1)}, f32[1,2,128,128]{3,2,1,0:T(8,128)S(1)}, u32[]{:S(2)}, u32[]{:S(2)}) collective-permute-start(f32[1,2,128,128]{3,2,1,0:T(8,128)S(1)} %get-tuple-element.24), channel_id=1, source_target_pairs={{0,24},{1,25},{8,16},{9,17},{16,8},{17,9},{24,0},{25,1},{2,26},{3,... | collective-permute-start | bytes 393224 | tf_op jit(solution)/shard_map/ppermute | solution.py:295
  20.6 7.2 %collective-permute-start.5 = (f32[1,2,128,128]{3,2,1,0:T(8,128)S(1)}, f32[1,2,128,128]{3,2,1,0:T(8,128)S(1)}, u32[]{:S(2)}, u32[]{:S(2)}) collective-permute-start(f32[1,2,128,128]{3,2,1,0:T(8,128)S(1)} %get-tuple-element.25), channel_id=1, source_target_pairs={{0,8},{1,17},{8,0},{9,25},{16,24},{17,1},{24,16},{25,9},{2,10},{3,... | collective-permute-start | bytes 393224 | tf_op jit(solution)/shard_map/ppermute | solution.py:295
  21.1 6.7 %collective-permute-start.6 = (f32[1,2,128,128]{3,2,1,0:T(8,128)S(1)}, f32[1,2,128,128]{3,2,1,0:T(8,128)S(1)}, u32[]{:S(2)}, u32[]{:S(2)}) collective-permute-start(f32[1,2,128,128]{3,2,1,0:T(8,128)S(1)} %get-tuple-element.26), channel_id=1, source_target_pairs={{0,16},{1,9},{8,24},{9,1},{16,0},{17,25},{24,8},{25,17},{2,18},{3,... | collective-permute-start | bytes 393224 | tf_op jit(solution)/shard_map/ppermute | solution.py:295
  21.7 6.1 %collective-permute-start.7 = (f32[1,2,128,128]{3,2,1,0:T(8,128)S(1)}, f32[1,2,128,128]{3,2,1,0:T(8,128)S(1)}, u32[]{:S(2)}, u32[]{:S(2)}) collective-permute-start(f32[1,2,128,128]{3,2,1,0:T(8,128)S(1)} %momentum.6.refs_0_), channel_id=1, source_target_pairs={{0,2},{2,4},{4,6},{6,7},{7,5},{5,3},{3,1},{1,0},{8,10},{10,12},{12... | collective-permute-start | bytes 393224 | tf_op jit(solution)/shard_map/ppermute | solution.py:364
  23.3 6.6 %collective-permute-start.13 = (f32[1,2,128,128]{3,2,1,0:T(8,128)S(1)}, f32[1,2,128,128]{3,2,1,0:T(8,128)S(1)}, u32[]{:S(2)}, u32[]{:S(2)}) collective-permute-start(f32[1,2,128,128]{3,2,1,0:T(8,128)S(1)} %momentum.9.refs_0_), channel_id=1, source_target_pairs={{2,0},{4,2},{6,4},{7,6},{5,7},{3,5},{1,3},{0,1},{10,8},{12,10},{14... | collective-permute-start | bytes 393224 | tf_op jit(solution)/shard_map/ppermute | solution.py:364
  27.8 2.2 %collective-permute-start.8 = (f32[1,2,128,128]{3,2,1,0:T(8,128)S(1)}, f32[1,2,128,128]{3,2,1,0:T(8,128)S(1)}, u32[]{:S(2)}, u32[]{:S(2)}) collective-permute-start(f32[1,2,128,128]{3,2,1,0:T(8,128)S(1)} %collective-permute-done.4.refs_0_), channel_id=1, source_target_pairs={{0,1},{1,0},{2,3},{3,2},{4,5},{5,4},{6,7},{7,6},{8,9},{9,8},{10,11... | collective-permute-start | bytes 393224 | tf_op jit(solution)/shard_map/ppermute | solution.py:374
  27.8 2.2 %collective-permute-start.9 = (f32[1,2,128,128]{3,2,1,0:T(8,128)S(1)}, f32[1,2,128,128]{3,2,1,0:T(8,128)S(1)}, u32[]{:S(2)}, u32[]{:S(2)}) collective-permute-start(f32[1,2,128,128]{3,2,1,0:T(8,128)S(1)} %collective-permute-done.5.refs_1_), channel_id=1, source_target_pairs={{0,1},{1,0},{2,3},{3,2},{4,5},{5,4},{6,7},{7,6},{8,9},{9,8},{10,11... | collective-permute-start | bytes 393224 | tf_op jit(solution)/shard_map/ppermute | solution.py:374
  28.3 3.8 %collective-permute-start.10 = (f32[1,2,128,128]{3,2,1,0:T(8,128)S(1)}, f32[1,2,128,128]{3,2,1,0:T(8,128)S(1)}, u32[]{:S(2)}, u32[]{:S(2)}) collective-permute-start(f32[1,2,128,128]{3,2,1,0:T(8,128)S(1)} %collective-permute-done.6.refs_0_), channel_id=1, source_target_pairs={{0,1},{1,0},{2,3},{3,2},{4,5},{5,4},{6,7},{7,6},{8,9},{9,8},{10,11... | collective-permute-start | bytes 393224 | tf_op jit(solution)/shard_map/ppermute | solution.py:374
  28.4 5.4 %collective-permute-start.11 = (f32[1,2,128,128]{3,2,1,0:T(8,128)S(1)}, f32[1,2,128,128]{3,2,1,0:T(8,128)S(1)}, u32[]{:S(2)}, u32[]{:S(2)}) collective-permute-start(f32[1,2,128,128]{3,2,1,0:T(8,128)S(1)} %collective-permute-done.7.refs_0_), channel_id=1, source_target_pairs={{0,2},{2,4},{4,6},{6,7},{7,5},{5,3},{3,1},{1,0},{8,10},{10,12},{12... | collective-permute-start | bytes 393224 | tf_op jit(solution)/shard_map/ppermute | solution.py:364
  29.9 6.3 %collective-permute-start.14 = (f32[1,2,128,128]{3,2,1,0:T(8,128)S(1)}, f32[1,2,128,128]{3,2,1,0:T(8,128)S(1)}, u32[]{:S(2)}, u32[]{:S(2)}) collective-permute-start(f32[1,2,128,128]{3,2,1,0:T(8,128)S(1)} %collective-permute-done.13.refs_0_), channel_id=1, source_target_pairs={{2,0},{4,2},{6,4},{7,6},{5,7},{3,5},{1,3},{0,1},{10,8},{12,10},{14... | collective-permute-start | bytes 393224 | tf_op jit(solution)/shard_map/ppermute | solution.py:364
  30.0 12.7 %collective-permute-start.12 = (f32[2,2,128,128]{3,2,1,0:T(8,128)S(1)}, f32[2,2,128,128]{3,2,1,0:T(8,128)S(1)}, u32[]{:S(2)}, u32[]{:S(2)}) collective-permute-start(f32[2,2,128,128]{3,2,1,0:T(8,128)S(1)} %momentum.7.refs_1_), channel_id=1, source_target_pairs={{0,2},{2,4},{4,6},{6,7},{7,5},{5,3},{3,1},{1,0},{8,10},{10,12},{12... | collective-permute-start | bytes 786440 | tf_op jit(solution)/shard_map/ppermute | solution.py:364
  32.1 12.3 %collective-permute-start.19 = (f32[2,2,128,128]{3,2,1,0:T(8,128)S(1)}, f32[2,2,128,128]{3,2,1,0:T(8,128)S(1)}, u32[]{:S(2)}, u32[]{:S(2)}) collective-permute-start(f32[2,2,128,128]{3,2,1,0:T(8,128)S(1)} %momentum.10.refs_1_), channel_id=1, source_target_pairs={{2,0},{4,2},{6,4},{7,6},{5,7},{3,5},{1,3},{0,1},{10,8},{12,10},{14... | collective-permute-start | bytes 786440 | tf_op jit(solution)/shard_map/ppermute | solution.py:364
  36.3 6.5 %collective-permute-start.15 = (f32[1,2,128,128]{3,2,1,0:T(8,128)S(1)}, f32[1,2,128,128]{3,2,1,0:T(8,128)S(1)}, u32[]{:S(2)}, u32[]{:S(2)}) collective-permute-start(f32[1,2,128,128]{3,2,1,0:T(8,128)S(1)} %momentum.11.refs_2_), channel_id=1, source_target_pairs={{2,0},{4,2},{6,4},{7,6},{5,7},{3,5},{1,3},{0,1},{10,8},{12,10},{14... | collective-permute-start | bytes 393224 | tf_op jit(solution)/shard_map/ppermute | solution.py:364
  36.3 8.1 %collective-permute-start.17 = (f32[1,2,128,128]{3,2,1,0:T(8,128)S(1)}, f32[1,2,128,128]{3,2,1,0:T(8,128)S(1)}, u32[]{:S(2)}, u32[]{:S(2)}) collective-permute-start(f32[1,2,128,128]{3,2,1,0:T(8,128)S(1)} %momentum.8.refs_2_), channel_id=1, source_target_pairs={{0,2},{2,4},{4,6},{6,7},{7,5},{5,3},{3,1},{1,0},{8,10},{10,12},{12... | collective-permute-start | bytes 393224 | tf_op jit(solution)/shard_map/ppermute | solution.py:364
  42.7 10.0 %collective-permute-start.16 = (f32[2,2,128,128]{3,2,1,0:T(8,128)S(1)}, f32[2,2,128,128]{3,2,1,0:T(8,128)S(1)}, u32[]{:S(2)}, u32[]{:S(2)}) collective-permute-start(f32[2,2,128,128]{3,2,1,0:T(8,128)S(1)} %collective-permute-done.12.refs_1_), channel_id=1, source_target_pairs={{0,2},{2,4},{4,6},{6,7},{7,5},{5,3},{3,1},{1,0},{8,10},{10,12},{12... | collective-permute-start | bytes 786440 | tf_op jit(solution)/shard_map/ppermute | solution.py:364
  44.3 9.1 %collective-permute-start.20 = (f32[2,2,128,128]{3,2,1,0:T(8,128)S(1)}, f32[2,2,128,128]{3,2,1,0:T(8,128)S(1)}, u32[]{:S(2)}, u32[]{:S(2)}) collective-permute-start(f32[2,2,128,128]{3,2,1,0:T(8,128)S(1)} %collective-permute-done.19.refs_1_), channel_id=1, source_target_pairs={{2,0},{4,2},{6,4},{7,6},{5,7},{3,5},{1,3},{0,1},{10,8},{12,10},{14... | collective-permute-start | bytes 786440 | tf_op jit(solution)/shard_map/ppermute | solution.py:364
  44.3 8.4 %collective-permute-start.18 = (f32[1,2,128,128]{3,2,1,0:T(8,128)S(1)}, f32[1,2,128,128]{3,2,1,0:T(8,128)S(1)}, u32[]{:S(2)}, u32[]{:S(2)}) collective-permute-start(f32[1,2,128,128]{3,2,1,0:T(8,128)S(1)} %collective-permute-done.17.refs_2_), channel_id=1, source_target_pairs={{0,2},{2,4},{4,6},{6,7},{7,5},{5,3},{3,1},{1,0},{8,10},{10,12},{12... | collective-permute-start | bytes 393224 | tf_op jit(solution)/shard_map/ppermute | solution.py:364
  46.4 7.1 %collective-permute-start.21 = (f32[1,2,128,128]{3,2,1,0:T(8,128)S(1)}, f32[1,2,128,128]{3,2,1,0:T(8,128)S(1)}, u32[]{:S(2)}, u32[]{:S(2)}) collective-permute-start(f32[1,2,128,128]{3,2,1,0:T(8,128)S(1)} %collective-permute-done.15.refs_2_), channel_id=1, source_target_pairs={{2,0},{4,2},{6,4},{7,6},{5,7},{3,5},{1,3},{0,1},{10,8},{12,10},{14... | collective-permute-start | bytes 393224 | tf_op jit(solution)/shard_map/ppermute | solution.py:364
  46.4 0.7 %copy-start = (s32[4]{0:T(128)S(1)}, s32[4]{0:T(128)}, u32[]{:S(2)}) copy-start(s32[4]{0:T(128)} %shift_ref.1) | copy-start | bytes 52
  46.4 0.7 %copy-start.1 = (f32[4]{0:T(128)S(1)}, f32[4]{0:T(128)}, u32[]{:S(2)}) copy-start(f32[4]{0:T(128)} %weight_ref.1) | copy-start | bytes 52
